TPU v7x, 512 devices: a whole 4x4x16 slice. The times are simulated.
512 devices in a mesh: dp: 128 (over z, x, core), tensor: 4 (over y).
Axes of the slice: x: 4, y: 4, z: 16, core: 2. Of those that a mesh axis runs over, the one named last changes fastest.
Arguments:
- tokens: bfloat16 [32768, 1536], P('dp'), may hold values from -6 to 6
- targets: bfloat16 [32768, 1536], P('dp'), may hold values from -6 to 6
- modulation: bfloat16 [256, 3, 1536], P('dp'), may hold values from -2.5 to 2.5
- live_block_count: int32 [128], P('dp'), may hold values from 2 to 4, as said below
- preferred_blocks: int32 [128], P('dp'), may hold values from 1 to 3, as said below
- last_block_rows: int32 [128, 2], P('dp'), may hold values from 1 to 64
- up_projection_weight: bfloat16 [1536, 6144], P('dp', 'tensor'), may hold values from -0.15625 to 0.15625
- down_weight_transposed: bfloat16 [1536, 6144], P('dp', 'tensor'), may hold values from -0.078125 to 0.078125
- adapter_input_factor: bfloat16 [1536, 64], replicated, may hold values from -0.15625 to 0.15625
- adapter_output_factor: bfloat16 [64, 6144], P(None, 'tensor'), may hold values from -0.75 to 0.75
Outputs:
- losses: float32 [128], P('dp')
- grad_tokens: bfloat16 [32768, 1536], P('dp')
- grad_lora_a: float32 [1536, 64], replicated
- grad_lora_b: float32 [64, 6144], P(None, 'tensor')
Inputs may be any that keep to these rules, and one draw needn't show every extreme that they name: `live_block_count`: device i of dp and device (i + 64) modulo 128 together hold 6 live blocks; some pair holds 4. `preferred_blocks`: at most live_block_count - 1 for each pair, so the loser has a block too.
All inputs are finite; a program needn't handle non-finite values.
Results may differ from a plain program's by a relative error of at most 0.035.
Values may be sent and summed in bfloat16 or wider, within the bound.
No kernel may reach another device: no remote copies, remote signals or barrier semaphores. Data moves between devices by JAX's collectives and lax.ppermute only.
A program may use at most 64 MiB of HBM per device.

v0:
```python
import jax
import jax.numpy as jnp
from jax import lax
from jax.sharding import PartitionSpec as P

BLK = 64
CAP = 4


EPS = 1e-06
BETA = 20.0
LOSS_SCALE = 4096.0


def settle_gradients(value):
    return lax.optimization_barrier(value.astype(jnp.bfloat16)).astype(jnp.float32)


def layer_norm(image_blocks):
    wide = image_blocks.astype(jnp.float32)
    center = wide - jnp.mean(wide, axis=-1, keepdims=True)
    inverse_deviation = lax.rsqrt(jnp.mean(center * center, axis=-1, keepdims=True) + EPS)
    return (center * inverse_deviation, inverse_deviation)


def gelu_and_slope(pre):

    def act(value):
        return jax.nn.gelu(value, approximate=True)

    value, back = jax.vjp(act, pre)
    return (value, back(jnp.ones_like(pre))[0])


def contract_trailing(left, right):
    return lax.dot_general(
        left, right, (((1,), (1,)), ((), ())), preferred_element_type=jnp.float32
    )


def contract_first(left, right):
    return lax.dot_general(
        left, right, (((0,), (0,)), ((), ())), preferred_element_type=jnp.float32
    )


def per_device(
    tokens,
    targets,
    modulation,
    live_block_count,
    preferred_blocks,
    last_block_rows,
    up_projection_weight,
    down_weight_transposed,
    adapter_input_factor,
    adapter_output_factor,
):
    width = tokens.shape[1]
    n_dp = lax.axis_size("dp")
    here = lax.axis_index("dp")
    count = live_block_count[0]
    wins = preferred_blocks[0]
    slots = jnp.arange(CAP, dtype=jnp.int32)
    flags = (slots >= wins).astype(jnp.int32)
    last = jnp.where(flags == 0, wins - 1, count - 1)
    tail = jnp.where(flags == 0, last_block_rows[0, 0], last_block_rows[0, 1])
    live = jnp.where(slots < count, jnp.where(slots == last, tail, BLK), 0)
    masks = (jnp.arange(BLK, dtype=jnp.int32)[None, :] < live[:, None]).astype(jnp.float32)
    own_counts = jnp.stack(
        [jnp.sum(jnp.where(flags == 0, live, 0)), jnp.sum(jnp.where(flags == 1, live, 0))]
    ).astype(jnp.float32)
    blocks_x = tokens.reshape(CAP, BLK, width)
    blocks_t = targets.reshape(CAP, BLK, width)
    blocks_mod = jnp.where(flags[:, None, None] == 0, modulation[0][None], modulation[1][None])
    homes = jnp.full((CAP,), here, jnp.int32)
    work_x, work_t, work_mod = (blocks_x, blocks_t, blocks_mod)
    work_mask, work_flag, work_home = (masks, flags, homes)
    spots = work_x.shape[0]
    count_rows = spots * BLK
    samples = 2 * n_dp
    ids = work_home * 2 + work_flag
    picks = (ids[:, None] == jnp.arange(samples, dtype=jnp.int32)[None, :]).astype(jnp.float32)
    modulation_vectors = work_mod.astype(jnp.float32)
    shift = modulation_vectors[:, None, 0]
    modulation_scale = 1.0 + modulation_vectors[:, None, 1]
    output_gate = modulation_vectors[:, None, 2]
    normalized_input, inverse_deviation = layer_norm(work_x)
    modulated_input = (
        (normalized_input * modulation_scale + shift)
        .astype(jnp.bfloat16)
        .reshape(count_rows, width)
    )
    w_up, w_down = (
        lax.all_gather(up_projection_weight, "dp", axis=0, tiled=True),
        lax.all_gather(down_weight_transposed, "dp", axis=0, tiled=True),
    )
    low_rank_hidden = jnp.dot(
        modulated_input, adapter_input_factor, preferred_element_type=jnp.float32
    ).astype(jnp.bfloat16)
    reference_preactivation = jnp.dot(modulated_input, w_up, preferred_element_type=jnp.float32)
    policy_preactivation = reference_preactivation + jnp.dot(
        low_rank_hidden, adapter_output_factor, preferred_element_type=jnp.float32
    )
    act_pol, policy_activation_slope = gelu_and_slope(policy_preactivation)
    hid_pol = act_pol.astype(jnp.bfloat16)
    hid_ref = jax.nn.gelu(reference_preactivation, approximate=True).astype(jnp.bfloat16)
    part_pol = settle_gradients(contract_trailing(hid_pol, w_down))
    part_ref = settle_gradients(contract_trailing(hid_ref, w_down))
    sum_pol, sum_ref = (
        lax.psum(part_pol.astype(jnp.bfloat16), "tensor").astype(jnp.float32),
        lax.psum(part_ref.astype(jnp.bfloat16), "tensor").astype(jnp.float32),
    )
    x_part = work_x.astype(jnp.float32)
    t_part = work_t.astype(jnp.float32)
    wmask = work_mask[:, :, None]
    miss_pol = x_part + output_gate * sum_pol.reshape(spots, BLK, width) - t_part
    miss_ref = x_part + output_gate * sum_ref.reshape(spots, BLK, width) - t_part
    vec_pol = jnp.sum(jnp.sum(wmask * miss_pol * miss_pol, axis=(1, 2))[:, None] * picks, axis=0)
    vec_ref = jnp.sum(jnp.sum(wmask * miss_ref * miss_ref, axis=(1, 2))[:, None] * picks, axis=0)
    owned = (jnp.arange(samples, dtype=jnp.int32) // 2 == here).astype(jnp.float32) * jnp.tile(
        own_counts, n_dp
    )
    tot_pol, tot_ref, tot_rows = lax.psum((vec_pol, vec_ref, owned), "dp")
    scale_rows = 1.0 / (width * tot_rows)
    pair_gap = ((tot_pol - tot_ref) * scale_rows).reshape(n_dp, 2)
    inside = -BETA * (pair_gap[:, 0] - pair_gap[:, 1])
    losses = lax.dynamic_slice_in_dim(jax.nn.softplus(-inside), here, 1)
    weight = BETA * LOSS_SCALE * jax.nn.sigmoid(-inside)
    coef = jnp.stack([weight, -weight], axis=1).reshape(samples) * scale_rows
    slot_coef = jnp.sum(picks * coef[None, :], axis=1)
    out_grad = slot_coef[:, None, None] * 2.0 * wmask * miss_pol
    dy_part = (output_gate * out_grad).astype(jnp.bfloat16).reshape(count_rows, width)
    dh = jnp.dot(dy_part, w_down, preferred_element_type=jnp.float32)
    preactivation_gradient = (dh * policy_activation_slope).astype(jnp.bfloat16)
    grad_b = contract_first(low_rank_hidden, preactivation_gradient)
    low_rank_gradient_piece = settle_gradients(
        contract_trailing(preactivation_gradient, adapter_output_factor)
    )
    dm_part = settle_gradients(contract_trailing(preactivation_gradient, w_up))
    modulation_gradient_sum, dlow_sum = (
        lax.psum(dm_part.astype(jnp.bfloat16), "tensor").astype(jnp.float32),
        lax.psum(low_rank_gradient_piece.astype(jnp.bfloat16), "tensor").astype(jnp.float32),
    )
    low_rank_gradient = dlow_sum.astype(jnp.bfloat16)
    modulation_gradient = modulation_gradient_sum + contract_trailing(
        low_rank_gradient, adapter_input_factor
    )
    dn = modulation_gradient.reshape(spots, BLK, width) * modulation_scale
    first_sum = jnp.sum(dn, axis=-1, keepdims=True)
    second_sum = jnp.sum(dn * normalized_input, axis=-1, keepdims=True)
    back_part = inverse_deviation * (dn - first_sum / width - normalized_input * second_sum / width)
    grad_part = (out_grad + back_part).astype(jnp.bfloat16)
    grad_a = contract_first(modulated_input, low_rank_gradient)
    sum_a, sum_b = lax.psum((grad_a, grad_b), "dp")
    return (losses, grad_part.reshape(CAP * BLK, width), sum_a / n_dp, sum_b / n_dp)


def solution(mesh):
    return jax.shard_map(
        per_device,
        mesh=mesh,
        in_specs=(
            P("dp", None),
            P("dp", None),
            P("dp", None, None),
            P("dp"),
            P("dp"),
            P("dp", None),
            P("dp", "tensor"),
            P("dp", "tensor"),
            P(),
            P(None, "tensor"),
        ),
        out_specs=(P("dp"), P("dp", None), P(), P(None, "tensor")),
        check_vma=False,
    )
```

profile of v0, /device:TPU:1, one launch (start us, length us, event | category | flops | bytes accessed | tf_op | source)
XLA Modules:
  0.0 1070.1 jit_solution(11939229913842427295)
XLA Ops:
  9.4 1.3 convert_reduce_fusion
  10.7 1.5 fusion.12
  13.8 147.7 %all-gather.5.cloned.1.call-done = bf16[128,12,1536]{2,1,0:T(8,128)(2,1)} async-done(((bf16[1,12,1536]{2,1,0:T(8,128)(2,1)}), bf16[128,12,1536]{2,1,0:T(8,128)(2,1)}) %all-gather.5.cloned.1.call-update) | async-done | bytes 4718608 | tf_op jit(solution)/shard_map/all_gather | solution.py:95
  161.5 8.2 reshape.200
  169.6 4.9 fusion.65
  174.5 129.5 %all-gather.7.cloned.1.call-done = bf16[128,12,1536]{2,1,0:T(8,128)(2,1)} async-done(((bf16[1,12,1536]{2,1,0:T(8,128)(2,1)}), bf16[128,12,1536]{2,1,0:T(8,128)(2,1)}) %all-gather.7.cloned.1.call-update) | async-done | bytes 4718608 | tf_op jit(solution)/shard_map/all_gather | solution.py:96
  304.0 8.2 reshape.202
  312.2 5.3 convolution_convert_fusion.1
  317.9 1.1 copy-done.6
  319.1 2.4 convolution_convert_fusion.2
  322.8 2.5 select_reduce_fusion.3
  325.9 1.3 add_convert_fusion
  327.9 54.0 %all-reduce.11.cloned.1.call-done = (bf16[256,1536]{1,0:T(8,128)(2,1)}, bf16[256,1536]{1,0:T(8,128)(2,1)}) async-done(((bf16[256,1536]{1,0:T(8,128)(2,1)}, bf16[256,1536]{1,0:T(8,128)(2,1)}), (bf16[256,1536]{1,0:T(8,128)(2,1)}, bf16[256,1536]{1,0:T(8,128)(2,1)})) %all-reduce.11.cloned.1.call-update) | async-done | bytes 1572880 | tf_op jit(solution)/shard_map/psum | solution.py:112
  381.9 3.3 fusion.28
  388.1 248.9 %all-reduce = (f32[256]{0:T(256)}, f32[256]{0:T(256)}, f32[256]{0:T(256)}) all-reduce(f32[256]{0:T(256)S(1)} %get-tuple-element.11, f32[256]{0:T(256)S(1)} %get-tuple-element.10, f32[256]{0:T(256)} %compare_select_fusion.2), channel_id=1, replica_groups=mesh['dp'=128,'tensor'=4] {'dp'}, use_global_device_ids=true, to_apply=%region_6.7 | all-reduce | flops 768 | bytes 6144 | tf_op jit(solution)/shard_map/psum | solution.py:124
  638.5 1.6 fusion.62
  640.1 0.9 copy.22
  641.0 0.9 copy.23
  642.7 1.0 reshape.197
  646.0 1.3 fusion.31
  647.4 4.3 fusion.1
  651.7 1.0 convolution_convert_fusion.3
  652.6 1.0 fusion.66
  653.6 12.9 %psum.69 = bf16[256,64]{0,1:T(8,128)(2,1)S(1)} all-reduce(bf16[256,64]{0,1:T(8,128)(2,1)} %convolution_convert_fusion.3), channel_id=1, replica_groups=mesh['dp'=128,'tensor'=4] {'tensor'}, use_global_device_ids=true, to_apply=%region_17.18 | all-reduce | flops 16384 | bytes 65536 | tf_op jit(solution)/shard_map/psum | solution.py:143
  666.6 1.0 fusion.67
  667.8 4.9 convolution_convert_fusion
  673.4 328.5 %all-reduce.9.cloned.1.call-done = (f32[1536,64]{0,1:T(8,128)}, f32[64,1536]{1,0:T(8,128)}) async-done(((f32[1536,64]{0,1:T(8,128)}, f32[64,1536]{1,0:T(8,128)}), (f32[1536,64]{0,1:T(8,128)}, f32[64,1536]{1,0:T(8,128)})) %all-reduce.9.cloned.1.call-update) | async-done | bytes 786448 | tf_op jit(solution)/shard_map/psum | solution.py:155
  1001.9 1.8 broadcast_multiply_fusion.1
  1003.7 1.8 broadcast_multiply_fusion
  1005.4 54.4 %all-reduce.7.cloned.1.call-done = bf16[256,1536]{1,0:T(8,128)(2,1)} async-done(((bf16[256,1536]{1,0:T(8,128)(2,1)}), bf16[256,1536]{1,0:T(8,128)(2,1)}) %all-reduce.7.cloned.1.call-update) | async-done | bytes 786448 | tf_op jit(solution)/shard_map/psum | solution.py:142
  1060.0 1.0 copy-done.10
  1061.7 1.9 fusion.11
  (90 shorter events, 14.5 us)
Async XLA Ops:
  7.2 6.2 copy-start
  7.2 5.8 copy-start.1
  7.2 5.0 copy-start.16
  7.2 154.3 %all-gather.5.cloned.1.call-start = ((), (), s32[]{:S(2)}) async-start(), calls=%async_computation.1 | async-start | bytes 6340608 | tf_op jit(solution)/shard_map/all_gather | solution.py:95
  7.9 296.0 %all-gather.7.cloned.1.call-start = ((), (), s32[]{:S(2)}) async-start(), calls=%async_computation.2 | async-start | bytes 6340608 | tf_op jit(solution)/shard_map/all_gather | solution.py:96
  8.7 373.3 %all-reduce.11.cloned.1.call-start = ((), (), s32[]{:S(2)}) async-start(), calls=%async_computation.4 | async-start | bytes 3145728 | tf_op jit(solution)/shard_map/psum | solution.py:112
  13.0 156.7 %copy-start.14 = (f32[4,1536]{1,0:T(4,128)}, f32[4,1536]{1,0:T(4,128)S(1)}, u32[]{:S(2)}) copy-start(f32[4,1536]{1,0:T(4,128)S(1)} %get-tuple-element.24) | copy-start | bytes 73732
  13.7 303.8 %copy-start.12 = (bf16[256,64]{0,1:T(8,128)(2,1)}, bf16[256,64]{0,1:T(8,128)(2,1)S(1)}, u32[]{:S(2)}) copy-start(bf16[256,64]{0,1:T(8,128)(2,1)S(1)} %convolution_convert_fusion.4) | copy-start | bytes 98308
  312.2 5.3 copy-start.8
  312.2 5.3 copy-start.9
  312.2 6.9 copy-start.4
  317.9 1.1 copy-start.6
  321.4 0.8 copy-start.22
  321.5 60.5 %copy-start.2 = (bf16[256,1536]{1,0:T(8,128)(2,1)S(1)}, bf16[256,1536]{1,0:T(8,128)(2,1)}, u32[]{:S(2)}) copy-start(bf16[256,1536]{1,0:T(8,128)(2,1)} %param.11) | copy-start | bytes 2359300
  321.5 680.4 %all-reduce.9.cloned.1.call-start = ((), (), s32[]{:S(2)}) async-start(), calls=%async_computation.3 | async-start | bytes 1572864 | tf_op jit(solution)/shard_map/psum | solution.py:155
  325.3 0.5 copy-start.17
  381.9 264.0 %copy-start.3 = (bf16[256,1536]{1,0:T(8,128)(2,1)S(1)}, bf16[256,1536]{1,0:T(8,128)(2,1)}, u32[]{:S(2)}) copy-start(bf16[256,1536]{1,0:T(8,128)(2,1)} %get-tuple-element.18) | copy-start | bytes 2359300
  641.0 1.0 copy-start.18
  641.9 3.2 copy-start.20
  646.0 1.4 copy-start.7
  647.4 5.3 copy-start.13
  651.7 1.0 copy-start.5
  667.6 5.1 copy-start.19
  667.6 5.1 copy-start.21
  667.6 392.2 %all-reduce.7.cloned.1.call-start = ((), (), s32[]{:S(2)}) async-start(), calls=%async_computation | async-start | bytes 1572864 | tf_op jit(solution)/shard_map/psum | solution.py:142
  672.7 387.1 %copy-start.15 = (f32[4,1536]{1,0:T(4,128)S(1)}, f32[4,1536]{1,0:T(4,128)}, u32[]{:S(2)}) copy-start(f32[4,1536]{1,0:T(4,128)} %copy-done.14) | copy-start | bytes 73732
  1059.8 1.1 copy-start.10
  1061.0 0.7 copy-start.11
Sparse Core Ops, SparseCore 0:
  11.2 150.2 all-gather.4
  164.6 139.3 all-gather.6
  321.6 60.2 all-reduce.10
  667.7 334.1 all-reduce.8
  1004.1 55.6 all-reduce.6
where the time goes:
time: 1070 us
  waiting for transfers between devices  716 us (67%)
  blocking collectives  262 us (24%)
  local copies, waits for them, and re-layouts  27.5 us (3%)
  matrix products  26.1 us (2%)
  other arithmetic  23.3 us (2%)
  between operations  15.4 us (1%)
    psum x1, waiting for transfers between devices, per_device(): sum_a, sum_b = lax.psum((grad_a, grad_b), 'dp')  329 us
    psum x1, blocking collectives, per_device(): tot_pol, tot_ref, tot_rows = lax.psum((vec_pol, vec_ref, owned), 'dp')  249 us
    all_gather x1, waiting for transfers between devices, per_device(): lax.all_gather(up_projection_weight, 'dp', axis=0, tiled=True)  148 us
    all_gather x1, waiting for transfers between devices, per_device(): lax.all_gather(down_weight_transposed, 'dp', axis=0, tiled=True)  129 us
    psum x1, waiting for transfers between devices, per_device(): lax.psum(dm_part.astype(jnp.bfloat16), 'tensor').astype(jnp.float32)  54.4 us
    psum x1, waiting for transfers between devices, per_device(): lax.psum(part_ref.astype(jnp.bfloat16), 'tensor').astype(jnp.float32)  54 us
  transfers between devices with their start and end apart: 5, of which 5 were waited for; matrix products, arithmetic and copies ran while one was open for 3% of the time, Pallas kernels for 0%

commit v1 on v0

v1 whole, which is shorter than its diff:
```python
import jax
import jax.numpy as jnp
from jax import lax
from jax.sharding import Mesh
from jax.sharding import PartitionSpec as P

BLK = 64
CAP = 4
EPS = 1e-06
BETA = 20.0
LOSS_SCALE = 4096.0
ROOT = 0.7978845608028654
CUBE = 0.044715
BF16 = jnp.bfloat16
F32 = jnp.float32
DP = ("z", "x", "c")
SWAP = [(0, 1), (1, 0)]


def gelu(pre):
    th = jnp.tanh(ROOT * (pre + CUBE * pre * pre * pre))
    return 0.5 * pre * (1.0 + th)


def gelu_and_slope(pre):
    square = pre * pre
    th = jnp.tanh(ROOT * (pre + CUBE * pre * square))
    half = 0.5 * (1.0 + th)
    slope = half + 0.5 * pre * (1.0 - th * th) * (ROOT * (1.0 + 3.0 * CUBE * square))
    return pre * half, slope


def rows_by_rows(left, right):
    return lax.dot_general(left, right, (((1,), (1,)), ((), ())), preferred_element_type=F32)


def columns_by_columns(left, right):
    return lax.dot_general(left, right, (((0,), (0,)), ((), ())), preferred_element_type=F32)


def product(left, right):
    return jnp.dot(left, right, preferred_element_type=F32)


def spread(value, axes, n):
    return lax.all_to_all(jnp.broadcast_to(value[None], (n, *value.shape)), axes, 0, 0, tiled=True)


def per_device(
    tokens,
    targets,
    modulation,
    live_block_count,
    preferred_blocks,
    last_block_rows,
    up_rows,
    down_rows,
    factor_in,
    factor_out,
):
    width = tokens.shape[1]
    n_z, n_x, n_c, n_t = (lax.axis_size(a) for a in ("z", "x", "c", "t"))
    n_dp = n_z * n_x * n_c
    core = lax.axis_index("c")
    group = lax.axis_index("t")
    thin, hidden = up_rows.shape
    half = hidden // n_c

    down_split = down_rows.reshape(thin, n_c, half).transpose(1, 0, 2)
    down_sent = jnp.broadcast_to(down_split[None], (n_x, n_c, thin, half)).reshape(n_x * n_c, thin, half)
    down_near = lax.all_to_all(down_sent, ("x", "c"), 0, 0, tiled=True)
    down_own = lax.all_gather(down_near.reshape(n_x * n_c * thin, half), "z", axis=0, tiled=True)

    up_keep = lax.dynamic_slice_in_dim(up_rows, core * half, half, axis=1)
    up_give = lax.dynamic_slice_in_dim(up_rows, (1 - core) * half, half, axis=1)
    up_got = lax.ppermute(up_give, "c", SWAP)
    up_pair = jnp.where(
        core == 0, jnp.concatenate([up_keep, up_got], 0), jnp.concatenate([up_got, up_keep], 0)
    )
    up_line = lax.all_gather(up_pair, "z", axis=0, tiled=True)
    up_all = spread(up_line, "x", n_x).reshape(n_x, n_z, n_c * thin, half)
    up_own = up_all.transpose(1, 0, 2, 3).reshape(width, half)
    up_other = lax.ppermute(up_own, "c", SWAP)
    down_other = lax.ppermute(down_own, "c", SWAP)

    count = live_block_count[0]
    wins = preferred_blocks[0]
    slots = jnp.arange(CAP, dtype=jnp.int32)
    flags = (slots >= wins).astype(jnp.int32)
    last = jnp.where(flags == 0, wins - 1, count - 1)
    tail = jnp.where(flags == 0, last_block_rows[0, 0], last_block_rows[0, 1])
    live = jnp.where(slots < count, jnp.where(slots == last, tail, BLK), 0)
    rows_first = jnp.sum(jnp.where(flags == 0, live, 0)).astype(F32)
    rows_second = jnp.sum(jnp.where(flags == 1, live, 0)).astype(F32)
    scale_first = 1.0 / (width * rows_first)
    scale_second = 1.0 / (width * rows_second)

    vectors = modulation.astype(F32)
    pick = (flags == 0)[:, None, None]
    shift = jnp.where(pick, vectors[0, 0][None, None], vectors[1, 0][None, None])
    scale = 1.0 + jnp.where(pick, vectors[0, 1][None, None], vectors[1, 1][None, None])

    def normalise(rows):
        wide = rows.astype(F32)
        center = wide - jnp.mean(wide, axis=-1, keepdims=True)
        inverse = lax.rsqrt(jnp.mean(center * center, axis=-1, keepdims=True) + EPS)
        return center * inverse, inverse

    normed, _ = normalise(tokens.reshape(CAP, BLK, width))
    modded = (normed * scale + shift).astype(BF16).reshape(CAP * BLK, width)
    low = product(modded, factor_in).astype(BF16)

    factor_own = lax.dynamic_slice_in_dim(factor_out, core * half, half, axis=1)
    factor_other = lax.dynamic_slice_in_dim(factor_out, (1 - core) * half, half, axis=1)

    def activate(w_up, factor):
        pre_ref = product(modded, w_up)
        pre_pol = pre_ref + product(low, factor)
        act, slope = gelu_and_slope(pre_pol)
        return act.astype(BF16), gelu(pre_ref).astype(BF16), slope

    pol_own, ref_own, slope_own = activate(up_own, factor_own)
    pol_other, ref_other, slope_other = activate(up_other, factor_other)

    part_pol = rows_by_rows(pol_own, down_own) + rows_by_rows(pol_other, down_other)
    part_ref = rows_by_rows(ref_own, down_own) + rows_by_rows(ref_other, down_other)
    parts = jnp.concatenate(
        [
            part_pol.astype(BF16).reshape(CAP, BLK, width),
            part_ref.astype(BF16).reshape(CAP, BLK, width),
        ],
        axis=1,
    )
    parts = lax.all_to_all(parts, "t", 0, 0, tiled=True)
    sums = jnp.sum(parts.astype(F32), axis=0)

    flag = (group >= wins).astype(jnp.int32)
    x_own = lax.dynamic_slice_in_dim(tokens, group * BLK, BLK, axis=0)
    t_own = lax.dynamic_slice_in_dim(targets, group * BLK, BLK, axis=0).astype(F32)
    vec_own = jnp.where(flag == 0, vectors[0], vectors[1])
    live_own = lax.dynamic_slice_in_dim(live, group, 1)
    mask = (jnp.arange(BLK, dtype=jnp.int32)[:, None] < live_own[None, :]).astype(F32)
    gate = vec_own[2][None]
    base = x_own.astype(F32) - t_own
    miss_pol = base + gate * sums[:BLK]
    miss_ref = base + gate * sums[BLK:]
    excess = jnp.sum(mask * (miss_pol - miss_ref) * (miss_pol + miss_ref))
    grad_unit = 2.0 * mask * miss_pol
    dy_unit = (gate * grad_unit).astype(BF16)
    high = excess.astype(BF16)
    rest = excess - high.astype(F32)
    middle = rest.astype(BF16)
    lowest = (rest - middle.astype(F32)).astype(BF16)
    note = jnp.zeros((16, width), BF16)
    line = jnp.arange(16, dtype=jnp.int32)[:, None]
    note = jnp.where(line == 0, high, jnp.where(line == 1, middle, jnp.where(line == 2, lowest, note)))
    shared = spread(jnp.concatenate([dy_unit, note], 0), "t", n_t)
    dy = shared[:, :BLK].reshape(CAP * BLK, width)
    excesses = jnp.sum(shared[:, BLK : BLK + 3, 0].astype(F32), axis=1)
    gap_first = jnp.sum(jnp.where(flags == 0, excesses, 0.0)) * scale_first
    gap_second = jnp.sum(jnp.where(flags == 1, excesses, 0.0)) * scale_second
    inside = -BETA * (gap_first - gap_second)
    losses = jax.nn.softplus(-inside)[None]
    weight = BETA * LOSS_SCALE * jax.nn.sigmoid(-inside)
    coef = jnp.where(flags == 0, weight * scale_first, -weight * scale_second)
    coef_rows = jnp.broadcast_to(coef[:, None], (CAP, BLK)).reshape(CAP * BLK, 1)
    coef_own = jnp.where(flag == 0, weight * scale_first, -weight * scale_second)

    dpre_own = (product(dy, down_own) * coef_rows * slope_own).astype(BF16)
    dpre_other = (product(dy, down_other) * coef_rows * slope_other).astype(BF16)
    dlow = (rows_by_rows(dpre_own, factor_own) + rows_by_rows(dpre_other, factor_other)).astype(BF16)
    dm_part = (
        rows_by_rows(dpre_own, up_own) + rows_by_rows(dpre_other, up_other) + rows_by_rows(dlow, factor_in)
    ).astype(BF16)
    grad_a = columns_by_columns(dlow, modded).astype(BF16)
    b_own = columns_by_columns(low, dpre_own).astype(BF16)
    b_other = columns_by_columns(low, dpre_other).astype(BF16)
    grad_b = jnp.where(
        core == 0, jnp.concatenate([b_own, b_other], 1), jnp.concatenate([b_other, b_own], 1)
    )
    rank = grad_a.shape[0]
    slab = rank // n_t
    back = lax.all_to_all(
        jnp.concatenate([dm_part.reshape(CAP, BLK, width), grad_a.reshape(n_t, slab, width)], 1),
        "t",
        0,
        0,
        tiled=True,
    )
    back = jnp.sum(back.astype(F32), axis=0)
    normed_own, inverse_own = normalise(x_own)
    dn = back[:BLK] * (1.0 + vec_own[1][None])
    mean_one = jnp.mean(dn, axis=-1, keepdims=True)
    mean_two = jnp.mean(dn * normed_own, axis=-1, keepdims=True)
    grad_block = coef_own * grad_unit + inverse_own * (dn - mean_one - normed_own * mean_two)

    pile = jnp.concatenate([grad_b, back[BLK:].astype(BF16)], 0)
    lines = pile.shape[0]
    share = lines * width // n_dp
    pieces = lax.all_to_all(pile.reshape(n_dp, share), DP, 0, 0, tiled=True)
    total = (jnp.sum(pieces.astype(F32), axis=0) / n_dp).astype(BF16)
    pile = spread(total, DP, n_dp).reshape(lines, width)
    sum_b = pile[:rank].astype(F32)
    final = spread(jnp.concatenate([grad_block.astype(BF16), pile[rank:]], 0), "t", n_t)
    grad_tokens = final[:, :BLK].reshape(CAP * BLK, width)
    sum_a = final[:, BLK:].reshape(rank, width).astype(F32).T
    return losses, grad_tokens, sum_a, sum_b


def solution(mesh):
    n_dp, n_t = mesh.devices.shape
    fine = Mesh(mesh.devices.reshape(n_dp // 8, 4, 2, n_t), ("z", "x", "c", "t"))
    return jax.shard_map(
        per_device,
        mesh=fine,
        in_specs=(
            P(DP, None),
            P(DP, None),
            P(DP, None, None),
            P(DP),
            P(DP),
            P(DP, None),
            P(DP, "t"),
            P(DP, "t"),
            P(),
            P(None, "t"),
        ),
        out_specs=(P(DP), P(DP, None), P(), P(None, "t")),
        check_vma=False,
    )
```

time: 1070 us -> 300 us (0.28)
  waiting for transfers between devices: 716 us -> 93.5 us
  blocking collectives: 262 us -> 72.6 us
  starting transfers between devices: 0.38 us -> 53.8 us
  local copies, waits for them, and re-layouts: 27.5 us -> 16.2 us
    psum x3 -> x0, waiting for transfers between devices: 437 us -> none  [the longest x1 329 us: per_device(): sum_a, sum_b = lax.psum((grad_a, grad_b), 'dp')]
    all_gather x2 -> x1, waiting for transfers between devices: 277 us -> 0.01 us  [per_device(): lax.all_gather(down_near.reshape(n_x * n_c * thin, half), 'z', axis=0, ti...]
    psum x2 -> x0, blocking collectives: 262 us -> none  [the longest x1 249 us: per_device(): tot_pol, tot_ref, tot_rows = lax.psum((vec_pol, vec_ref, owned), 'dp')]
    all_to_all x0 -> x6, waiting for transfers between devices: none -> 92.6 us  [the longest x3 44.6 us: spread(): lax.all_to_all(jnp.broadcast_to(value[None], (n, *value.shape)), axes, 0,...]
    all_to_all x0 -> x2, blocking collectives: none -> 40.7 us  [the longest x1 25.6 us: spread(): lax.all_to_all(jnp.broadcast_to(value[None], (n, *value.shape)), axes, 0,...]
    all_to_all x0 -> x6, starting transfers between devices: none -> 37.3 us  [the longest x3 16.1 us: spread(): lax.all_to_all(jnp.broadcast_to(value[None], (n, *value.shape)), axes, 0,...]
    all_gather x0 -> x1, blocking collectives: none -> 31.9 us  [per_device(): up_line = lax.all_gather(up_pair, 'z', axis=0, tiled=True)]
    ppermute x0 -> x3, starting transfers between devices: none -> 16.4 us  [the longest x1 8.91 us: per_device(): up_other = lax.ppermute(up_own, 'c', SWAP)]
  transfers between devices with their start and end apart: 5 -> 10, of which waited for: 5 -> 7; matrix products, arithmetic and copies ran while one was open for 3% -> 6% of each run, Pallas kernels for 0% -> 0%
where the time goes in v1:
time: 300 us; the launch traced here: 298 us
  waiting for transfers between devices  93.5 us (31%)
  blocking collectives  72.6 us (24%)
  starting transfers between devices  53.8 us (18%)
  other arithmetic  22.6 us (8%)
  between operations  21.3 us (7%)
  matrix products  17.8 us (6%)
  local copies, waits for them, and re-layouts  16.2 us (5%)
    all_to_all x3, waiting for transfers between devices, spread(): lax.all_to_all(jnp.broadcast_to(value[None], (n, *value.shape)), axes, 0,...  44.6 us
    all_gather x1, blocking collectives, per_device(): up_line = lax.all_gather(up_pair, 'z', axis=0, tiled=True)  31.9 us
    all_to_all x1, blocking collectives, spread(): lax.all_to_all(jnp.broadcast_to(value[None], (n, *value.shape)), axes, 0,...  25.6 us
    all_to_all x1, waiting for transfers between devices, per_device(): pieces = lax.all_to_all(pile.reshape(n_dp, share), DP, 0, 0, tiled=True)  20.4 us
    all_to_all x3, starting transfers between devices, spread(): lax.all_to_all(jnp.broadcast_to(value[None], (n, *value.shape)), axes, 0,...  16.1 us
    all_to_all x1, waiting for transfers between devices, per_device(): parts = lax.all_to_all(parts, 't', 0, 0, tiled=True)  15.6 us
    all_to_all x1, blocking collectives, per_device(): down_near = lax.all_to_all(down_sent, ('x', 'c'), 0, 0, tiled=True)  15.2 us
    all_to_all x1, starting transfers between devices, per_device(): pieces = lax.all_to_all(pile.reshape(n_dp, share), DP, 0, 0, tiled=True)  13 us
  transfers between devices with their start and end apart: 10, of which 7 were waited for; matrix products, arithmetic and copies ran while one was open for 6% of the time, Pallas kernels for 0%

profile of v1, /device:TPU:1, one launch (start us, length us, event | category | flops | bytes accessed | tf_op | source)
XLA Modules:
  0.0 297.8 jit_solution(1041288502173520968)
XLA Ops:
  8.1 15.2 %all_to_all.46 = bf16[8,12,768]{2,1,0:T(8,128)(2,1)S(1)} all-to-all(bf16[8,12,768]{2,1,0:T(8,128)(2,1)S(1)} %bitcast.75), channel_id=1, replica_groups=mesh['z'=16,'x'=4,'c'=2,'t'=4] {'x','c'}, dimensions={0} | all-to-all | bytes 294912 | tf_op jit(solution)/shard_map/all_to_all | solution.py:71
  24.8 2.8 collective-permute-start
  28.5 31.9 %all_gather.6 = bf16[384,768]{1,0:T(8,128)(2,1)S(1)} all-gather(bf16[24,768]{1,0:T(8,128)(2,1)S(1)} %maximum_select_fusion.1), channel_id=1, replica_groups=mesh['z'=16,'x'=4,'c'=2,'t'=4] {'z'}, dimensions={0}, use_global_device_ids=true | all-gather | bytes 626688 | tf_op jit(solution)/shard_map/all_gather | solution.py:80
  60.5 25.6 %all_to_all.47 = bf16[4,384,768]{2,1,0:T(8,128)(2,1)S(1)} all-to-all(bf16[4,384,768]{2,1,0:T(8,128)(2,1)S(1)} %broadcast_in_dim.173), channel_id=1, replica_groups=mesh['z'=16,'x'=4,'c'=2,'t'=4] {'x'}, dimensions={0} | all-to-all | bytes 4718592 | tf_op jit(solution)/shard_map/all_to_all | solution.py:46
  86.4 8.9 %collective-permute-start.1 = (bf16[1536,768]{1,0:T(8,128)(2,1)S(1)}, bf16[1536,768]{1,0:T(8,128)(2,1)}, u32[]{:S(2)}, u32[]{:S(2)}) collective-permute-start(bf16[1536,768]{1,0:T(8,128)(2,1)S(1)} %bitcast.65), channel_id=1, source_target_pairs={{0,4},{4,0},{1,5},{5,1},{2,6},{6,2},{3,7},{7,3},{8,12},{12,8},{9,1... | collective-permute-start | bytes 7077896 | tf_op jit(solution)/shard_map/ppermute | solution.py:83
  96.4 4.7 %collective-permute-start.2 = (bf16[1536,768]{1,0:T(8,128)(2,1)}, bf16[1536,768]{1,0:T(8,128)(2,1)S(1)}, u32[]{:S(2)}, u32[]{:S(2)}) collective-permute-start(bf16[1536,768]{1,0:T(8,128)(2,1)} %all-gather.2.cloned.1.call-done), channel_id=1, source_target_pairs={{0,4},{4,0},{1,5},{5,1},{2,6},{6,2},{3,7},{7,3},{8,12},{12,8},{9,1... | collective-permute-start | bytes 7077896 | tf_op jit(solution)/shard_map/ppermute | solution.py:84
  101.8 1.5 convolution_convert_fusion.3
  104.4 2.7 fusion.88
  111.5 1.3 pad_maximum_fusion
  112.8 4.5 %all-to-all-start.2 = ((bf16[4,128,1536]{2,1,0:T(8,128)(2,1)}), bf16[4,128,1536]{2,1,0:T(8,128)(2,1)}, u32[]{:S(2)}, u32[]{:S(2)}) async-start(bf16[4,128,1536]{2,1,0:T(8,128)(2,1)} %pad_maximum_fusion), calls=%async_computation.2 | async-start | bytes 3145728 | tf_op jit(solution)/shard_map/all_to_all | solution.py:134
  118.6 2.0 fusion.68
  122.7 15.6 %all-to-all-done.2 = bf16[4,128,1536]{2,1,0:T(8,128)(2,1)} async-done(((bf16[4,128,1536]{2,1,0:T(8,128)(2,1)}), bf16[4,128,1536]{2,1,0:T(8,128)(2,1)}, u32[]{:S(2)}, u32[]{:S(2)}) %all-to-all-start.2) | async-done | bytes 1572896 | tf_op jit(solution)/shard_map/all_to_all | solution.py:134
  138.2 1.7 convert_reduce_fusion
  140.9 2.5 fusion.33
  145.7 1.1 broadcast_in_dim.182
  146.9 4.3 %all-to-all-start.3 = ((bf16[4,80,1536]{2,1,0:T(8,128)(2,1)}), bf16[4,80,1536]{2,1,0:T(8,128)(2,1)}, u32[]{:S(2)}, u32[]{:S(2)}) async-start(bf16[4,80,1536]{2,1,0:T(8,128)(2,1)} %broadcast_in_dim.182), calls=%async_computation.3 | async-start | bytes 1966080 | tf_op jit(solution)/shard_map/all_to_all | solution.py:46
  152.5 12.4 %all-to-all-done.3 = bf16[4,80,1536]{2,1,0:T(8,128)(2,1)} async-done(((bf16[4,80,1536]{2,1,0:T(8,128)(2,1)}), bf16[4,80,1536]{2,1,0:T(8,128)(2,1)}, u32[]{:S(2)}, u32[]{:S(2)}) %all-to-all-start.3) | async-done | bytes 983072 | tf_op jit(solution)/shard_map/all_to_all | solution.py:46
  167.9 1.2 slice.93
  169.0 2.9 fusion.11
  175.6 2.5 convolution_add_fusion.1
  179.6 3.7 %all-to-all-start.4 = ((bf16[4,80,1536]{2,1,0:T(8,128)(2,1)}), bf16[4,80,1536]{2,1,0:T(8,128)(2,1)S(1)}, u32[]{:S(2)}, u32[]{:S(2)}) async-start(bf16[4,80,1536]{2,1,0:T(8,128)(2,1)} %pad_maximum_fusion.1), calls=%async_computation.4 | async-start | bytes 1966080 | tf_op jit(solution)/shard_map/all_to_all | solution.py:183
  183.8 12.1 %all-to-all-done.4 = bf16[4,80,1536]{2,1,0:T(8,128)(2,1)S(1)} async-done(((bf16[4,80,1536]{2,1,0:T(8,128)(2,1)}), bf16[4,80,1536]{2,1,0:T(8,128)(2,1)S(1)}, u32[]{:S(2)}, u32[]{:S(2)}) %all-to-all-start.4) | async-done | bytes 983072 | tf_op jit(solution)/shard_map/all_to_all | solution.py:183
  197.1 2.2 reduce.17
  200.3 13.0 %all-to-all-start.5 = ((bf16[128,2,480]{2,1,0:T(2,128)(2,1)}), bf16[128,2,480]{2,1,0:T(2,128)(2,1)S(1)}, u32[]{:S(2)}, u32[]{:S(2)}) async-start(bf16[128,2,480]{2,1,0:T(2,128)(2,1)} %reshape.279), calls=%async_computation.5 | async-start | bytes 524288 | tf_op jit(solution)/shard_map/all_to_all | solution.py:200
  213.3 20.4 %all-to-all-done.5 = bf16[128,2,480]{2,1,0:T(2,128)(2,1)S(1)} async-done(((bf16[128,2,480]{2,1,0:T(2,128)(2,1)}), bf16[128,2,480]{2,1,0:T(2,128)(2,1)S(1)}, u32[]{:S(2)}, u32[]{:S(2)}) %all-to-all-start.5) | async-done | bytes 245792 | tf_op jit(solution)/shard_map/all_to_all | solution.py:200
  235.0 2.2 reduce.18
  238.2 8.3 %all-to-all-start.6 = ((bf16[128,2,480]{2,1,0:T(2,128)(2,1)}), bf16[128,2,480]{2,1,0:T(2,128)(2,1)S(1)}, u32[]{:S(2)}, u32[]{:S(2)}) async-start(bf16[128,2,480]{2,1,0:T(2,128)(2,1)} %reshape.281), calls=%async_computation.6 | async-start | bytes 524288 | tf_op jit(solution)/shard_map/all_to_all | solution.py:46
  246.8 1.3 fusion.32
  248.0 19.0 %all-to-all-done.6 = bf16[128,2,480]{2,1,0:T(2,128)(2,1)S(1)} async-done(((bf16[128,2,480]{2,1,0:T(2,128)(2,1)}), bf16[128,2,480]{2,1,0:T(2,128)(2,1)S(1)}, u32[]{:S(2)}, u32[]{:S(2)}) %all-to-all-start.6) | async-done | bytes 245792 | tf_op jit(solution)/shard_map/all_to_all | solution.py:46
  267.4 1.6 reduce.10
  270.5 3.5 %all-to-all-start.7 = ((bf16[4,80,1536]{2,1,0:T(8,128)(2,1)}), bf16[4,80,1536]{2,1,0:T(8,128)(2,1)S(1)}, u32[]{:S(2)}, u32[]{:S(2)}) async-start(bf16[4,80,1536]{2,1,0:T(8,128)(2,1)} %broadcast_in_dim.189), calls=%async_computation.7 | async-start | bytes 1966080 | tf_op jit(solution)/shard_map/all_to_all | solution.py:46
  274.9 13.1 %all-to-all-done.7 = bf16[4,80,1536]{2,1,0:T(8,128)(2,1)S(1)} async-done(((bf16[4,80,1536]{2,1,0:T(8,128)(2,1)}), bf16[4,80,1536]{2,1,0:T(8,128)(2,1)S(1)}, u32[]{:S(2)}, u32[]{:S(2)}) %all-to-all-start.7) | async-done | bytes 983072 | tf_op jit(solution)/shard_map/all_to_all | solution.py:46
  (116 shorter events, 30.7 us)
Async XLA Ops:
  7.2 96.9 %copy-start = (bf16[64,1536]{1,0:T(8,128)(2,1)S(1)}, bf16[64,1536]{1,0:T(8,128)(2,1)}, u32[]{:S(2)}) copy-start(bf16[64,1536]{1,0:T(8,128)(2,1)} %param.19) | copy-start | bytes 589828
  7.2 89.2 %all-gather.2.cloned.1.call-start = ((), (), s32[]{:S(2)}) async-start(), calls=%async_computation.8 | async-start | bytes 2506752 | tf_op jit(solution)/shard_map/all_gather | solution.py:72
  24.8 3.7 %collective-permute-start = (bf16[12,768]{1,0:T(8,128)(2,1)S(1)}, bf16[12,768]{1,0:T(8,128)(2,1)S(1)}, u32[]{:S(2)}, u32[]{:S(2)}) collective-permute-start(bf16[12,768]{1,0:T(8,128)(2,1)S(1)} %get-tuple-element.21), channel_id=1, source_target_pairs={{0,4},{4,0},{1,5},{5,1},{2,6},{6,2},{3,7},{7,3},{8,12},{12,8},{9,1... | collective-permute-start | bytes 55304 | tf_op jit(solution)/shard_map/ppermute | solution.py:76
  86.1 9.8 %copy-start.14 = (bf16[2,3,1536]{2,0,1:T(2,128)(2,1)S(1)}, bf16[2,3,1536]{2,0,1:T(2,128)(2,1)}, u32[]{:S(2)}) copy-start(bf16[2,3,1536]{2,0,1:T(2,128)(2,1)} %param.12) | copy-start | bytes 55300
  86.1 10.0 %copy-start.1 = (bf16[256,1536]{1,0:T(8,128)(2,1)S(1)}, bf16[256,1536]{1,0:T(8,128)(2,1)}, u32[]{:S(2)}) copy-start(bf16[256,1536]{1,0:T(8,128)(2,1)} %param.10) | copy-start | bytes 2359300
  86.4 18.0 %collective-permute-start.1 = (bf16[1536,768]{1,0:T(8,128)(2,1)S(1)}, bf16[1536,768]{1,0:T(8,128)(2,1)}, u32[]{:S(2)}, u32[]{:S(2)}) collective-permute-start(bf16[1536,768]{1,0:T(8,128)(2,1)S(1)} %bitcast.65), channel_id=1, source_target_pairs={{0,4},{4,0},{1,5},{5,1},{2,6},{6,2},{3,7},{7,3},{8,12},{12,8},{9,1... | collective-permute-start | bytes 7077896 | tf_op jit(solution)/shard_map/ppermute | solution.py:83
  96.4 12.8 %collective-permute-start.2 = (bf16[1536,768]{1,0:T(8,128)(2,1)}, bf16[1536,768]{1,0:T(8,128)(2,1)S(1)}, u32[]{:S(2)}, u32[]{:S(2)}) collective-permute-start(bf16[1536,768]{1,0:T(8,128)(2,1)} %all-gather.2.cloned.1.call-done), channel_id=1, source_target_pairs={{0,4},{4,0},{1,5},{5,1},{2,6},{6,2},{3,7},{7,3},{8,12},{12,8},{9,1... | collective-permute-start | bytes 7077896 | tf_op jit(solution)/shard_map/ppermute | solution.py:84
  101.8 2.6 copy-start.4
  104.4 4.0 %copy-start.12 = (f32[256,768]{1,0:T(8,128)}, f32[256,768]{1,0:T(8,128)S(1)}, u32[]{:S(2)}) copy-start(f32[256,768]{1,0:T(8,128)S(1)} %convolution_add_fusion.5) | copy-start | bytes 2359300
  104.4 3.1 %copy-start.16 = (bf16[1536,768]{1,0:T(8,128)(2,1)S(1)}, bf16[1536,768]{1,0:T(8,128)(2,1)}, u32[]{:S(2)}) copy-start(bf16[1536,768]{1,0:T(8,128)(2,1)} %all-gather.2.cloned.1.call-done) | copy-start | bytes 7077892
  107.5 2.6 copy-start.10
  109.2 1.4 copy-start.2
  112.8 4.5 %copy-start.15 = (s32[1,2]{1,0:T(1,128)S(1)}, s32[1,2]{1,0:T(1,128)}, u32[]{:S(2)}) copy-start(s32[1,2]{1,0:T(1,128)} %param.15) | copy-start | bytes 28
  112.8 25.4 %all-to-all-start.2 = ((bf16[4,128,1536]{2,1,0:T(8,128)(2,1)}), bf16[4,128,1536]{2,1,0:T(8,128)(2,1)}, u32[]{:S(2)}, u32[]{:S(2)}) async-start(bf16[4,128,1536]{2,1,0:T(8,128)(2,1)} %pad_maximum_fusion), calls=%async_computation.2 | async-start | bytes 3145728 | tf_op jit(solution)/shard_map/all_to_all | solution.py:134
  140.0 0.9 copy-start.6
  146.9 18.0 %all-to-all-start.3 = ((bf16[4,80,1536]{2,1,0:T(8,128)(2,1)}), bf16[4,80,1536]{2,1,0:T(8,128)(2,1)}, u32[]{:S(2)}, u32[]{:S(2)}) async-start(bf16[4,80,1536]{2,1,0:T(8,128)(2,1)} %broadcast_in_dim.182), calls=%async_computation.3 | async-start | bytes 1966080 | tf_op jit(solution)/shard_map/all_to_all | solution.py:46
  171.9 1.1 copy-start.8
  172.2 1.7 copy-start.3
  172.2 1.8 copy-start.11
  174.0 1.3 copy-start.5
  175.6 2.6 copy-start.13
  178.6 4.9 %copy-start.9 = (bf16[256,768]{1,0:T(8,128)(2,1)S(1)}, bf16[256,768]{1,0:T(8,128)(2,1)}, u32[]{:S(2)}) copy-start(bf16[256,768]{1,0:T(8,128)(2,1)} %copy-done.8) | copy-start | bytes 1179652
  179.6 16.2 %all-to-all-start.4 = ((bf16[4,80,1536]{2,1,0:T(8,128)(2,1)}), bf16[4,80,1536]{2,1,0:T(8,128)(2,1)S(1)}, u32[]{:S(2)}, u32[]{:S(2)}) async-start(bf16[4,80,1536]{2,1,0:T(8,128)(2,1)} %pad_maximum_fusion.1), calls=%async_computation.4 | async-start | bytes 1966080 | tf_op jit(solution)/shard_map/all_to_all | solution.py:183
  200.3 33.5 %all-to-all-start.5 = ((bf16[128,2,480]{2,1,0:T(2,128)(2,1)}), bf16[128,2,480]{2,1,0:T(2,128)(2,1)S(1)}, u32[]{:S(2)}, u32[]{:S(2)}) async-start(bf16[128,2,480]{2,1,0:T(2,128)(2,1)} %reshape.279), calls=%async_computation.5 | async-start | bytes 524288 | tf_op jit(solution)/shard_map/all_to_all | solution.py:200
  213.3 33.4 %copy-start.7 = (f32[128,1536]{1,0:T(8,128)S(1)}, f32[128,1536]{1,0:T(8,128)}, u32[]{:S(2)}) copy-start(f32[128,1536]{1,0:T(8,128)} %copy-done.6) | copy-start | bytes 2359300
  238.2 28.9 %all-to-all-start.6 = ((bf16[128,2,480]{2,1,0:T(2,128)(2,1)}), bf16[128,2,480]{2,1,0:T(2,128)(2,1)S(1)}, u32[]{:S(2)}, u32[]{:S(2)}) async-start(bf16[128,2,480]{2,1,0:T(2,128)(2,1)} %reshape.281), calls=%async_computation.6 | async-start | bytes 524288 | tf_op jit(solution)/shard_map/all_to_all | solution.py:46
  270.5 17.5 %all-to-all-start.7 = ((bf16[4,80,1536]{2,1,0:T(8,128)(2,1)}), bf16[4,80,1536]{2,1,0:T(8,128)(2,1)S(1)}, u32[]{:S(2)}, u32[]{:S(2)}) async-start(bf16[4,80,1536]{2,1,0:T(8,128)(2,1)} %broadcast_in_dim.189), calls=%async_computation.7 | async-start | bytes 1966080 | tf_op jit(solution)/shard_map/all_to_all | solution.py:46
Sparse Core Ops, SparseCore 0:
  24.1 66.0 all-gather.1

commit v2 on v1

--- a/solution.py
+++ b/solution.py
@@ -14,6 +14,8 @@
 BF16 = jnp.bfloat16
 F32 = jnp.float32
 DP = ("z", "x", "c")
+CHIPS = ("z", "x")
+LANES = 128
 SWAP = [(0, 1), (1, 0)]
 
 
@@ -66,21 +68,24 @@
     thin, hidden = up_rows.shape
     half = hidden // n_c
 
-    down_split = down_rows.reshape(thin, n_c, half).transpose(1, 0, 2)
-    down_sent = jnp.broadcast_to(down_split[None], (n_x, n_c, thin, half)).reshape(n_x * n_c, thin, half)
-    down_near = lax.all_to_all(down_sent, ("x", "c"), 0, 0, tiled=True)
-    down_own = lax.all_gather(down_near.reshape(n_x * n_c * thin, half), "z", axis=0, tiled=True)
-
-    up_keep = lax.dynamic_slice_in_dim(up_rows, core * half, half, axis=1)
-    up_give = lax.dynamic_slice_in_dim(up_rows, (1 - core) * half, half, axis=1)
-    up_got = lax.ppermute(up_give, "c", SWAP)
-    up_pair = jnp.where(
-        core == 0, jnp.concatenate([up_keep, up_got], 0), jnp.concatenate([up_got, up_keep], 0)
-    )
+    both = jnp.concatenate([up_rows, down_rows], axis=0)
+    keep = lax.dynamic_slice_in_dim(both, core * half, half, axis=1)
+    got = lax.ppermute(lax.dynamic_slice_in_dim(both, (1 - core) * half, half, axis=1), "c", SWAP)
+    first = jnp.where(core == 0, keep, got)
+    second = jnp.where(core == 0, got, keep)
+    up_pair = jnp.concatenate([first[:thin], second[:thin]], axis=0)
+    down_pair = jnp.concatenate([first[thin:], second[thin:]], axis=0)
+
+    def whole(line):
+        rows = spread(line, "x", n_x).reshape(n_x, n_z, n_c * thin, half)
+        return rows.transpose(1, 0, 2, 3).reshape(width, half)
+
     up_line = lax.all_gather(up_pair, "z", axis=0, tiled=True)
-    up_all = spread(up_line, "x", n_x).reshape(n_x, n_z, n_c * thin, half)
-    up_own = up_all.transpose(1, 0, 2, 3).reshape(width, half)
+    down_pair, up_line = lax.optimization_barrier((down_pair, up_line))
+    down_line = lax.all_gather(down_pair, "z", axis=0, tiled=True)
+    up_own = whole(up_line)
     up_other = lax.ppermute(up_own, "c", SWAP)
+    down_own = whole(down_line)
     down_other = lax.ppermute(down_own, "c", SWAP)
 
     count = live_block_count[0]
@@ -151,12 +156,11 @@
     rest = excess - high.astype(F32)
     middle = rest.astype(BF16)
     lowest = (rest - middle.astype(F32)).astype(BF16)
-    note = jnp.zeros((16, width), BF16)
-    line = jnp.arange(16, dtype=jnp.int32)[:, None]
-    note = jnp.where(line == 0, high, jnp.where(line == 1, middle, jnp.where(line == 2, lowest, note)))
-    shared = spread(jnp.concatenate([dy_unit, note], 0), "t", n_t)
-    dy = shared[:, :BLK].reshape(CAP * BLK, width)
-    excesses = jnp.sum(shared[:, BLK : BLK + 3, 0].astype(F32), axis=1)
+    lane = lax.broadcasted_iota(jnp.int32, (BLK, LANES), 1)
+    note = jnp.where(lane == 0, high, jnp.where(lane == 1, middle, lowest))
+    shared = spread(jnp.concatenate([dy_unit, note], 1), "t", n_t)
+    dy = shared[:, :, :width].reshape(CAP * BLK, width)
+    excesses = jnp.sum(shared[:, 0, width : width + 3].astype(F32), axis=1)
     gap_first = jnp.sum(jnp.where(flags == 0, excesses, 0.0)) * scale_first
     gap_second = jnp.sum(jnp.where(flags == 1, excesses, 0.0)) * scale_second
     inside = -BETA * (gap_first - gap_second)
@@ -172,38 +176,37 @@
     dm_part = (
         rows_by_rows(dpre_own, up_own) + rows_by_rows(dpre_other, up_other) + rows_by_rows(dlow, factor_in)
     ).astype(BF16)
-    grad_a = columns_by_columns(dlow, modded).astype(BF16)
-    b_own = columns_by_columns(low, dpre_own).astype(BF16)
-    b_other = columns_by_columns(low, dpre_other).astype(BF16)
-    grad_b = jnp.where(
-        core == 0, jnp.concatenate([b_own, b_other], 1), jnp.concatenate([b_other, b_own], 1)
-    )
+    grad_a = columns_by_columns(dlow, modded)
+    b_own = columns_by_columns(low, dpre_own)
+    b_other = columns_by_columns(low, dpre_other)
     rank = grad_a.shape[0]
-    slab = rank // n_t
-    back = lax.all_to_all(
-        jnp.concatenate([dm_part.reshape(CAP, BLK, width), grad_a.reshape(n_t, slab, width)], 1),
-        "t",
-        0,
-        0,
-        tiled=True,
-    )
+    middle_column = width // n_c
+    a_own = lax.dynamic_slice_in_dim(grad_a, core * middle_column, middle_column, axis=1)
+    a_other = lax.dynamic_slice_in_dim(grad_a, (1 - core) * middle_column, middle_column, axis=1)
+    given = lax.ppermute(jnp.concatenate([b_other, a_other], 0).astype(BF16), "c", SWAP)
+    pile = (jnp.concatenate([b_own, a_own], 0) + given.astype(F32)).astype(BF16)
+
+    chips = n_z * n_x
+    pieces = lax.all_to_all(pile.reshape(chips, 2 * rank // chips, half), CHIPS, 0, 0, tiled=True)
+    total = jnp.sum(pieces.astype(F32), axis=0) / n_dp
+    place = lax.axis_index("z") * n_x + lax.axis_index("x")
+    total = jnp.where(place < chips // 2, total, lax.psum(total, "t")).astype(BF16)
+    mine = spread(total, CHIPS, chips).reshape(2 * rank, half)
+    theirs = lax.ppermute(mine, "c", SWAP)
+    ends = jnp.concatenate([mine, theirs], 1)
+    flipped = jnp.concatenate([theirs, mine], 1)
+    ends = jnp.where(core == 0, ends, flipped).astype(F32)
+    sum_b = ends[:rank]
+    sum_a = ends[rank:].T
+
+    back = lax.all_to_all(dm_part.reshape(CAP, BLK, width), "t", 0, 0, tiled=True)
     back = jnp.sum(back.astype(F32), axis=0)
     normed_own, inverse_own = normalise(x_own)
-    dn = back[:BLK] * (1.0 + vec_own[1][None])
+    dn = back * (1.0 + vec_own[1][None])
     mean_one = jnp.mean(dn, axis=-1, keepdims=True)
     mean_two = jnp.mean(dn * normed_own, axis=-1, keepdims=True)
     grad_block = coef_own * grad_unit + inverse_own * (dn - mean_one - normed_own * mean_two)
-
-    pile = jnp.concatenate([grad_b, back[BLK:].astype(BF16)], 0)
-    lines = pile.shape[0]
-    share = lines * width // n_dp
-    pieces = lax.all_to_all(pile.reshape(n_dp, share), DP, 0, 0, tiled=True)
-    total = (jnp.sum(pieces.astype(F32), axis=0) / n_dp).astype(BF16)
-    pile = spread(total, DP, n_dp).reshape(lines, width)
-    sum_b = pile[:rank].astype(F32)
-    final = spread(jnp.concatenate([grad_block.astype(BF16), pile[rank:]], 0), "t", n_t)
-    grad_tokens = final[:, :BLK].reshape(CAP * BLK, width)
-    sum_a = final[:, BLK:].reshape(rank, width).astype(F32).T
+    grad_tokens = spread(grad_block.astype(BF16), "t", n_t).reshape(CAP * BLK, width)
     return losses, grad_tokens, sum_a, sum_b
 
 

time: 300 us -> 277 us (0.923); the launches traced: 298 us -> 271 us
  starting transfers between devices: 53.8 us -> 91 us
  waiting for transfers between devices: 93.5 us -> 64 us
  blocking collectives: 72.6 us -> 56.8 us
  between operations: 21.3 us -> 7.91 us
  other arithmetic: 22.6 us -> 15.5 us
    all_to_all x2 -> x0, blocking collectives: 40.7 us -> none  [the longest x1 25.6 us: spread(): lax.all_to_all(jnp.broadcast_to(value[None], (n, *value.shape)), axes, 0,...]
    all_gather x0 -> x1, blocking collectives: none -> 23.3 us  [per_device(): down_line = lax.all_gather(down_pair, 'z', axis=0, tiled=True)]
    ppermute x1 -> x3, starting transfers between devices: 2.85 us -> 21.8 us  [the longest x1 9.25 us: per_device(): theirs = lax.ppermute(mine, 'c', SWAP)]
    all_to_all x3 -> x5, waiting for transfers between devices: 44.6 us -> 25.6 us  [spread(): lax.all_to_all(jnp.broadcast_to(value[None], (n, *value.shape)), axes, 0,...]
    all_to_all x2, waiting for transfers between devices: 32.5 us -> 20.4 us  [the longest x1 15.9 us: per_device(): lax.all_to_all(pile.reshape(chips, 2 * rank // chips, half), CHIPS, 0, 0,...]
    ppermute x1, starting transfers between devices: 4.67 us -> 15.2 us  [per_device(): down_other = lax.ppermute(down_own, 'c', SWAP)]
    ppermute x1, starting transfers between devices: 8.91 us -> 16.1 us  [per_device(): up_other = lax.ppermute(up_own, 'c', SWAP)]
    psum x0 -> x1, blocking collectives: none -> 6.97 us  [per_device(): lax.psum(total, 't')]
  transfers between devices with their start and end apart: 10 -> 13, of which waited for: 7 -> 8; matrix products, arithmetic and copies ran while one was open for 6% -> 7% of each run, Pallas kernels for 0% -> 0%
where the time goes in v2:
time: 277 us; the launch traced here: 271 us
  starting transfers between devices  91 us (33%)
  waiting for transfers between devices  64 us (23%)
  blocking collectives  56.8 us (21%)
  local copies, waits for them, and re-layouts  19.1 us (7%)
  matrix products  17.2 us (6%)
  other arithmetic  15.5 us (6%)
  between operations  7.91 us (3%)
    all_gather x1, blocking collectives, per_device(): up_line = lax.all_gather(up_pair, 'z', axis=0, tiled=True)  26.5 us
    all_to_all x5, waiting for transfers between devices, spread(): lax.all_to_all(jnp.broadcast_to(value[None], (n, *value.shape)), axes, 0,...  25.6 us
    all_gather x1, blocking collectives, per_device(): down_line = lax.all_gather(down_pair, 'z', axis=0, tiled=True)  23.3 us
    all_to_all x5, starting transfers between devices, spread(): lax.all_to_all(jnp.broadcast_to(value[None], (n, *value.shape)), axes, 0,...  21.7 us
    ppermute x1, starting transfers between devices, per_device(): up_other = lax.ppermute(up_own, 'c', SWAP)  16.1 us
    all_to_all x1, waiting for transfers between devices, per_device(): lax.all_to_all(pile.reshape(chips, 2 * rank // chips, half), CHIPS, 0, 0,...  15.9 us
    all_to_all x1, waiting for transfers between devices, per_device(): parts = lax.all_to_all(parts, 't', 0, 0, tiled=True)  15.4 us
    ppermute x1, starting transfers between devices, per_device(): down_other = lax.ppermute(down_own, 'c', SWAP)  15.2 us
  transfers between devices with their start and end apart: 13, of which 8 were waited for; matrix products, arithmetic and copies ran while one was open for 7% of the time, Pallas kernels for 0%

profile of v2, /device:TPU:1, one launch (start us, length us, event | category | flops | bytes accessed | tf_op | source)
XLA Modules:
  0.0 271.4 jit_solution(2985914142022283810)
XLA Ops:
  1.5 8.8 %collective-permute-start = (bf16[24,768]{1,0:T(8,128)(2,1)S(1)}, bf16[24,768]{1,0:T(8,128)(2,1)S(1)}, u32[]{:S(2)}, u32[]{:S(2)}) collective-permute-start(bf16[24,768]{1,0:T(8,128)(2,1)S(1)} %fusion.63), channel_id=1, source_target_pairs={{0,4},{4,0},{1,5},{5,1},{2,6},{6,2},{3,7},{7,3},{8,12},{12,8},{9,1... | collective-permute-start | bytes 110600 | tf_op jit(solution)/shard_map/ppermute | solution.py:73
  12.2 26.5 %all_gather.6 = bf16[384,768]{1,0:T(8,128)(2,1)S(1)} all-gather(bf16[24,768]{1,0:T(8,128)(2,1)S(1)} %pad_maximum_fusion.4), channel_id=1, replica_groups=mesh['z'=16,'x'=4,'c'=2,'t'=4] {'z'}, dimensions={0}, use_global_device_ids=true | all-gather | bytes 626688 | tf_op jit(solution)/shard_map/all_gather | solution.py:83
  38.7 1.6 broadcast_in_dim.153
  40.2 4.0 %all-to-all-start = ((bf16[4,384,768]{2,1,0:T(8,128)(2,1)}), bf16[4,384,768]{2,1,0:T(8,128)(2,1)S(1)}, u32[]{:S(2)}, u32[]{:S(2)}) async-start(bf16[4,384,768]{2,1,0:T(8,128)(2,1)} %broadcast_in_dim.153), calls=%async_computation | async-start | bytes 4718592 | tf_op jit(solution)/shard_map/all_to_all | solution.py:48
  44.3 23.3 %all_gather.7 = bf16[384,768]{1,0:T(8,128)(2,1)S(1)} all-gather(bf16[24,768]{1,0:T(8,128)(2,1)S(1)} %pad_maximum_fusion.3), channel_id=1, replica_groups=mesh['z'=16,'x'=4,'c'=2,'t'=4] {'z'}, dimensions={0}, use_global_device_ids=true | all-gather | bytes 626688 | tf_op jit(solution)/shard_map/all_gather | solution.py:85
  67.5 1.7 broadcast_in_dim.154
  69.7 4.5 %all-to-all-start.1 = ((bf16[4,384,768]{2,1,0:T(8,128)(2,1)}), bf16[4,384,768]{2,1,0:T(8,128)(2,1)}, u32[]{:S(2)}, u32[]{:S(2)}) async-start(bf16[4,384,768]{2,1,0:T(8,128)(2,1)} %broadcast_in_dim.154), calls=%async_computation.1 | async-start | bytes 4718592 | tf_op jit(solution)/shard_map/all_to_all | solution.py:48
  75.2 1.9 copy.26
  77.1 16.1 %collective-permute-start.1 = (bf16[1536,768]{1,0:T(8,128)(2,1)S(1)}, bf16[1536,768]{1,0:T(8,128)(2,1)}, u32[]{:S(2)}, u32[]{:S(2)}) collective-permute-start(bf16[1536,768]{1,0:T(8,128)(2,1)S(1)} %bitcast.63), channel_id=1, source_target_pairs={{0,4},{4,0},{1,5},{5,1},{2,6},{6,2},{3,7},{7,3},{8,12},{12,8},{9,1... | collective-permute-start | bytes 7077896 | tf_op jit(solution)/shard_map/ppermute | solution.py:87
  93.3 1.9 copy.27
  95.3 15.2 %collective-permute-start.2 = (bf16[1536,768]{1,0:T(8,128)(2,1)S(1)}, bf16[1536,768]{1,0:T(8,128)(2,1)S(1)}, u32[]{:S(2)}, u32[]{:S(2)}) collective-permute-start(bf16[1536,768]{1,0:T(8,128)(2,1)S(1)} %bitcast.70), channel_id=1, source_target_pairs={{0,4},{4,0},{1,5},{5,1},{2,6},{6,2},{3,7},{7,3},{8,12},{12,8},{9,1... | collective-permute-start | bytes 7077896 | tf_op jit(solution)/shard_map/ppermute | solution.py:89
  114.4 2.4 fusion.94
  119.7 1.3 pad_maximum_fusion
  121.0 4.5 %all-to-all-start.2 = ((bf16[4,128,1536]{2,1,0:T(8,128)(2,1)}), bf16[4,128,1536]{2,1,0:T(8,128)(2,1)}, u32[]{:S(2)}, u32[]{:S(2)}) async-start(bf16[4,128,1536]{2,1,0:T(8,128)(2,1)} %pad_maximum_fusion), calls=%async_computation.2 | async-start | bytes 3145728 | tf_op jit(solution)/shard_map/all_to_all | solution.py:139
  126.7 2.0 fusion.71
  130.8 15.4 %all-to-all-done.2 = bf16[4,128,1536]{2,1,0:T(8,128)(2,1)} async-done(((bf16[4,128,1536]{2,1,0:T(8,128)(2,1)}), bf16[4,128,1536]{2,1,0:T(8,128)(2,1)}, u32[]{:S(2)}, u32[]{:S(2)}) %all-to-all-start.2) | async-done | bytes 1572896 | tf_op jit(solution)/shard_map/all_to_all | solution.py:139
  146.2 1.7 convert_reduce_fusion
  148.9 2.5 fusion.33
  154.7 4.4 %all-to-all-start.3 = ((bf16[4,64,1664]{2,1,0:T(8,128)(2,1)}), bf16[4,64,1664]{2,1,0:T(8,128)(2,1)}, u32[]{:S(2)}, u32[]{:S(2)}) async-start(bf16[4,64,1664]{2,1,0:T(8,128)(2,1)} %broadcast_in_dim.158), calls=%async_computation.3 | async-start | bytes 1703936 | tf_op jit(solution)/shard_map/all_to_all | solution.py:48
  160.5 10.6 %all-to-all-done.3 = bf16[4,64,1664]{2,1,0:T(8,128)(2,1)} async-done(((bf16[4,64,1664]{2,1,0:T(8,128)(2,1)}), bf16[4,64,1664]{2,1,0:T(8,128)(2,1)}, u32[]{:S(2)}, u32[]{:S(2)}) %all-to-all-start.3) | async-done | bytes 852000 | tf_op jit(solution)/shard_map/all_to_all | solution.py:48
  175.3 2.9 %fusion.11 = bf16[256,768]{1,0:T(8,128)(2,1)S(1)} fusion(bf16[256,1536]{1,0:T(8,128)(2,1)S(1)} %bitcast.74, bf16[1536,768]{1,0:T(8,128)(2,1)} %bitcast.73, f32[256,768]{1,0:T(8,128)} %copy-done.14, f32[256]{0:T(256)S(1)} %mul.337), kind=kOutput, calls=%fused_computation.24 | convolution fusion | flops 607715328 | bytes 4326400 | tf_op jit(solution)/shard_map/dot_general | solution.py:44
  181.9 2.6 convolution_add_fusion.1
  185.8 3.5 %all-to-all-start.4 = ((bf16[4,64,1536]{2,1,0:T(8,128)(2,1)}), bf16[4,64,1536]{2,1,0:T(8,128)(2,1)S(1)}, u32[]{:S(2)}, u32[]{:S(2)}) async-start(bf16[4,64,1536]{2,1,0:T(8,128)(2,1)} %bitcast.17), calls=%async_computation.4 | async-start | bytes 1572864 | tf_op jit(solution)/shard_map/all_to_all | solution.py:202
  189.3 3.8 %collective-permute-start.3 = (bf16[128,768]{1,0:T(8,128)(2,1)S(1)}, bf16[128,768]{1,0:T(8,128)(2,1)S(1)}, u32[]{:S(2)}, u32[]{:S(2)}) collective-permute-start(bf16[128,768]{1,0:T(8,128)(2,1)S(1)} %pad_maximum_fusion.2), channel_id=1, source_target_pairs={{0,4},{4,0},{1,5},{5,1},{2,6},{6,2},{3,7},{7,3},{8,12},{12,8},{9,1... | collective-permute-start | bytes 589832 | tf_op jit(solution)/shard_map/ppermute | solution.py:186
  195.0 4.4 %all-to-all-done.4 = bf16[4,64,1536]{2,1,0:T(8,128)(2,1)S(1)} async-done(((bf16[4,64,1536]{2,1,0:T(8,128)(2,1)}), bf16[4,64,1536]{2,1,0:T(8,128)(2,1)S(1)}, u32[]{:S(2)}, u32[]{:S(2)}) %all-to-all-start.4) | async-done | bytes 786464 | tf_op jit(solution)/shard_map/all_to_all | solution.py:202
  199.4 8.3 %all-to-all-start.6 = ((bf16[64,2,768]{2,1,0:T(2,128)(2,1)}), bf16[64,2,768]{2,1,0:T(2,128)(2,1)S(1)}, u32[]{:S(2)}, u32[]{:S(2)}) async-start(bf16[64,2,768]{2,1,0:T(2,128)(2,1)} %reshape.232), calls=%async_computation.6 | async-start | bytes 393216 | tf_op jit(solution)/shard_map/all_to_all | solution.py:190
  208.1 15.9 %all-to-all-done.6 = bf16[64,2,768]{2,1,0:T(2,128)(2,1)S(1)} async-done(((bf16[64,2,768]{2,1,0:T(2,128)(2,1)}), bf16[64,2,768]{2,1,0:T(2,128)(2,1)S(1)}, u32[]{:S(2)}, u32[]{:S(2)}) %all-to-all-start.6) | async-done | bytes 196640 | tf_op jit(solution)/shard_map/all_to_all | solution.py:190
  224.2 7.0 %psum.7 = bf16[2,768]{1,0:T(2,128)(2,1)S(1)} all-reduce(f32[2,768]{1,0:T(2,128)S(1)} %broadcast_multiply_fusion), channel_id=1, replica_groups=mesh['z'=16,'x'=4,'c'=2,'t'=4] {'t'}, use_global_device_ids=true, to_apply=%region_15.16 | all-reduce | flops 1536 | bytes 9216 | tf_op jit(solution)/shard_map/psum | solution.py:193
  232.0 5.2 %all-to-all-start.7 = ((bf16[64,2,768]{2,1,0:T(2,128)(2,1)}), bf16[64,2,768]{2,1,0:T(2,128)(2,1)S(1)}, u32[]{:S(2)}, u32[]{:S(2)}) async-start(bf16[64,2,768]{2,1,0:T(2,128)(2,1)} %broadcast_in_dim.165), calls=%async_computation.7 | async-start | bytes 393216 | tf_op jit(solution)/shard_map/all_to_all | solution.py:48
  238.5 15.0 %all-to-all-done.7 = bf16[64,2,768]{2,1,0:T(2,128)(2,1)S(1)} async-done(((bf16[64,2,768]{2,1,0:T(2,128)(2,1)}), bf16[64,2,768]{2,1,0:T(2,128)(2,1)S(1)}, u32[]{:S(2)}, u32[]{:S(2)}) %all-to-all-start.7) | async-done | bytes 196640 | tf_op jit(solution)/shard_map/all_to_all | solution.py:48
  254.5 3.5 %all-to-all-start.5 = ((bf16[4,64,1536]{2,1,0:T(8,128)(2,1)}), bf16[4,64,1536]{2,1,0:T(8,128)(2,1)S(1)}, u32[]{:S(2)}, u32[]{:S(2)}) async-start(bf16[4,64,1536]{2,1,0:T(8,128)(2,1)} %broadcast_in_dim.164), calls=%async_computation.5 | async-start | bytes 1572864 | tf_op jit(solution)/shard_map/all_to_all | solution.py:48
  258.1 9.3 %collective-permute-start.4 = (bf16[128,768]{1,0:T(8,128)(2,1)S(1)}, bf16[128,768]{1,0:T(8,128)(2,1)S(1)}, u32[]{:S(2)}, u32[]{:S(2)}) collective-permute-start(bf16[128,768]{1,0:T(8,128)(2,1)S(1)} %reshape.233), channel_id=1, source_target_pairs={{0,4},{4,0},{1,5},{5,1},{2,6},{6,2},{3,7},{7,3},{8,12},{12,8},{9,1... | collective-permute-start | bytes 589832 | tf_op jit(solution)/shard_map/ppermute | solution.py:195
  (116 shorter events, 31.9 us)
Async XLA Ops:
  0.6 111.7 %copy-start = (bf16[64,1536]{1,0:T(8,128)(2,1)S(1)}, bf16[64,1536]{1,0:T(8,128)(2,1)}, u32[]{:S(2)}) copy-start(bf16[64,1536]{1,0:T(8,128)(2,1)} %param.19) | copy-start | bytes 589828
  1.5 9.6 %collective-permute-start = (bf16[24,768]{1,0:T(8,128)(2,1)S(1)}, bf16[24,768]{1,0:T(8,128)(2,1)S(1)}, u32[]{:S(2)}, u32[]{:S(2)}) collective-permute-start(bf16[24,768]{1,0:T(8,128)(2,1)S(1)} %fusion.63), channel_id=1, source_target_pairs={{0,4},{4,0},{1,5},{5,1},{2,6},{6,2},{3,7},{7,3},{8,12},{12,8},{9,1... | collective-permute-start | bytes 110600 | tf_op jit(solution)/shard_map/ppermute | solution.py:73
  40.2 27.3 %all-to-all-start = ((bf16[4,384,768]{2,1,0:T(8,128)(2,1)}), bf16[4,384,768]{2,1,0:T(8,128)(2,1)S(1)}, u32[]{:S(2)}, u32[]{:S(2)}) async-start(bf16[4,384,768]{2,1,0:T(8,128)(2,1)} %broadcast_in_dim.153), calls=%async_computation | async-start | bytes 4718592 | tf_op jit(solution)/shard_map/all_to_all | solution.py:48
  67.5 2.1 copy-start.2
  69.2 5.6 %copy-start.17 = (bf16[2,3,1536]{2,0,1:T(2,128)(2,1)S(1)}, bf16[2,3,1536]{2,0,1:T(2,128)(2,1)}, u32[]{:S(2)}) copy-start(bf16[2,3,1536]{2,0,1:T(2,128)(2,1)} %param.12) | copy-start | bytes 55300
  69.2 5.7 %copy-start.1 = (bf16[256,1536]{1,0:T(8,128)(2,1)S(1)}, bf16[256,1536]{1,0:T(8,128)(2,1)}, u32[]{:S(2)}) copy-start(bf16[256,1536]{1,0:T(8,128)(2,1)} %param.10) | copy-start | bytes 2359300
  69.7 23.6 %all-to-all-start.1 = ((bf16[4,384,768]{2,1,0:T(8,128)(2,1)}), bf16[4,384,768]{2,1,0:T(8,128)(2,1)}, u32[]{:S(2)}, u32[]{:S(2)}) async-start(bf16[4,384,768]{2,1,0:T(8,128)(2,1)} %broadcast_in_dim.154), calls=%async_computation.1 | async-start | bytes 4718592 | tf_op jit(solution)/shard_map/all_to_all | solution.py:48
  77.1 37.3 %collective-permute-start.1 = (bf16[1536,768]{1,0:T(8,128)(2,1)S(1)}, bf16[1536,768]{1,0:T(8,128)(2,1)}, u32[]{:S(2)}, u32[]{:S(2)}) collective-permute-start(bf16[1536,768]{1,0:T(8,128)(2,1)S(1)} %bitcast.63), channel_id=1, source_target_pairs={{0,4},{4,0},{1,5},{5,1},{2,6},{6,2},{3,7},{7,3},{8,12},{12,8},{9,1... | collective-permute-start | bytes 7077896 | tf_op jit(solution)/shard_map/ppermute | solution.py:87
  95.2 18.3 %copy-start.13 = (bf16[16,4,24,768]{3,2,1,0:T(8,128)(2,1)}, bf16[16,4,24,768]{3,2,1,0:T(8,128)(2,1)S(1)}, u32[]{:S(2)}) copy-start(bf16[16,4,24,768]{3,2,1,0:T(8,128)(2,1)S(1)} %copy.27) | copy-start | bytes 7077892
  95.2 15.9 %copy-start.15 = (bf16[1536,64]{0,1:T(8,128)(2,1)S(1)}, bf16[1536,64]{0,1:T(8,128)(2,1)}, u32[]{:S(2)}) copy-start(bf16[1536,64]{0,1:T(8,128)(2,1)} %param.18) | copy-start | bytes 589828
  95.3 21.9 %collective-permute-start.2 = (bf16[1536,768]{1,0:T(8,128)(2,1)S(1)}, bf16[1536,768]{1,0:T(8,128)(2,1)S(1)}, u32[]{:S(2)}, u32[]{:S(2)}) collective-permute-start(bf16[1536,768]{1,0:T(8,128)(2,1)S(1)} %bitcast.70), channel_id=1, source_target_pairs={{0,4},{4,0},{1,5},{5,1},{2,6},{6,2},{3,7},{7,3},{8,12},{12,8},{9,1... | collective-permute-start | bytes 7077896 | tf_op jit(solution)/shard_map/ppermute | solution.py:89
  111.2 3.2 %copy-start.5 = (bf16[256,1536]{1,0:T(8,128)(2,1)}, bf16[256,1536]{1,0:T(8,128)(2,1)S(1)}, u32[]{:S(2)}) copy-start(bf16[256,1536]{1,0:T(8,128)(2,1)S(1)} %fusion.8) | copy-start | bytes 2359300
  112.6 0.9 copy-start.14
  117.1 0.9 copy-start.11
  117.1 1.7 copy-start.3
  121.0 4.5 %copy-start.18 = (s32[1,2]{1,0:T(1,128)S(1)}, s32[1,2]{1,0:T(1,128)}, u32[]{:S(2)}) copy-start(s32[1,2]{1,0:T(1,128)} %param.15) | copy-start | bytes 28
  121.0 25.2 %all-to-all-start.2 = ((bf16[4,128,1536]{2,1,0:T(8,128)(2,1)}), bf16[4,128,1536]{2,1,0:T(8,128)(2,1)}, u32[]{:S(2)}, u32[]{:S(2)}) async-start(bf16[4,128,1536]{2,1,0:T(8,128)(2,1)} %pad_maximum_fusion), calls=%async_computation.2 | async-start | bytes 3145728 | tf_op jit(solution)/shard_map/all_to_all | solution.py:139
  148.0 1.0 copy-start.7
  154.7 16.4 %all-to-all-start.3 = ((bf16[4,64,1664]{2,1,0:T(8,128)(2,1)}), bf16[4,64,1664]{2,1,0:T(8,128)(2,1)}, u32[]{:S(2)}, u32[]{:S(2)}) async-start(bf16[4,64,1664]{2,1,0:T(8,128)(2,1)} %broadcast_in_dim.158), calls=%async_computation.3 | async-start | bytes 1703936 | tf_op jit(solution)/shard_map/all_to_all | solution.py:48
  178.2 1.1 copy-start.9
  178.2 1.8 copy-start.4
  178.2 2.0 copy-start.12
  180.2 1.5 copy-start.6
  181.9 2.6 copy-start.16
  184.5 8.7 %copy-start.10 = (bf16[256,768]{1,0:T(8,128)(2,1)S(1)}, bf16[256,768]{1,0:T(8,128)(2,1)}, u32[]{:S(2)}) copy-start(bf16[256,768]{1,0:T(8,128)(2,1)} %copy-done.9) | copy-start | bytes 1179652
  185.8 13.6 %all-to-all-start.4 = ((bf16[4,64,1536]{2,1,0:T(8,128)(2,1)}), bf16[4,64,1536]{2,1,0:T(8,128)(2,1)S(1)}, u32[]{:S(2)}, u32[]{:S(2)}) async-start(bf16[4,64,1536]{2,1,0:T(8,128)(2,1)} %bitcast.17), calls=%async_computation.4 | async-start | bytes 1572864 | tf_op jit(solution)/shard_map/all_to_all | solution.py:202
  189.3 4.8 %collective-permute-start.3 = (bf16[128,768]{1,0:T(8,128)(2,1)S(1)}, bf16[128,768]{1,0:T(8,128)(2,1)S(1)}, u32[]{:S(2)}, u32[]{:S(2)}) collective-permute-start(bf16[128,768]{1,0:T(8,128)(2,1)S(1)} %pad_maximum_fusion.2), channel_id=1, source_target_pairs={{0,4},{4,0},{1,5},{5,1},{2,6},{6,2},{3,7},{7,3},{8,12},{12,8},{9,1... | collective-permute-start | bytes 589832 | tf_op jit(solution)/shard_map/ppermute | solution.py:186
  193.2 44.1 %copy-start.8 = (f32[128,1536]{1,0:T(8,128)S(1)}, f32[128,1536]{1,0:T(8,128)}, u32[]{:S(2)}) copy-start(f32[128,1536]{1,0:T(8,128)} %copy-done.7) | copy-start | bytes 2359300
  199.4 24.6 %all-to-all-start.6 = ((bf16[64,2,768]{2,1,0:T(2,128)(2,1)}), bf16[64,2,768]{2,1,0:T(2,128)(2,1)S(1)}, u32[]{:S(2)}, u32[]{:S(2)}) async-start(bf16[64,2,768]{2,1,0:T(2,128)(2,1)} %reshape.232), calls=%async_computation.6 | async-start | bytes 393216 | tf_op jit(solution)/shard_map/all_to_all | solution.py:190
  232.0 21.5 %all-to-all-start.7 = ((bf16[64,2,768]{2,1,0:T(2,128)(2,1)}), bf16[64,2,768]{2,1,0:T(2,128)(2,1)S(1)}, u32[]{:S(2)}, u32[]{:S(2)}) async-start(bf16[64,2,768]{2,1,0:T(2,128)(2,1)} %broadcast_in_dim.165), calls=%async_computation.7 | async-start | bytes 393216 | tf_op jit(solution)/shard_map/all_to_all | solution.py:48
  254.5 12.9 %all-to-all-start.5 = ((bf16[4,64,1536]{2,1,0:T(8,128)(2,1)}), bf16[4,64,1536]{2,1,0:T(8,128)(2,1)S(1)}, u32[]{:S(2)}, u32[]{:S(2)}) async-start(bf16[4,64,1536]{2,1,0:T(8,128)(2,1)} %broadcast_in_dim.164), calls=%async_computation.5 | async-start | bytes 1572864 | tf_op jit(solution)/shard_map/all_to_all | solution.py:48
  258.1 10.3 %collective-permute-start.4 = (bf16[128,768]{1,0:T(8,128)(2,1)S(1)}, bf16[128,768]{1,0:T(8,128)(2,1)S(1)}, u32[]{:S(2)}, u32[]{:S(2)}) collective-permute-start(bf16[128,768]{1,0:T(8,128)(2,1)S(1)} %reshape.233), channel_id=1, source_target_pairs={{0,4},{4,0},{1,5},{5,1},{2,6},{6,2},{3,7},{7,3},{8,12},{12,8},{9,1... | collective-permute-start | bytes 589832 | tf_op jit(solution)/shard_map/ppermute | solution.py:195

commit v3 on v2

--- a/solution.py
+++ b/solution.py
@@ -15,7 +15,6 @@
 F32 = jnp.float32
 DP = ("z", "x", "c")
 CHIPS = ("z", "x")
-LANES = 128
 SWAP = [(0, 1), (1, 0)]
 
 
@@ -68,24 +67,22 @@
     thin, hidden = up_rows.shape
     half = hidden // n_c
 
-    both = jnp.concatenate([up_rows, down_rows], axis=0)
-    keep = lax.dynamic_slice_in_dim(both, core * half, half, axis=1)
-    got = lax.ppermute(lax.dynamic_slice_in_dim(both, (1 - core) * half, half, axis=1), "c", SWAP)
-    first = jnp.where(core == 0, keep, got)
-    second = jnp.where(core == 0, got, keep)
-    up_pair = jnp.concatenate([first[:thin], second[:thin]], axis=0)
-    down_pair = jnp.concatenate([first[thin:], second[thin:]], axis=0)
-
-    def whole(line):
-        rows = spread(line, "x", n_x).reshape(n_x, n_z, n_c * thin, half)
-        return rows.transpose(1, 0, 2, 3).reshape(width, half)
-
+    down_split = down_rows.reshape(thin, n_c, half).transpose(1, 0, 2)
+    down_sent = jnp.broadcast_to(down_split[None], (n_x, n_c, thin, half)).reshape(n_x * n_c, thin, half)
+    down_near = lax.all_to_all(down_sent, ("x", "c"), 0, 0, tiled=True)
+    down_own = lax.all_gather(down_near.reshape(n_x * n_c * thin, half), "z", axis=0, tiled=True)
+
+    up_rows, down_near = lax.optimization_barrier((up_rows, down_near))
+    up_keep = lax.dynamic_slice_in_dim(up_rows, core * half, half, axis=1)
+    up_give = lax.dynamic_slice_in_dim(up_rows, (1 - core) * half, half, axis=1)
+    up_got = lax.ppermute(up_give, "c", SWAP)
+    up_pair = jnp.where(
+        core == 0, jnp.concatenate([up_keep, up_got], 0), jnp.concatenate([up_got, up_keep], 0)
+    )
     up_line = lax.all_gather(up_pair, "z", axis=0, tiled=True)
-    down_pair, up_line = lax.optimization_barrier((down_pair, up_line))
-    down_line = lax.all_gather(down_pair, "z", axis=0, tiled=True)
-    up_own = whole(up_line)
+    up_all = spread(up_line, "x", n_x).reshape(n_x, n_z, n_c * thin, half)
+    up_own = up_all.transpose(1, 0, 2, 3).reshape(width, half)
     up_other = lax.ppermute(up_own, "c", SWAP)
-    down_own = whole(down_line)
     down_other = lax.ppermute(down_own, "c", SWAP)
 
     count = live_block_count[0]
@@ -127,17 +124,12 @@
     pol_own, ref_own, slope_own = activate(up_own, factor_own)
     pol_other, ref_other, slope_other = activate(up_other, factor_other)
 
-    part_pol = rows_by_rows(pol_own, down_own) + rows_by_rows(pol_other, down_other)
-    part_ref = rows_by_rows(ref_own, down_own) + rows_by_rows(ref_other, down_other)
-    parts = jnp.concatenate(
-        [
-            part_pol.astype(BF16).reshape(CAP, BLK, width),
-            part_ref.astype(BF16).reshape(CAP, BLK, width),
-        ],
-        axis=1,
-    )
-    parts = lax.all_to_all(parts, "t", 0, 0, tiled=True)
-    sums = jnp.sum(parts.astype(F32), axis=0)
+    part_ref = (rows_by_rows(ref_own, down_own) + rows_by_rows(ref_other, down_other)).astype(BF16)
+    part_ref, pol_other = lax.optimization_barrier((part_ref, pol_other))
+    sum_ref = lax.psum_scatter(part_ref, "t", scatter_dimension=0, tiled=True).astype(F32)
+    part_pol = (rows_by_rows(pol_own, down_own) + rows_by_rows(pol_other, down_other)).astype(BF16)
+    sum_pol = lax.all_to_all(part_pol.reshape(CAP, BLK, width), "t", 0, 0, tiled=True)
+    sum_pol = jnp.sum(sum_pol.astype(F32), axis=0)
 
     flag = (group >= wins).astype(jnp.int32)
     x_own = lax.dynamic_slice_in_dim(tokens, group * BLK, BLK, axis=0)
@@ -147,50 +139,63 @@
     mask = (jnp.arange(BLK, dtype=jnp.int32)[:, None] < live_own[None, :]).astype(F32)
     gate = vec_own[2][None]
     base = x_own.astype(F32) - t_own
-    miss_pol = base + gate * sums[:BLK]
-    miss_ref = base + gate * sums[BLK:]
+    miss_pol = base + gate * sum_pol
+    grad_unit = 2.0 * mask * miss_pol
+    dy = spread((gate * grad_unit).astype(BF16), "t", n_t).reshape(CAP * BLK, width)
+
+    dpre_own = (product(dy, down_own) * slope_own).astype(BF16)
+    dpre_other = (product(dy, down_other) * slope_other).astype(BF16)
+    dlow_part = (rows_by_rows(factor_own, dpre_own) + rows_by_rows(factor_other, dpre_other)).astype(BF16)
+    rank = dlow_part.shape[0]
+
+    miss_ref = base + gate * sum_ref
     excess = jnp.sum(mask * (miss_pol - miss_ref) * (miss_pol + miss_ref))
-    grad_unit = 2.0 * mask * miss_pol
-    dy_unit = (gate * grad_unit).astype(BF16)
     high = excess.astype(BF16)
     rest = excess - high.astype(F32)
     middle = rest.astype(BF16)
     lowest = (rest - middle.astype(F32)).astype(BF16)
-    lane = lax.broadcasted_iota(jnp.int32, (BLK, LANES), 1)
+    lane = lax.broadcasted_iota(jnp.int32, (16, CAP * BLK), 1)
     note = jnp.where(lane == 0, high, jnp.where(lane == 1, middle, lowest))
-    shared = spread(jnp.concatenate([dy_unit, note], 1), "t", n_t)
-    dy = shared[:, :, :width].reshape(CAP * BLK, width)
-    excesses = jnp.sum(shared[:, 0, width : width + 3].astype(F32), axis=1)
+    shared = spread(jnp.concatenate([dlow_part, note], 0), "t", n_t)
+
+    dm_part = (
+        rows_by_rows(dpre_own, up_own)
+        + rows_by_rows(dpre_other, up_other)
+        + lax.dot_general(dlow_part, factor_in, (((0,), (1,)), ((), ())), preferred_element_type=F32)
+    ).astype(BF16)
+    dm_sum = lax.psum_scatter(dm_part, "t", scatter_dimension=0, tiled=True).astype(F32)
+
+    row_flags = jnp.broadcast_to(flags[:, None], (CAP, BLK)).reshape(CAP * BLK, 1)
+    low_split = jnp.concatenate(
+        [jnp.where(row_flags == 0, low, jnp.zeros_like(low)), jnp.where(row_flags == 1, low, jnp.zeros_like(low))], 1
+    )
+    b_own = columns_by_columns(low_split, dpre_own)
+    b_other = columns_by_columns(low_split, dpre_other)
+
+    excesses = jnp.sum(shared[:, rank, :3].astype(F32), axis=1)
     gap_first = jnp.sum(jnp.where(flags == 0, excesses, 0.0)) * scale_first
     gap_second = jnp.sum(jnp.where(flags == 1, excesses, 0.0)) * scale_second
     inside = -BETA * (gap_first - gap_second)
     losses = jax.nn.softplus(-inside)[None]
     weight = BETA * LOSS_SCALE * jax.nn.sigmoid(-inside)
-    coef = jnp.where(flags == 0, weight * scale_first, -weight * scale_second)
-    coef_rows = jnp.broadcast_to(coef[:, None], (CAP, BLK)).reshape(CAP * BLK, 1)
-    coef_own = jnp.where(flag == 0, weight * scale_first, -weight * scale_second)
-
-    dpre_own = (product(dy, down_own) * coef_rows * slope_own).astype(BF16)
-    dpre_other = (product(dy, down_other) * coef_rows * slope_other).astype(BF16)
-    dlow = (rows_by_rows(dpre_own, factor_own) + rows_by_rows(dpre_other, factor_other)).astype(BF16)
-    dm_part = (
-        rows_by_rows(dpre_own, up_own) + rows_by_rows(dpre_other, up_other) + rows_by_rows(dlow, factor_in)
-    ).astype(BF16)
-    grad_a = columns_by_columns(dlow, modded)
-    b_own = columns_by_columns(low, dpre_own)
-    b_other = columns_by_columns(low, dpre_other)
-    rank = grad_a.shape[0]
+    coef_first = weight * scale_first
+    coef_second = -weight * scale_second
+    coef_rows = jnp.where(row_flags.reshape(1, CAP * BLK) == 0, coef_first, coef_second)
+    coef_own = jnp.where(flag == 0, coef_first, coef_second)
+
+    dlow = (jnp.sum(shared[:, :rank].astype(F32), axis=0) * coef_rows).astype(BF16)
+    grad_a = product(dlow, modded)
     middle_column = width // n_c
     a_own = lax.dynamic_slice_in_dim(grad_a, core * middle_column, middle_column, axis=1)
     a_other = lax.dynamic_slice_in_dim(grad_a, (1 - core) * middle_column, middle_column, axis=1)
+    b_own = coef_first * b_own[:rank] + coef_second * b_own[rank:]
+    b_other = coef_first * b_other[:rank] + coef_second * b_other[rank:]
     given = lax.ppermute(jnp.concatenate([b_other, a_other], 0).astype(BF16), "c", SWAP)
     pile = (jnp.concatenate([b_own, a_own], 0) + given.astype(F32)).astype(BF16)
 
     chips = n_z * n_x
     pieces = lax.all_to_all(pile.reshape(chips, 2 * rank // chips, half), CHIPS, 0, 0, tiled=True)
-    total = jnp.sum(pieces.astype(F32), axis=0) / n_dp
-    place = lax.axis_index("z") * n_x + lax.axis_index("x")
-    total = jnp.where(place < chips // 2, total, lax.psum(total, "t")).astype(BF16)
+    total = (jnp.sum(pieces.astype(F32), axis=0) / n_dp).astype(BF16)
     mine = spread(total, CHIPS, chips).reshape(2 * rank, half)
     theirs = lax.ppermute(mine, "c", SWAP)
     ends = jnp.concatenate([mine, theirs], 1)
@@ -199,14 +204,19 @@
     sum_b = ends[:rank]
     sum_a = ends[rank:].T
 
-    back = lax.all_to_all(dm_part.reshape(CAP, BLK, width), "t", 0, 0, tiled=True)
-    back = jnp.sum(back.astype(F32), axis=0)
     normed_own, inverse_own = normalise(x_own)
-    dn = back * (1.0 + vec_own[1][None])
+    dn = dm_sum * (1.0 + vec_own[1][None])
     mean_one = jnp.mean(dn, axis=-1, keepdims=True)
     mean_two = jnp.mean(dn * normed_own, axis=-1, keepdims=True)
-    grad_block = coef_own * grad_unit + inverse_own * (dn - mean_one - normed_own * mean_two)
-    grad_tokens = spread(grad_block.astype(BF16), "t", n_t).reshape(CAP * BLK, width)
+    grad_block = coef_own * (grad_unit + inverse_own * (dn - mean_one - normed_own * mean_two))
+    grad_block = grad_block.astype(BF16)
+    blocks = [grad_block]
+    for step in range(1, n_t):
+        blocks.append(lax.ppermute(grad_block, "t", [(i, (i + step) % n_t) for i in range(n_t)]))
+    blocks = jnp.stack(blocks)
+    grad_tokens = jnp.concatenate(
+        [lax.dynamic_index_in_dim(blocks, (group - slot) % n_t, 0, False) for slot in range(n_t)], 0
+    )
     return losses, grad_tokens, sum_a, sum_b
 
 

time: 277 us -> 312 us (1.13); the launches traced: 271 us -> 310 us
  waiting for transfers between devices: 64 us -> 105 us
  starting transfers between devices: 91 us -> 72.5 us
  between operations: 7.91 us -> 21.4 us
  matrix products: 17.2 us -> 29.1 us
  blocking collectives: 56.8 us -> 47 us
    reduce_scatter x0 -> x2, waiting for transfers between devices: none -> 35.4 us  [the longest x1 33.4 us: per_device(): lax.psum_scatter(dm_part, 't', scatter_dimension=0, tiled=True).astype(F32)]
    all_gather x1 -> x0, blocking collectives: 23.3 us -> none  [per_device(): down_line = lax.all_gather(down_pair, 'z', axis=0, tiled=True)]
    all_to_all x0 -> x1, blocking collectives: none -> 15.2 us  [per_device(): down_near = lax.all_to_all(down_sent, ('x', 'c'), 0, 0, tiled=True)]
    ppermute x1, starting transfers between devices: 15.2 us -> 1.91 us  [per_device(): down_other = lax.ppermute(down_own, 'c', SWAP)]
    all_to_all x2 -> x1, waiting for transfers between devices: 19.8 us -> 8.85 us  [per_device(): lax.all_to_all(part_pol.reshape(CAP, BLK, width), 't', 0, 0, tiled=True)]
    all_to_all x5 -> x4, waiting for transfers between devices: 25.6 us -> 34.3 us  [spread(): lax.all_to_all(jnp.broadcast_to(value[None], (n, *value.shape)), axes, 0,...]
    all_to_all x1, starting transfers between devices: 8.28 us -> 15.3 us  [per_device(): lax.all_to_all(pile.reshape(chips, 2 * rank // chips, half), CHIPS, 0, 0,...]
    psum x1 -> x0, blocking collectives: 6.97 us -> none  [per_device(): lax.psum(total, 't')]
  transfers between devices with their start and end apart: 13 -> 17, of which waited for: 8 -> 13; matrix products, arithmetic and copies ran while one was open for 7% -> 14% of each run, Pallas kernels for 0% -> 0%
where the time goes in v3:
time: 312 us; the launch traced here: 310 us
  waiting for transfers between devices  105 us (34%)
  starting transfers between devices  72.5 us (23%)
  blocking collectives  47 us (15%)
  matrix products  29.1 us (9%)
  between operations  21.4 us (7%)
  other arithmetic  18.4 us (6%)
  local copies, waits for them, and re-layouts  17.3 us (6%)
    all_to_all x4, waiting for transfers between devices, spread(): lax.all_to_all(jnp.broadcast_to(value[None], (n, *value.shape)), axes, 0,...  34.3 us
    reduce_scatter x1, waiting for transfers between devices, per_device(): lax.psum_scatter(dm_part, 't', scatter_dimension=0, tiled=True).astype(F32)  33.4 us
    all_gather x1, blocking collectives, per_device(): up_line = lax.all_gather(up_pair, 'z', axis=0, tiled=True)  31.9 us
    all_to_all x4, starting transfers between devices, spread(): lax.all_to_all(jnp.broadcast_to(value[None], (n, *value.shape)), axes, 0,...  17.8 us
    all_to_all x1, waiting for transfers between devices, per_device(): lax.all_to_all(pile.reshape(chips, 2 * rank // chips, half), CHIPS, 0, 0,...  17.5 us
    all_to_all x1, starting transfers between devices, per_device(): lax.all_to_all(pile.reshape(chips, 2 * rank // chips, half), CHIPS, 0, 0,...  15.3 us
    all_to_all x1, blocking collectives, per_device(): down_near = lax.all_to_all(down_sent, ('x', 'c'), 0, 0, tiled=True)  15.2 us
    dot_general x8, matrix products, rows_by_rows(): lax.dot_general(left, right, (((1,), (1,)), ((), ())), preferred_element_...  14.1 us
  transfers between devices with their start and end apart: 17, of which 13 were waited for; matrix products, arithmetic and copies ran while one was open for 14% of the time, Pallas kernels for 0%

profile of v3, /device:TPU:1, one launch (start us, length us, event | category | flops | bytes accessed | tf_op | source)
XLA Modules:
  0.0 310.4 jit_solution(4341786213150913987)
XLA Ops:
  8.1 15.2 %all_to_all.35 = bf16[8,12,768]{2,1,0:T(8,128)(2,1)S(1)} all-to-all(bf16[8,12,768]{2,1,0:T(8,128)(2,1)S(1)} %bitcast.73), channel_id=1, replica_groups=mesh['z'=16,'x'=4,'c'=2,'t'=4] {'x','c'}, dimensions={0} | all-to-all | bytes 294912 | tf_op jit(solution)/shard_map/all_to_all | solution.py:72
  24.8 2.8 collective-permute-start
  28.5 31.9 %all_gather.6 = bf16[384,768]{1,0:T(8,128)(2,1)S(1)} all-gather(bf16[24,768]{1,0:T(8,128)(2,1)S(1)} %maximum_select_fusion.1), channel_id=1, replica_groups=mesh['z'=16,'x'=4,'c'=2,'t'=4] {'z'}, dimensions={0}, use_global_device_ids=true | all-gather | bytes 626688 | tf_op jit(solution)/shard_map/all_gather | solution.py:82
  62.0 3.8 %all-to-all-start.1 = ((bf16[4,384,768]{2,1,0:T(8,128)(2,1)}), bf16[4,384,768]{2,1,0:T(8,128)(2,1)S(1)}, u32[]{:S(2)}, u32[]{:S(2)}) async-start(bf16[4,384,768]{2,1,0:T(8,128)(2,1)} %broadcast_in_dim.169), calls=%async_computation.1 | async-start | bytes 4718592 | tf_op jit(solution)/shard_map/all_to_all | solution.py:47
  67.7 20.8 %all-to-all-done.1 = bf16[4,384,768]{2,1,0:T(8,128)(2,1)S(1)} async-done(((bf16[4,384,768]{2,1,0:T(8,128)(2,1)}), bf16[4,384,768]{2,1,0:T(8,128)(2,1)S(1)}, u32[]{:S(2)}, u32[]{:S(2)}) %all-to-all-start.1) | async-done | bytes 2359328 | tf_op jit(solution)/shard_map/all_to_all | solution.py:47
  91.9 9.2 %collective-permute-start.1 = (bf16[1536,768]{1,0:T(8,128)(2,1)S(1)}, bf16[1536,768]{1,0:T(8,128)(2,1)}, u32[]{:S(2)}, u32[]{:S(2)}) collective-permute-start(bf16[1536,768]{1,0:T(8,128)(2,1)S(1)} %bitcast.67), channel_id=1, source_target_pairs={{0,4},{4,0},{1,5},{5,1},{2,6},{6,2},{3,7},{7,3},{8,12},{12,8},{9,1... | collective-permute-start | bytes 7077896 | tf_op jit(solution)/shard_map/ppermute | solution.py:85
  104.4 2.5 select_reduce_fusion
  114.9 2.7 fusion.88
  119.9 2.1 fusion.33
  122.0 3.4 %fusion.1 = bf16[256,1536]{1,0:T(8,128)(2,1)} fusion(f32[256,1536]{1,0:T(8,128)S(1)} %fusion.35, bf16[1536,768]{1,0:T(8,128)(2,1)} %collective-permute-done.2, f32[256,768]{1,0:T(8,128)S(1)} %fusion.88), kind=kOutput, calls=%fused_computation.5 | convolution fusion | flops 606535680 | bytes 5505024 | tf_op jit(solution)/shard_map/dot_general | solution.py:35
  125.4 3.9 %fusion.2 = bf16[256,1536]{1,0:T(8,128)(2,1)} fusion(f32[256,1536]{1,0:T(8,128)} %fusion.33, bf16[256,768]{1,0:T(8,128)(2,1)} %get-tuple-element.8, bf16[1536,768]{1,0:T(8,128)(2,1)} %collective-permute-done.2), kind=kOutput, calls=%fused_computation.6 | convolution fusion | flops 604766208 | bytes 5111808 | tf_op jit(solution)/shard_map/dot_general | solution.py:35
  129.3 4.9 %all-to-all-start.2 = ((bf16[4,64,1536]{2,1,0:T(8,128)(2,1)}), bf16[4,64,1536]{2,1,0:T(8,128)(2,1)}, u32[]{:S(2)}, u32[]{:S(2)}) async-start(bf16[4,64,1536]{2,1,0:T(8,128)(2,1)} %bitcast.71), calls=%async_computation.2 | async-start | bytes 1572864 | tf_op jit(solution)/shard_map/all_to_all | solution.py:131
  137.0 8.8 %all-to-all-done.2 = bf16[4,64,1536]{2,1,0:T(8,128)(2,1)} async-done(((bf16[4,64,1536]{2,1,0:T(8,128)(2,1)}), bf16[4,64,1536]{2,1,0:T(8,128)(2,1)}, u32[]{:S(2)}, u32[]{:S(2)}) %all-to-all-start.2) | async-done | bytes 786464 | tf_op jit(solution)/shard_map/all_to_all | solution.py:131
  150.8 4.2 %all-to-all-start.3 = ((bf16[4,64,1536]{2,1,0:T(8,128)(2,1)}), bf16[4,64,1536]{2,1,0:T(8,128)(2,1)}, u32[]{:S(2)}, u32[]{:S(2)}) async-start(bf16[4,64,1536]{2,1,0:T(8,128)(2,1)} %broadcast_in_dim.170), calls=%async_computation.3 | async-start | bytes 1572864 | tf_op jit(solution)/shard_map/all_to_all | solution.py:47
  155.8 9.6 %all-to-all-done.3 = bf16[4,64,1536]{2,1,0:T(8,128)(2,1)} async-done(((bf16[4,64,1536]{2,1,0:T(8,128)(2,1)}), bf16[4,64,1536]{2,1,0:T(8,128)(2,1)}, u32[]{:S(2)}, u32[]{:S(2)}) %all-to-all-start.3) | async-done | bytes 786464 | tf_op jit(solution)/shard_map/all_to_all | solution.py:47
  165.4 3.1 %fusion.9 = bf16[256,768]{1,0:T(8,128)(2,1)S(1)} fusion(bf16[256,1536]{1,0:T(8,128)(2,1)} %bitcast.13, bf16[1536,768]{1,0:T(8,128)(2,1)} %all-gather.2.cloned.1.call-done, f32[256,768]{1,0:T(8,128)} %copy-done.13), kind=kOutput, calls=%fused_computation.20 | convolution fusion | flops 607518720 | bytes 4325376 | tf_op jit(solution)/shard_map/dot_general | solution.py:43
  168.8 2.9 fusion.10
  172.9 2.5 convolution_add_fusion.1
  181.2 33.4 %reduce-scatter.5.cloned.1.call-done = bf16[64,1536]{1,0:T(8,128)(2,1)} async-done(((bf16[256,1536]{1,0:T(8,128)(2,1)}), bf16[64,1536]{1,0:T(8,128)(2,1)}) %reduce-scatter.5.cloned.1.call-update) | async-done | bytes 196624 | tf_op jit(solution)/shard_map/reduce_scatter | solution.py:166
  214.6 2.1 fusion.26
  218.8 3.5 %all-to-all-start.4 = ((bf16[4,80,256]{2,1,0:T(8,128)(2,1)}), bf16[4,80,256]{2,1,0:T(8,128)(2,1)S(1)}, u32[]{:S(2)}, u32[]{:S(2)}) async-start(bf16[4,80,256]{2,1,0:T(8,128)(2,1)} %broadcast_in_dim.174), calls=%async_computation.5 | async-start | bytes 327680 | tf_op jit(solution)/shard_map/all_to_all | solution.py:47
  223.3 3.8 %all-to-all-done.4 = bf16[4,80,256]{2,1,0:T(8,128)(2,1)S(1)} async-done(((bf16[4,80,256]{2,1,0:T(8,128)(2,1)}), bf16[4,80,256]{2,1,0:T(8,128)(2,1)S(1)}, u32[]{:S(2)}, u32[]{:S(2)}) %all-to-all-start.4) | async-done | bytes 163872 | tf_op jit(solution)/shard_map/all_to_all | solution.py:47
  230.4 5.0 %collective-permute-start.6 = (bf16[128,768]{1,0:T(8,128)(2,1)S(1)}, bf16[128,768]{1,0:T(8,128)(2,1)S(1)}, u32[]{:S(2)}, u32[]{:S(2)}) collective-permute-start(bf16[128,768]{1,0:T(8,128)(2,1)S(1)} %pad_maximum_fusion.2), channel_id=1, source_target_pairs={{0,4},{4,0},{1,5},{5,1},{2,6},{6,2},{3,7},{7,3},{8,12},{12,8},{9,1... | collective-permute-start | bytes 589832 | tf_op jit(solution)/shard_map/ppermute | solution.py:193
  237.2 15.3 %all-to-all-start.5 = ((bf16[64,2,768]{2,1,0:T(2,128)(2,1)}), bf16[64,2,768]{2,1,0:T(2,128)(2,1)S(1)}, u32[]{:S(2)}, u32[]{:S(2)}) async-start(bf16[64,2,768]{2,1,0:T(2,128)(2,1)} %reshape.251), calls=%async_computation.7 | async-start | bytes 393216 | tf_op jit(solution)/shard_map/all_to_all | solution.py:197
  252.5 17.5 %all-to-all-done.5 = bf16[64,2,768]{2,1,0:T(2,128)(2,1)S(1)} async-done(((bf16[64,2,768]{2,1,0:T(2,128)(2,1)}), bf16[64,2,768]{2,1,0:T(2,128)(2,1)S(1)}, u32[]{:S(2)}, u32[]{:S(2)}) %all-to-all-start.5) | async-done | bytes 196640 | tf_op jit(solution)/shard_map/all_to_all | solution.py:197
  271.1 6.3 %all-to-all-start.6 = ((bf16[64,2,768]{2,1,0:T(2,128)(2,1)}), bf16[64,2,768]{2,1,0:T(2,128)(2,1)S(1)}, u32[]{:S(2)}, u32[]{:S(2)}) async-start(bf16[64,2,768]{2,1,0:T(2,128)(2,1)} %broadcast_in_dim.183), calls=%async_computation.8 | async-start | bytes 393216 | tf_op jit(solution)/shard_map/all_to_all | solution.py:47
  278.7 2.2 collective-permute-start.3
  280.9 3.7 %collective-permute-start.4 = (bf16[64,1536]{1,0:T(8,128)(2,1)S(1)}, bf16[64,1536]{1,0:T(8,128)(2,1)S(1)}, u32[]{:S(2)}, u32[]{:S(2)}) collective-permute-start(bf16[64,1536]{1,0:T(8,128)(2,1)S(1)} %fusion.31), channel_id=1, source_target_pairs={{0,2},{1,3},{2,0},{3,1},{4,6},{5,7},{6,4},{7,5},{8,10},{9,11},{10,... | collective-permute-start | bytes 589832 | tf_op jit(solution)/shard_map/ppermute | solution.py:215
  284.6 2.5 collective-permute-start.5
  287.3 3.7 %collective-permute-done.4 = bf16[64,1536]{1,0:T(8,128)(2,1)S(1)} collective-permute-done((bf16[64,1536]{1,0:T(8,128)(2,1)S(1)}, bf16[64,1536]{1,0:T(8,128)(2,1)S(1)}, u32[]{:S(2)}, u32[]{:S(2)}) %collective-permute-start.4) | collective-permute-done | bytes 196640 | tf_op jit(solution)/shard_map/ppermute | solution.py:215
  291.0 2.2 collective-permute-done.5
  293.5 7.1 %collective-permute-start.7 = (bf16[128,768]{1,0:T(8,128)(2,1)S(1)}, bf16[128,768]{1,0:T(8,128)(2,1)S(1)}, u32[]{:S(2)}, u32[]{:S(2)}) collective-permute-start(bf16[128,768]{1,0:T(8,128)(2,1)S(1)} %reshape.252), channel_id=1, source_target_pairs={{0,4},{4,0},{1,5},{5,1},{2,6},{6,2},{3,7},{7,3},{8,12},{12,8},{9,1... | collective-permute-start | bytes 589832 | tf_op jit(solution)/shard_map/ppermute | solution.py:200
  (156 shorter events, 46.3 us)
Async XLA Ops:
  7.2 107.3 %copy-start = (bf16[64,1536]{1,0:T(8,128)(2,1)S(1)}, bf16[64,1536]{1,0:T(8,128)(2,1)}, u32[]{:S(2)}) copy-start(bf16[64,1536]{1,0:T(8,128)(2,1)} %param.19) | copy-start | bytes 589828
  7.2 95.3 %all-gather.2.cloned.1.call-start = ((), (), s32[]{:S(2)}) async-start(), calls=%async_computation.9 | async-start | bytes 2506752 | tf_op jit(solution)/shard_map/all_gather | solution.py:73
  24.8 3.7 %collective-permute-start = (bf16[12,768]{1,0:T(8,128)(2,1)S(1)}, bf16[12,768]{1,0:T(8,128)(2,1)S(1)}, u32[]{:S(2)}, u32[]{:S(2)}) collective-permute-start(bf16[12,768]{1,0:T(8,128)(2,1)S(1)} %get-tuple-element.33), channel_id=1, source_target_pairs={{0,4},{4,0},{1,5},{5,1},{2,6},{6,2},{3,7},{7,3},{8,12},{12,8},{9,1... | collective-permute-start | bytes 55304 | tf_op jit(solution)/shard_map/ppermute | solution.py:78
  62.0 26.5 %all-to-all-start.1 = ((bf16[4,384,768]{2,1,0:T(8,128)(2,1)}), bf16[4,384,768]{2,1,0:T(8,128)(2,1)S(1)}, u32[]{:S(2)}, u32[]{:S(2)}) async-start(bf16[4,384,768]{2,1,0:T(8,128)(2,1)} %broadcast_in_dim.169), calls=%async_computation.1 | async-start | bytes 4718592 | tf_op jit(solution)/shard_map/all_to_all | solution.py:47
  66.4 34.8 %copy-start.19 = (f32[2,3,1536]{2,0,1:T(2,128)}, f32[2,3,1536]{2,0,1:T(2,128)S(1)}, u32[]{:S(2)}) copy-start(f32[2,3,1536]{2,0,1:T(2,128)S(1)} %convert_element_type.143) | copy-start | bytes 110596
  91.9 22.9 %collective-permute-start.1 = (bf16[1536,768]{1,0:T(8,128)(2,1)S(1)}, bf16[1536,768]{1,0:T(8,128)(2,1)}, u32[]{:S(2)}, u32[]{:S(2)}) collective-permute-start(bf16[1536,768]{1,0:T(8,128)(2,1)S(1)} %bitcast.67), channel_id=1, source_target_pairs={{0,4},{4,0},{1,5},{5,1},{2,6},{6,2},{3,7},{7,3},{8,12},{12,8},{9,1... | collective-permute-start | bytes 7077896 | tf_op jit(solution)/shard_map/ppermute | solution.py:85
  102.5 19.5 %collective-permute-start.2 = (bf16[1536,768]{1,0:T(8,128)(2,1)}, bf16[1536,768]{1,0:T(8,128)(2,1)}, u32[]{:S(2)}, u32[]{:S(2)}) collective-permute-start(bf16[1536,768]{1,0:T(8,128)(2,1)} %all-gather.2.cloned.1.call-done), channel_id=1, source_target_pairs={{0,4},{4,0},{1,5},{5,1},{2,6},{6,2},{3,7},{7,3},{8,12},{12,8},{9,1... | collective-permute-start | bytes 7077896 | tf_op jit(solution)/shard_map/ppermute | solution.py:86
  129.3 16.5 %all-to-all-start.2 = ((bf16[4,64,1536]{2,1,0:T(8,128)(2,1)}), bf16[4,64,1536]{2,1,0:T(8,128)(2,1)}, u32[]{:S(2)}, u32[]{:S(2)}) async-start(bf16[4,64,1536]{2,1,0:T(8,128)(2,1)} %bitcast.71), calls=%async_computation.2 | async-start | bytes 1572864 | tf_op jit(solution)/shard_map/all_to_all | solution.py:131
  150.8 14.6 %all-to-all-start.3 = ((bf16[4,64,1536]{2,1,0:T(8,128)(2,1)}), bf16[4,64,1536]{2,1,0:T(8,128)(2,1)}, u32[]{:S(2)}, u32[]{:S(2)}) async-start(bf16[4,64,1536]{2,1,0:T(8,128)(2,1)} %broadcast_in_dim.170), calls=%async_computation.3 | async-start | bytes 1572864 | tf_op jit(solution)/shard_map/all_to_all | solution.py:47
  155.0 26.2 %reduce-scatter.3.cloned.1.call-start = ((), (), s32[]{:S(2)}) async-start(), calls=%async_computation.10 | async-start | bytes 983040 | tf_op jit(solution)/shard_map/reduce_scatter | solution.py:129
  155.7 58.9 %reduce-scatter.5.cloned.1.call-start = ((), (), s32[]{:S(2)}) async-start(), calls=%async_computation.11 | async-start | bytes 983040 | tf_op jit(solution)/shard_map/reduce_scatter | solution.py:166
  175.5 39.1 %copy-start.6 = (f32[64,1536]{1,0:T(8,128)S(1)}, f32[64,1536]{1,0:T(8,128)}, u32[]{:S(2)}) copy-start(f32[64,1536]{1,0:T(8,128)} %copy-done.5) | copy-start | bytes 1179652
  175.5 39.1 %copy-start.21 = (f32[64]{0:T(128)S(1)}, f32[64]{0:T(128)}, u32[]{:S(2)}) copy-start(f32[64]{0:T(128)} %get-tuple-element.46) | copy-start | bytes 772
  176.8 41.4 %copy-start.15 = (bf16[64,256]{1,0:T(8,128)(2,1)S(1)}, bf16[64,256]{1,0:T(8,128)(2,1)}, u32[]{:S(2)}) copy-start(bf16[64,256]{1,0:T(8,128)(2,1)} %copy-done.14) | copy-start | bytes 98308
  176.8 45.6 %copy-start.8 = (bf16[256,768]{1,0:T(8,128)(2,1)S(1)}, bf16[256,768]{1,0:T(8,128)(2,1)}, u32[]{:S(2)}) copy-start(bf16[256,768]{1,0:T(8,128)(2,1)} %copy-done.7) | copy-start | bytes 1179652
  176.8 45.6 %copy-start.17 = (bf16[256,64]{0,1:T(8,128)(2,1)S(1)}, bf16[256,64]{0,1:T(8,128)(2,1)}, u32[]{:S(2)}) copy-start(bf16[256,64]{0,1:T(8,128)(2,1)} %get-tuple-element.34) | copy-start | bytes 98308
  178.9 39.2 %copy-start.24 = (f32[64]{0:T(128)}, f32[64]{0:T(128)S(1)}, u32[]{:S(2)}) copy-start(f32[64]{0:T(128)S(1)} %add_rsqrt_fusion.1) | copy-start | bytes 772
  179.2 50.8 %copy-start.4 = (bf16[256,1536]{1,0:T(8,128)(2,1)S(1)}, bf16[256,1536]{1,0:T(8,128)(2,1)}, u32[]{:S(2)}) copy-start(bf16[256,1536]{1,0:T(8,128)(2,1)} %copy-done.3) | copy-start | bytes 2359300
  218.8 8.3 %all-to-all-start.4 = ((bf16[4,80,256]{2,1,0:T(8,128)(2,1)}), bf16[4,80,256]{2,1,0:T(8,128)(2,1)S(1)}, u32[]{:S(2)}, u32[]{:S(2)}) async-start(bf16[4,80,256]{2,1,0:T(8,128)(2,1)} %broadcast_in_dim.174), calls=%async_computation.5 | async-start | bytes 327680 | tf_op jit(solution)/shard_map/all_to_all | solution.py:47
  230.2 22.2 %copy-start.29 = (f32[64]{0:T(128)S(1)}, f32[64]{0:T(128)}, u32[]{:S(2)}) copy-start(f32[64]{0:T(128)} %get-tuple-element.10) | copy-start | bytes 772
  230.3 22.2 %copy-start.28 = (f32[64]{0:T(128)S(1)}, f32[64]{0:T(128)}, u32[]{:S(2)}) copy-start(f32[64]{0:T(128)} %get-tuple-element.12) | copy-start | bytes 772
  230.3 47.0 %copy-start.12 = (bf16[64,1536]{1,0:T(8,128)(2,1)S(1)}, bf16[64,1536]{1,0:T(8,128)(2,1)}, u32[]{:S(2)}) copy-start(bf16[64,1536]{1,0:T(8,128)(2,1)} %reduce-scatter.5.cloned.1.call-done) | copy-start | bytes 589828
  230.3 47.0 %copy-start.22 = (f32[64]{0:T(128)S(1)}, f32[64]{0:T(128)}, u32[]{:S(2)}) copy-start(f32[64]{0:T(128)} %get-tuple-element.46) | copy-start | bytes 772
  230.3 47.0 %copy-start.23 = (f32[64]{0:T(128)S(1)}, f32[64]{0:T(128)}, u32[]{:S(2)}) copy-start(f32[64]{0:T(128)} %get-tuple-element.45) | copy-start | bytes 772
  230.4 47.0 %copy-start.25 = (f32[64]{0:T(128)S(1)}, f32[64]{0:T(128)}, u32[]{:S(2)}) copy-start(f32[64]{0:T(128)} %copy-done.24) | copy-start | bytes 772
  230.4 6.0 %collective-permute-start.6 = (bf16[128,768]{1,0:T(8,128)(2,1)S(1)}, bf16[128,768]{1,0:T(8,128)(2,1)S(1)}, u32[]{:S(2)}, u32[]{:S(2)}) collective-permute-start(bf16[128,768]{1,0:T(8,128)(2,1)S(1)} %pad_maximum_fusion.2), channel_id=1, source_target_pairs={{0,4},{4,0},{1,5},{5,1},{2,6},{6,2},{3,7},{7,3},{8,12},{12,8},{9,1... | collective-permute-start | bytes 589832 | tf_op jit(solution)/shard_map/ppermute | solution.py:193
  237.2 32.9 %all-to-all-start.5 = ((bf16[64,2,768]{2,1,0:T(2,128)(2,1)}), bf16[64,2,768]{2,1,0:T(2,128)(2,1)S(1)}, u32[]{:S(2)}, u32[]{:S(2)}) async-start(bf16[64,2,768]{2,1,0:T(2,128)(2,1)} %reshape.251), calls=%async_computation.7 | async-start | bytes 393216 | tf_op jit(solution)/shard_map/all_to_all | solution.py:197
  271.1 22.4 %all-to-all-start.6 = ((bf16[64,2,768]{2,1,0:T(2,128)(2,1)}), bf16[64,2,768]{2,1,0:T(2,128)(2,1)S(1)}, u32[]{:S(2)}, u32[]{:S(2)}) async-start(bf16[64,2,768]{2,1,0:T(2,128)(2,1)} %broadcast_in_dim.183), calls=%async_computation.8 | async-start | bytes 393216 | tf_op jit(solution)/shard_map/all_to_all | solution.py:47
  278.7 8.6 %collective-permute-start.3 = (bf16[64,1536]{1,0:T(8,128)(2,1)S(1)}, bf16[64,1536]{1,0:T(8,128)(2,1)S(1)}, u32[]{:S(2)}, u32[]{:S(2)}) collective-permute-start(bf16[64,1536]{1,0:T(8,128)(2,1)S(1)} %fusion.31), channel_id=1, source_target_pairs={{0,1},{1,2},{2,3},{3,0},{4,5},{5,6},{6,7},{7,4},{8,9},{9,10},{10,1... | collective-permute-start | bytes 589832 | tf_op jit(solution)/shard_map/ppermute | solution.py:215
  280.9 10.1 %collective-permute-start.4 = (bf16[64,1536]{1,0:T(8,128)(2,1)S(1)}, bf16[64,1536]{1,0:T(8,128)(2,1)S(1)}, u32[]{:S(2)}, u32[]{:S(2)}) collective-permute-start(bf16[64,1536]{1,0:T(8,128)(2,1)S(1)} %fusion.31), channel_id=1, source_target_pairs={{0,2},{1,3},{2,0},{3,1},{4,6},{5,7},{6,4},{7,5},{8,10},{9,11},{10,... | collective-permute-start | bytes 589832 | tf_op jit(solution)/shard_map/ppermute | solution.py:215
  284.6 8.6 %collective-permute-start.5 = (bf16[64,1536]{1,0:T(8,128)(2,1)S(1)}, bf16[64,1536]{1,0:T(8,128)(2,1)S(1)}, u32[]{:S(2)}, u32[]{:S(2)}) collective-permute-start(bf16[64,1536]{1,0:T(8,128)(2,1)S(1)} %fusion.31), channel_id=1, source_target_pairs={{0,3},{1,0},{2,1},{3,2},{4,7},{5,4},{6,5},{7,6},{8,11},{9,8},{10,9... | collective-permute-start | bytes 589832 | tf_op jit(solution)/shard_map/ppermute | solution.py:215
  293.5 8.1 %collective-permute-start.7 = (bf16[128,768]{1,0:T(8,128)(2,1)S(1)}, bf16[128,768]{1,0:T(8,128)(2,1)S(1)}, u32[]{:S(2)}, u32[]{:S(2)}) collective-permute-start(bf16[128,768]{1,0:T(8,128)(2,1)S(1)} %reshape.252), channel_id=1, source_target_pairs={{0,4},{4,0},{1,5},{5,1},{2,6},{6,2},{3,7},{7,3},{8,12},{12,8},{9,1... | collective-permute-start | bytes 589832 | tf_op jit(solution)/shard_map/ppermute | solution.py:200
  (18 other events, 78.3 us)
Sparse Core Ops, SparseCore 0:
  24.1 66.0 all-gather.1
  158.7 22.4 reduce-scatter.2
  184.6 29.9 reduce-scatter.4

commit v4 on v2

v4 whole, which is shorter than its diff:
```python
import jax
import jax.numpy as jnp
from jax import lax
from jax.experimental import pallas as pl
from jax.experimental.pallas import tpu as pltpu
from jax.sharding import Mesh
from jax.sharding import PartitionSpec as P

BLK = 64
CAP = 4
EPS = 1e-06
BETA = 20.0
LOSS_SCALE = 4096.0
ROOT = 0.7978845608028654
CUBE = 0.044715
BF16 = jnp.bfloat16
F32 = jnp.float32
DP = ("z", "x", "c")
CHIPS = ("z", "x")
SWAP = [(0, 1), (1, 0)]
EARLY = 16
NOTE = 16
VMEM_LIMIT = 40 * 1024 * 1024
SMEM = pltpu.SMEM


def gelu(pre):
    th = jnp.tanh(ROOT * (pre + CUBE * pre * pre * pre))
    return 0.5 * pre * (1.0 + th)


def gelu_and_slope(pre):
    square = pre * pre
    th = jnp.tanh(ROOT * (pre + CUBE * pre * square))
    half = 0.5 * (1.0 + th)
    slope = half + 0.5 * pre * (1.0 - th * th) * (ROOT * (1.0 + 3.0 * CUBE * square))
    return pre * half, slope


def rows_by_rows(left, right):
    return lax.dot_general(left, right, (((1,), (1,)), ((), ())), preferred_element_type=F32)


def product(left, right):
    return jnp.dot(left, right, preferred_element_type=F32)


def spread(value, axes, n):
    return lax.all_to_all(jnp.broadcast_to(value[None], (n, *value.shape)), axes, 0, 0, tiled=True)


def normalise(rows):
    wide = rows.astype(F32)
    center = wide - jnp.mean(wide, axis=-1, keepdims=True)
    inverse = lax.rsqrt(jnp.mean(center * center, axis=-1, keepdims=True) + EPS)
    return center * inverse, inverse


def params():
    return pltpu.CompilerParams(vmem_limit_bytes=VMEM_LIMIT)


def cost(flops, moved, tanh=0):
    return pl.CostEstimate(flops=flops, bytes_accessed=moved, transcendentals=tanh)


def whole(shape):
    return pl.BlockSpec(shape, lambda *_: (0,) * len(shape))


def input_kernel(wins_ref, x_ref, mod_ref, a_ref, modded_ref, low_ref, split_ref):
    wins = wins_ref[0]
    for slot in range(CAP):
        rows = slice(slot * BLK, (slot + 1) * BLK)
        normed, _ = normalise(x_ref[rows])
        first = slot < wins
        shift = jnp.where(first, mod_ref[0:1].astype(F32), mod_ref[3:4].astype(F32))
        scale = 1.0 + jnp.where(first, mod_ref[1:2].astype(F32), mod_ref[4:5].astype(F32))
        modded_ref[rows] = (normed * scale + shift).astype(BF16)
    modded = modded_ref[...]
    low_ref[...] = rows_by_rows(modded, a_ref[...]).astype(BF16)
    turned = rows_by_rows(a_ref[...], modded)
    second = lax.broadcasted_iota(jnp.int32, turned.shape, 1) // BLK >= wins
    rank = turned.shape[0]
    split_ref[:rank] = jnp.where(second, 0.0, turned).astype(BF16)
    split_ref[rank:] = jnp.where(second, turned, 0.0).astype(BF16)


def prepare(wins, tokens, mod, a_turned):
    rows, width = tokens.shape
    rank = a_turned.shape[0]
    return pl.pallas_call(
        input_kernel,
        out_shape=[
            jax.ShapeDtypeStruct((rows, width), BF16),
            jax.ShapeDtypeStruct((rows, rank), BF16),
            jax.ShapeDtypeStruct((2 * rank, rows), BF16),
        ],
        in_specs=[pl.BlockSpec(memory_space=SMEM)] + [pl.BlockSpec(memory_space=pltpu.VMEM)] * 3,
        compiler_params=params(),
        cost_estimate=cost(4 * rows * width * rank, 4 * rows * width),
    )(wins, tokens, mod, a_turned)


def up_kernel(modded_ref, low_ref, up_ref, b_ref, pol_ref, ref_ref, slope_ref):
    pre_ref = product(modded_ref[...], up_ref[...])
    pre_pol = pre_ref + product(low_ref[...], b_ref[...])
    act, slope = gelu_and_slope(pre_pol)
    pol_ref[...] = act.astype(BF16)
    slope_ref[...] = slope
    ref_ref[...] = gelu(pre_ref).astype(BF16)


def activate(modded, low, up, factor):
    rows, width = modded.shape
    rank, half = factor.shape
    step = 256
    cut = pl.BlockSpec((rows, step), lambda i: (0, i))
    return pl.pallas_call(
        up_kernel,
        grid=(half // step,),
        out_shape=[
            jax.ShapeDtypeStruct((rows, half), BF16),
            jax.ShapeDtypeStruct((rows, half), BF16),
            jax.ShapeDtypeStruct((rows, half), F32),
        ],
        in_specs=[
            whole((rows, width)),
            whole((rows, rank)),
            pl.BlockSpec((width, step), lambda i: (0, i)),
            pl.BlockSpec((rank, step), lambda i: (0, i)),
        ],
        out_specs=[cut, cut, cut],
        compiler_params=params(),
        cost_estimate=cost(2 * rows * width * half, 2 * width * half + 10 * rows * half, 2 * rows * half),
    )(modded, low, up, factor)


def down_kernel(left_ref, right_ref, own_ref, other_ref, out_ref):
    total = rows_by_rows(left_ref[...], own_ref[...]) + rows_by_rows(right_ref[...], other_ref[...])
    out_ref[...] = total.astype(BF16)


def lower(left, right, own, other):
    rows, half = left.shape
    width = own.shape[0]
    step = 512
    cut = pl.BlockSpec((step, half), lambda i: (i, 0))
    return pl.pallas_call(
        down_kernel,
        grid=(width // step,),
        out_shape=jax.ShapeDtypeStruct((rows, width), BF16),
        in_specs=[whole((rows, half)), whole((rows, half)), cut, cut],
        out_specs=pl.BlockSpec((rows, step), lambda i: (0, i)),
        compiler_params=params(),
        cost_estimate=cost(4 * rows * width * half, 4 * width * half + 2 * rows * width),
    )(left, right, own, other)


def miss_kernel(got_ref, ref_ref, x_ref, t_ref, gate_ref, mask_ref, unit_ref, send_ref):
    total = jnp.sum(got_ref[...].astype(F32), axis=0)
    gate = gate_ref[...]
    unit = 2.0 * mask_ref[...] * (x_ref[...].astype(F32) - t_ref[...].astype(F32) + gate * total)
    unit_ref[...] = unit
    dy = (gate * unit).astype(BF16)
    for peer in range(send_ref.shape[0]):
        send_ref[peer, :BLK] = dy
        send_ref[peer, BLK:] = ref_ref[peer]


def miss(got, part_ref, x_own, t_own, gate, mask):
    groups, rows, width = got.shape
    return pl.pallas_call(
        miss_kernel,
        out_shape=[
            jax.ShapeDtypeStruct((rows, width), F32),
            jax.ShapeDtypeStruct((groups, 2 * rows, width), BF16),
        ],
        compiler_params=params(),
        cost_estimate=cost(20 * rows * width, 8 * groups * rows * width),
    )(got, part_ref, x_own, t_own, gate, mask)


def back_kernel(
    got_ref, unit_ref, x_ref, t_ref, gate_ref, mask_ref, own_ref, other_ref, bo_ref, bt_ref, so_ref, st_ref,
    do_ref, dt_ref, dlow_ref, send_ref, turned_scr, straight_scr,
):
    step = pl.program_id(0)
    width = got_ref.shape[2]
    dy = got_ref[:, :BLK].reshape(CAP * BLK, width)
    d_own = (product(dy, own_ref[...]) * so_ref[...]).astype(BF16)
    d_other = (product(dy, other_ref[...]) * st_ref[...]).astype(BF16)
    do_ref[...] = d_own
    dt_ref[...] = d_other
    turned = rows_by_rows(bo_ref[...], d_own) + rows_by_rows(bt_ref[...], d_other)
    straight = rows_by_rows(d_own, bo_ref[...]) + rows_by_rows(d_other, bt_ref[...])

    @pl.when(step == 0)
    def _():
        turned_scr[...] = turned
        straight_scr[...] = straight

    @pl.when(step > 0)
    def _():
        turned_scr[...] += turned
        straight_scr[...] += straight

    @pl.when(step == pl.num_programs(0) - 1)
    def _():
        rank = turned_scr.shape[0]
        dlow_ref[...] = straight_scr[...].astype(BF16)
        mask = mask_ref[...]
        base = x_ref[...].astype(F32) - t_ref[...].astype(F32)
        miss_ref = mask * (base + gate_ref[...] * jnp.sum(got_ref[:, BLK:].astype(F32), axis=0))
        miss_pol = 0.5 * unit_ref[...]
        parts = jnp.sum((miss_pol - miss_ref) * (miss_pol + miss_ref), axis=1, keepdims=True)
        excess = jnp.broadcast_to(jnp.sum(parts, axis=0, keepdims=True), (NOTE, CAP * BLK))
        high = excess.astype(BF16)
        rest = excess - high.astype(F32)
        middle = rest.astype(BF16)
        lowest = rest - middle.astype(F32)
        line = lax.broadcasted_iota(jnp.int32, excess.shape, 0)
        note = jnp.where(line == 0, high.astype(F32), jnp.where(line == 1, middle.astype(F32), lowest)).astype(BF16)
        total = turned_scr[...].astype(BF16)
        for peer in range(send_ref.shape[0]):
            send_ref[peer, :rank] = total
            send_ref[peer, rank:] = note


def backward(got, unit, x_own, t_own, gate, mask, own, other, b_own, b_other, s_own, s_other):
    groups, _, width = got.shape
    half = own.shape[1]
    rank = b_own.shape[0]
    rows = CAP * BLK
    step = 256
    weight = pl.BlockSpec((width, step), lambda i: (0, i))
    factor = pl.BlockSpec((rank, step), lambda i: (0, i))
    cut = pl.BlockSpec((rows, step), lambda i: (0, i))
    block = whole((BLK, width))
    return pl.pallas_call(
        back_kernel,
        grid=(half // step,),
        out_shape=[
            jax.ShapeDtypeStruct((rows, half), BF16),
            jax.ShapeDtypeStruct((rows, half), BF16),
            jax.ShapeDtypeStruct((rows, rank), BF16),
            jax.ShapeDtypeStruct((groups, rank + NOTE, rows), BF16),
        ],
        in_specs=[
            whole(got.shape), block, block, block, whole((1, width)), whole((BLK, 1)),
            weight, weight, factor, factor, cut, cut,
        ],
        out_specs=[cut, cut, whole((rows, rank)), whole((groups, rank + NOTE, rows))],
        scratch_shapes=[pltpu.VMEM((rank, rows), F32), pltpu.VMEM((rows, rank), F32)],
        compiler_params=params(),
        cost_estimate=cost(4 * rows * width * half, 4 * width * half + 12 * rows * half),
    )(got, unit, x_own, t_own, gate, mask, own, other, b_own, b_other, s_own, s_other)


def factor_kernel(split_ref, do_ref, dt_ref, own_ref, other_ref):
    own_ref[...] = product(split_ref[...], do_ref[...])
    other_ref[...] = product(split_ref[...], dt_ref[...])


def factor_terms(split, d_own, d_other):
    lines, rows = split.shape
    half = d_own.shape[1]
    return pl.pallas_call(
        factor_kernel,
        out_shape=[jax.ShapeDtypeStruct((lines, half), F32)] * 2,
        compiler_params=params(),
        cost_estimate=cost(4 * lines * rows * half, 8 * lines * half),
    )(split, d_own, d_other)


def pile_kernel(
    ints_ref, scales_ref, got_ref, modded_ref, own_ref, other_ref, keep_ref, give_ref, facts_ref
):
    wins = ints_ref[0]
    core = ints_ref[1]
    groups, lines, rows = got_ref.shape
    rank = lines - NOTE
    half = own_ref.shape[1]
    gap_first = jnp.zeros((1, rows), F32)
    gap_second = jnp.zeros((1, rows), F32)
    for slot in range(groups):
        note = got_ref[slot, rank:].astype(F32)
        excess = note[0:1] + note[1:2] + note[2:3]
        gap_first += jnp.where(slot < wins, excess, 0.0)
        gap_second += jnp.where(slot < wins, 0.0, excess)
    scale_first = scales_ref[0]
    scale_second = scales_ref[1]
    inside = -BETA * (gap_first * scale_first - gap_second * scale_second)
    losses = jnp.maximum(-inside, 0.0) + jnp.log1p(jnp.exp(-jnp.abs(inside)))
    weight = BETA * LOSS_SCALE * jax.nn.sigmoid(-inside)
    first = weight * scale_first
    second = -weight * scale_second
    line = lax.broadcasted_iota(jnp.int32, facts_ref.shape, 0)
    facts_ref[...] = jnp.where(line == 0, losses, jnp.where(line == 1, first, second))
    slot = lax.broadcasted_iota(jnp.int32, (1, rows), 1) // BLK
    total = jnp.sum(got_ref[:, :rank].astype(F32), axis=0)
    dlow = (total * jnp.where(slot < wins, first, second)).astype(BF16)
    one = first[:, :1]
    two = second[:, :1]
    near = modded_ref[:, pl.ds(pl.multiple_of(core * half, 128), half)]
    far = modded_ref[:, pl.ds(pl.multiple_of((1 - core) * half, 128), half)]
    keep_ref[:rank] = one * own_ref[:rank] + two * own_ref[rank:]
    keep_ref[rank:] = product(dlow, near)
    give_ref[:rank] = (one * other_ref[:rank] + two * other_ref[rank:]).astype(BF16)
    give_ref[rank:] = product(dlow, far).astype(BF16)


def piles(ints, scales, got, modded, b_own, b_other):
    lines, half = b_own.shape
    rows = got.shape[2]
    return pl.pallas_call(
        pile_kernel,
        out_shape=[
            jax.ShapeDtypeStruct((lines, half), F32),
            jax.ShapeDtypeStruct((lines, half), BF16),
            jax.ShapeDtypeStruct((8, rows), F32),
        ],
        in_specs=[pl.BlockSpec(memory_space=SMEM)] * 2 + [pl.BlockSpec(memory_space=pltpu.VMEM)] * 4,
        compiler_params=params(),
        cost_estimate=cost(2 * lines * half * rows, 16 * lines * half),
    )(ints, scales, got, modded, b_own, b_other)


def dm_kernel(after_ref, do_ref, dt_ref, dlow_ref, own_ref, other_ref, a_ref, out_ref):
    total = rows_by_rows(do_ref[...], own_ref[...]) + rows_by_rows(dt_ref[...], other_ref[...])
    out_ref[...] = (total + product(dlow_ref[...], a_ref[...])).astype(BF16)


def dm_terms(after, d_own, d_other, dlow, own, other, a_turned):
    rows, half = d_own.shape
    width = own.shape[0]
    rank = dlow.shape[1]
    step = 512
    cut = pl.BlockSpec((step, half), lambda i: (i, 0))
    return pl.pallas_call(
        dm_kernel,
        grid=(width // step,),
        out_shape=jax.ShapeDtypeStruct((rows, width), BF16),
        in_specs=[
            pl.BlockSpec(memory_space=pl.ANY),
            whole((rows, half)),
            whole((rows, half)),
            whole((rows, rank)),
            cut,
            cut,
            pl.BlockSpec((rank, step), lambda i: (0, i)),
        ],
        out_specs=pl.BlockSpec((rows, step), lambda i: (0, i)),
        compiler_params=params(),
        cost_estimate=cost(4 * rows * width * half, 4 * width * half + 2 * rows * width),
    )(after, d_own, d_other, dlow, own, other, a_turned)


def token_kernel(one_ref, two_ref, three_ref, four_ref, x_ref, scale_ref, unit_ref, coef_ref, out_ref):
    total = one_ref[...].astype(F32) + two_ref[...].astype(F32)
    total = total + three_ref[...].astype(F32) + four_ref[...].astype(F32)
    normed, inverse = normalise(x_ref[...])
    dn = total * scale_ref[...]
    mean_one = jnp.mean(dn, axis=-1, keepdims=True)
    mean_two = jnp.mean(dn * normed, axis=-1, keepdims=True)
    grad = coef_ref[...] * (unit_ref[...] + inverse * (dn - mean_one - normed * mean_two))
    out_ref[...] = grad.astype(BF16)


def token_gradient(pieces, x_own, scale, unit, coef):
    rows, width = x_own.shape
    return pl.pallas_call(
        token_kernel,
        out_shape=jax.ShapeDtypeStruct((rows, width), BF16),
        compiler_params=params(),
        cost_estimate=cost(20 * rows * width, 20 * rows * width),
    )(*pieces, x_own, scale, unit, coef)


def per_device(
    tokens,
    targets,
    modulation,
    live_block_count,
    preferred_blocks,
    last_block_rows,
    up_rows,
    down_rows,
    factor_in,
    factor_out,
):
    width = tokens.shape[1]
    n_z, n_x, n_c, n_t = (lax.axis_size(a) for a in ("z", "x", "c", "t"))
    n_dp = n_z * n_x * n_c
    core = lax.axis_index("c")
    group = lax.axis_index("t")
    thin, hidden = up_rows.shape
    half = hidden // n_c
    pair = n_c * thin
    rank = factor_in.shape[1]

    both = jnp.concatenate([up_rows, down_rows], axis=0)
    keep = lax.dynamic_slice_in_dim(both, core * half, half, axis=1)
    got = lax.ppermute(lax.dynamic_slice_in_dim(both, (1 - core) * half, half, axis=1), "c", SWAP)
    first = jnp.where(core == 0, keep, got)
    second = jnp.where(core == 0, got, keep)
    up_pair = jnp.concatenate([first[:thin], second[:thin]], axis=0)
    down_pair = jnp.concatenate([first[thin:], second[thin:]], axis=0)
    line_one = lax.all_gather(jnp.concatenate([up_pair, down_pair[:EARLY]], 0), "z", axis=0, tiled=True)
    down_late, line_one = lax.optimization_barrier((down_pair[EARLY:], line_one))
    line_two = lax.all_gather(down_late, "z", axis=0, tiled=True)
    near_one = spread(line_one, "x", n_x).reshape(n_x, n_z, pair + EARLY, half).transpose(1, 0, 2, 3)
    near_two = spread(line_two, "x", n_x).reshape(n_x, n_z, pair - EARLY, half).transpose(1, 0, 2, 3)
    up_own = near_one[:, :, :pair].reshape(width, half)
    up_other = lax.ppermute(up_own, "c", SWAP)
    down_own = jnp.concatenate([near_one[:, :, pair:], near_two], axis=2).reshape(width, half)
    down_other = lax.ppermute(down_own, "c", SWAP)

    count = live_block_count[0]
    wins = preferred_blocks[0]
    slots = jnp.arange(CAP, dtype=jnp.int32)
    flags = (slots >= wins).astype(jnp.int32)
    last = jnp.where(flags == 0, wins - 1, count - 1)
    tail = jnp.where(flags == 0, last_block_rows[0, 0], last_block_rows[0, 1])
    live = jnp.where(slots < count, jnp.where(slots == last, tail, BLK), 0)
    rows_first = jnp.sum(jnp.where(flags == 0, live, 0)).astype(F32)
    rows_second = jnp.sum(jnp.where(flags == 1, live, 0)).astype(F32)
    scales = 1.0 / (width * jnp.stack([rows_first, rows_second]))

    own_first = group < wins
    x_own = lax.dynamic_slice_in_dim(tokens, group * BLK, BLK, axis=0)
    t_own = lax.dynamic_slice_in_dim(targets, group * BLK, BLK, axis=0)
    vec_own = jnp.where(own_first, modulation[0], modulation[1]).astype(F32)
    live_own = lax.dynamic_slice_in_dim(live, group, 1)
    mask = (jnp.arange(BLK, dtype=jnp.int32)[:, None] < live_own[None, :]).astype(F32)
    gate = vec_own[2:3]
    scale_own = 1.0 + vec_own[1:2]

    a_turned = factor_in.T
    factor_own = lax.dynamic_slice_in_dim(factor_out, core * half, half, axis=1)
    factor_other = lax.dynamic_slice_in_dim(factor_out, (1 - core) * half, half, axis=1)
    modded, low, low_split = prepare(preferred_blocks, tokens, modulation.reshape(6, width), a_turned)

    pol_own, ref_own, slope_own = activate(modded, low, up_own, factor_own)
    pol_other, ref_other, slope_other = activate(modded, low, up_other, factor_other)
    part_pol = lower(pol_own, pol_other, down_own, down_other).reshape(CAP, BLK, width)
    got_pol = lax.all_to_all(part_pol, "t", 0, 0, tiled=True)
    part_ref = lower(ref_own, ref_other, down_own, down_other).reshape(CAP, BLK, width)

    unit, send = miss(got_pol, part_ref, x_own, t_own, gate, mask)
    got_dy = lax.all_to_all(send, "t", 0, 0, tiled=True)
    d_own, d_other, dlow_part, send = backward(
        got_dy, unit, x_own, t_own, gate, mask, down_own, down_other, factor_own, factor_other, slope_own, slope_other
    )
    got_low = lax.all_to_all(send, "t", 0, 0, tiled=True)
    b_own, b_other = factor_terms(low_split, d_own, d_other)
    keep, give, facts = piles(
        jnp.stack([wins, core]).astype(jnp.int32), scales, got_low, modded, b_own, b_other
    )
    losses = facts[0, :1]
    coef_own = jnp.where(own_first, facts[1:2, :1], facts[2:3, :1])
    pile = (keep + lax.ppermute(give, "c", SWAP).astype(F32)).astype(BF16)

    chips = n_z * n_x
    pieces = lax.all_to_all(pile.reshape(chips, 2 * rank // chips, half), CHIPS, 0, 0, tiled=True)
    total = (jnp.sum(pieces.astype(F32), axis=0) / n_dp).astype(BF16)
    mine = spread(total, CHIPS, chips).reshape(2 * rank, half)
    theirs = lax.ppermute(mine, "c", SWAP)
    ends = jnp.concatenate([mine, theirs], 1)
    flipped = jnp.concatenate([theirs, mine], 1)
    ends = jnp.where(core == 0, ends, flipped).astype(F32)
    sum_b = ends[:rank]
    sum_a = ends[rank:].T

    dm_part = dm_terms(pile, d_own, d_other, dlow_part, up_own, up_other, a_turned).reshape(CAP, BLK, width)
    turns = [[(i, (i + step) % n_t) for i in range(n_t)] for step in range(n_t)]
    chunks = [lax.dynamic_index_in_dim(dm_part, (group + step) % n_t, 0, False) for step in range(n_t)]
    chunks = [chunks[0]] + [lax.ppermute(chunks[step], "t", turns[step]) for step in range(1, n_t)]
    grad_block = token_gradient(chunks, x_own, scale_own, unit, coef_own)
    blocks = [grad_block] + [lax.ppermute(grad_block, "t", turns[step]) for step in range(1, n_t)]
    blocks = jnp.stack(blocks)
    grad_tokens = jnp.concatenate(
        [lax.dynamic_index_in_dim(blocks, (group - slot) % n_t, 0, False) for slot in range(n_t)], 0
    )
    return losses, grad_tokens, sum_a, sum_b


def solution(mesh):
    n_dp, n_t = mesh.devices.shape
    fine = Mesh(mesh.devices.reshape(n_dp // 8, 4, 2, n_t), ("z", "x", "c", "t"))
    return jax.shard_map(
        per_device,
        mesh=fine,
        in_specs=(
            P(DP, None),
            P(DP, None),
            P(DP, None, None),
            P(DP),
            P(DP),
            P(DP, None),
            P(DP, "t"),
            P(DP, "t"),
            P(),
            P(None, "t"),
        ),
        out_specs=(P(DP), P(DP, None), P(), P(None, "t")),
        check_vma=False,
    )
```

time: 277 us -> 267 us (0.964); the launches traced: 271 us -> 265 us
  waiting for transfers between devices: 64 us -> 34.3 us
  Pallas kernels: 0 us -> 26.9 us
  matrix products: 17.2 us -> 0 us
  blocking collectives: 56.8 us -> 72.8 us
  local copies, waits for them, and re-layouts: 19.1 us -> 31.2 us
  other arithmetic: 15.5 us -> 8.83 us
  starting transfers between devices: 91 us -> 86 us
    pallas_call x0 -> x11, Pallas kernels: none -> 26.9 us  [the longest x2 7.15 us: activate(): pl.pallas_call(up_kernel, grid=(half // step,), out_shape=[jax.ShapeDtype...]
    all_to_all x0 -> x1, blocking collectives: none -> 22.1 us  [per_device(): got_dy = lax.all_to_all(send, 't', 0, 0, tiled=True)]
    ppermute x1 -> x7, starting transfers between devices: 3.78 us -> 22.6 us  [the longest x3 9.63 us: per_device(): lax.ppermute(chunks[step], 't', turns[step])]
    dot_general x19 -> x0, matrix products: 17.2 us -> none  [the longest x9 8.53 us: rows_by_rows(): lax.dot_general(left, right, (((1,), (1,)), ((), ())), preferred_element_...]
    all_to_all x2, waiting for transfers between devices: 19.8 us -> 4.26 us  [the longest x1 3.89 us: per_device(): got_pol = lax.all_to_all(part_pol, 't', 0, 0, tiled=True)]
    all_to_all x1, waiting for transfers between devices: 15.9 us -> 3.62 us  [per_device(): lax.all_to_all(pile.reshape(chips, 2 * rank // chips, half), CHIPS, 0, 0,...]
    unnamed x40 -> x71, local copies, waits for them, and re-layouts: 4.12 us -> 16.4 us
    ppermute x1, starting transfers between devices: 15.2 us -> 4.4 us  [per_device(): down_other = lax.ppermute(down_own, 'c', SWAP)]
  transfers between devices with their start and end apart: 13 -> 17, of which waited for: 8 -> 9; matrix products, arithmetic and copies ran while one was open for 7% -> 6% of each run, Pallas kernels for 0% -> 6%
where the time goes in v4:
time: 267 us; the launch traced here: 265 us
  starting transfers between devices  86 us (32%)
  blocking collectives  72.8 us (27%)
  waiting for transfers between devices  34.3 us (13%)
  local copies, waits for them, and re-layouts  31.2 us (12%)
  Pallas kernels  26.9 us (10%)
  other arithmetic  8.83 us (3%)
  between operations  5.23 us (2%)
    all_gather x1, blocking collectives, per_device(): lax.all_gather(jnp.concatenate([up_pair, down_pair[:EARLY]], 0), 'z', axi...  29.2 us
    all_to_all x1, blocking collectives, per_device(): got_dy = lax.all_to_all(send, 't', 0, 0, tiled=True)  22.1 us
    all_gather x1, blocking collectives, per_device(): line_two = lax.all_gather(down_late, 'z', axis=0, tiled=True)  21.6 us
    all_to_all x3, starting transfers between devices, spread(): lax.all_to_all(jnp.broadcast_to(value[None], (n, *value.shape)), axes, 0,...  19.3 us
    all_to_all x3, waiting for transfers between devices, spread(): lax.all_to_all(jnp.broadcast_to(value[None], (n, *value.shape)), axes, 0,...  17.6 us
    unnamed x71, local copies, waits for them, and re-layouts  16.4 us
    ppermute x1, starting transfers between devices, per_device(): up_other = lax.ppermute(up_own, 'c', SWAP)  9.74 us
    ppermute x3, starting transfers between devices, per_device(): lax.ppermute(chunks[step], 't', turns[step])  9.63 us
  transfers between devices with their start and end apart: 17, of which 9 were waited for; matrix products, arithmetic and copies ran while one was open for 6% of the time, Pallas kernels for 6%

profile of v4, /device:TPU:1, one launch (start us, length us, event | category | flops | bytes accessed | tf_op | source)
XLA Modules:
  0.0 265.2 jit_solution(7654346400170198047)
XLA Ops:
  1.5 8.8 %collective-permute-start = (bf16[24,768]{1,0:T(8,128)(2,1)S(1)}, bf16[24,768]{1,0:T(8,128)(2,1)S(1)}, u32[]{:S(2)}, u32[]{:S(2)}) collective-permute-start(bf16[24,768]{1,0:T(8,128)(2,1)S(1)} %fusion.3), channel_id=1, source_target_pairs={{0,4},{4,0},{1,5},{5,1},{2,6},{6,2},{3,7},{7,3},{8,12},{12,8},{9,1... | collective-permute-start | bytes 110600 | tf_op jit(solution)/shard_map/ppermute | solution.py:404
  12.1 29.2 %all_gather.6 = bf16[640,768]{1,0:T(8,128)(2,1)S(1)} all-gather(bf16[40,768]{1,0:T(8,128)(2,1)S(1)} %fusion.1), channel_id=1, replica_groups=mesh['z'=16,'x'=4,'c'=2,'t'=4] {'z'}, dimensions={0}, use_global_device_ids=true | all-gather | bytes 1044480 | tf_op jit(solution)/shard_map/all_gather | solution.py:409
  41.2 2.2 broadcast_in_dim.46
  43.4 4.9 %all-to-all-start = ((bf16[4,640,768]{2,1,0:T(8,128)(2,1)}), bf16[4,640,768]{2,1,0:T(8,128)(2,1)}, u32[]{:S(2)}, u32[]{:S(2)}) async-start(bf16[4,640,768]{2,1,0:T(8,128)(2,1)} %broadcast_in_dim.46), calls=%async_computation | async-start | bytes 7864320 | tf_op jit(solution)/shard_map/all_to_all | solution.py:49
  48.3 21.6 %all_gather.7 = bf16[128,768]{1,0:T(8,128)(2,1)S(1)} all-gather(bf16[8,768]{1,0:T(8,128)(2,1)S(1)} %slice.82), channel_id=1, replica_groups=mesh['z'=16,'x'=4,'c'=2,'t'=4] {'z'}, dimensions={0}, use_global_device_ids=true | all-gather | bytes 208896 | tf_op jit(solution)/shard_map/all_gather | solution.py:411
  69.9 17.6 %all-to-all-done = bf16[4,640,768]{2,1,0:T(8,128)(2,1)} async-done(((bf16[4,640,768]{2,1,0:T(8,128)(2,1)}), bf16[4,640,768]{2,1,0:T(8,128)(2,1)}, u32[]{:S(2)}, u32[]{:S(2)}) %all-to-all-start) | async-done | bytes 3932192 | tf_op jit(solution)/shard_map/all_to_all | solution.py:49
  88.4 3.5 %all-to-all-start.1 = ((bf16[4,128,768]{2,1,0:T(8,128)(2,1)}), bf16[4,128,768]{2,1,0:T(8,128)(2,1)S(1)}, u32[]{:S(2)}, u32[]{:S(2)}) async-start(bf16[4,128,768]{2,1,0:T(8,128)(2,1)} %broadcast_in_dim.47), calls=%async_computation.1 | async-start | bytes 1572864 | tf_op jit(solution)/shard_map/all_to_all | solution.py:49
  96.9 9.7 %collective-permute-start.1 = (bf16[1536,768]{1,0:T(8,128)(2,1)}, bf16[1536,768]{1,0:T(8,128)(2,1)}, u32[]{:S(2)}, u32[]{:S(2)}) collective-permute-start(bf16[1536,768]{1,0:T(8,128)(2,1)} %bitcast.10.up_ref.own_ref), channel_id=1, source_target_pairs={{0,4},{4,0},{1,5},{5,1},{2,6},{6,2},{3,7},{7,3},{8,12},{12,8},{9,1... | collective-permute-start | bytes 7077896 | tf_op jit(solution)/shard_map/ppermute | solution.py:415
  107.2 4.4 %collective-permute-start.2 = (bf16[1536,768]{1,0:T(8,128)(2,1)S(1)}, bf16[1536,768]{1,0:T(8,128)(2,1)}, u32[]{:S(2)}, u32[]{:S(2)}) collective-permute-start(bf16[1536,768]{1,0:T(8,128)(2,1)S(1)} %bitcast.53), channel_id=1, source_target_pairs={{0,4},{4,0},{1,5},{5,1},{2,6},{6,2},{3,7},{7,3},{8,12},{12,8},{9,1... | collective-permute-start | bytes 7077896 | tf_op jit(solution)/shard_map/ppermute | solution.py:417
  113.5 2.0 select_reduce_fusion
  122.3 3.6 %shard_map.130 = (bf16[256,768]{1,0:T(8,128)(2,1)S(1)}, bf16[256,768]{1,0:T(8,128)(2,1)S(1)}, f32[256,768]{1,0:T(8,128)S(1)}) custom-call(bf16[256,1536]{1,0:T(8,128)(2,1)S(1)} %get-tuple-element.26.modded_ref, bf16[256,64]{1,0:T(8,128)(2,1)S(1)} %get-tuple-element.27.low_ref, bf16[1536,768]{1,0:T(8,128)(2,1)} %bitcast.10.up_ref.own_ref, ...), custom_call_target="tpu_custom_call" | custom-call | flops 603979776 | bytes 4325376 | tf_op jit(solution)/shard_map/pallas_call | solution.py:119
  127.6 3.6 %shard_map.131 = (bf16[256,768]{1,0:T(8,128)(2,1)S(1)}, bf16[256,768]{1,0:T(8,128)(2,1)S(1)}, f32[256,768]{1,0:T(8,128)S(1)}) custom-call(bf16[256,1536]{1,0:T(8,128)(2,1)S(1)} %get-tuple-element.26.modded_ref, bf16[256,64]{1,0:T(8,128)(2,1)S(1)} %get-tuple-element.27.low_ref, bf16[1536,768]{1,0:T(8,128)(2,1)} %collective-permute-done.1.up_ref.other_ref, ...), custom_call_target="tpu_custom_call" | custom-call | flops 603979776 | bytes 4325376 | tf_op jit(solution)/shard_map/pallas_call | solution.py:119
  132.8 3.5 %shard_map.132 = bf16[256,1536]{1,0:T(8,128)(2,1)S(1)} custom-call(bf16[256,768]{1,0:T(8,128)(2,1)S(1)} %get-tuple-element.29.left_ref, bf16[256,768]{1,0:T(8,128)(2,1)S(1)} %get-tuple-element.30.right_ref, bf16[1536,768]{1,0:T(8,128)(2,1)S(1)} %bitcast.54, bf16[1536,768]{1,0:T(8,128)(2,1)} %collective-permute-done.2.other_ref), custom_call_target="tpu_custom_call" | custom-call | flops 1207959552 | bytes 5505024 | tf_op jit(solution)/shard_map/pallas_call | solution.py:149
  137.2 4.2 %all-to-all-start.2 = ((bf16[4,64,1536]{2,1,0:T(8,128)(2,1)}), bf16[4,64,1536]{2,1,0:T(8,128)(2,1)}, u32[]{:S(2)}, u32[]{:S(2)}) async-start(bf16[4,64,1536]{2,1,0:T(8,128)(2,1)} %bitcast.57), calls=%async_computation.2 | async-start | bytes 1572864 | tf_op jit(solution)/shard_map/all_to_all | solution.py:447
  145.4 3.5 %shard_map.133 = bf16[256,1536]{1,0:T(8,128)(2,1)S(1)} custom-call(bf16[256,768]{1,0:T(8,128)(2,1)S(1)} %copy-done.23, bf16[256,768]{1,0:T(8,128)(2,1)S(1)} %copy-done.25, bf16[1536,768]{1,0:T(8,128)(2,1)S(1)} %bitcast.55, bf16[1536,768]{1,0:T(8,128)(2,1)} %collective-permute-done.2.other_ref), custom_call_target="tpu_custom_call" | custom-call | flops 1207959552 | bytes 5505024 | tf_op jit(solution)/shard_map/pallas_call | solution.py:149
  149.8 3.9 %all-to-all-done.2.got_ref = bf16[4,64,1536]{2,1,0:T(8,128)(2,1)} async-done(((bf16[4,64,1536]{2,1,0:T(8,128)(2,1)}), bf16[4,64,1536]{2,1,0:T(8,128)(2,1)}, u32[]{:S(2)}, u32[]{:S(2)}) %all-to-all-start.2) | async-done | bytes 786464 | tf_op jit(solution)/shard_map/all_to_all | solution.py:447
  157.2 22.1 %all_to_all.35.got_ref = bf16[4,128,1536]{2,1,0:T(8,128)(2,1)S(1)} all-to-all(bf16[4,128,1536]{2,1,0:T(8,128)(2,1)S(1)} %get-tuple-element.34), channel_id=1, replica_groups=mesh['z'=16,'x'=4,'c'=2,'t'=4] {'t'}, dimensions={0} | all-to-all | bytes 3145728 | tf_op jit(solution)/shard_map/all_to_all | solution.py:451
  179.3 4.5 %shard_map.135 = (bf16[256,768]{1,0:T(8,128)(2,1)S(1)}, bf16[256,768]{1,0:T(8,128)(2,1)S(1)}, bf16[256,64]{1,0:T(8,128)(2,1)S(1)}, bf16[4,80,256]{2,1,0:T(8,128)(2,1)S(1)}) custom-call(bf16[4,128,1536]{2,1,0:T(8,128)(2,1)S(1)} %all_to_all.35.got_ref, f32[64,1536]{1,0:T(8,128)S(1)} %get-tuple-element.35.unit_ref, ...), custom_call_target="tpu_custom_call" | custom-call | flops 1207959552 | bytes 7077888 | tf_op jit(solution)/shard_map/pallas_call | solution.py:240
  186.6 3.5 %all-to-all-start.4 = ((bf16[4,80,256]{2,1,0:T(8,128)(2,1)}), bf16[4,80,256]{2,1,0:T(8,128)(2,1)S(1)}, u32[]{:S(2)}, u32[]{:S(2)}) async-start(bf16[4,80,256]{2,1,0:T(8,128)(2,1)} %copy-done.28), calls=%async_computation.4 | async-start | bytes 327680 | tf_op jit(solution)/shard_map/all_to_all | solution.py:455
  195.8 5.1 %collective-permute-start.3 = (bf16[128,768]{1,0:T(8,128)(2,1)S(1)}, bf16[128,768]{1,0:T(8,128)(2,1)S(1)}, u32[]{:S(2)}, u32[]{:S(2)}) collective-permute-start(bf16[128,768]{1,0:T(8,128)(2,1)S(1)} %get-tuple-element.46), channel_id=1, source_target_pairs={{0,4},{4,0},{1,5},{5,1},{2,6},{6,2},{3,7},{7,3},{8,12},{12,8},{9,1... | collective-permute-start | bytes 589832 | tf_op jit(solution)/shard_map/ppermute | solution.py:462
  202.8 7.6 %all-to-all-start.5 = ((bf16[64,2,768]{2,1,0:T(2,128)(2,1)}), bf16[64,2,768]{2,1,0:T(2,128)(2,1)S(1)}, u32[]{:S(2)}, u32[]{:S(2)}) async-start(bf16[64,2,768]{2,1,0:T(2,128)(2,1)} %reshape.75), calls=%async_computation.5 | async-start | bytes 393216 | tf_op jit(solution)/shard_map/all_to_all | solution.py:465
  210.5 4.1 %shard_map.138 = bf16[256,1536]{1,0:T(8,128)(2,1)S(1)} custom-call(bf16[128,768]{1,0:T(8,128)(2,1)S(1)} %add_convert_fusion.after_ref, bf16[256,768]{1,0:T(8,128)(2,1)S(1)} %copy-done.7, bf16[256,768]{1,0:T(8,128)(2,1)S(1)} %copy-done.10, bf16[256,64]{1,0:T(8,128)(2,1)S(1)} %copy-done.30, bf16[1536,768]{1,0:T(8,128)(2,1)} %bitcast.10.up_ref.own_ref, ...), custom_call_target="tpu_custom_call" | custom-call | flops 1207959552 | bytes 5505024 | tf_op jit(solution)/shard_map/pallas_call | solution.py:340
  214.7 2.3 collective-permute-start.4
  217.0 4.2 %collective-permute-start.5 = (bf16[64,1536]{1,0:T(8,128)(2,1)S(1)}, bf16[64,1536]{1,0:T(8,128)(2,1)S(1)}, u32[]{:S(2)}, u32[]{:S(2)}) collective-permute-start(bf16[64,1536]{1,0:T(8,128)(2,1)S(1)} %get-tuple-element.58), channel_id=1, source_target_pairs={{0,2},{1,3},{2,0},{3,1},{4,6},{5,7},{6,4},{7,5},{8,10},{9,11},{10,... | collective-permute-start | bytes 589832 | tf_op jit(solution)/shard_map/ppermute | solution.py:478
  221.2 3.1 %collective-permute-start.6 = (bf16[64,1536]{1,0:T(8,128)(2,1)S(1)}, bf16[64,1536]{1,0:T(8,128)(2,1)S(1)}, u32[]{:S(2)}, u32[]{:S(2)}) collective-permute-start(bf16[64,1536]{1,0:T(8,128)(2,1)S(1)} %get-tuple-element.57), channel_id=1, source_target_pairs={{0,3},{1,0},{2,1},{3,2},{4,7},{5,4},{6,5},{7,6},{8,11},{9,8},{10,9... | collective-permute-start | bytes 589832 | tf_op jit(solution)/shard_map/ppermute | solution.py:478
  224.3 3.6 %all-to-all-done.5 = bf16[64,2,768]{2,1,0:T(2,128)(2,1)S(1)} async-done(((bf16[64,2,768]{2,1,0:T(2,128)(2,1)}), bf16[64,2,768]{2,1,0:T(2,128)(2,1)S(1)}, u32[]{:S(2)}, u32[]{:S(2)}) %all-to-all-start.5) | async-done | bytes 196640 | tf_op jit(solution)/shard_map/all_to_all | solution.py:465
  228.9 10.9 %all-to-all-start.6 = ((bf16[64,2,768]{2,1,0:T(2,128)(2,1)}), bf16[64,2,768]{2,1,0:T(2,128)(2,1)S(1)}, u32[]{:S(2)}, u32[]{:S(2)}) async-start(bf16[64,2,768]{2,1,0:T(2,128)(2,1)} %broadcast_in_dim.48), calls=%async_computation.6 | async-start | bytes 393216 | tf_op jit(solution)/shard_map/all_to_all | solution.py:49
  244.0 4.0 %collective-permute-start.8 = (bf16[64,1536]{1,0:T(8,128)(2,1)S(1)}, bf16[64,1536]{1,0:T(8,128)(2,1)S(1)}, u32[]{:S(2)}, u32[]{:S(2)}) collective-permute-start(bf16[64,1536]{1,0:T(8,128)(2,1)S(1)} %shard_map.139), channel_id=1, source_target_pairs={{0,2},{1,3},{2,0},{3,1},{4,6},{5,7},{6,4},{7,5},{8,10},{9,11},{10,... | collective-permute-start | bytes 589832 | tf_op jit(solution)/shard_map/ppermute | solution.py:480
  248.0 2.0 collective-permute-start.7
  250.1 2.2 collective-permute-done.8
  252.3 4.7 %collective-permute-done.7 = bf16[64,1536]{1,0:T(8,128)(2,1)S(1)} collective-permute-done((bf16[64,1536]{1,0:T(8,128)(2,1)S(1)}, bf16[64,1536]{1,0:T(8,128)(2,1)S(1)}, u32[]{:S(2)}, u32[]{:S(2)}) %collective-permute-start.7) | collective-permute-done | bytes 196640 | tf_op jit(solution)/shard_map/ppermute | solution.py:480
  257.2 6.0 %collective-permute-start.10 = (bf16[128,768]{1,0:T(8,128)(2,1)S(1)}, bf16[128,768]{1,0:T(8,128)(2,1)S(1)}, u32[]{:S(2)}, u32[]{:S(2)}) collective-permute-start(bf16[128,768]{1,0:T(8,128)(2,1)S(1)} %reshape.76), channel_id=1, source_target_pairs={{0,4},{4,0},{1,5},{5,1},{2,6},{6,2},{3,7},{7,3},{8,12},{12,8},{9,1... | collective-permute-start | bytes 589832 | tf_op jit(solution)/shard_map/ppermute | solution.py:468
  (123 shorter events, 44.3 us)
Async XLA Ops:
  1.5 9.6 %collective-permute-start = (bf16[24,768]{1,0:T(8,128)(2,1)S(1)}, bf16[24,768]{1,0:T(8,128)(2,1)S(1)}, u32[]{:S(2)}, u32[]{:S(2)}) collective-permute-start(bf16[24,768]{1,0:T(8,128)(2,1)S(1)} %fusion.3), channel_id=1, source_target_pairs={{0,4},{4,0},{1,5},{5,1},{2,6},{6,2},{3,7},{7,3},{8,12},{12,8},{9,1... | collective-permute-start | bytes 110600 | tf_op jit(solution)/shard_map/ppermute | solution.py:404
  43.4 44.0 %all-to-all-start = ((bf16[4,640,768]{2,1,0:T(8,128)(2,1)}), bf16[4,640,768]{2,1,0:T(8,128)(2,1)}, u32[]{:S(2)}, u32[]{:S(2)}) async-start(bf16[4,640,768]{2,1,0:T(8,128)(2,1)} %broadcast_in_dim.46), calls=%async_computation | async-start | bytes 7864320 | tf_op jit(solution)/shard_map/all_to_all | solution.py:49
  88.4 18.3 %all-to-all-start.1 = ((bf16[4,128,768]{2,1,0:T(8,128)(2,1)}), bf16[4,128,768]{2,1,0:T(8,128)(2,1)S(1)}, u32[]{:S(2)}, u32[]{:S(2)}) async-start(bf16[4,128,768]{2,1,0:T(8,128)(2,1)} %broadcast_in_dim.47), calls=%async_computation.1 | async-start | bytes 1572864 | tf_op jit(solution)/shard_map/all_to_all | solution.py:49
  96.9 30.6 %collective-permute-start.1 = (bf16[1536,768]{1,0:T(8,128)(2,1)}, bf16[1536,768]{1,0:T(8,128)(2,1)}, u32[]{:S(2)}, u32[]{:S(2)}) collective-permute-start(bf16[1536,768]{1,0:T(8,128)(2,1)} %bitcast.10.up_ref.own_ref), channel_id=1, source_target_pairs={{0,4},{4,0},{1,5},{5,1},{2,6},{6,2},{3,7},{7,3},{8,12},{12,8},{9,1... | collective-permute-start | bytes 7077896 | tf_op jit(solution)/shard_map/ppermute | solution.py:415
  106.9 6.1 %copy-start.34 = (s32[1,2]{1,0:T(1,128)S(1)}, s32[1,2]{1,0:T(1,128)}, u32[]{:S(2)}) copy-start(s32[1,2]{1,0:T(1,128)} %param.15) | copy-start | bytes 28
  106.9 9.2 %copy-start.16 = (bf16[1536,64]{0,1:T(8,128)(2,1)S(1)}, bf16[1536,64]{0,1:T(8,128)(2,1)}, u32[]{:S(2)}) copy-start(bf16[1536,64]{0,1:T(8,128)(2,1)} %param.18) | copy-start | bytes 589828
  107.2 25.7 %collective-permute-start.2 = (bf16[1536,768]{1,0:T(8,128)(2,1)S(1)}, bf16[1536,768]{1,0:T(8,128)(2,1)}, u32[]{:S(2)}, u32[]{:S(2)}) collective-permute-start(bf16[1536,768]{1,0:T(8,128)(2,1)S(1)} %bitcast.53), channel_id=1, source_target_pairs={{0,4},{4,0},{1,5},{5,1},{2,6},{6,2},{3,7},{7,3},{8,12},{12,8},{9,1... | collective-permute-start | bytes 7077896 | tf_op jit(solution)/shard_map/ppermute | solution.py:417
  119.8 11.3 %copy-start.12 = (bf16[64,768]{1,0:T(8,128)(2,1)}, bf16[64,768]{1,0:T(8,128)(2,1)S(1)}, u32[]{:S(2)}) copy-start(bf16[64,768]{1,0:T(8,128)(2,1)S(1)} %get-tuple-element.61.b_ref.bt_ref) | copy-start | bytes 294916
  119.8 11.3 %copy-start.14 = (bf16[64,768]{1,0:T(8,128)(2,1)}, bf16[64,768]{1,0:T(8,128)(2,1)S(1)}, u32[]{:S(2)}) copy-start(bf16[64,768]{1,0:T(8,128)(2,1)S(1)} %get-tuple-element.62.b_ref.bo_ref) | copy-start | bytes 294916
  137.2 16.4 %all-to-all-start.2 = ((bf16[4,64,1536]{2,1,0:T(8,128)(2,1)}), bf16[4,64,1536]{2,1,0:T(8,128)(2,1)}, u32[]{:S(2)}, u32[]{:S(2)}) async-start(bf16[4,64,1536]{2,1,0:T(8,128)(2,1)} %bitcast.57), calls=%async_computation.2 | async-start | bytes 1572864 | tf_op jit(solution)/shard_map/all_to_all | solution.py:447
  155.5 23.8 %copy-start.13 = (bf16[64,768]{1,0:T(8,128)(2,1)S(1)}, bf16[64,768]{1,0:T(8,128)(2,1)}, u32[]{:S(2)}) copy-start(bf16[64,768]{1,0:T(8,128)(2,1)} %copy-done.12) | copy-start | bytes 294916
  155.6 23.8 %copy-start.15 = (bf16[64,768]{1,0:T(8,128)(2,1)S(1)}, bf16[64,768]{1,0:T(8,128)(2,1)}, u32[]{:S(2)}) copy-start(bf16[64,768]{1,0:T(8,128)(2,1)} %copy-done.14) | copy-start | bytes 294916
  155.6 23.8 %copy-start.19 = (f32[256,768]{1,0:T(8,128)S(1)}, f32[256,768]{1,0:T(8,128)}, u32[]{:S(2)}) copy-start(f32[256,768]{1,0:T(8,128)} %copy-done.18) | copy-start | bytes 2359300
  155.6 23.8 %copy-start.21 = (f32[256,768]{1,0:T(8,128)S(1)}, f32[256,768]{1,0:T(8,128)}, u32[]{:S(2)}) copy-start(f32[256,768]{1,0:T(8,128)} %copy-done.20) | copy-start | bytes 2359300
  155.6 23.8 %copy-start.27 = (f32[64,1]{1,0:T(8,128)S(1)}, f32[64,1]{1,0:T(8,128)}, u32[]{:S(2)}) copy-start(f32[64,1]{1,0:T(8,128)} %fusion.4.mask_ref) | copy-start | bytes 772
  157.2 26.6 %copy-start.3 = (f32[64,1536]{1,0:T(8,128)}, f32[64,1536]{1,0:T(8,128)S(1)}, u32[]{:S(2)}) copy-start(f32[64,1536]{1,0:T(8,128)S(1)} %get-tuple-element.35.unit_ref) | copy-start | bytes 1179652
  186.6 23.8 %copy-start.17 = (bf16[1536,64]{0,1:T(8,128)(2,1)S(1)}, bf16[1536,64]{0,1:T(8,128)(2,1)}, u32[]{:S(2)}) copy-start(bf16[1536,64]{0,1:T(8,128)(2,1)} %param.18) | copy-start | bytes 589828
  186.6 23.8 %copy-start.30 = (bf16[256,64]{1,0:T(8,128)(2,1)S(1)}, bf16[256,64]{1,0:T(8,128)(2,1)}, u32[]{:S(2)}) copy-start(bf16[256,64]{1,0:T(8,128)(2,1)} %copy-done.29) | copy-start | bytes 98308
  186.6 8.5 %all-to-all-start.4 = ((bf16[4,80,256]{2,1,0:T(8,128)(2,1)}), bf16[4,80,256]{2,1,0:T(8,128)(2,1)S(1)}, u32[]{:S(2)}, u32[]{:S(2)}) async-start(bf16[4,80,256]{2,1,0:T(8,128)(2,1)} %copy-done.28), calls=%async_computation.4 | async-start | bytes 327680 | tf_op jit(solution)/shard_map/all_to_all | solution.py:455
  194.4 16.1 %copy-start.7 = (bf16[256,768]{1,0:T(8,128)(2,1)S(1)}, bf16[256,768]{1,0:T(8,128)(2,1)}, u32[]{:S(2)}) copy-start(bf16[256,768]{1,0:T(8,128)(2,1)} %copy-done.5) | copy-start | bytes 1179652
  194.4 16.1 %copy-start.10 = (bf16[256,768]{1,0:T(8,128)(2,1)S(1)}, bf16[256,768]{1,0:T(8,128)(2,1)}, u32[]{:S(2)}) copy-start(bf16[256,768]{1,0:T(8,128)(2,1)} %copy-done.8) | copy-start | bytes 1179652
  195.8 6.1 %collective-permute-start.3 = (bf16[128,768]{1,0:T(8,128)(2,1)S(1)}, bf16[128,768]{1,0:T(8,128)(2,1)S(1)}, u32[]{:S(2)}, u32[]{:S(2)}) collective-permute-start(bf16[128,768]{1,0:T(8,128)(2,1)S(1)} %get-tuple-element.46), channel_id=1, source_target_pairs={{0,4},{4,0},{1,5},{5,1},{2,6},{6,2},{3,7},{7,3},{8,12},{12,8},{9,1... | collective-permute-start | bytes 589832 | tf_op jit(solution)/shard_map/ppermute | solution.py:462
  202.8 25.2 %all-to-all-start.5 = ((bf16[64,2,768]{2,1,0:T(2,128)(2,1)}), bf16[64,2,768]{2,1,0:T(2,128)(2,1)S(1)}, u32[]{:S(2)}, u32[]{:S(2)}) async-start(bf16[64,2,768]{2,1,0:T(2,128)(2,1)} %reshape.75), calls=%async_computation.5 | async-start | bytes 393216 | tf_op jit(solution)/shard_map/all_to_all | solution.py:465
  214.6 27.0 %copy-start.4 = (f32[64,1536]{1,0:T(8,128)S(1)}, f32[64,1536]{1,0:T(8,128)}, u32[]{:S(2)}) copy-start(f32[64,1536]{1,0:T(8,128)} %copy-done.3) | copy-start | bytes 1179652
  214.7 26.9 %collective-permute-start.4 = (bf16[64,1536]{1,0:T(8,128)(2,1)S(1)}, bf16[64,1536]{1,0:T(8,128)(2,1)S(1)}, u32[]{:S(2)}, u32[]{:S(2)}) collective-permute-start(bf16[64,1536]{1,0:T(8,128)(2,1)S(1)} %get-tuple-element.59), channel_id=1, source_target_pairs={{0,1},{1,2},{2,3},{3,0},{4,5},{5,6},{6,7},{7,4},{8,9},{9,10},{10,1... | collective-permute-start | bytes 589832 | tf_op jit(solution)/shard_map/ppermute | solution.py:478
  217.0 24.6 %collective-permute-start.5 = (bf16[64,1536]{1,0:T(8,128)(2,1)S(1)}, bf16[64,1536]{1,0:T(8,128)(2,1)S(1)}, u32[]{:S(2)}, u32[]{:S(2)}) collective-permute-start(bf16[64,1536]{1,0:T(8,128)(2,1)S(1)} %get-tuple-element.58), channel_id=1, source_target_pairs={{0,2},{1,3},{2,0},{3,1},{4,6},{5,7},{6,4},{7,5},{8,10},{9,11},{10,... | collective-permute-start | bytes 589832 | tf_op jit(solution)/shard_map/ppermute | solution.py:478
  221.2 20.4 %collective-permute-start.6 = (bf16[64,1536]{1,0:T(8,128)(2,1)S(1)}, bf16[64,1536]{1,0:T(8,128)(2,1)S(1)}, u32[]{:S(2)}, u32[]{:S(2)}) collective-permute-start(bf16[64,1536]{1,0:T(8,128)(2,1)S(1)} %get-tuple-element.57), channel_id=1, source_target_pairs={{0,3},{1,0},{2,1},{3,2},{4,7},{5,4},{6,5},{7,6},{8,11},{9,8},{10,9... | collective-permute-start | bytes 589832 | tf_op jit(solution)/shard_map/ppermute | solution.py:478
  228.9 28.2 %all-to-all-start.6 = ((bf16[64,2,768]{2,1,0:T(2,128)(2,1)}), bf16[64,2,768]{2,1,0:T(2,128)(2,1)S(1)}, u32[]{:S(2)}, u32[]{:S(2)}) async-start(bf16[64,2,768]{2,1,0:T(2,128)(2,1)} %broadcast_in_dim.48), calls=%async_computation.6 | async-start | bytes 393216 | tf_op jit(solution)/shard_map/all_to_all | solution.py:49
  242.1 7.9 %collective-permute-start.9 = (bf16[64,1536]{1,0:T(8,128)(2,1)S(1)}, bf16[64,1536]{1,0:T(8,128)(2,1)S(1)}, u32[]{:S(2)}, u32[]{:S(2)}) collective-permute-start(bf16[64,1536]{1,0:T(8,128)(2,1)S(1)} %shard_map.139), channel_id=1, source_target_pairs={{0,3},{1,0},{2,1},{3,2},{4,7},{5,4},{6,5},{7,6},{8,11},{9,8},{10,9... | collective-permute-start | bytes 589832 | tf_op jit(solution)/shard_map/ppermute | solution.py:480
  244.0 8.2 %collective-permute-start.8 = (bf16[64,1536]{1,0:T(8,128)(2,1)S(1)}, bf16[64,1536]{1,0:T(8,128)(2,1)S(1)}, u32[]{:S(2)}, u32[]{:S(2)}) collective-permute-start(bf16[64,1536]{1,0:T(8,128)(2,1)S(1)} %shard_map.139), channel_id=1, source_target_pairs={{0,2},{1,3},{2,0},{3,1},{4,6},{5,7},{6,4},{7,5},{8,10},{9,11},{10,... | collective-permute-start | bytes 589832 | tf_op jit(solution)/shard_map/ppermute | solution.py:480
  248.0 8.9 %collective-permute-start.7 = (bf16[64,1536]{1,0:T(8,128)(2,1)S(1)}, bf16[64,1536]{1,0:T(8,128)(2,1)S(1)}, u32[]{:S(2)}, u32[]{:S(2)}) collective-permute-start(bf16[64,1536]{1,0:T(8,128)(2,1)S(1)} %shard_map.139), channel_id=1, source_target_pairs={{0,1},{1,2},{2,3},{3,0},{4,5},{5,6},{6,7},{7,4},{8,9},{9,10},{10,1... | collective-permute-start | bytes 589832 | tf_op jit(solution)/shard_map/ppermute | solution.py:480
  257.2 7.0 %collective-permute-start.10 = (bf16[128,768]{1,0:T(8,128)(2,1)S(1)}, bf16[128,768]{1,0:T(8,128)(2,1)S(1)}, u32[]{:S(2)}, u32[]{:S(2)}) collective-permute-start(bf16[128,768]{1,0:T(8,128)(2,1)S(1)} %reshape.76), channel_id=1, source_target_pairs={{0,4},{4,0},{1,5},{5,1},{2,6},{6,2},{3,7},{7,3},{8,12},{12,8},{9,1... | collective-permute-start | bytes 589832 | tf_op jit(solution)/shard_map/ppermute | solution.py:468
  (20 other events, 22.4 us)

commit v5 on v4

--- a/solution.py
+++ b/solution.py
@@ -18,9 +18,9 @@
 DP = ("z", "x", "c")
 CHIPS = ("z", "x")
 SWAP = [(0, 1), (1, 0)]
-EARLY = 16
+LATE = 8
 NOTE = 16
-VMEM_LIMIT = 40 * 1024 * 1024
+VMEM_LIMIT = 56 * 1024 * 1024
 SMEM = pltpu.SMEM
 
 
@@ -100,6 +100,20 @@
         compiler_params=params(),
         cost_estimate=cost(4 * rows * width * rank, 4 * rows * width),
     )(wins, tokens, mod, a_turned)
+
+
+def after_kernel(*refs):
+    refs[-1][...] = refs[0][...]
+
+
+def after(value, others):
+    return pl.pallas_call(
+        after_kernel,
+        out_shape=jax.ShapeDtypeStruct(value.shape, value.dtype),
+        in_specs=[pl.BlockSpec(memory_space=pltpu.VMEM)] + [pl.BlockSpec(memory_space=pl.ANY)] * len(others),
+        compiler_params=params(),
+        cost_estimate=cost(0, 4 * value.size),
+    )(value, *others)
 
 
 def up_kernel(modded_ref, low_ref, up_ref, b_ref, pol_ref, ref_ref, slope_ref):
@@ -406,16 +420,6 @@
     second = jnp.where(core == 0, got, keep)
     up_pair = jnp.concatenate([first[:thin], second[:thin]], axis=0)
     down_pair = jnp.concatenate([first[thin:], second[thin:]], axis=0)
-    line_one = lax.all_gather(jnp.concatenate([up_pair, down_pair[:EARLY]], 0), "z", axis=0, tiled=True)
-    down_late, line_one = lax.optimization_barrier((down_pair[EARLY:], line_one))
-    line_two = lax.all_gather(down_late, "z", axis=0, tiled=True)
-    near_one = spread(line_one, "x", n_x).reshape(n_x, n_z, pair + EARLY, half).transpose(1, 0, 2, 3)
-    near_two = spread(line_two, "x", n_x).reshape(n_x, n_z, pair - EARLY, half).transpose(1, 0, 2, 3)
-    up_own = near_one[:, :, :pair].reshape(width, half)
-    up_other = lax.ppermute(up_own, "c", SWAP)
-    down_own = jnp.concatenate([near_one[:, :, pair:], near_two], axis=2).reshape(width, half)
-    down_other = lax.ppermute(down_own, "c", SWAP)
-
     count = live_block_count[0]
     wins = preferred_blocks[0]
     slots = jnp.arange(CAP, dtype=jnp.int32)
@@ -440,6 +444,23 @@
     factor_own = lax.dynamic_slice_in_dim(factor_out, core * half, half, axis=1)
     factor_other = lax.dynamic_slice_in_dim(factor_out, (1 - core) * half, half, axis=1)
     modded, low, low_split = prepare(preferred_blocks, tokens, modulation.reshape(6, width), a_turned)
+
+    early = pair - LATE
+    line = lax.all_gather(jnp.concatenate([up_pair, down_pair[:early]], 0), "z", axis=0, tiled=True)
+    line = line.reshape(n_z, pair + early, half)
+    line = jnp.concatenate([line[:, :pair].reshape(n_z * pair, half), line[:, pair:].reshape(n_z * early, half)], 0)
+    near = spread(line, "x", n_x)
+    late = spread(down_pair[early:], "x", n_x).reshape(n_x * LATE, half)
+    late = after(late, [modded, low, low_split, factor_own, factor_other, x_own, t_own, gate, scale_own, mask])
+    late = lax.all_gather(late, "z", axis=0, tiled=True).reshape(n_z, n_x, LATE, half)
+
+    def arrange(block, late):
+        up = block[:, : n_z * pair].reshape(n_x, n_z, pair, half).transpose(1, 0, 2, 3).reshape(width, half)
+        down = block[:, n_z * pair :].reshape(n_x, n_z, early, half).transpose(1, 0, 2, 3)
+        return up, jnp.concatenate([down, late], axis=2).reshape(width, half)
+
+    up_own, down_own = arrange(near, late)
+    up_other, down_other = arrange(lax.ppermute(near, "c", SWAP), lax.ppermute(late, "c", SWAP))
 
     pol_own, ref_own, slope_own = activate(modded, low, up_own, factor_own)
     pol_other, ref_other, slope_other = activate(modded, low, up_other, factor_other)

time: 267 us -> 319 us (1.19)
  blocking collectives: 72.8 us -> 120 us
  Pallas kernels: 26.9 us -> 46.7 us
  waiting for transfers between devices: 34.3 us -> 15.3 us
  starting transfers between devices: 86 us -> 92.5 us
  local copies, waits for them, and re-layouts: 31.2 us -> 27.7 us
    all_to_all x0 -> x1, blocking collectives: none -> 42.9 us  [spread(): lax.all_to_all(jnp.broadcast_to(value[None], (n, *value.shape)), axes, 0,...]
    all_to_all x3 -> x2, waiting for transfers between devices: 17.6 us -> 0.01 us  [spread(): lax.all_to_all(jnp.broadcast_to(value[None], (n, *value.shape)), axes, 0,...]
    unnamed x71 -> x21, local copies, waits for them, and re-layouts: 16.4 us -> 2.96 us
    ppermute x2, starting transfers between devices: 14.1 us -> 19.7 us  [the longest x1 10 us: per_device(): lax.ppermute(near, 'c', SWAP)]
    transpose x0 -> x2, local copies, waits for them, and re-layouts: none -> 3.43 us  [arrange(): block[:, :n_z * pair].reshape(n_x, n_z, pair, half).transpose(1, 0, 2, 3)]
    all_to_all x1, waiting for transfers between devices: 3.89 us -> 7.11 us  [per_device(): got_pol = lax.all_to_all(part_pol, 't', 0, 0, tiled=True)]
    concatenate x1 -> x2, local copies, waits for them, and re-layouts: 0.25 us -> 3.45 us  [arrange(): return (up, jnp.concatenate([down, late], axis=2).reshape(width, half))]
    all_to_all x3 -> x2, starting transfers between devices: 19.3 us -> 17.1 us  [spread(): lax.all_to_all(jnp.broadcast_to(value[None], (n, *value.shape)), axes, 0,...]
  transfers between devices with their start and end apart: 17 -> 16, of which waited for: 9 -> 8; matrix products, arithmetic and copies ran while one was open for 6% -> 8% of each run, Pallas kernels for 6% -> 8%
where the time goes in v5:
time: 319 us; the launch traced here: 318 us
  blocking collectives  120 us (38%)
  starting transfers between devices  92.5 us (29%)
  Pallas kernels  46.7 us (15%)
  local copies, waits for them, and re-layouts  27.7 us (9%)
  waiting for transfers between devices  15.3 us (5%)
  other arithmetic  10.5 us (3%)
  between operations  4.84 us (2%)
    all_to_all x1, blocking collectives, spread(): lax.all_to_all(jnp.broadcast_to(value[None], (n, *value.shape)), axes, 0,...  42.9 us
    all_gather x1, blocking collectives, per_device(): lax.all_gather(jnp.concatenate([up_pair, down_pair[:early]], 0), 'z', axi...  29.2 us
    all_to_all x1, blocking collectives, per_device(): got_dy = lax.all_to_all(send, 't', 0, 0, tiled=True)  24.1 us
    all_gather x1, blocking collectives, per_device(): lax.all_gather(late, 'z', axis=0, tiled=True).reshape(n_z, n_x, LATE, half)  23.9 us
    all_to_all x2, starting transfers between devices, spread(): lax.all_to_all(jnp.broadcast_to(value[None], (n, *value.shape)), axes, 0,...  17.1 us
    all_to_all x1, starting transfers between devices, per_device(): lax.all_to_all(pile.reshape(chips, 2 * rank // chips, half), CHIPS, 0, 0,...  10.6 us
    pallas_call x2, Pallas kernels, lower(): pl.pallas_call(down_kernel, grid=(width // step,), out_shape=jax.ShapeDty...  10 us
    ppermute x1, starting transfers between devices, per_device(): lax.ppermute(near, 'c', SWAP)  10 us
  transfers between devices with their start and end apart: 16, of which 8 were waited for; matrix products, arithmetic and copies ran while one was open for 8% of the time, Pallas kernels for 8%

profile of v5, /device:TPU:1, one launch (start us, length us, event | category | flops | bytes accessed | tf_op | source)
XLA Modules:
  0.0 317.5 jit_solution(14279583989259015180)
XLA Ops:
  1.5 8.8 %collective-permute-start = (bf16[24,768]{1,0:T(8,128)(2,1)S(1)}, bf16[24,768]{1,0:T(8,128)(2,1)S(1)}, u32[]{:S(2)}, u32[]{:S(2)}) collective-permute-start(bf16[24,768]{1,0:T(8,128)(2,1)S(1)} %fusion.2), channel_id=1, source_target_pairs={{0,4},{4,0},{1,5},{5,1},{2,6},{6,2},{3,7},{7,3},{8,12},{12,8},{9,1... | collective-permute-start | bytes 110600 | tf_op jit(solution)/shard_map/ppermute | solution.py:418
  12.1 29.2 %all_gather.6 = bf16[640,768]{1,0:T(8,128)(2,1)S(1)} all-gather(bf16[40,768]{1,0:T(8,128)(2,1)S(1)} %fusion.1), channel_id=1, replica_groups=mesh['z'=16,'x'=4,'c'=2,'t'=4] {'z'}, dimensions={0}, use_global_device_ids=true | all-gather | bytes 1044480 | tf_op jit(solution)/shard_map/all_gather | solution.py:449
  41.7 42.9 %all_to_all.35 = bf16[4,640,768]{2,1,0:T(8,128)(2,1)} all-to-all(bf16[4,640,768]{2,1,0:T(8,128)(2,1)S(1)} %broadcast_in_dim.46), channel_id=1, replica_groups=mesh['z'=16,'x'=4,'c'=2,'t'=4] {'x'}, dimensions={0} | all-to-all | bytes 7864320 | tf_op jit(solution)/shard_map/all_to_all | solution.py:49
  84.6 10.0 %collective-permute-start.1 = (bf16[4,640,768]{2,1,0:T(8,128)(2,1)}, bf16[4,640,768]{2,1,0:T(8,128)(2,1)}, u32[]{:S(2)}, u32[]{:S(2)}) collective-permute-start(bf16[4,640,768]{2,1,0:T(8,128)(2,1)} %all_to_all.35), channel_id=1, source_target_pairs={{0,4},{4,0},{1,5},{5,1},{2,6},{6,2},{3,7},{7,3},{8,12},{12,8},{9,1... | collective-permute-start | bytes 11796488 | tf_op jit(solution)/shard_map/ppermute | solution.py:463
  102.8 3.3 %all-to-all-start.1 = ((bf16[4,8,768]{2,1,0:T(8,128)(2,1)}), bf16[4,8,768]{2,1,0:T(8,128)(2,1)S(1)}, u32[]{:S(2)}, u32[]{:S(2)}) async-start(bf16[4,8,768]{2,1,0:T(8,128)(2,1)} %broadcast_in_dim.47), calls=%async_computation.1 | async-start | bytes 98304 | tf_op jit(solution)/shard_map/all_to_all | solution.py:49
  108.0 2.8 shard_map.129
  112.8 23.9 %all_gather.7 = bf16[512,768]{1,0:T(8,128)(2,1)S(1)} all-gather(bf16[32,768]{1,0:T(8,128)(2,1)} %shard_map.132), channel_id=1, replica_groups=mesh['z'=16,'x'=4,'c'=2,'t'=4] {'z'}, dimensions={0}, use_global_device_ids=true | all-gather | bytes 835584 | tf_op jit(solution)/shard_map/all_gather | solution.py:455
  136.7 9.6 %collective-permute-start.2 = (bf16[16,4,8,768]{3,2,0,1:T(8,128)(2,1)S(1)}, bf16[16,4,8,768]{3,2,0,1:T(8,128)(2,1)S(1)}, u32[]{:S(2)}, u32[]{:S(2)}) collective-permute-start(bf16[16,4,8,768]{3,2,0,1:T(8,128)(2,1)S(1)} %copy.18), channel_id=1, source_target_pairs={{0,4},{4,0},{1,5},{5,1},{2,6},{6,2},{3,7},{7,3},{8,12},{12,8},{9,1... | collective-permute-start | bytes 2359304 | tf_op jit(solution)/shard_map/ppermute | solution.py:463
  153.4 4.8 %shard_map.130 = (bf16[256,768]{1,0:T(8,128)(2,1)}, bf16[256,768]{1,0:T(8,128)(2,1)}, f32[256,768]{1,0:T(8,128)}) custom-call(bf16[256,1536]{1,0:T(8,128)(2,1)} %get-tuple-element.24.modded_ref.refs_1_, bf16[256,64]{1,0:T(8,128)(2,1)} %get-tuple-element.25.low_ref.refs_2_, bf16[1536,768]{1,0:T(8,128)(2,1)} %bitcast.72, ...), custom_call_target="tpu_custom_call" | custom-call | flops 603979776 | bytes 4325376 | tf_op jit(solution)/shard_map/pallas_call | solution.py:133
  165.1 4.8 %shard_map.131 = (bf16[256,768]{1,0:T(8,128)(2,1)}, bf16[256,768]{1,0:T(8,128)(2,1)}, f32[256,768]{1,0:T(8,128)}) custom-call(bf16[256,1536]{1,0:T(8,128)(2,1)} %get-tuple-element.24.modded_ref.refs_1_, bf16[256,64]{1,0:T(8,128)(2,1)} %get-tuple-element.25.low_ref.refs_2_, bf16[1536,768]{1,0:T(8,128)(2,1)} %bitcast.74, ...), custom_call_target="tpu_custom_call" | custom-call | flops 603979776 | bytes 4325376 | tf_op jit(solution)/shard_map/pallas_call | solution.py:133
  169.9 5.0 %shard_map.133 = bf16[256,1536]{1,0:T(8,128)(2,1)} custom-call(bf16[256,768]{1,0:T(8,128)(2,1)} %get-tuple-element.26.left_ref, bf16[256,768]{1,0:T(8,128)(2,1)} %get-tuple-element.27.right_ref, bf16[1536,768]{1,0:T(8,128)(2,1)} %bitcast.66, bf16[1536,768]{1,0:T(8,128)(2,1)} %bitcast.69), custom_call_target="tpu_custom_call" | custom-call | flops 1207959552 | bytes 5505024 | tf_op jit(solution)/shard_map/pallas_call | solution.py:163
  174.9 4.2 %all-to-all-start.2 = ((bf16[4,64,1536]{2,1,0:T(8,128)(2,1)}), bf16[4,64,1536]{2,1,0:T(8,128)(2,1)S(1)}, u32[]{:S(2)}, u32[]{:S(2)}) async-start(bf16[4,64,1536]{2,1,0:T(8,128)(2,1)} %bitcast.86), calls=%async_computation.2 | async-start | bytes 1572864 | tf_op jit(solution)/shard_map/all_to_all | solution.py:468
  179.1 5.0 %shard_map.134 = bf16[256,1536]{1,0:T(8,128)(2,1)} custom-call(bf16[256,768]{1,0:T(8,128)(2,1)} %get-tuple-element.29.left_ref, bf16[256,768]{1,0:T(8,128)(2,1)} %get-tuple-element.30.right_ref, bf16[1536,768]{1,0:T(8,128)(2,1)} %bitcast.67, bf16[1536,768]{1,0:T(8,128)(2,1)} %bitcast.70), custom_call_target="tpu_custom_call" | custom-call | flops 1207959552 | bytes 5505024 | tf_op jit(solution)/shard_map/pallas_call | solution.py:163
  184.1 7.1 %all-to-all-done.2.got_ref = bf16[4,64,1536]{2,1,0:T(8,128)(2,1)S(1)} async-done(((bf16[4,64,1536]{2,1,0:T(8,128)(2,1)}), bf16[4,64,1536]{2,1,0:T(8,128)(2,1)S(1)}, u32[]{:S(2)}, u32[]{:S(2)}) %all-to-all-start.2) | async-done | bytes 786464 | tf_op jit(solution)/shard_map/all_to_all | solution.py:468
  192.1 3.1 shard_map.135
  195.2 24.1 %all_to_all.36.got_ref = bf16[4,128,1536]{2,1,0:T(8,128)(2,1)} all-to-all(bf16[4,128,1536]{2,1,0:T(8,128)(2,1)} %get-tuple-element.31), channel_id=1, replica_groups=mesh['z'=16,'x'=4,'c'=2,'t'=4] {'t'}, dimensions={0} | all-to-all | bytes 3145728 | tf_op jit(solution)/shard_map/all_to_all | solution.py:472
  219.2 7.0 %shard_map.136 = (bf16[256,768]{1,0:T(8,128)(2,1)}, bf16[256,768]{1,0:T(8,128)(2,1)}, bf16[256,64]{1,0:T(8,128)(2,1)}, bf16[4,80,256]{2,1,0:T(8,128)(2,1)}) custom-call(bf16[4,128,1536]{2,1,0:T(8,128)(2,1)} %all_to_all.36.got_ref, f32[64,1536]{1,0:T(8,128)} %get-tuple-element.32.unit_ref, bf16[64,1536]{1,0:T(8,128)(2,1)} %get-tuple-element.75.refs_6_.x_ref, ...), custom_call_target="tpu_custom_call" | custom-call | flops 1207959552 | bytes 7077888 | tf_op jit(solution)/shard_map/pallas_call | solution.py:254
  226.3 3.4 %all-to-all-start.4 = ((bf16[4,80,256]{2,1,0:T(8,128)(2,1)}), bf16[4,80,256]{2,1,0:T(8,128)(2,1)S(1)}, u32[]{:S(2)}, u32[]{:S(2)}) async-start(bf16[4,80,256]{2,1,0:T(8,128)(2,1)} %get-tuple-element.35), calls=%async_computation.4 | async-start | bytes 327680 | tf_op jit(solution)/shard_map/all_to_all | solution.py:476
  232.0 2.3 shard_map.137
  235.3 2.6 shard_map.138
  237.8 5.1 %collective-permute-start.3 = (bf16[128,768]{1,0:T(8,128)(2,1)}, bf16[128,768]{1,0:T(8,128)(2,1)S(1)}, u32[]{:S(2)}, u32[]{:S(2)}) collective-permute-start(bf16[128,768]{1,0:T(8,128)(2,1)} %get-tuple-element.42), channel_id=1, source_target_pairs={{0,4},{4,0},{1,5},{5,1},{2,6},{6,2},{3,7},{7,3},{8,12},{12,8},{9,1... | collective-permute-start | bytes 589832 | tf_op jit(solution)/shard_map/ppermute | solution.py:483
  246.0 10.6 %all-to-all-start.5 = ((bf16[64,2,768]{2,1,0:T(2,128)(2,1)}), bf16[64,2,768]{2,1,0:T(2,128)(2,1)S(1)}, u32[]{:S(2)}, u32[]{:S(2)}) async-start(bf16[64,2,768]{2,1,0:T(2,128)(2,1)} %reshape.111), calls=%async_computation.5 | async-start | bytes 393216 | tf_op jit(solution)/shard_map/all_to_all | solution.py:486
  256.6 5.4 %shard_map.139 = bf16[256,1536]{1,0:T(8,128)(2,1)} custom-call(bf16[128,768]{1,0:T(8,128)(2,1)} %copy-done.1, bf16[256,768]{1,0:T(8,128)(2,1)} %get-tuple-element.36.do_ref, bf16[256,768]{1,0:T(8,128)(2,1)} %get-tuple-element.37.dt_ref, bf16[256,64]{1,0:T(8,128)(2,1)} %get-tuple-element.43.dlow_ref, bf16[1536,768]{1,0:T(8,128)(2,1)} %bitcast.73, ...), custom_call_target="tpu_custom_call" | custom-call | flops 1207959552 | bytes 5505024 | tf_op jit(solution)/shard_map/pallas_call | solution.py:354
  264.0 2.2 collective-permute-start.4
  266.2 4.2 %collective-permute-start.5 = (bf16[64,1536]{1,0:T(8,128)(2,1)S(1)}, bf16[64,1536]{1,0:T(8,128)(2,1)S(1)}, u32[]{:S(2)}, u32[]{:S(2)}) collective-permute-start(bf16[64,1536]{1,0:T(8,128)(2,1)S(1)} %get-tuple-element.54), channel_id=1, source_target_pairs={{0,2},{1,3},{2,0},{3,1},{4,6},{5,7},{6,4},{7,5},{8,10},{9,11},{10,... | collective-permute-start | bytes 589832 | tf_op jit(solution)/shard_map/ppermute | solution.py:499
  270.4 3.1 collective-permute-start.6
  275.2 13.8 %all-to-all-start.6 = ((bf16[64,2,768]{2,1,0:T(2,128)(2,1)}), bf16[64,2,768]{2,1,0:T(2,128)(2,1)S(1)}, u32[]{:S(2)}, u32[]{:S(2)}) async-start(bf16[64,2,768]{2,1,0:T(2,128)(2,1)} %broadcast_in_dim.48), calls=%async_computation.6 | async-start | bytes 393216 | tf_op jit(solution)/shard_map/all_to_all | solution.py:49
  292.4 2.6 shard_map.140
  297.2 2.9 collective-permute-start.8
  300.1 4.0 %collective-permute-start.9 = (bf16[64,1536]{1,0:T(8,128)(2,1)}, bf16[64,1536]{1,0:T(8,128)(2,1)S(1)}, u32[]{:S(2)}, u32[]{:S(2)}) collective-permute-start(bf16[64,1536]{1,0:T(8,128)(2,1)} %shard_map.140), channel_id=1, source_target_pairs={{0,3},{1,0},{2,1},{3,2},{4,7},{5,4},{6,5},{7,6},{8,11},{9,8},{10,9... | collective-permute-start | bytes 589832 | tf_op jit(solution)/shard_map/ppermute | solution.py:501
  306.1 2.9 collective-permute-done.9
  310.2 5.2 %collective-permute-start.10 = (bf16[128,768]{1,0:T(8,128)(2,1)S(1)}, bf16[128,768]{1,0:T(8,128)(2,1)S(1)}, u32[]{:S(2)}, u32[]{:S(2)}) collective-permute-start(bf16[128,768]{1,0:T(8,128)(2,1)S(1)} %reshape.112), channel_id=1, source_target_pairs={{0,4},{4,0},{1,5},{5,1},{2,6},{6,2},{3,7},{7,3},{8,12},{12,8},{9,1... | collective-permute-start | bytes 589832 | tf_op jit(solution)/shard_map/ppermute | solution.py:489
  (82 shorter events, 47.0 us)
Async XLA Ops:
  1.5 9.6 %collective-permute-start = (bf16[24,768]{1,0:T(8,128)(2,1)S(1)}, bf16[24,768]{1,0:T(8,128)(2,1)S(1)}, u32[]{:S(2)}, u32[]{:S(2)}) collective-permute-start(bf16[24,768]{1,0:T(8,128)(2,1)S(1)} %fusion.2), channel_id=1, source_target_pairs={{0,4},{4,0},{1,5},{5,1},{2,6},{6,2},{3,7},{7,3},{8,12},{12,8},{9,1... | collective-permute-start | bytes 110600 | tf_op jit(solution)/shard_map/ppermute | solution.py:418
  41.6 54.2 %copy-start.9 = (s32[1,2]{1,0:T(1,128)S(1)}, s32[1,2]{1,0:T(1,128)}, u32[]{:S(2)}) copy-start(s32[1,2]{1,0:T(1,128)} %param.15) | copy-start | bytes 28
  41.7 57.3 %copy-start.4 = (bf16[64,1536]{1,0:T(8,128)(2,1)S(1)}, bf16[64,1536]{1,0:T(8,128)(2,1)}, u32[]{:S(2)}) copy-start(bf16[64,1536]{1,0:T(8,128)(2,1)} %param.19) | copy-start | bytes 589828
  41.7 59.8 %copy-start.8 = (bf16[2,3,1536]{2,0,1:T(2,128)(2,1)S(1)}, bf16[2,3,1536]{2,0,1:T(2,128)(2,1)}, u32[]{:S(2)}) copy-start(bf16[2,3,1536]{2,0,1:T(2,128)(2,1)} %param.12) | copy-start | bytes 55300
  84.6 73.6 %collective-permute-start.1 = (bf16[4,640,768]{2,1,0:T(8,128)(2,1)}, bf16[4,640,768]{2,1,0:T(8,128)(2,1)}, u32[]{:S(2)}, u32[]{:S(2)}) collective-permute-start(bf16[4,640,768]{2,1,0:T(8,128)(2,1)} %all_to_all.35), channel_id=1, source_target_pairs={{0,4},{4,0},{1,5},{5,1},{2,6},{6,2},{3,7},{7,3},{8,12},{12,8},{9,1... | collective-permute-start | bytes 11796488 | tf_op jit(solution)/shard_map/ppermute | solution.py:463
  102.8 8.0 %all-to-all-start.1 = ((bf16[4,8,768]{2,1,0:T(8,128)(2,1)}), bf16[4,8,768]{2,1,0:T(8,128)(2,1)S(1)}, u32[]{:S(2)}, u32[]{:S(2)}) async-start(bf16[4,8,768]{2,1,0:T(8,128)(2,1)} %broadcast_in_dim.47), calls=%async_computation.1 | async-start | bytes 98304 | tf_op jit(solution)/shard_map/all_to_all | solution.py:49
  110.8 0.6 copy-start.3
  136.7 22.9 %collective-permute-start.2 = (bf16[16,4,8,768]{3,2,0,1:T(8,128)(2,1)S(1)}, bf16[16,4,8,768]{3,2,0,1:T(8,128)(2,1)S(1)}, u32[]{:S(2)}, u32[]{:S(2)}) collective-permute-start(bf16[16,4,8,768]{3,2,0,1:T(8,128)(2,1)S(1)} %copy.18), channel_id=1, source_target_pairs={{0,4},{4,0},{1,5},{5,1},{2,6},{6,2},{3,7},{7,3},{8,12},{12,8},{9,1... | collective-permute-start | bytes 2359304 | tf_op jit(solution)/shard_map/ppermute | solution.py:463
  174.9 16.3 %all-to-all-start.2 = ((bf16[4,64,1536]{2,1,0:T(8,128)(2,1)}), bf16[4,64,1536]{2,1,0:T(8,128)(2,1)S(1)}, u32[]{:S(2)}, u32[]{:S(2)}) async-start(bf16[4,64,1536]{2,1,0:T(8,128)(2,1)} %bitcast.86), calls=%async_computation.2 | async-start | bytes 1572864 | tf_op jit(solution)/shard_map/all_to_all | solution.py:468
  191.2 0.9 copy-start
  226.3 8.3 %all-to-all-start.4 = ((bf16[4,80,256]{2,1,0:T(8,128)(2,1)}), bf16[4,80,256]{2,1,0:T(8,128)(2,1)S(1)}, u32[]{:S(2)}, u32[]{:S(2)}) async-start(bf16[4,80,256]{2,1,0:T(8,128)(2,1)} %get-tuple-element.35), calls=%async_computation.4 | async-start | bytes 327680 | tf_op jit(solution)/shard_map/all_to_all | solution.py:476
  234.6 0.7 copy-start.2
  237.8 6.3 %collective-permute-start.3 = (bf16[128,768]{1,0:T(8,128)(2,1)}, bf16[128,768]{1,0:T(8,128)(2,1)S(1)}, u32[]{:S(2)}, u32[]{:S(2)}) collective-permute-start(bf16[128,768]{1,0:T(8,128)(2,1)} %get-tuple-element.42), channel_id=1, source_target_pairs={{0,4},{4,0},{1,5},{5,1},{2,6},{6,2},{3,7},{7,3},{8,12},{12,8},{9,1... | collective-permute-start | bytes 589832 | tf_op jit(solution)/shard_map/ppermute | solution.py:483
  245.2 11.4 %copy-start.1 = (bf16[128,768]{1,0:T(8,128)(2,1)}, bf16[128,768]{1,0:T(8,128)(2,1)S(1)}, u32[]{:S(2)}) copy-start(bf16[128,768]{1,0:T(8,128)(2,1)S(1)} %add_convert_fusion.after_ref) | copy-start | bytes 589828
  246.0 28.2 %all-to-all-start.5 = ((bf16[64,2,768]{2,1,0:T(2,128)(2,1)}), bf16[64,2,768]{2,1,0:T(2,128)(2,1)S(1)}, u32[]{:S(2)}, u32[]{:S(2)}) async-start(bf16[64,2,768]{2,1,0:T(2,128)(2,1)} %reshape.111), calls=%async_computation.5 | async-start | bytes 393216 | tf_op jit(solution)/shard_map/all_to_all | solution.py:486
  264.0 27.6 %collective-permute-start.4 = (bf16[64,1536]{1,0:T(8,128)(2,1)S(1)}, bf16[64,1536]{1,0:T(8,128)(2,1)S(1)}, u32[]{:S(2)}, u32[]{:S(2)}) collective-permute-start(bf16[64,1536]{1,0:T(8,128)(2,1)S(1)} %get-tuple-element.55), channel_id=1, source_target_pairs={{0,1},{1,2},{2,3},{3,0},{4,5},{5,6},{6,7},{7,4},{8,9},{9,10},{10,1... | collective-permute-start | bytes 589832 | tf_op jit(solution)/shard_map/ppermute | solution.py:499
  266.2 25.4 %collective-permute-start.5 = (bf16[64,1536]{1,0:T(8,128)(2,1)S(1)}, bf16[64,1536]{1,0:T(8,128)(2,1)S(1)}, u32[]{:S(2)}, u32[]{:S(2)}) collective-permute-start(bf16[64,1536]{1,0:T(8,128)(2,1)S(1)} %get-tuple-element.54), channel_id=1, source_target_pairs={{0,2},{1,3},{2,0},{3,1},{4,6},{5,7},{6,4},{7,5},{8,10},{9,11},{10,... | collective-permute-start | bytes 589832 | tf_op jit(solution)/shard_map/ppermute | solution.py:499
  270.4 21.2 %collective-permute-start.6 = (bf16[64,1536]{1,0:T(8,128)(2,1)S(1)}, bf16[64,1536]{1,0:T(8,128)(2,1)S(1)}, u32[]{:S(2)}, u32[]{:S(2)}) collective-permute-start(bf16[64,1536]{1,0:T(8,128)(2,1)S(1)} %get-tuple-element.53), channel_id=1, source_target_pairs={{0,3},{1,0},{2,1},{3,2},{4,7},{5,4},{6,5},{7,6},{8,11},{9,8},{10,9... | collective-permute-start | bytes 589832 | tf_op jit(solution)/shard_map/ppermute | solution.py:499
  275.2 35.0 %all-to-all-start.6 = ((bf16[64,2,768]{2,1,0:T(2,128)(2,1)}), bf16[64,2,768]{2,1,0:T(2,128)(2,1)S(1)}, u32[]{:S(2)}, u32[]{:S(2)}) async-start(bf16[64,2,768]{2,1,0:T(2,128)(2,1)} %broadcast_in_dim.48), calls=%async_computation.6 | async-start | bytes 393216 | tf_op jit(solution)/shard_map/all_to_all | solution.py:49
  291.6 0.7 copy-start.5
  291.6 0.7 copy-start.6
  291.6 0.8 copy-start.7
  295.0 9.2 %collective-permute-start.7 = (bf16[64,1536]{1,0:T(8,128)(2,1)}, bf16[64,1536]{1,0:T(8,128)(2,1)S(1)}, u32[]{:S(2)}, u32[]{:S(2)}) collective-permute-start(bf16[64,1536]{1,0:T(8,128)(2,1)} %shard_map.140), channel_id=1, source_target_pairs={{0,1},{1,2},{2,3},{3,0},{4,5},{5,6},{6,7},{7,4},{8,9},{9,10},{10,1... | collective-permute-start | bytes 589832 | tf_op jit(solution)/shard_map/ppermute | solution.py:501
  297.2 8.9 %collective-permute-start.8 = (bf16[64,1536]{1,0:T(8,128)(2,1)}, bf16[64,1536]{1,0:T(8,128)(2,1)S(1)}, u32[]{:S(2)}, u32[]{:S(2)}) collective-permute-start(bf16[64,1536]{1,0:T(8,128)(2,1)} %shard_map.140), channel_id=1, source_target_pairs={{0,2},{1,3},{2,0},{3,1},{4,6},{5,7},{6,4},{7,5},{8,10},{9,11},{10,... | collective-permute-start | bytes 589832 | tf_op jit(solution)/shard_map/ppermute | solution.py:501
  300.1 8.9 %collective-permute-start.9 = (bf16[64,1536]{1,0:T(8,128)(2,1)}, bf16[64,1536]{1,0:T(8,128)(2,1)S(1)}, u32[]{:S(2)}, u32[]{:S(2)}) collective-permute-start(bf16[64,1536]{1,0:T(8,128)(2,1)} %shard_map.140), channel_id=1, source_target_pairs={{0,3},{1,0},{2,1},{3,2},{4,7},{5,4},{6,5},{7,6},{8,11},{9,8},{10,9... | collective-permute-start | bytes 589832 | tf_op jit(solution)/shard_map/ppermute | solution.py:501
  310.2 6.2 %collective-permute-start.10 = (bf16[128,768]{1,0:T(8,128)(2,1)S(1)}, bf16[128,768]{1,0:T(8,128)(2,1)S(1)}, u32[]{:S(2)}, u32[]{:S(2)}) collective-permute-start(bf16[128,768]{1,0:T(8,128)(2,1)S(1)} %reshape.112), channel_id=1, source_target_pairs={{0,4},{4,0},{1,5},{5,1},{2,6},{6,2},{3,7},{7,3},{8,12},{12,8},{9,1... | collective-permute-start | bytes 589832 | tf_op jit(solution)/shard_map/ppermute | solution.py:489

commit v6 on v4

--- a/solution.py
+++ b/solution.py
@@ -18,7 +18,6 @@
 DP = ("z", "x", "c")
 CHIPS = ("z", "x")
 SWAP = [(0, 1), (1, 0)]
-EARLY = 16
 NOTE = 16
 VMEM_LIMIT = 40 * 1024 * 1024
 SMEM = pltpu.SMEM
@@ -102,6 +101,20 @@
     )(wins, tokens, mod, a_turned)
 
 
+def after_kernel(*refs):
+    del refs
+
+
+def after(value, others):
+    return pl.pallas_call(
+        after_kernel,
+        out_shape=jax.ShapeDtypeStruct(value.shape, value.dtype),
+        in_specs=[pl.BlockSpec(memory_space=pl.ANY)] * (1 + len(others)),
+        out_specs=pl.BlockSpec(memory_space=pl.ANY),
+        input_output_aliases={0: 0},
+    )(value, *others)
+
+
 def up_kernel(modded_ref, low_ref, up_ref, b_ref, pol_ref, ref_ref, slope_ref):
     pre_ref = product(modded_ref[...], up_ref[...])
     pre_pol = pre_ref + product(low_ref[...], b_ref[...])
@@ -111,7 +124,7 @@
     ref_ref[...] = gelu(pre_ref).astype(BF16)
 
 
-def activate(modded, low, up, factor):
+def activate(modded, low, weights, factor):
     rows, width = modded.shape
     rank, half = factor.shape
     step = 256
@@ -133,7 +146,7 @@
         out_specs=[cut, cut, cut],
         compiler_params=params(),
         cost_estimate=cost(2 * rows * width * half, 2 * width * half + 10 * rows * half, 2 * rows * half),
-    )(modded, low, up, factor)
+    )(modded, low, weights, factor)
 
 
 def down_kernel(left_ref, right_ref, own_ref, other_ref, out_ref):
@@ -145,7 +158,7 @@
     rows, half = left.shape
     width = own.shape[0]
     step = 512
-    cut = pl.BlockSpec((step, half), lambda i: (i, 0))
+    cut = pl.BlockSpec((step, half), lambda i: (i, 1))
     return pl.pallas_call(
         down_kernel,
         grid=(width // step,),
@@ -229,11 +242,11 @@
 
 def backward(got, unit, x_own, t_own, gate, mask, own, other, b_own, b_other, s_own, s_other):
     groups, _, width = got.shape
-    half = own.shape[1]
+    half = s_own.shape[1]
     rank = b_own.shape[0]
     rows = CAP * BLK
     step = 256
-    weight = pl.BlockSpec((width, step), lambda i: (0, i))
+    weight = pl.BlockSpec((width, step), lambda i: (0, half // step + i))
     factor = pl.BlockSpec((rank, step), lambda i: (0, i))
     cut = pl.BlockSpec((rows, step), lambda i: (0, i))
     block = whole((BLK, width))
@@ -396,25 +409,13 @@
     group = lax.axis_index("t")
     thin, hidden = up_rows.shape
     half = hidden // n_c
-    pair = n_c * thin
     rank = factor_in.shape[1]
 
-    both = jnp.concatenate([up_rows, down_rows], axis=0)
-    keep = lax.dynamic_slice_in_dim(both, core * half, half, axis=1)
-    got = lax.ppermute(lax.dynamic_slice_in_dim(both, (1 - core) * half, half, axis=1), "c", SWAP)
-    first = jnp.where(core == 0, keep, got)
-    second = jnp.where(core == 0, got, keep)
-    up_pair = jnp.concatenate([first[:thin], second[:thin]], axis=0)
-    down_pair = jnp.concatenate([first[thin:], second[thin:]], axis=0)
-    line_one = lax.all_gather(jnp.concatenate([up_pair, down_pair[:EARLY]], 0), "z", axis=0, tiled=True)
-    down_late, line_one = lax.optimization_barrier((down_pair[EARLY:], line_one))
-    line_two = lax.all_gather(down_late, "z", axis=0, tiled=True)
-    near_one = spread(line_one, "x", n_x).reshape(n_x, n_z, pair + EARLY, half).transpose(1, 0, 2, 3)
-    near_two = spread(line_two, "x", n_x).reshape(n_x, n_z, pair - EARLY, half).transpose(1, 0, 2, 3)
-    up_own = near_one[:, :, :pair].reshape(width, half)
-    up_other = lax.ppermute(up_own, "c", SWAP)
-    down_own = jnp.concatenate([near_one[:, :, pair:], near_two], axis=2).reshape(width, half)
-    down_other = lax.ppermute(down_own, "c", SWAP)
+    sent = jnp.stack([up_rows.reshape(thin, n_c, half), down_rows.reshape(thin, n_c, half)], axis=2)
+    sent = sent.reshape(thin, n_c, 2 * half).transpose(1, 0, 2)
+    sent = jnp.broadcast_to(sent[None], (n_x, n_c, thin, 2 * half)).reshape(n_x * n_c, thin, 2 * half)
+    near = lax.all_to_all(sent, ("x", "c"), 0, 0, tiled=True).reshape(n_x * n_c * thin, 2 * half)
+    own = lax.all_gather(near, "z", axis=0, tiled=True)
 
     count = live_block_count[0]
     wins = preferred_blocks[0]
@@ -441,16 +442,19 @@
     factor_other = lax.dynamic_slice_in_dim(factor_out, (1 - core) * half, half, axis=1)
     modded, low, low_split = prepare(preferred_blocks, tokens, modulation.reshape(6, width), a_turned)
 
-    pol_own, ref_own, slope_own = activate(modded, low, up_own, factor_own)
-    pol_other, ref_other, slope_other = activate(modded, low, up_other, factor_other)
-    part_pol = lower(pol_own, pol_other, down_own, down_other).reshape(CAP, BLK, width)
+    own = after(own, [modded, low, low_split, factor_own, factor_other, x_own, t_own, gate, scale_own, mask])
+    other = lax.ppermute(own, "c", SWAP)
+
+    pol_own, ref_own, slope_own = activate(modded, low, own, factor_own)
+    pol_other, ref_other, slope_other = activate(modded, low, other, factor_other)
+    part_pol = lower(pol_own, pol_other, own, other).reshape(CAP, BLK, width)
     got_pol = lax.all_to_all(part_pol, "t", 0, 0, tiled=True)
-    part_ref = lower(ref_own, ref_other, down_own, down_other).reshape(CAP, BLK, width)
+    part_ref = lower(ref_own, ref_other, own, other).reshape(CAP, BLK, width)
 
     unit, send = miss(got_pol, part_ref, x_own, t_own, gate, mask)
     got_dy = lax.all_to_all(send, "t", 0, 0, tiled=True)
     d_own, d_other, dlow_part, send = backward(
-        got_dy, unit, x_own, t_own, gate, mask, down_own, down_other, factor_own, factor_other, slope_own, slope_other
+        got_dy, unit, x_own, t_own, gate, mask, own, other, factor_own, factor_other, slope_own, slope_other
     )
     got_low = lax.all_to_all(send, "t", 0, 0, tiled=True)
     b_own, b_other = factor_terms(low_split, d_own, d_other)
@@ -472,7 +476,7 @@
     sum_b = ends[:rank]
     sum_a = ends[rank:].T
 
-    dm_part = dm_terms(pile, d_own, d_other, dlow_part, up_own, up_other, a_turned).reshape(CAP, BLK, width)
+    dm_part = dm_terms(pile, d_own, d_other, dlow_part, own, other, a_turned).reshape(CAP, BLK, width)
     turns = [[(i, (i + step) % n_t) for i in range(n_t)] for step in range(n_t)]
     chunks = [lax.dynamic_index_in_dim(dm_part, (group + step) % n_t, 0, False) for step in range(n_t)]
     chunks = [chunks[0]] + [lax.ppermute(chunks[step], "t", turns[step]) for step in range(1, n_t)]

time: 267 us -> 260 us (0.974)
  waiting for transfers between devices: 34.3 us -> 80 us
  blocking collectives: 72.8 us -> 39.2 us
  starting transfers between devices: 86 us -> 67.4 us
  between operations: 5.23 us -> 18.6 us
  Pallas kernels: 26.9 us -> 19.8 us
  local copies, waits for them, and re-layouts: 31.2 us -> 27.7 us
  other arithmetic: 8.83 us -> 5.61 us
    all_gather x0 -> x1, waiting for transfers between devices: none -> 60.7 us  [per_device(): own = lax.all_gather(near, 'z', axis=0, tiled=True)]
    all_gather x2 -> x0, blocking collectives: 50.8 us -> none  [the longest x1 29.2 us: per_device(): lax.all_gather(jnp.concatenate([up_pair, down_pair[:EARLY]], 0), 'z', axi...]
    all_to_all x3 -> x1, waiting for transfers between devices: 17.6 us -> 0.01 us  [spread(): lax.all_to_all(jnp.broadcast_to(value[None], (n, *value.shape)), axes, 0,...]
    all_to_all x0 -> x1, blocking collectives: none -> 17.5 us  [per_device(): lax.all_to_all(sent, ('x', 'c'), 0, 0, tiled=True)]
    ppermute x3 -> x1, starting transfers between devices: 22.9 us -> 10.6 us  [per_device(): other = lax.ppermute(own, 'c', SWAP)]
    all_to_all x3 -> x1, starting transfers between devices: 19.3 us -> 12.6 us  [spread(): lax.all_to_all(jnp.broadcast_to(value[None], (n, *value.shape)), axes, 0,...]
    slice x5 -> x0, local copies, waits for them, and re-layouts: 5.05 us -> none  [the longest x2 3.5 us: per_device(): up_own = near_one[:, :, :pair].reshape(width, half)]
    broadcast_in_dim x3 -> x1, local copies, waits for them, and re-layouts: 3.91 us -> 0.78 us  [spread(): jnp.broadcast_to(value[None], (n, *value.shape))]
  transfers between devices with their start and end apart: 17 -> 14, of which waited for: 9 -> 9; matrix products, arithmetic and copies ran while one was open for 6% -> 4% of each run, Pallas kernels for 6% -> 3%
where the time goes in v6:
time: 260 us; the launch traced here: 258 us
  waiting for transfers between devices  80 us (31%)
  starting transfers between devices  67.4 us (26%)
  blocking collectives  39.2 us (15%)
  local copies, waits for them, and re-layouts  27.7 us (11%)
  Pallas kernels  19.8 us (8%)
  between operations  18.6 us (7%)
  other arithmetic  5.61 us (2%)
    all_gather x1, waiting for transfers between devices, per_device(): own = lax.all_gather(near, 'z', axis=0, tiled=True)  60.7 us
    all_to_all x1, blocking collectives, per_device(): got_dy = lax.all_to_all(send, 't', 0, 0, tiled=True)  21.7 us
    unnamed x71, local copies, waits for them, and re-layouts  18.3 us
    all_to_all x1, blocking collectives, per_device(): lax.all_to_all(sent, ('x', 'c'), 0, 0, tiled=True)  17.5 us
    all_to_all x1, starting transfers between devices, spread(): lax.all_to_all(jnp.broadcast_to(value[None], (n, *value.shape)), axes, 0,...  12.6 us
    ppermute x1, starting transfers between devices, per_device(): other = lax.ppermute(own, 'c', SWAP)  10.6 us
    all_to_all x1, starting transfers between devices, per_device(): lax.all_to_all(pile.reshape(chips, 2 * rank // chips, half), CHIPS, 0, 0,...  9.98 us
    ppermute x3, starting transfers between devices, per_device(): lax.ppermute(grad_block, 't', turns[step])  8.94 us
  transfers between devices with their start and end apart: 14, of which 9 were waited for; matrix products, arithmetic and copies ran while one was open for 4% of the time, Pallas kernels for 3%

profile of v6, /device:TPU:1, one launch (start us, length us, event | category | flops | bytes accessed | tf_op | source)
XLA Modules:
  0.0 258.2 jit_solution(3278079590460279335)
XLA Ops:
  9.3 17.5 %all_to_all.30 = bf16[8,12,1536]{2,1,0:T(8,128)(2,1)S(1)} all-to-all(bf16[8,12,1536]{2,1,0:T(8,128)(2,1)S(1)} %bitcast.52), channel_id=1, replica_groups=mesh['z'=16,'x'=4,'c'=2,'t'=4] {'x','c'}, dimensions={0} | all-to-all | bytes 589824 | tf_op jit(solution)/shard_map/all_to_all | solution.py:417
  38.3 60.7 %all-gather.2.cloned.1.call-done.refs_0_ = bf16[1536,1536]{1,0:T(8,128)(2,1)} async-done(((bf16[96,1536]{1,0:T(8,128)(2,1)}), bf16[1536,1536]{1,0:T(8,128)(2,1)}) %all-gather.2.cloned.1.call-update) | async-done | bytes 4718608 | tf_op jit(solution)/shard_map/all_gather | solution.py:418
  99.0 10.6 %collective-permute-start = (bf16[1536,1536]{1,0:T(8,128)(2,1)}, bf16[1536,1536]{1,0:T(8,128)(2,1)S(1)}, u32[]{:S(2)}, u32[]{:S(2)}) collective-permute-start(bf16[1536,1536]{1,0:T(8,128)(2,1)} %shard_map.130.up_ref.own_ref), channel_id=1, source_target_pairs={{0,4},{4,0},{1,5},{5,1},{2,6},{6,2},{3,7},{7,3},{8,12},{12,8},{9,1... | collective-permute-start | bytes 14155784 | tf_op jit(solution)/shard_map/ppermute | solution.py:446
  109.7 2.3 copy-done
  112.0 2.1 shard_map.131
  114.9 2.4 collective-permute-done.up_ref.other_ref
  117.4 2.1 shard_map.132
  119.6 2.9 %shard_map.133 = bf16[256,1536]{1,0:T(8,128)(2,1)} custom-call(bf16[256,768]{1,0:T(8,128)(2,1)S(1)} %get-tuple-element.27.left_ref, bf16[256,768]{1,0:T(8,128)(2,1)S(1)} %get-tuple-element.28.right_ref, bf16[1536,1536]{1,0:T(8,128)(2,1)S(1)} %copy-done.1, bf16[1536,1536]{1,0:T(8,128)(2,1)S(1)} %collective-permute-done.up_ref.other_ref), custom_call_target="tpu_custom_call" | custom-call | flops 1207959552 | bytes 5505024 | tf_op jit(solution)/shard_map/pallas_call | solution.py:162
  122.5 3.9 %all-to-all-start.1 = ((bf16[4,64,1536]{2,1,0:T(8,128)(2,1)}), bf16[4,64,1536]{2,1,0:T(8,128)(2,1)S(1)}, u32[]{:S(2)}, u32[]{:S(2)}) async-start(bf16[4,64,1536]{2,1,0:T(8,128)(2,1)} %bitcast.13), calls=%async_computation.1 | async-start | bytes 1572864 | tf_op jit(solution)/shard_map/all_to_all | solution.py:451
  126.4 2.3 copy-done.2
  128.7 2.3 copy-done.6
  132.1 2.2 shard_map.134
  134.3 3.8 %all-to-all-done.1.got_ref = bf16[4,64,1536]{2,1,0:T(8,128)(2,1)S(1)} async-done(((bf16[4,64,1536]{2,1,0:T(8,128)(2,1)}), bf16[4,64,1536]{2,1,0:T(8,128)(2,1)S(1)}, u32[]{:S(2)}, u32[]{:S(2)}) %all-to-all-start.1) | async-done | bytes 786464 | tf_op jit(solution)/shard_map/all_to_all | solution.py:451
  139.3 21.7 %all_to_all.31.got_ref = bf16[4,128,1536]{2,1,0:T(8,128)(2,1)S(1)} all-to-all(bf16[4,128,1536]{2,1,0:T(8,128)(2,1)S(1)} %get-tuple-element.31), channel_id=1, replica_groups=mesh['z'=16,'x'=4,'c'=2,'t'=4] {'t'}, dimensions={0} | all-to-all | bytes 3145728 | tf_op jit(solution)/shard_map/all_to_all | solution.py:455
  161.0 2.3 copy-done.3
  163.3 5.1 %shard_map.136 = (bf16[256,768]{1,0:T(8,128)(2,1)S(1)}, bf16[256,768]{1,0:T(8,128)(2,1)S(1)}, bf16[256,64]{1,0:T(8,128)(2,1)S(1)}, bf16[4,80,256]{2,1,0:T(8,128)(2,1)}) custom-call(bf16[4,128,1536]{2,1,0:T(8,128)(2,1)S(1)} %all_to_all.31.got_ref, f32[64,1536]{1,0:T(8,128)S(1)} %get-tuple-element.32.unit_ref, bf16[64,1536]{1,0:T(8,128)(2,1)S(1)} %copy-done.10, ...), custom_call_target="tpu_custom_call" | custom-call | flops 1207959552 | bytes 7077888 | tf_op jit(solution)/shard_map/pallas_call | solution.py:253
  168.4 3.3 %all-to-all-start.3 = ((bf16[4,80,256]{2,1,0:T(8,128)(2,1)}), bf16[4,80,256]{2,1,0:T(8,128)(2,1)S(1)}, u32[]{:S(2)}, u32[]{:S(2)}) async-start(bf16[4,80,256]{2,1,0:T(8,128)(2,1)} %get-tuple-element.35), calls=%async_computation.3 | async-start | bytes 327680 | tf_op jit(solution)/shard_map/all_to_all | solution.py:459
  174.3 2.4 all-to-all-done.3.got_ref
  177.5 5.6 %collective-permute-start.1 = (bf16[128,768]{1,0:T(8,128)(2,1)S(1)}, bf16[128,768]{1,0:T(8,128)(2,1)S(1)}, u32[]{:S(2)}, u32[]{:S(2)}) collective-permute-start(bf16[128,768]{1,0:T(8,128)(2,1)S(1)} %get-tuple-element.42), channel_id=1, source_target_pairs={{0,4},{4,0},{1,5},{5,1},{2,6},{6,2},{3,7},{7,3},{8,12},{12,8},{9,1... | collective-permute-start | bytes 589832 | tf_op jit(solution)/shard_map/ppermute | solution.py:466
  185.0 10.0 %all-to-all-start.4 = ((bf16[64,2,768]{2,1,0:T(2,128)(2,1)}), bf16[64,2,768]{2,1,0:T(2,128)(2,1)S(1)}, u32[]{:S(2)}, u32[]{:S(2)}) async-start(bf16[64,2,768]{2,1,0:T(2,128)(2,1)} %reshape.70), calls=%async_computation.4 | async-start | bytes 393216 | tf_op jit(solution)/shard_map/all_to_all | solution.py:469
  195.0 2.3 copy-done.4
  197.4 2.3 copy-done.7
  199.7 2.4 shard_map.139
  202.2 2.2 collective-permute-start.2
  204.4 3.7 %collective-permute-start.3 = (bf16[64,1536]{1,0:T(8,128)(2,1)S(1)}, bf16[64,1536]{1,0:T(8,128)(2,1)S(1)}, u32[]{:S(2)}, u32[]{:S(2)}) collective-permute-start(bf16[64,1536]{1,0:T(8,128)(2,1)S(1)} %get-tuple-element.54), channel_id=1, source_target_pairs={{0,2},{1,3},{2,0},{3,1},{4,6},{5,7},{6,4},{7,5},{8,10},{9,11},{10,... | collective-permute-start | bytes 589832 | tf_op jit(solution)/shard_map/ppermute | solution.py:482
  208.1 2.5 collective-permute-start.4
  213.6 12.6 %all-to-all-start.5 = ((bf16[64,2,768]{2,1,0:T(2,128)(2,1)}), bf16[64,2,768]{2,1,0:T(2,128)(2,1)S(1)}, u32[]{:S(2)}, u32[]{:S(2)}) async-start(bf16[64,2,768]{2,1,0:T(2,128)(2,1)} %broadcast_in_dim.41), calls=%async_computation.5 | async-start | bytes 393216 | tf_op jit(solution)/shard_map/all_to_all | solution.py:48
  228.5 2.8 %collective-permute-start.7 = (bf16[64,1536]{1,0:T(8,128)(2,1)S(1)}, bf16[64,1536]{1,0:T(8,128)(2,1)S(1)}, u32[]{:S(2)}, u32[]{:S(2)}) collective-permute-start(bf16[64,1536]{1,0:T(8,128)(2,1)S(1)} %shard_map.140), channel_id=1, source_target_pairs={{0,3},{1,0},{2,1},{3,2},{4,7},{5,4},{6,5},{7,6},{8,11},{9,8},{10,9... | collective-permute-start | bytes 589832 | tf_op jit(solution)/shard_map/ppermute | solution.py:484
  231.3 3.7 %collective-permute-start.6 = (bf16[64,1536]{1,0:T(8,128)(2,1)S(1)}, bf16[64,1536]{1,0:T(8,128)(2,1)S(1)}, u32[]{:S(2)}, u32[]{:S(2)}) collective-permute-start(bf16[64,1536]{1,0:T(8,128)(2,1)S(1)} %shard_map.140), channel_id=1, source_target_pairs={{0,2},{1,3},{2,0},{3,1},{4,6},{5,7},{6,4},{7,5},{8,10},{9,11},{10,... | collective-permute-start | bytes 589832 | tf_op jit(solution)/shard_map/ppermute | solution.py:484
  235.0 2.5 collective-permute-start.5
  239.5 5.6 %collective-permute-done.5 = bf16[64,1536]{1,0:T(8,128)(2,1)S(1)} collective-permute-done((bf16[64,1536]{1,0:T(8,128)(2,1)S(1)}, bf16[64,1536]{1,0:T(8,128)(2,1)S(1)}, u32[]{:S(2)}, u32[]{:S(2)}) %collective-permute-start.5) | collective-permute-done | bytes 196640 | tf_op jit(solution)/shard_map/ppermute | solution.py:484
  245.3 3.9 %collective-permute-start.8 = (bf16[128,768]{1,0:T(8,128)(2,1)S(1)}, bf16[128,768]{1,0:T(8,128)(2,1)S(1)}, u32[]{:S(2)}, u32[]{:S(2)}) collective-permute-start(bf16[128,768]{1,0:T(8,128)(2,1)S(1)} %reshape.71), channel_id=1, source_target_pairs={{0,4},{4,0},{1,5},{5,1},{2,6},{6,2},{3,7},{7,3},{8,12},{12,8},{9,1... | collective-permute-start | bytes 589832 | tf_op jit(solution)/shard_map/ppermute | solution.py:472
  (113 shorter events, 27.3 us)
Async XLA Ops:
  7.2 21.7 %copy-start.33 = (bf16[2,3,1536]{2,0,1:T(2,128)(2,1)S(1)}, bf16[2,3,1536]{2,0,1:T(2,128)(2,1)}, u32[]{:S(2)}) copy-start(bf16[2,3,1536]{2,0,1:T(2,128)(2,1)} %param.12) | copy-start | bytes 55300
  7.2 21.8 %copy-start.34 = (s32[1,2]{1,0:T(1,128)S(1)}, s32[1,2]{1,0:T(1,128)}, u32[]{:S(2)}) copy-start(s32[1,2]{1,0:T(1,128)} %param.15) | copy-start | bytes 28
  7.2 91.8 %all-gather.2.cloned.1.call-start = ((), (), s32[]{:S(2)}) async-start(), calls=%async_computation.6 | async-start | bytes 5013504 | tf_op jit(solution)/shard_map/all_gather | solution.py:418
  8.1 24.1 %copy-start.14 = (bf16[256,1536]{1,0:T(8,128)(2,1)S(1)}, bf16[256,1536]{1,0:T(8,128)(2,1)}, u32[]{:S(2)}) copy-start(bf16[256,1536]{1,0:T(8,128)(2,1)} %x_ref.1) | copy-start | bytes 2359300
  8.1 24.1 %copy-start.15 = (bf16[1536,64]{0,1:T(8,128)(2,1)S(1)}, bf16[1536,64]{0,1:T(8,128)(2,1)}, u32[]{:S(2)}) copy-start(bf16[1536,64]{0,1:T(8,128)(2,1)} %param.18) | copy-start | bytes 589828
  9.3 26.0 %copy-start.32 = (bf16[64,1536]{1,0:T(8,128)(2,1)S(1)}, bf16[64,1536]{1,0:T(8,128)(2,1)}, u32[]{:S(2)}) copy-start(bf16[64,1536]{1,0:T(8,128)(2,1)} %param.19) | copy-start | bytes 589828
  99.0 10.6 %copy-start.9 = (bf16[256,1536]{1,0:T(8,128)(2,1)S(1)}, bf16[256,1536]{1,0:T(8,128)(2,1)}, u32[]{:S(2)}) copy-start(bf16[256,1536]{1,0:T(8,128)(2,1)} %copy-done.8) | copy-start | bytes 2359300
  99.0 10.7 %copy-start.13 = (bf16[64,768]{1,0:T(8,128)(2,1)S(1)}, bf16[64,768]{1,0:T(8,128)(2,1)}, u32[]{:S(2)}) copy-start(bf16[64,768]{1,0:T(8,128)(2,1)} %get-tuple-element.58.refs_4_.b_ref.bo_ref) | copy-start | bytes 294916
  99.0 10.7 %copy-start.21 = (bf16[256,64]{1,0:T(8,128)(2,1)S(1)}, bf16[256,64]{1,0:T(8,128)(2,1)}, u32[]{:S(2)}) copy-start(bf16[256,64]{1,0:T(8,128)(2,1)} %copy-done.20) | copy-start | bytes 98308
  99.0 18.4 %collective-permute-start = (bf16[1536,1536]{1,0:T(8,128)(2,1)}, bf16[1536,1536]{1,0:T(8,128)(2,1)S(1)}, u32[]{:S(2)}, u32[]{:S(2)}) collective-permute-start(bf16[1536,1536]{1,0:T(8,128)(2,1)} %shard_map.130.up_ref.own_ref), channel_id=1, source_target_pairs={{0,4},{4,0},{1,5},{5,1},{2,6},{6,2},{3,7},{7,3},{8,12},{12,8},{9,1... | collective-permute-start | bytes 14155784 | tf_op jit(solution)/shard_map/ppermute | solution.py:446
  112.0 5.4 %copy-start.12 = (bf16[64,768]{1,0:T(8,128)(2,1)S(1)}, bf16[64,768]{1,0:T(8,128)(2,1)}, u32[]{:S(2)}) copy-start(bf16[64,768]{1,0:T(8,128)(2,1)} %get-tuple-element.57.refs_5_.b_ref.bt_ref) | copy-start | bytes 294916
  114.9 4.6 %copy-start.16 = (f32[256,768]{1,0:T(8,128)}, f32[256,768]{1,0:T(8,128)S(1)}, u32[]{:S(2)}) copy-start(f32[256,768]{1,0:T(8,128)S(1)} %get-tuple-element.33.so_ref) | copy-start | bytes 2359300
  114.9 4.7 %copy-start.1 = (bf16[1536,1536]{1,0:T(8,128)(2,1)S(1)}, bf16[1536,1536]{1,0:T(8,128)(2,1)}, u32[]{:S(2)}) copy-start(bf16[1536,1536]{1,0:T(8,128)(2,1)} %shard_map.130.up_ref.own_ref) | copy-start | bytes 14155780
  122.5 15.6 %all-to-all-start.1 = ((bf16[4,64,1536]{2,1,0:T(8,128)(2,1)}), bf16[4,64,1536]{2,1,0:T(8,128)(2,1)S(1)}, u32[]{:S(2)}, u32[]{:S(2)}) async-start(bf16[4,64,1536]{2,1,0:T(8,128)(2,1)} %bitcast.13), calls=%async_computation.1 | async-start | bytes 1572864 | tf_op jit(solution)/shard_map/all_to_all | solution.py:451
  132.1 6.0 %copy-start.10 = (bf16[64,1536]{1,0:T(8,128)(2,1)S(1)}, bf16[64,1536]{1,0:T(8,128)(2,1)}, u32[]{:S(2)}) copy-start(bf16[64,1536]{1,0:T(8,128)(2,1)} %get-tuple-element.67.refs_6_.x_ref) | copy-start | bytes 589828
  132.1 6.1 %copy-start.11 = (bf16[64,1536]{1,0:T(8,128)(2,1)S(1)}, bf16[64,1536]{1,0:T(8,128)(2,1)}, u32[]{:S(2)}) copy-start(bf16[64,1536]{1,0:T(8,128)(2,1)} %get-tuple-element.66.refs_7_.t_ref) | copy-start | bytes 589828
  132.1 6.1 %copy-start.30 = (f32[1,1536]{1,0:T(1,128)S(1)}, f32[1,1536]{1,0:T(1,128)}, u32[]{:S(2)}) copy-start(f32[1,1536]{1,0:T(1,128)} %get-tuple-element.60.refs_8_.gate_ref) | copy-start | bytes 18436
  139.3 21.7 %copy-start.17 = (f32[256,768]{1,0:T(8,128)S(1)}, f32[256,768]{1,0:T(8,128)}, u32[]{:S(2)}) copy-start(f32[256,768]{1,0:T(8,128)} %copy-done.16) | copy-start | bytes 2359300
  139.3 21.7 %copy-start.19 = (f32[256,768]{1,0:T(8,128)S(1)}, f32[256,768]{1,0:T(8,128)}, u32[]{:S(2)}) copy-start(f32[256,768]{1,0:T(8,128)} %copy-done.18) | copy-start | bytes 2359300
  139.3 21.7 %copy-start.23 = (f32[64,1]{1,0:T(8,128)S(1)}, f32[64,1]{1,0:T(8,128)}, u32[]{:S(2)}) copy-start(f32[64,1]{1,0:T(8,128)} %fusion.1.refs_10_.mask_ref) | copy-start | bytes 772
  168.4 8.3 %all-to-all-start.3 = ((bf16[4,80,256]{2,1,0:T(8,128)(2,1)}), bf16[4,80,256]{2,1,0:T(8,128)(2,1)S(1)}, u32[]{:S(2)}, u32[]{:S(2)}) async-start(bf16[4,80,256]{2,1,0:T(8,128)(2,1)} %get-tuple-element.35), calls=%async_computation.3 | async-start | bytes 327680 | tf_op jit(solution)/shard_map/all_to_all | solution.py:459
  177.5 6.7 %collective-permute-start.1 = (bf16[128,768]{1,0:T(8,128)(2,1)S(1)}, bf16[128,768]{1,0:T(8,128)(2,1)S(1)}, u32[]{:S(2)}, u32[]{:S(2)}) collective-permute-start(bf16[128,768]{1,0:T(8,128)(2,1)S(1)} %get-tuple-element.42), channel_id=1, source_target_pairs={{0,4},{4,0},{1,5},{5,1},{2,6},{6,2},{3,7},{7,3},{8,12},{12,8},{9,1... | collective-permute-start | bytes 589832 | tf_op jit(solution)/shard_map/ppermute | solution.py:466
  185.0 27.6 %all-to-all-start.4 = ((bf16[64,2,768]{2,1,0:T(2,128)(2,1)}), bf16[64,2,768]{2,1,0:T(2,128)(2,1)S(1)}, u32[]{:S(2)}, u32[]{:S(2)}) async-start(bf16[64,2,768]{2,1,0:T(2,128)(2,1)} %reshape.70), calls=%async_computation.4 | async-start | bytes 393216 | tf_op jit(solution)/shard_map/all_to_all | solution.py:469
  202.1 25.9 %copy-start.31 = (f32[1,1536]{1,0:T(1,128)S(1)}, f32[1,1536]{1,0:T(1,128)}, u32[]{:S(2)}) copy-start(f32[1,1536]{1,0:T(1,128)} %get-tuple-element.59.refs_9_.scale_ref) | copy-start | bytes 18436
  202.2 25.8 %collective-permute-start.2 = (bf16[64,1536]{1,0:T(8,128)(2,1)S(1)}, bf16[64,1536]{1,0:T(8,128)(2,1)S(1)}, u32[]{:S(2)}, u32[]{:S(2)}) collective-permute-start(bf16[64,1536]{1,0:T(8,128)(2,1)S(1)} %get-tuple-element.55), channel_id=1, source_target_pairs={{0,1},{1,2},{2,3},{3,0},{4,5},{5,6},{6,7},{7,4},{8,9},{9,10},{10,1... | collective-permute-start | bytes 589832 | tf_op jit(solution)/shard_map/ppermute | solution.py:482
  204.4 23.6 %collective-permute-start.3 = (bf16[64,1536]{1,0:T(8,128)(2,1)S(1)}, bf16[64,1536]{1,0:T(8,128)(2,1)S(1)}, u32[]{:S(2)}, u32[]{:S(2)}) collective-permute-start(bf16[64,1536]{1,0:T(8,128)(2,1)S(1)} %get-tuple-element.54), channel_id=1, source_target_pairs={{0,2},{1,3},{2,0},{3,1},{4,6},{5,7},{6,4},{7,5},{8,10},{9,11},{10,... | collective-permute-start | bytes 589832 | tf_op jit(solution)/shard_map/ppermute | solution.py:482
  208.1 19.9 %collective-permute-start.4 = (bf16[64,1536]{1,0:T(8,128)(2,1)S(1)}, bf16[64,1536]{1,0:T(8,128)(2,1)S(1)}, u32[]{:S(2)}, u32[]{:S(2)}) collective-permute-start(bf16[64,1536]{1,0:T(8,128)(2,1)S(1)} %get-tuple-element.53), channel_id=1, source_target_pairs={{0,3},{1,0},{2,1},{3,2},{4,7},{5,4},{6,5},{7,6},{8,11},{9,8},{10,9... | collective-permute-start | bytes 589832 | tf_op jit(solution)/shard_map/ppermute | solution.py:482
  213.6 31.7 %all-to-all-start.5 = ((bf16[64,2,768]{2,1,0:T(2,128)(2,1)}), bf16[64,2,768]{2,1,0:T(2,128)(2,1)S(1)}, u32[]{:S(2)}, u32[]{:S(2)}) async-start(bf16[64,2,768]{2,1,0:T(2,128)(2,1)} %broadcast_in_dim.41), calls=%async_computation.5 | async-start | bytes 393216 | tf_op jit(solution)/shard_map/all_to_all | solution.py:48
  228.5 9.0 %collective-permute-start.7 = (bf16[64,1536]{1,0:T(8,128)(2,1)S(1)}, bf16[64,1536]{1,0:T(8,128)(2,1)S(1)}, u32[]{:S(2)}, u32[]{:S(2)}) collective-permute-start(bf16[64,1536]{1,0:T(8,128)(2,1)S(1)} %shard_map.140), channel_id=1, source_target_pairs={{0,3},{1,0},{2,1},{3,2},{4,7},{5,4},{6,5},{7,6},{8,11},{9,8},{10,9... | collective-permute-start | bytes 589832 | tf_op jit(solution)/shard_map/ppermute | solution.py:484
  231.3 8.2 %collective-permute-start.6 = (bf16[64,1536]{1,0:T(8,128)(2,1)S(1)}, bf16[64,1536]{1,0:T(8,128)(2,1)S(1)}, u32[]{:S(2)}, u32[]{:S(2)}) collective-permute-start(bf16[64,1536]{1,0:T(8,128)(2,1)S(1)} %shard_map.140), channel_id=1, source_target_pairs={{0,2},{1,3},{2,0},{3,1},{4,6},{5,7},{6,4},{7,5},{8,10},{9,11},{10,... | collective-permute-start | bytes 589832 | tf_op jit(solution)/shard_map/ppermute | solution.py:484
  235.0 10.1 %collective-permute-start.5 = (bf16[64,1536]{1,0:T(8,128)(2,1)S(1)}, bf16[64,1536]{1,0:T(8,128)(2,1)S(1)}, u32[]{:S(2)}, u32[]{:S(2)}) collective-permute-start(bf16[64,1536]{1,0:T(8,128)(2,1)S(1)} %shard_map.140), channel_id=1, source_target_pairs={{0,1},{1,2},{2,3},{3,0},{4,5},{5,6},{6,7},{7,4},{8,9},{9,10},{10,1... | collective-permute-start | bytes 589832 | tf_op jit(solution)/shard_map/ppermute | solution.py:484
  245.3 5.0 %collective-permute-start.8 = (bf16[128,768]{1,0:T(8,128)(2,1)S(1)}, bf16[128,768]{1,0:T(8,128)(2,1)S(1)}, u32[]{:S(2)}, u32[]{:S(2)}) collective-permute-start(bf16[128,768]{1,0:T(8,128)(2,1)S(1)} %reshape.71), channel_id=1, source_target_pairs={{0,4},{4,0},{1,5},{5,1},{2,6},{6,2},{3,7},{7,3},{8,12},{12,8},{9,1... | collective-permute-start | bytes 589832 | tf_op jit(solution)/shard_map/ppermute | solution.py:472
  (17 other events, 37.6 us)
Sparse Core Ops, SparseCore 0:
  27.7 71.2 all-gather.1

commit v7 on v6

--- a/solution.py
+++ b/solution.py
@@ -16,10 +16,9 @@
 BF16 = jnp.bfloat16
 F32 = jnp.float32
 DP = ("z", "x", "c")
-CHIPS = ("z", "x")
 SWAP = [(0, 1), (1, 0)]
 NOTE = 16
-VMEM_LIMIT = 40 * 1024 * 1024
+VMEM_LIMIT = 24 * 1024 * 1024
 SMEM = pltpu.SMEM
 
 
@@ -287,7 +286,7 @@
 
 
 def pile_kernel(
-    ints_ref, scales_ref, got_ref, modded_ref, own_ref, other_ref, keep_ref, give_ref, facts_ref
+    ints_ref, scales_ref, got_ref, modded_ref, own_ref, other_ref, pile_ref, facts_ref
 ):
     wins = ints_ref[0]
     core = ints_ref[1]
@@ -315,27 +314,25 @@
     dlow = (total * jnp.where(slot < wins, first, second)).astype(BF16)
     one = first[:, :1]
     two = second[:, :1]
-    near = modded_ref[:, pl.ds(pl.multiple_of(core * half, 128), half)]
-    far = modded_ref[:, pl.ds(pl.multiple_of((1 - core) * half, 128), half)]
-    keep_ref[:rank] = one * own_ref[:rank] + two * own_ref[rank:]
-    keep_ref[rank:] = product(dlow, near)
-    give_ref[:rank] = (one * other_ref[:rank] + two * other_ref[rank:]).astype(BF16)
-    give_ref[rank:] = product(dlow, far).astype(BF16)
+    near = pl.ds(pl.multiple_of(core * half, 128), half)
+    far = pl.ds(pl.multiple_of((1 - core) * half, 128), half)
+    pile_ref[:rank, near] = (one * own_ref[:rank] + two * own_ref[rank:]).astype(BF16)
+    pile_ref[:rank, far] = (one * other_ref[:rank] + two * other_ref[rank:]).astype(BF16)
+    pile_ref[rank:] = product(dlow, modded_ref[...]).astype(BF16)
 
 
 def piles(ints, scales, got, modded, b_own, b_other):
     lines, half = b_own.shape
-    rows = got.shape[2]
+    rows, width = modded.shape
     return pl.pallas_call(
         pile_kernel,
         out_shape=[
-            jax.ShapeDtypeStruct((lines, half), F32),
-            jax.ShapeDtypeStruct((lines, half), BF16),
+            jax.ShapeDtypeStruct((lines, width), BF16),
             jax.ShapeDtypeStruct((8, rows), F32),
         ],
         in_specs=[pl.BlockSpec(memory_space=SMEM)] * 2 + [pl.BlockSpec(memory_space=pltpu.VMEM)] * 4,
         compiler_params=params(),
-        cost_estimate=cost(2 * lines * half * rows, 16 * lines * half),
+        cost_estimate=cost(lines * width * rows, 16 * lines * half),
     )(ints, scales, got, modded, b_own, b_other)
 
 
@@ -458,23 +455,22 @@
     )
     got_low = lax.all_to_all(send, "t", 0, 0, tiled=True)
     b_own, b_other = factor_terms(low_split, d_own, d_other)
-    keep, give, facts = piles(
+    pile, facts = piles(
         jnp.stack([wins, core]).astype(jnp.int32), scales, got_low, modded, b_own, b_other
     )
     losses = facts[0, :1]
     coef_own = jnp.where(own_first, facts[1:2, :1], facts[2:3, :1])
-    pile = (keep + lax.ppermute(give, "c", SWAP).astype(F32)).astype(BF16)
-
-    chips = n_z * n_x
-    pieces = lax.all_to_all(pile.reshape(chips, 2 * rank // chips, half), CHIPS, 0, 0, tiled=True)
+
+    across = n_x * n_c
+    lines = 2 * rank // across
+    pieces = lax.all_to_all(pile.reshape(across, lines, width), ("x", "c"), 0, 0, tiled=True)
+    pieces = jnp.sum(pieces.astype(F32), axis=0).astype(BF16)
+    pieces = lax.all_to_all(pieces.reshape(n_z, lines // n_z, width), "z", 0, 0, tiled=True)
     total = (jnp.sum(pieces.astype(F32), axis=0) / n_dp).astype(BF16)
-    mine = spread(total, CHIPS, chips).reshape(2 * rank, half)
-    theirs = lax.ppermute(mine, "c", SWAP)
-    ends = jnp.concatenate([mine, theirs], 1)
-    flipped = jnp.concatenate([theirs, mine], 1)
-    ends = jnp.where(core == 0, ends, flipped).astype(F32)
-    sum_b = ends[:rank]
-    sum_a = ends[rank:].T
+    total = spread(total, "z", n_z).reshape(lines, width)
+    total = spread(total, ("x", "c"), across).reshape(2 * rank, width).astype(F32)
+    sum_b = total[:rank]
+    sum_a = total[rank:].T
 
     dm_part = dm_terms(pile, d_own, d_other, dlow_part, own, other, a_turned).reshape(CAP, BLK, width)
     turns = [[(i, (i + step) % n_t) for i in range(n_t)] for step in range(n_t)]

time: 260 us -> 284 us (1.092)
  waiting for transfers between devices: 80 us -> 105 us
  blocking collectives: 39.2 us -> 17.5 us
  local copies, waits for them, and re-layouts: 27.7 us -> 41.4 us
  starting transfers between devices: 67.4 us -> 73 us
    all_to_all x1 -> x0, blocking collectives: 21.7 us -> none  [per_device(): got_dy = lax.all_to_all(send, 't', 0, 0, tiled=True)]
    all_to_all x1 -> x2, waiting for transfers between devices: 0.01 us -> 18.6 us  [spread(): lax.all_to_all(jnp.broadcast_to(value[None], (n, *value.shape)), axes, 0,...]
    all_to_all x1 -> x3, waiting for transfers between devices: 1.92 us -> 19.2 us  [the longest x1 19.1 us: per_device(): got_dy = lax.all_to_all(send, 't', 0, 0, tiled=True)]
    unnamed x71 -> x96, local copies, waits for them, and re-layouts: 18.3 us -> 32.3 us
    ppermute x2 -> x0, starting transfers between devices: 9.53 us -> none  [the longest x1 5.62 us: per_device(): pile = (keep + lax.ppermute(give, 'c', SWAP).astype(F32)).astype(BF16)]
    all_to_all x1 -> x3, starting transfers between devices: 9.98 us -> 18.1 us  [the longest x1 7.89 us: per_device(): lax.all_to_all(pile.reshape(across, lines, width), ('x', 'c'), 0, 0, tile...]
    ppermute x3, waiting for transfers between devices: 7.51 us -> 0.01 us  [per_device(): lax.ppermute(grad_block, 't', turns[step])]
    all_to_all x1 -> x2, starting transfers between devices: 12.6 us -> 19.7 us  [spread(): lax.all_to_all(jnp.broadcast_to(value[None], (n, *value.shape)), axes, 0,...]
  transfers between devices with their start and end apart: 14 -> 15, of which waited for: 9 -> 8; matrix products, arithmetic and copies ran while one was open for 4% -> 5% of each run, Pallas kernels for 3% -> 3%
where the time goes in v7:
time: 284 us; the launch traced here: 282 us
  waiting for transfers between devices  105 us (37%)
  starting transfers between devices  73 us (26%)
  local copies, waits for them, and re-layouts  41.4 us (15%)
  Pallas kernels  18.9 us (7%)
  between operations  18.6 us (7%)
  blocking collectives  17.5 us (6%)
  other arithmetic  7.83 us (3%)
    all_gather x1, waiting for transfers between devices, per_device(): own = lax.all_gather(near, 'z', axis=0, tiled=True)  60.7 us
    unnamed x96, local copies, waits for them, and re-layouts  32.3 us
    all_to_all x2, starting transfers between devices, spread(): lax.all_to_all(jnp.broadcast_to(value[None], (n, *value.shape)), axes, 0,...  19.7 us
    all_to_all x1, waiting for transfers between devices, per_device(): got_dy = lax.all_to_all(send, 't', 0, 0, tiled=True)  19.1 us
    all_to_all x2, waiting for transfers between devices, spread(): lax.all_to_all(jnp.broadcast_to(value[None], (n, *value.shape)), axes, 0,...  18.6 us
    all_to_all x1, blocking collectives, per_device(): lax.all_to_all(sent, ('x', 'c'), 0, 0, tiled=True)  17.5 us
    ppermute x1, starting transfers between devices, per_device(): other = lax.ppermute(own, 'c', SWAP)  10.6 us
    ppermute x3, starting transfers between devices, per_device(): lax.ppermute(grad_block, 't', turns[step])  8.94 us
  transfers between devices with their start and end apart: 15, of which 8 were waited for; matrix products, arithmetic and copies ran while one was open for 5% of the time, Pallas kernels for 3%

profile of v7, /device:TPU:1, one launch (start us, length us, event | category | flops | bytes accessed | tf_op | source)
XLA Modules:
  0.0 282.4 jit_solution(806815358108991185)
XLA Ops:
  9.3 17.5 %all_to_all.40 = bf16[8,12,1536]{2,1,0:T(8,128)(2,1)S(1)} all-to-all(bf16[8,12,1536]{2,1,0:T(8,128)(2,1)S(1)} %bitcast.59), channel_id=1, replica_groups=mesh['z'=16,'x'=4,'c'=2,'t'=4] {'x','c'}, dimensions={0} | all-to-all | bytes 589824 | tf_op jit(solution)/shard_map/all_to_all | solution.py:414
  38.3 60.7 %all-gather.2.cloned.1.call-done.refs_0_ = bf16[1536,1536]{1,0:T(8,128)(2,1)} async-done(((bf16[96,1536]{1,0:T(8,128)(2,1)}), bf16[1536,1536]{1,0:T(8,128)(2,1)}) %all-gather.2.cloned.1.call-update) | async-done | bytes 4718608 | tf_op jit(solution)/shard_map/all_gather | solution.py:415
  99.0 10.6 %collective-permute-start = (bf16[1536,1536]{1,0:T(8,128)(2,1)}, bf16[1536,1536]{1,0:T(8,128)(2,1)S(1)}, u32[]{:S(2)}, u32[]{:S(2)}) collective-permute-start(bf16[1536,1536]{1,0:T(8,128)(2,1)} %shard_map.130.up_ref.own_ref), channel_id=1, source_target_pairs={{0,4},{4,0},{1,5},{5,1},{2,6},{6,2},{3,7},{7,3},{8,12},{12,8},{9,1... | collective-permute-start | bytes 14155784 | tf_op jit(solution)/shard_map/ppermute | solution.py:443
  109.7 2.3 copy-done
  115.1 2.3 collective-permute-done.up_ref.other_ref
  120.5 2.9 %shard_map.133 = bf16[256,1536]{1,0:T(8,128)(2,1)} custom-call(bf16[256,768]{1,0:T(8,128)(2,1)S(1)} %get-tuple-element.26.left_ref, bf16[256,768]{1,0:T(8,128)(2,1)S(1)} %get-tuple-element.27.right_ref, bf16[1536,1536]{1,0:T(8,128)(2,1)S(1)} %copy-done.1, bf16[1536,1536]{1,0:T(8,128)(2,1)S(1)} %collective-permute-done.up_ref.other_ref), custom_call_target="tpu_custom_call" | custom-call | flops 1207959552 | bytes 5505024 | tf_op jit(solution)/shard_map/pallas_call | solution.py:161
  123.4 3.8 %all-to-all-start.1 = ((bf16[4,64,1536]{2,1,0:T(8,128)(2,1)}), bf16[4,64,1536]{2,1,0:T(8,128)(2,1)S(1)}, u32[]{:S(2)}, u32[]{:S(2)}) async-start(bf16[4,64,1536]{2,1,0:T(8,128)(2,1)} %bitcast.13), calls=%async_computation.1 | async-start | bytes 1572864 | tf_op jit(solution)/shard_map/all_to_all | solution.py:448
  127.2 2.3 copy-done.2
  129.5 2.3 copy-done.6
  133.8 2.2 shard_map.134
  136.1 2.8 all-to-all-done.1.got_ref
  141.2 3.6 %all-to-all-start.2 = ((bf16[4,128,1536]{2,1,0:T(8,128)(2,1)}), bf16[4,128,1536]{2,1,0:T(8,128)(2,1)S(1)}, u32[]{:S(2)}, u32[]{:S(2)}) async-start(bf16[4,128,1536]{2,1,0:T(8,128)(2,1)} %copy-done.17), calls=%async_computation.2 | async-start | bytes 3145728 | tf_op jit(solution)/shard_map/all_to_all | solution.py:452
  144.9 19.1 %all-to-all-done.2.got_ref = bf16[4,128,1536]{2,1,0:T(8,128)(2,1)S(1)} async-done(((bf16[4,128,1536]{2,1,0:T(8,128)(2,1)}), bf16[4,128,1536]{2,1,0:T(8,128)(2,1)S(1)}, u32[]{:S(2)}, u32[]{:S(2)}) %all-to-all-start.2) | async-done | bytes 1572896 | tf_op jit(solution)/shard_map/all_to_all | solution.py:452
  163.9 2.3 copy-done.3
  166.3 2.3 copy-done.7
  172.6 3.4 %shard_map.136 = (bf16[256,768]{1,0:T(8,128)(2,1)S(1)}, bf16[256,768]{1,0:T(8,128)(2,1)S(1)}, bf16[256,64]{1,0:T(8,128)(2,1)S(1)}, bf16[4,80,256]{2,1,0:T(8,128)(2,1)S(1)}) custom-call(bf16[4,128,1536]{2,1,0:T(8,128)(2,1)S(1)} %all-to-all-done.2.got_ref, f32[64,1536]{1,0:T(8,128)S(1)} %copy-done.19, bf16[64,1536]{1,0:T(8,128)(2,1)S(1)} %copy-done.11, ...), custom_call_target="tpu_custom_call" | custom-call | flops 1207959552 | bytes 7077888 | tf_op jit(solution)/shard_map/pallas_call | solution.py:252
  178.1 3.3 %all-to-all-start.3 = ((bf16[4,80,256]{2,1,0:T(8,128)(2,1)}), bf16[4,80,256]{2,1,0:T(8,128)(2,1)S(1)}, u32[]{:S(2)}, u32[]{:S(2)}) async-start(bf16[4,80,256]{2,1,0:T(8,128)(2,1)} %copy-done.37), calls=%async_computation.3 | async-start | bytes 327680 | tf_op jit(solution)/shard_map/all_to_all | solution.py:456
  188.0 7.9 %all-to-all-start.4 = ((bf16[8,16,1536]{2,1,0:T(8,128)(2,1)}), bf16[8,16,1536]{2,1,0:T(8,128)(2,1)}, u32[]{:S(2)}, u32[]{:S(2)}) async-start(bf16[8,16,1536]{2,1,0:T(8,128)(2,1)} %bitcast.30), calls=%async_computation.4 | async-start | bytes 786432 | tf_op jit(solution)/shard_map/all_to_all | solution.py:466
  195.9 2.3 copy-done.4
  198.2 2.3 copy-done.8
  200.5 2.4 shard_map.139
  203.1 2.3 collective-permute-start.1
  205.4 3.7 %collective-permute-start.2 = (bf16[64,1536]{1,0:T(8,128)(2,1)S(1)}, bf16[64,1536]{1,0:T(8,128)(2,1)S(1)}, u32[]{:S(2)}, u32[]{:S(2)}) collective-permute-start(bf16[64,1536]{1,0:T(8,128)(2,1)S(1)} %get-tuple-element.50), channel_id=1, source_target_pairs={{0,2},{1,3},{2,0},{3,1},{4,6},{5,7},{6,4},{7,5},{8,10},{9,11},{10,... | collective-permute-start | bytes 589832 | tf_op jit(solution)/shard_map/ppermute | solution.py:478
  209.1 2.5 collective-permute-start.3
  214.4 6.6 %all-to-all-start.5 = ((bf16[16,2,768]{2,1,0:T(2,128)(2,1)}), bf16[16,2,768]{2,1,0:T(2,128)(2,1)S(1)}, u32[]{:S(2)}, u32[]{:S(2)}) async-start(bf16[16,2,768]{2,1,0:T(2,128)(2,1)} %reshape.84), calls=%async_computation.5 | async-start | bytes 98304 | tf_op jit(solution)/shard_map/all_to_all | solution.py:468
  223.6 2.8 collective-permute-start.6
  226.3 3.7 %collective-permute-start.5 = (bf16[64,1536]{1,0:T(8,128)(2,1)S(1)}, bf16[64,1536]{1,0:T(8,128)(2,1)S(1)}, u32[]{:S(2)}, u32[]{:S(2)}) collective-permute-start(bf16[64,1536]{1,0:T(8,128)(2,1)S(1)} %shard_map.140), channel_id=1, source_target_pairs={{0,2},{1,3},{2,0},{3,1},{4,6},{5,7},{6,4},{7,5},{8,10},{9,11},{10,... | collective-permute-start | bytes 589832 | tf_op jit(solution)/shard_map/ppermute | solution.py:480
  230.0 2.5 collective-permute-start.4
  234.3 11.3 %all-to-all-start.6 = ((bf16[16,2,768]{2,1,0:T(2,128)(2,1)}), bf16[16,2,768]{2,1,0:T(2,128)(2,1)S(1)}, u32[]{:S(2)}, u32[]{:S(2)}) async-start(bf16[16,2,768]{2,1,0:T(2,128)(2,1)} %reshape.86), calls=%async_computation.6 | async-start | bytes 98304 | tf_op jit(solution)/shard_map/all_to_all | solution.py:47
  245.8 11.5 %all-to-all-done.6 = bf16[16,2,768]{2,1,0:T(2,128)(2,1)S(1)} async-done(((bf16[16,2,768]{2,1,0:T(2,128)(2,1)}), bf16[16,2,768]{2,1,0:T(2,128)(2,1)S(1)}, u32[]{:S(2)}, u32[]{:S(2)}) %all-to-all-start.6) | async-done | bytes 49184 | tf_op jit(solution)/shard_map/all_to_all | solution.py:47
  258.1 8.4 %all-to-all-start.7 = ((bf16[8,16,1536]{2,1,0:T(8,128)(2,1)}), bf16[8,16,1536]{2,1,0:T(8,128)(2,1)S(1)}, u32[]{:S(2)}, u32[]{:S(2)}) async-start(bf16[8,16,1536]{2,1,0:T(8,128)(2,1)} %broadcast_in_dim.50), calls=%async_computation.7 | async-start | bytes 786432 | tf_op jit(solution)/shard_map/all_to_all | solution.py:47
  267.5 7.1 %all-to-all-done.7 = bf16[8,16,1536]{2,1,0:T(8,128)(2,1)S(1)} async-done(((bf16[8,16,1536]{2,1,0:T(8,128)(2,1)}), bf16[8,16,1536]{2,1,0:T(8,128)(2,1)S(1)}, u32[]{:S(2)}, u32[]{:S(2)}) %all-to-all-start.7) | async-done | bytes 393248 | tf_op jit(solution)/shard_map/all_to_all | solution.py:47
  (140 shorter events, 42.5 us)
Async XLA Ops:
  7.2 21.7 %copy-start.43 = (bf16[2,3,1536]{2,0,1:T(2,128)(2,1)S(1)}, bf16[2,3,1536]{2,0,1:T(2,128)(2,1)}, u32[]{:S(2)}) copy-start(bf16[2,3,1536]{2,0,1:T(2,128)(2,1)} %param.12) | copy-start | bytes 55300
  7.2 21.8 %copy-start.44 = (s32[1,2]{1,0:T(1,128)S(1)}, s32[1,2]{1,0:T(1,128)}, u32[]{:S(2)}) copy-start(s32[1,2]{1,0:T(1,128)} %param.15) | copy-start | bytes 28
  7.2 91.8 %all-gather.2.cloned.1.call-start = ((), (), s32[]{:S(2)}) async-start(), calls=%async_computation.8 | async-start | bytes 5013504 | tf_op jit(solution)/shard_map/all_gather | solution.py:415
  8.1 24.1 %copy-start.21 = (bf16[256,1536]{1,0:T(8,128)(2,1)S(1)}, bf16[256,1536]{1,0:T(8,128)(2,1)}, u32[]{:S(2)}) copy-start(bf16[256,1536]{1,0:T(8,128)(2,1)} %x_ref.1) | copy-start | bytes 2359300
  8.1 24.1 %copy-start.22 = (bf16[1536,64]{0,1:T(8,128)(2,1)S(1)}, bf16[1536,64]{0,1:T(8,128)(2,1)}, u32[]{:S(2)}) copy-start(bf16[1536,64]{0,1:T(8,128)(2,1)} %param.18) | copy-start | bytes 589828
  9.3 26.0 %copy-start.42 = (bf16[64,1536]{1,0:T(8,128)(2,1)S(1)}, bf16[64,1536]{1,0:T(8,128)(2,1)}, u32[]{:S(2)}) copy-start(bf16[64,1536]{1,0:T(8,128)(2,1)} %param.19) | copy-start | bytes 589828
  99.0 10.6 %copy-start.10 = (bf16[256,1536]{1,0:T(8,128)(2,1)S(1)}, bf16[256,1536]{1,0:T(8,128)(2,1)}, u32[]{:S(2)}) copy-start(bf16[256,1536]{1,0:T(8,128)(2,1)} %copy-done.9) | copy-start | bytes 2359300
  99.0 10.7 %copy-start.14 = (bf16[64,768]{1,0:T(8,128)(2,1)S(1)}, bf16[64,768]{1,0:T(8,128)(2,1)}, u32[]{:S(2)}) copy-start(bf16[64,768]{1,0:T(8,128)(2,1)} %get-tuple-element.56.refs_4_.b_ref.bo_ref) | copy-start | bytes 294916
  99.0 10.7 %copy-start.28 = (bf16[256,64]{1,0:T(8,128)(2,1)S(1)}, bf16[256,64]{1,0:T(8,128)(2,1)}, u32[]{:S(2)}) copy-start(bf16[256,64]{1,0:T(8,128)(2,1)} %copy-done.27) | copy-start | bytes 98308
  99.0 18.4 %collective-permute-start = (bf16[1536,1536]{1,0:T(8,128)(2,1)}, bf16[1536,1536]{1,0:T(8,128)(2,1)S(1)}, u32[]{:S(2)}, u32[]{:S(2)}) collective-permute-start(bf16[1536,1536]{1,0:T(8,128)(2,1)} %shard_map.130.up_ref.own_ref), channel_id=1, source_target_pairs={{0,4},{4,0},{1,5},{5,1},{2,6},{6,2},{3,7},{7,3},{8,12},{12,8},{9,1... | collective-permute-start | bytes 14155784 | tf_op jit(solution)/shard_map/ppermute | solution.py:443
  112.0 5.4 %copy-start.13 = (bf16[64,768]{1,0:T(8,128)(2,1)S(1)}, bf16[64,768]{1,0:T(8,128)(2,1)}, u32[]{:S(2)}) copy-start(bf16[64,768]{1,0:T(8,128)(2,1)} %get-tuple-element.55.refs_5_.b_ref.bt_ref) | copy-start | bytes 294916
  115.1 5.4 %copy-start.1 = (bf16[1536,1536]{1,0:T(8,128)(2,1)S(1)}, bf16[1536,1536]{1,0:T(8,128)(2,1)}, u32[]{:S(2)}) copy-start(bf16[1536,1536]{1,0:T(8,128)(2,1)} %shard_map.130.up_ref.own_ref) | copy-start | bytes 14155780
  123.4 15.5 %all-to-all-start.1 = ((bf16[4,64,1536]{2,1,0:T(8,128)(2,1)}), bf16[4,64,1536]{2,1,0:T(8,128)(2,1)S(1)}, u32[]{:S(2)}, u32[]{:S(2)}) async-start(bf16[4,64,1536]{2,1,0:T(8,128)(2,1)} %bitcast.13), calls=%async_computation.1 | async-start | bytes 1572864 | tf_op jit(solution)/shard_map/all_to_all | solution.py:448
  133.8 5.1 %copy-start.11 = (bf16[64,1536]{1,0:T(8,128)(2,1)S(1)}, bf16[64,1536]{1,0:T(8,128)(2,1)}, u32[]{:S(2)}) copy-start(bf16[64,1536]{1,0:T(8,128)(2,1)} %get-tuple-element.65.refs_6_.x_ref) | copy-start | bytes 589828
  133.8 5.1 %copy-start.12 = (bf16[64,1536]{1,0:T(8,128)(2,1)S(1)}, bf16[64,1536]{1,0:T(8,128)(2,1)}, u32[]{:S(2)}) copy-start(bf16[64,1536]{1,0:T(8,128)(2,1)} %get-tuple-element.64.refs_7_.t_ref) | copy-start | bytes 589828
  133.8 5.1 %copy-start.29 = (f32[64,1]{1,0:T(8,128)S(1)}, f32[64,1]{1,0:T(8,128)}, u32[]{:S(2)}) copy-start(f32[64,1]{1,0:T(8,128)} %fusion.refs_10_.mask_ref) | copy-start | bytes 772
  133.8 5.1 %copy-start.38 = (f32[1,1536]{1,0:T(1,128)S(1)}, f32[1,1536]{1,0:T(1,128)}, u32[]{:S(2)}) copy-start(f32[1,1536]{1,0:T(1,128)} %get-tuple-element.58.refs_8_.gate_ref) | copy-start | bytes 18436
  141.2 22.8 %all-to-all-start.2 = ((bf16[4,128,1536]{2,1,0:T(8,128)(2,1)}), bf16[4,128,1536]{2,1,0:T(8,128)(2,1)S(1)}, u32[]{:S(2)}, u32[]{:S(2)}) async-start(bf16[4,128,1536]{2,1,0:T(8,128)(2,1)} %copy-done.17), calls=%async_computation.2 | async-start | bytes 3145728 | tf_op jit(solution)/shard_map/all_to_all | solution.py:452
  178.1 8.3 %all-to-all-start.3 = ((bf16[4,80,256]{2,1,0:T(8,128)(2,1)}), bf16[4,80,256]{2,1,0:T(8,128)(2,1)S(1)}, u32[]{:S(2)}, u32[]{:S(2)}) async-start(bf16[4,80,256]{2,1,0:T(8,128)(2,1)} %copy-done.37), calls=%async_computation.3 | async-start | bytes 327680 | tf_op jit(solution)/shard_map/all_to_all | solution.py:456
  184.6 11.2 %copy-start.40 = (bf16[256,64]{1,0:T(8,128)(2,1)S(1)}, bf16[256,64]{1,0:T(8,128)(2,1)}, u32[]{:S(2)}) copy-start(bf16[256,64]{1,0:T(8,128)(2,1)} %copy-done.39) | copy-start | bytes 98308
  188.0 23.7 %all-to-all-start.4 = ((bf16[8,16,1536]{2,1,0:T(8,128)(2,1)}), bf16[8,16,1536]{2,1,0:T(8,128)(2,1)}, u32[]{:S(2)}, u32[]{:S(2)}) async-start(bf16[8,16,1536]{2,1,0:T(8,128)(2,1)} %bitcast.30), calls=%async_computation.4 | async-start | bytes 786432 | tf_op jit(solution)/shard_map/all_to_all | solution.py:466
  203.0 20.1 %copy-start.20 = (f32[64,1536]{1,0:T(8,128)S(1)}, f32[64,1536]{1,0:T(8,128)}, u32[]{:S(2)}) copy-start(f32[64,1536]{1,0:T(8,128)} %copy-done.18) | copy-start | bytes 1179652
  203.0 20.1 %copy-start.41 = (f32[1,1536]{1,0:T(1,128)S(1)}, f32[1,1536]{1,0:T(1,128)}, u32[]{:S(2)}) copy-start(f32[1,1536]{1,0:T(1,128)} %get-tuple-element.57.refs_9_.scale_ref) | copy-start | bytes 18436
  203.1 20.0 %collective-permute-start.1 = (bf16[64,1536]{1,0:T(8,128)(2,1)S(1)}, bf16[64,1536]{1,0:T(8,128)(2,1)S(1)}, u32[]{:S(2)}, u32[]{:S(2)}) collective-permute-start(bf16[64,1536]{1,0:T(8,128)(2,1)S(1)} %get-tuple-element.51), channel_id=1, source_target_pairs={{0,1},{1,2},{2,3},{3,0},{4,5},{5,6},{6,7},{7,4},{8,9},{9,10},{10,1... | collective-permute-start | bytes 589832 | tf_op jit(solution)/shard_map/ppermute | solution.py:478
  205.4 17.6 %collective-permute-start.2 = (bf16[64,1536]{1,0:T(8,128)(2,1)S(1)}, bf16[64,1536]{1,0:T(8,128)(2,1)S(1)}, u32[]{:S(2)}, u32[]{:S(2)}) collective-permute-start(bf16[64,1536]{1,0:T(8,128)(2,1)S(1)} %get-tuple-element.50), channel_id=1, source_target_pairs={{0,2},{1,3},{2,0},{3,1},{4,6},{5,7},{6,4},{7,5},{8,10},{9,11},{10,... | collective-permute-start | bytes 589832 | tf_op jit(solution)/shard_map/ppermute | solution.py:478
  209.1 14.0 %collective-permute-start.3 = (bf16[64,1536]{1,0:T(8,128)(2,1)S(1)}, bf16[64,1536]{1,0:T(8,128)(2,1)S(1)}, u32[]{:S(2)}, u32[]{:S(2)}) collective-permute-start(bf16[64,1536]{1,0:T(8,128)(2,1)S(1)} %get-tuple-element.49), channel_id=1, source_target_pairs={{0,3},{1,0},{2,1},{3,2},{4,7},{5,4},{6,5},{7,6},{8,11},{9,8},{10,9... | collective-permute-start | bytes 589832 | tf_op jit(solution)/shard_map/ppermute | solution.py:478
  214.4 18.2 %all-to-all-start.5 = ((bf16[16,2,768]{2,1,0:T(2,128)(2,1)}), bf16[16,2,768]{2,1,0:T(2,128)(2,1)S(1)}, u32[]{:S(2)}, u32[]{:S(2)}) async-start(bf16[16,2,768]{2,1,0:T(2,128)(2,1)} %reshape.84), calls=%async_computation.5 | async-start | bytes 98304 | tf_op jit(solution)/shard_map/all_to_all | solution.py:468
  223.6 22.1 %collective-permute-start.6 = (bf16[64,1536]{1,0:T(8,128)(2,1)S(1)}, bf16[64,1536]{1,0:T(8,128)(2,1)S(1)}, u32[]{:S(2)}, u32[]{:S(2)}) collective-permute-start(bf16[64,1536]{1,0:T(8,128)(2,1)S(1)} %shard_map.140), channel_id=1, source_target_pairs={{0,3},{1,0},{2,1},{3,2},{4,7},{5,4},{6,5},{7,6},{8,11},{9,8},{10,9... | collective-permute-start | bytes 589832 | tf_op jit(solution)/shard_map/ppermute | solution.py:480
  226.3 19.3 %collective-permute-start.5 = (bf16[64,1536]{1,0:T(8,128)(2,1)S(1)}, bf16[64,1536]{1,0:T(8,128)(2,1)S(1)}, u32[]{:S(2)}, u32[]{:S(2)}) collective-permute-start(bf16[64,1536]{1,0:T(8,128)(2,1)S(1)} %shard_map.140), channel_id=1, source_target_pairs={{0,2},{1,3},{2,0},{3,1},{4,6},{5,7},{6,4},{7,5},{8,10},{9,11},{10,... | collective-permute-start | bytes 589832 | tf_op jit(solution)/shard_map/ppermute | solution.py:480
  230.0 15.6 %collective-permute-start.4 = (bf16[64,1536]{1,0:T(8,128)(2,1)S(1)}, bf16[64,1536]{1,0:T(8,128)(2,1)S(1)}, u32[]{:S(2)}, u32[]{:S(2)}) collective-permute-start(bf16[64,1536]{1,0:T(8,128)(2,1)S(1)} %shard_map.140), channel_id=1, source_target_pairs={{0,1},{1,2},{2,3},{3,0},{4,5},{5,6},{6,7},{7,4},{8,9},{9,10},{10,1... | collective-permute-start | bytes 589832 | tf_op jit(solution)/shard_map/ppermute | solution.py:480
  234.3 23.0 %all-to-all-start.6 = ((bf16[16,2,768]{2,1,0:T(2,128)(2,1)}), bf16[16,2,768]{2,1,0:T(2,128)(2,1)S(1)}, u32[]{:S(2)}, u32[]{:S(2)}) async-start(bf16[16,2,768]{2,1,0:T(2,128)(2,1)} %reshape.86), calls=%async_computation.6 | async-start | bytes 98304 | tf_op jit(solution)/shard_map/all_to_all | solution.py:47
  258.1 16.4 %all-to-all-start.7 = ((bf16[8,16,1536]{2,1,0:T(8,128)(2,1)}), bf16[8,16,1536]{2,1,0:T(8,128)(2,1)S(1)}, u32[]{:S(2)}, u32[]{:S(2)}) async-start(bf16[8,16,1536]{2,1,0:T(8,128)(2,1)} %broadcast_in_dim.50), calls=%async_computation.7 | async-start | bytes 786432 | tf_op jit(solution)/shard_map/all_to_all | solution.py:47
  (28 other events, 48.7 us)
Sparse Core Ops, SparseCore 0:
  27.7 71.2 all-gather.1

commit v8 on v6

--- a/solution.py
+++ b/solution.py
@@ -170,37 +170,33 @@
     )(left, right, own, other)
 
 
-def miss_kernel(got_ref, ref_ref, x_ref, t_ref, gate_ref, mask_ref, unit_ref, send_ref):
+def miss_kernel(got_ref, x_ref, t_ref, gate_ref, mask_ref, unit_ref, dy_ref):
     total = jnp.sum(got_ref[...].astype(F32), axis=0)
     gate = gate_ref[...]
     unit = 2.0 * mask_ref[...] * (x_ref[...].astype(F32) - t_ref[...].astype(F32) + gate * total)
     unit_ref[...] = unit
-    dy = (gate * unit).astype(BF16)
-    for peer in range(send_ref.shape[0]):
-        send_ref[peer, :BLK] = dy
-        send_ref[peer, BLK:] = ref_ref[peer]
-
-
-def miss(got, part_ref, x_own, t_own, gate, mask):
+    dy_ref[...] = (gate * unit).astype(BF16)
+
+
+def miss(got, x_own, t_own, gate, mask):
     groups, rows, width = got.shape
     return pl.pallas_call(
         miss_kernel,
         out_shape=[
             jax.ShapeDtypeStruct((rows, width), F32),
-            jax.ShapeDtypeStruct((groups, 2 * rows, width), BF16),
-        ],
-        compiler_params=params(),
-        cost_estimate=cost(20 * rows * width, 8 * groups * rows * width),
-    )(got, part_ref, x_own, t_own, gate, mask)
+            jax.ShapeDtypeStruct((rows, width), BF16),
+        ],
+        compiler_params=params(),
+        cost_estimate=cost(20 * rows * width, 4 * groups * rows * width),
+    )(got, x_own, t_own, gate, mask)
 
 
 def back_kernel(
-    got_ref, unit_ref, x_ref, t_ref, gate_ref, mask_ref, own_ref, other_ref, bo_ref, bt_ref, so_ref, st_ref,
+    dy_ref, got_ref, unit_ref, x_ref, t_ref, gate_ref, mask_ref, own_ref, other_ref, bo_ref, bt_ref, so_ref, st_ref,
     do_ref, dt_ref, dlow_ref, send_ref, turned_scr, straight_scr,
 ):
     step = pl.program_id(0)
-    width = got_ref.shape[2]
-    dy = got_ref[:, :BLK].reshape(CAP * BLK, width)
+    dy = dy_ref[...]
     d_own = (product(dy, own_ref[...]) * so_ref[...]).astype(BF16)
     d_other = (product(dy, other_ref[...]) * st_ref[...]).astype(BF16)
     do_ref[...] = d_own
@@ -224,7 +220,7 @@
         dlow_ref[...] = straight_scr[...].astype(BF16)
         mask = mask_ref[...]
         base = x_ref[...].astype(F32) - t_ref[...].astype(F32)
-        miss_ref = mask * (base + gate_ref[...] * jnp.sum(got_ref[:, BLK:].astype(F32), axis=0))
+        miss_ref = mask * (base + gate_ref[...] * jnp.sum(got_ref[...].astype(F32), axis=0))
         miss_pol = 0.5 * unit_ref[...]
         parts = jnp.sum((miss_pol - miss_ref) * (miss_pol + miss_ref), axis=1, keepdims=True)
         excess = jnp.broadcast_to(jnp.sum(parts, axis=0, keepdims=True), (NOTE, CAP * BLK))
@@ -240,7 +236,7 @@
             send_ref[peer, rank:] = note
 
 
-def backward(got, unit, x_own, t_own, gate, mask, own, other, b_own, b_other, s_own, s_other):
+def backward(dy, got, unit, x_own, t_own, gate, mask, own, other, b_own, b_other, s_own, s_other):
     groups, _, width = got.shape
     half = s_own.shape[1]
     rank = b_own.shape[0]
@@ -260,14 +256,14 @@
             jax.ShapeDtypeStruct((groups, rank + NOTE, rows), BF16),
         ],
         in_specs=[
-            whole(got.shape), block, block, block, whole((1, width)), whole((BLK, 1)),
+            whole(dy.shape), whole(got.shape), block, block, block, whole((1, width)), whole((BLK, 1)),
             weight, weight, factor, factor, cut, cut,
         ],
         out_specs=[cut, cut, whole((rows, rank)), whole((groups, rank + NOTE, rows))],
         scratch_shapes=[pltpu.VMEM((rank, rows), F32), pltpu.VMEM((rows, rank), F32)],
         compiler_params=params(),
         cost_estimate=cost(4 * rows * width * half, 4 * width * half + 12 * rows * half),
-    )(got, unit, x_own, t_own, gate, mask, own, other, b_own, b_other, s_own, s_other)
+    )(dy, got, unit, x_own, t_own, gate, mask, own, other, b_own, b_other, s_own, s_other)
 
 
 def factor_kernel(split_ref, do_ref, dt_ref, own_ref, other_ref):
@@ -339,12 +335,12 @@
     )(ints, scales, got, modded, b_own, b_other)
 
 
-def dm_kernel(after_ref, do_ref, dt_ref, dlow_ref, own_ref, other_ref, a_ref, out_ref):
+def dm_kernel(do_ref, dt_ref, dlow_ref, own_ref, other_ref, a_ref, out_ref):
     total = rows_by_rows(do_ref[...], own_ref[...]) + rows_by_rows(dt_ref[...], other_ref[...])
     out_ref[...] = (total + product(dlow_ref[...], a_ref[...])).astype(BF16)
 
 
-def dm_terms(after, d_own, d_other, dlow, own, other, a_turned):
+def dm_terms(d_own, d_other, dlow, own, other, a_turned):
     rows, half = d_own.shape
     width = own.shape[0]
     rank = dlow.shape[1]
@@ -355,7 +351,6 @@
         grid=(width // step,),
         out_shape=jax.ShapeDtypeStruct((rows, width), BF16),
         in_specs=[
-            pl.BlockSpec(memory_space=pl.ANY),
             whole((rows, half)),
             whole((rows, half)),
             whole((rows, rank)),
@@ -366,7 +361,7 @@
         out_specs=pl.BlockSpec((rows, step), lambda i: (0, i)),
         compiler_params=params(),
         cost_estimate=cost(4 * rows * width * half, 4 * width * half + 2 * rows * width),
-    )(after, d_own, d_other, dlow, own, other, a_turned)
+    )(d_own, d_other, dlow, own, other, a_turned)
 
 
 def token_kernel(one_ref, two_ref, three_ref, four_ref, x_ref, scale_ref, unit_ref, coef_ref, out_ref):
@@ -451,13 +446,15 @@
     got_pol = lax.all_to_all(part_pol, "t", 0, 0, tiled=True)
     part_ref = lower(ref_own, ref_other, own, other).reshape(CAP, BLK, width)
 
-    unit, send = miss(got_pol, part_ref, x_own, t_own, gate, mask)
-    got_dy = lax.all_to_all(send, "t", 0, 0, tiled=True)
+    unit, dy = miss(got_pol, x_own, t_own, gate, mask)
+    dy = lax.all_gather(dy, "t", axis=0, tiled=True)
+    got_ref = lax.all_to_all(part_ref, "t", 0, 0, tiled=True)
     d_own, d_other, dlow_part, send = backward(
-        got_dy, unit, x_own, t_own, gate, mask, own, other, factor_own, factor_other, slope_own, slope_other
+        dy, got_ref, unit, x_own, t_own, gate, mask, own, other, factor_own, factor_other, slope_own, slope_other
     )
     got_low = lax.all_to_all(send, "t", 0, 0, tiled=True)
     b_own, b_other = factor_terms(low_split, d_own, d_other)
+    dm_part = dm_terms(d_own, d_other, dlow_part, own, other, a_turned)
     keep, give, facts = piles(
         jnp.stack([wins, core]).astype(jnp.int32), scales, got_low, modded, b_own, b_other
     )
@@ -476,16 +473,12 @@
     sum_b = ends[:rank]
     sum_a = ends[rank:].T
 
-    dm_part = dm_terms(pile, d_own, d_other, dlow_part, own, other, a_turned).reshape(CAP, BLK, width)
+    dm_part = after(dm_part, [pile]).reshape(CAP, BLK, width)
     turns = [[(i, (i + step) % n_t) for i in range(n_t)] for step in range(n_t)]
     chunks = [lax.dynamic_index_in_dim(dm_part, (group + step) % n_t, 0, False) for step in range(n_t)]
     chunks = [chunks[0]] + [lax.ppermute(chunks[step], "t", turns[step]) for step in range(1, n_t)]
     grad_block = token_gradient(chunks, x_own, scale_own, unit, coef_own)
-    blocks = [grad_block] + [lax.ppermute(grad_block, "t", turns[step]) for step in range(1, n_t)]
-    blocks = jnp.stack(blocks)
-    grad_tokens = jnp.concatenate(
-        [lax.dynamic_index_in_dim(blocks, (group - slot) % n_t, 0, False) for slot in range(n_t)], 0
-    )
+    grad_tokens = lax.all_gather(grad_block, "t", axis=0, tiled=True)
     return losses, grad_tokens, sum_a, sum_b
 
 

time: 260 us -> 276 us (1.062)
  blocking collectives: 39.2 us -> 72.7 us
  starting transfers between devices: 67.4 us -> 49.4 us
  local copies, waits for them, and re-layouts: 27.7 us -> 37.3 us
  waiting for transfers between devices: 80 us -> 71 us
    all_gather x0 -> x2, blocking collectives: none -> 28 us  [the longest x1 16.3 us: per_device(): dy = lax.all_gather(dy, 't', axis=0, tiled=True)]
    ppermute x3 -> x0, starting transfers between devices: 8.94 us -> none  [per_device(): lax.ppermute(grad_block, 't', turns[step])]
    unnamed x71 -> x78, local copies, waits for them, and re-layouts: 18.3 us -> 25.9 us
    ppermute x3 -> x0, waiting for transfers between devices: 7.51 us -> none  [per_device(): lax.ppermute(grad_block, 't', turns[step])]
    all_to_all x1, starting transfers between devices: 9.98 us -> 3.49 us  [per_device(): got_ref = lax.all_to_all(part_ref, 't', 0, 0, tiled=True)]
    all_to_all x1, starting transfers between devices: 12.6 us -> 6.28 us  [spread(): lax.all_to_all(jnp.broadcast_to(value[None], (n, *value.shape)), axes, 0,...]
    all_to_all x1, blocking collectives: 21.7 us -> 27.4 us  [per_device(): lax.all_to_all(pile.reshape(chips, 2 * rank // chips, half), CHIPS, 0, 0,...]
    all_gather x1, waiting for transfers between devices: 60.7 us -> 56.3 us  [per_device(): own = lax.all_gather(near, 'z', axis=0, tiled=True)]
  transfers between devices with their start and end apart: 14 -> 11, of which waited for: 9 -> 7; matrix products, arithmetic and copies ran while one was open for 4% -> 4% of each run, Pallas kernels for 3% -> 3%
where the time goes in v8:
time: 276 us; the launch traced here: 273 us
  blocking collectives  72.7 us (26%)
  waiting for transfers between devices  71 us (26%)
  starting transfers between devices  49.4 us (18%)
  local copies, waits for them, and re-layouts  37.3 us (14%)
  Pallas kernels  19.8 us (7%)
  between operations  18.5 us (7%)
  other arithmetic  4.56 us (2%)
    all_gather x1, waiting for transfers between devices, per_device(): own = lax.all_gather(near, 'z', axis=0, tiled=True)  56.3 us
    all_to_all x1, blocking collectives, per_device(): lax.all_to_all(pile.reshape(chips, 2 * rank // chips, half), CHIPS, 0, 0,...  27.4 us
    unnamed x78, local copies, waits for them, and re-layouts  25.9 us
    all_to_all x1, blocking collectives, per_device(): lax.all_to_all(sent, ('x', 'c'), 0, 0, tiled=True)  17.3 us
    all_gather x1, blocking collectives, per_device(): dy = lax.all_gather(dy, 't', axis=0, tiled=True)  16.3 us
    all_gather x1, blocking collectives, per_device(): grad_tokens = lax.all_gather(grad_block, 't', axis=0, tiled=True)  11.7 us
    ppermute x1, starting transfers between devices, per_device(): other = lax.ppermute(own, 'c', SWAP)  10.6 us
    ppermute x3, starting transfers between devices, per_device(): lax.ppermute(chunks[step], 't', turns[step])  8.42 us
  transfers between devices with their start and end apart: 11, of which 7 were waited for; matrix products, arithmetic and copies ran while one was open for 4% of the time, Pallas kernels for 3%

profile of v8, /device:TPU:1, one launch (start us, length us, event | category | flops | bytes accessed | tf_op | source)
XLA Modules:
  0.0 273.2 jit_solution(17697761420404764330)
XLA Ops:
  9.2 17.3 %all_to_all.30 = bf16[8,12,1536]{2,1,0:T(8,128)(2,1)S(1)} all-to-all(bf16[8,12,1536]{2,1,0:T(8,128)(2,1)S(1)} %bitcast.38), channel_id=1, replica_groups=mesh['z'=16,'x'=4,'c'=2,'t'=4] {'x','c'}, dimensions={0} | all-to-all | bytes 589824 | tf_op jit(solution)/shard_map/all_to_all | solution.py:412
  30.7 2.0 select_reduce_fusion
  42.5 56.3 %all-gather.2.cloned.1.call-done.refs_0_ = bf16[1536,1536]{1,0:T(8,128)(2,1)} async-done(((bf16[96,1536]{1,0:T(8,128)(2,1)}), bf16[1536,1536]{1,0:T(8,128)(2,1)}) %all-gather.2.cloned.1.call-update) | async-done | bytes 4718608 | tf_op jit(solution)/shard_map/all_gather | solution.py:413
  98.8 10.6 %collective-permute-start = (bf16[1536,1536]{1,0:T(8,128)(2,1)}, bf16[1536,1536]{1,0:T(8,128)(2,1)S(1)}, u32[]{:S(2)}, u32[]{:S(2)}) collective-permute-start(bf16[1536,1536]{1,0:T(8,128)(2,1)} %shard_map.130.up_ref.own_ref), channel_id=1, source_target_pairs={{0,4},{4,0},{1,5},{5,1},{2,6},{6,2},{3,7},{7,3},{8,12},{12,8},{9,1... | collective-permute-start | bytes 14155784 | tf_op jit(solution)/shard_map/ppermute | solution.py:441
  109.4 2.3 copy-done
  111.8 2.1 shard_map.131
  113.9 3.2 %collective-permute-done.up_ref.other_ref = bf16[1536,1536]{1,0:T(8,128)(2,1)S(1)} collective-permute-done((bf16[1536,1536]{1,0:T(8,128)(2,1)}, bf16[1536,1536]{1,0:T(8,128)(2,1)S(1)}, u32[]{:S(2)}, u32[]{:S(2)}) %collective-permute-start) | collective-permute-done | bytes 4718624 | tf_op jit(solution)/shard_map/ppermute | solution.py:441
  117.1 2.2 shard_map.132
  119.3 2.9 %shard_map.133 = bf16[256,1536]{1,0:T(8,128)(2,1)} custom-call(bf16[256,768]{1,0:T(8,128)(2,1)S(1)} %get-tuple-element.27.left_ref, bf16[256,768]{1,0:T(8,128)(2,1)S(1)} %get-tuple-element.28.right_ref, bf16[1536,1536]{1,0:T(8,128)(2,1)S(1)} %copy-done.1, bf16[1536,1536]{1,0:T(8,128)(2,1)S(1)} %collective-permute-done.up_ref.other_ref), custom_call_target="tpu_custom_call" | custom-call | flops 1207959552 | bytes 5505024 | tf_op jit(solution)/shard_map/pallas_call | solution.py:162
  122.2 3.8 %all-to-all-start.1 = ((bf16[4,64,1536]{2,1,0:T(8,128)(2,1)}), bf16[4,64,1536]{2,1,0:T(8,128)(2,1)S(1)}, u32[]{:S(2)}, u32[]{:S(2)}) async-start(bf16[4,64,1536]{2,1,0:T(8,128)(2,1)} %bitcast.13), calls=%async_computation.1 | async-start | bytes 1572864 | tf_op jit(solution)/shard_map/all_to_all | solution.py:446
  126.0 2.3 copy-done.2
  128.3 2.3 copy-done.6
  130.7 2.9 %shard_map.135 = bf16[256,1536]{1,0:T(8,128)(2,1)} custom-call(bf16[256,768]{1,0:T(8,128)(2,1)S(1)} %get-tuple-element.30.left_ref, bf16[256,768]{1,0:T(8,128)(2,1)S(1)} %get-tuple-element.31.right_ref, bf16[1536,1536]{1,0:T(8,128)(2,1)S(1)} %copy-done.2, bf16[1536,1536]{1,0:T(8,128)(2,1)S(1)} %copy-done.6), custom_call_target="tpu_custom_call" | custom-call | flops 1207959552 | bytes 5505024 | tf_op jit(solution)/shard_map/pallas_call | solution.py:162
  133.6 4.1 %all-to-all-done.1.got_ref = bf16[4,64,1536]{2,1,0:T(8,128)(2,1)S(1)} async-done(((bf16[4,64,1536]{2,1,0:T(8,128)(2,1)}), bf16[4,64,1536]{2,1,0:T(8,128)(2,1)S(1)}, u32[]{:S(2)}, u32[]{:S(2)}) %all-to-all-start.1) | async-done | bytes 786464 | tf_op jit(solution)/shard_map/all_to_all | solution.py:446
  137.7 3.5 %all-to-all-start.2 = ((bf16[4,64,1536]{2,1,0:T(8,128)(2,1)}), bf16[4,64,1536]{2,1,0:T(8,128)(2,1)S(1)}, u32[]{:S(2)}, u32[]{:S(2)}) async-start(bf16[4,64,1536]{2,1,0:T(8,128)(2,1)} %bitcast.14), calls=%async_computation.2 | async-start | bytes 1572864 | tf_op jit(solution)/shard_map/all_to_all | solution.py:451
  142.3 16.3 %all_gather.10.dy_ref = bf16[256,1536]{1,0:T(8,128)(2,1)S(1)} all-gather(bf16[64,1536]{1,0:T(8,128)(2,1)S(1)} %get-tuple-element.29), channel_id=1, replica_groups=mesh['z'=16,'x'=4,'c'=2,'t'=4] {'t'}, dimensions={0}, use_global_device_ids=true | all-gather | bytes 983040 | tf_op jit(solution)/shard_map/all_gather | solution.py:450
  158.6 2.3 copy-done.3
  164.2 4.4 %shard_map.136 = (bf16[256,768]{1,0:T(8,128)(2,1)S(1)}, bf16[256,768]{1,0:T(8,128)(2,1)S(1)}, bf16[256,64]{1,0:T(8,128)(2,1)S(1)}, bf16[4,80,256]{2,1,0:T(8,128)(2,1)S(1)}) custom-call(bf16[256,1536]{1,0:T(8,128)(2,1)S(1)} %all_gather.10.dy_ref, bf16[4,64,1536]{2,1,0:T(8,128)(2,1)S(1)} %all-to-all-done.2.got_ref, f32[64,1536]{1,0:T(8,128)S(1)} %copy-done.19, ...), custom_call_target="tpu_custom_call" | custom-call | flops 1207959552 | bytes 7077888 | tf_op jit(solution)/shard_map/pallas_call | solution.py:249
  170.0 4.4 %all-to-all-start.3 = ((bf16[4,80,256]{2,1,0:T(8,128)(2,1)}), bf16[4,80,256]{2,1,0:T(8,128)(2,1)S(1)}, u32[]{:S(2)}, u32[]{:S(2)}) async-start(bf16[4,80,256]{2,1,0:T(8,128)(2,1)} %copy-done.33), calls=%async_computation.3 | async-start | bytes 327680 | tf_op jit(solution)/shard_map/all_to_all | solution.py:455
  177.2 2.3 all-to-all-done.3.got_ref
  180.2 7.6 %collective-permute-start.1 = (bf16[128,768]{1,0:T(8,128)(2,1)S(1)}, bf16[128,768]{1,0:T(8,128)(2,1)S(1)}, u32[]{:S(2)}, u32[]{:S(2)}) collective-permute-start(bf16[128,768]{1,0:T(8,128)(2,1)S(1)} %get-tuple-element.43), channel_id=1, source_target_pairs={{0,4},{4,0},{1,5},{5,1},{2,6},{6,2},{3,7},{7,3},{8,12},{12,8},{9,1... | collective-permute-start | bytes 589832 | tf_op jit(solution)/shard_map/ppermute | solution.py:463
  189.0 27.4 %all_to_all.31 = bf16[64,2,768]{2,1,0:T(2,128)(2,1)S(1)} all-to-all(bf16[64,2,768]{2,1,0:T(2,128)(2,1)S(1)} %reshape.70), channel_id=1, replica_groups=mesh['z'=16,'x'=4,'c'=2,'t'=4] {'z','x'}, dimensions={0} | all-to-all | bytes 393216 | tf_op jit(solution)/shard_map/all_to_all | solution.py:466
  217.4 6.3 %all-to-all-start.5 = ((bf16[64,2,768]{2,1,0:T(2,128)(2,1)}), bf16[64,2,768]{2,1,0:T(2,128)(2,1)S(1)}, u32[]{:S(2)}, u32[]{:S(2)}) async-start(bf16[64,2,768]{2,1,0:T(2,128)(2,1)} %broadcast_in_dim.41), calls=%async_computation.5 | async-start | bytes 393216 | tf_op jit(solution)/shard_map/all_to_all | solution.py:48
  223.8 2.3 copy-done.4
  226.1 2.3 copy-done.7
  228.4 2.4 shard_map.139.refs_0_
  233.0 2.2 collective-permute-start.2
  235.2 3.7 %collective-permute-start.3 = (bf16[64,1536]{1,0:T(8,128)(2,1)S(1)}, bf16[64,1536]{1,0:T(8,128)(2,1)S(1)}, u32[]{:S(2)}, u32[]{:S(2)}) collective-permute-start(bf16[64,1536]{1,0:T(8,128)(2,1)S(1)} %get-tuple-element.50), channel_id=1, source_target_pairs={{0,2},{1,3},{2,0},{3,1},{4,6},{5,7},{6,4},{7,5},{8,10},{9,11},{10,... | collective-permute-start | bytes 589832 | tf_op jit(solution)/shard_map/ppermute | solution.py:479
  238.9 2.5 collective-permute-start.4
  243.3 2.1 collective-permute-done.3.three_ref
  247.9 4.8 %collective-permute-start.5 = (bf16[128,768]{1,0:T(8,128)(2,1)S(1)}, bf16[128,768]{1,0:T(8,128)(2,1)S(1)}, u32[]{:S(2)}, u32[]{:S(2)}) collective-permute-start(bf16[128,768]{1,0:T(8,128)(2,1)S(1)} %reshape.71), channel_id=1, source_target_pairs={{0,4},{4,0},{1,5},{5,1},{2,6},{6,2},{3,7},{7,3},{8,12},{12,8},{9,1... | collective-permute-start | bytes 589832 | tf_op jit(solution)/shard_map/ppermute | solution.py:469
  252.7 11.7 %all_gather.11 = bf16[256,1536]{1,0:T(8,128)(2,1)S(1)} all-gather(bf16[64,1536]{1,0:T(8,128)(2,1)S(1)} %shard_map.141), channel_id=1, replica_groups=mesh['z'=16,'x'=4,'c'=2,'t'=4] {'t'}, dimensions={0}, use_global_device_ids=true | all-gather | bytes 983040 | tf_op jit(solution)/shard_map/all_gather | solution.py:481
  (114 shorter events, 31.8 us)
Async XLA Ops:
  7.2 34.6 %copy-start.37 = (bf16[2,3,1536]{2,0,1:T(2,128)(2,1)S(1)}, bf16[2,3,1536]{2,0,1:T(2,128)(2,1)}, u32[]{:S(2)}) copy-start(bf16[2,3,1536]{2,0,1:T(2,128)(2,1)} %param.12) | copy-start | bytes 55300
  7.2 91.6 %all-gather.2.cloned.1.call-start = ((), (), s32[]{:S(2)}) async-start(), calls=%async_computation.6 | async-start | bytes 5013504 | tf_op jit(solution)/shard_map/all_gather | solution.py:413
  37.2 4.6 %copy-start.28 = (bf16[256,64]{1,0:T(8,128)(2,1)}, bf16[256,64]{1,0:T(8,128)(2,1)S(1)}, u32[]{:S(2)}) copy-start(bf16[256,64]{1,0:T(8,128)(2,1)S(1)} %get-tuple-element.25.refs_2_.low_ref) | copy-start | bytes 98308
  37.2 4.6 %copy-start.31 = (bf16[128,256]{1,0:T(8,128)(2,1)}, bf16[128,256]{1,0:T(8,128)(2,1)S(1)}, u32[]{:S(2)}) copy-start(bf16[128,256]{1,0:T(8,128)(2,1)S(1)} %get-tuple-element.26.refs_3_.split_ref) | copy-start | bytes 196612
  98.8 10.6 %copy-start.9 = (bf16[256,1536]{1,0:T(8,128)(2,1)S(1)}, bf16[256,1536]{1,0:T(8,128)(2,1)}, u32[]{:S(2)}) copy-start(bf16[256,1536]{1,0:T(8,128)(2,1)} %copy-done.8) | copy-start | bytes 2359300
  98.8 10.7 %copy-start.14 = (bf16[64,768]{1,0:T(8,128)(2,1)S(1)}, bf16[64,768]{1,0:T(8,128)(2,1)}, u32[]{:S(2)}) copy-start(bf16[64,768]{1,0:T(8,128)(2,1)} %get-tuple-element.54.refs_4_.b_ref.bo_ref) | copy-start | bytes 294916
  98.8 10.7 %copy-start.29 = (bf16[256,64]{1,0:T(8,128)(2,1)S(1)}, bf16[256,64]{1,0:T(8,128)(2,1)}, u32[]{:S(2)}) copy-start(bf16[256,64]{1,0:T(8,128)(2,1)} %copy-done.28) | copy-start | bytes 98308
  98.8 18.4 %collective-permute-start = (bf16[1536,1536]{1,0:T(8,128)(2,1)}, bf16[1536,1536]{1,0:T(8,128)(2,1)S(1)}, u32[]{:S(2)}, u32[]{:S(2)}) collective-permute-start(bf16[1536,1536]{1,0:T(8,128)(2,1)} %shard_map.130.up_ref.own_ref), channel_id=1, source_target_pairs={{0,4},{4,0},{1,5},{5,1},{2,6},{6,2},{3,7},{7,3},{8,12},{12,8},{9,1... | collective-permute-start | bytes 14155784 | tf_op jit(solution)/shard_map/ppermute | solution.py:441
  111.8 5.4 %copy-start.13 = (bf16[64,768]{1,0:T(8,128)(2,1)S(1)}, bf16[64,768]{1,0:T(8,128)(2,1)}, u32[]{:S(2)}) copy-start(bf16[64,768]{1,0:T(8,128)(2,1)} %get-tuple-element.53.refs_5_.b_ref.bt_ref) | copy-start | bytes 294916
  111.8 7.5 %copy-start.1 = (bf16[1536,1536]{1,0:T(8,128)(2,1)S(1)}, bf16[1536,1536]{1,0:T(8,128)(2,1)}, u32[]{:S(2)}) copy-start(bf16[1536,1536]{1,0:T(8,128)(2,1)} %shard_map.130.up_ref.own_ref) | copy-start | bytes 14155780
  113.9 8.3 %copy-start.24 = (f32[256,768]{1,0:T(8,128)}, f32[256,768]{1,0:T(8,128)S(1)}, u32[]{:S(2)}) copy-start(f32[256,768]{1,0:T(8,128)S(1)} %get-tuple-element.33.so_ref) | copy-start | bytes 2359300
  117.1 5.1 %copy-start.5 = (bf16[1536,1536]{1,0:T(8,128)(2,1)}, bf16[1536,1536]{1,0:T(8,128)(2,1)S(1)}, u32[]{:S(2)}) copy-start(bf16[1536,1536]{1,0:T(8,128)(2,1)S(1)} %collective-permute-done.up_ref.other_ref) | copy-start | bytes 14155780
  119.3 2.9 %copy-start.26 = (f32[256,768]{1,0:T(8,128)}, f32[256,768]{1,0:T(8,128)S(1)}, u32[]{:S(2)}) copy-start(f32[256,768]{1,0:T(8,128)S(1)} %get-tuple-element.34.st_ref) | copy-start | bytes 2359300
  122.2 15.5 %all-to-all-start.1 = ((bf16[4,64,1536]{2,1,0:T(8,128)(2,1)}), bf16[4,64,1536]{2,1,0:T(8,128)(2,1)S(1)}, u32[]{:S(2)}, u32[]{:S(2)}) async-start(bf16[4,64,1536]{2,1,0:T(8,128)(2,1)} %bitcast.13), calls=%async_computation.1 | async-start | bytes 1572864 | tf_op jit(solution)/shard_map/all_to_all | solution.py:446
  130.6 10.5 %copy-start.11 = (bf16[64,1536]{1,0:T(8,128)(2,1)S(1)}, bf16[64,1536]{1,0:T(8,128)(2,1)}, u32[]{:S(2)}) copy-start(bf16[64,1536]{1,0:T(8,128)(2,1)} %get-tuple-element.63.refs_6_.x_ref) | copy-start | bytes 589828
  130.6 10.6 %copy-start.12 = (bf16[64,1536]{1,0:T(8,128)(2,1)S(1)}, bf16[64,1536]{1,0:T(8,128)(2,1)}, u32[]{:S(2)}) copy-start(bf16[64,1536]{1,0:T(8,128)(2,1)} %get-tuple-element.62.refs_7_.t_ref) | copy-start | bytes 589828
  130.6 10.6 %copy-start.30 = (f32[64,1]{1,0:T(8,128)S(1)}, f32[64,1]{1,0:T(8,128)}, u32[]{:S(2)}) copy-start(f32[64,1]{1,0:T(8,128)} %fusion.1.refs_10_.mask_ref) | copy-start | bytes 772
  130.7 10.6 %copy-start.34 = (f32[1,1536]{1,0:T(1,128)S(1)}, f32[1,1536]{1,0:T(1,128)}, u32[]{:S(2)}) copy-start(f32[1,1536]{1,0:T(1,128)} %get-tuple-element.56.refs_8_.gate_ref) | copy-start | bytes 18436
  137.7 20.9 %all-to-all-start.2 = ((bf16[4,64,1536]{2,1,0:T(8,128)(2,1)}), bf16[4,64,1536]{2,1,0:T(8,128)(2,1)S(1)}, u32[]{:S(2)}, u32[]{:S(2)}) async-start(bf16[4,64,1536]{2,1,0:T(8,128)(2,1)} %bitcast.14), calls=%async_computation.2 | async-start | bytes 1572864 | tf_op jit(solution)/shard_map/all_to_all | solution.py:451
  164.2 11.7 %copy-start.32 = (bf16[128,256]{1,0:T(8,128)(2,1)S(1)}, bf16[128,256]{1,0:T(8,128)(2,1)}, u32[]{:S(2)}) copy-start(bf16[128,256]{1,0:T(8,128)(2,1)} %copy-done.31) | copy-start | bytes 196612
  170.0 53.7 %copy-start.23 = (bf16[1536,64]{0,1:T(8,128)(2,1)S(1)}, bf16[1536,64]{0,1:T(8,128)(2,1)}, u32[]{:S(2)}) copy-start(bf16[1536,64]{0,1:T(8,128)(2,1)} %param.18) | copy-start | bytes 589828
  170.0 9.4 %all-to-all-start.3 = ((bf16[4,80,256]{2,1,0:T(8,128)(2,1)}), bf16[4,80,256]{2,1,0:T(8,128)(2,1)S(1)}, u32[]{:S(2)}, u32[]{:S(2)}) async-start(bf16[4,80,256]{2,1,0:T(8,128)(2,1)} %copy-done.33), calls=%async_computation.3 | async-start | bytes 327680 | tf_op jit(solution)/shard_map/all_to_all | solution.py:455
  176.9 46.9 %copy-start.17 = (bf16[256,768]{1,0:T(8,128)(2,1)S(1)}, bf16[256,768]{1,0:T(8,128)(2,1)}, u32[]{:S(2)}) copy-start(bf16[256,768]{1,0:T(8,128)(2,1)} %copy-done.15) | copy-start | bytes 1179652
  180.2 8.6 %collective-permute-start.1 = (bf16[128,768]{1,0:T(8,128)(2,1)S(1)}, bf16[128,768]{1,0:T(8,128)(2,1)S(1)}, u32[]{:S(2)}, u32[]{:S(2)}) collective-permute-start(bf16[128,768]{1,0:T(8,128)(2,1)S(1)} %get-tuple-element.43), channel_id=1, source_target_pairs={{0,4},{4,0},{1,5},{5,1},{2,6},{6,2},{3,7},{7,3},{8,12},{12,8},{9,1... | collective-permute-start | bytes 589832 | tf_op jit(solution)/shard_map/ppermute | solution.py:463
  188.9 42.0 %copy-start.36 = (bf16[128,768]{1,0:T(8,128)(2,1)}, bf16[128,768]{1,0:T(8,128)(2,1)S(1)}, u32[]{:S(2)}) copy-start(bf16[128,768]{1,0:T(8,128)(2,1)S(1)} %add_convert_fusion.refs_1_) | copy-start | bytes 589828
  217.4 30.4 %all-to-all-start.5 = ((bf16[64,2,768]{2,1,0:T(2,128)(2,1)}), bf16[64,2,768]{2,1,0:T(2,128)(2,1)S(1)}, u32[]{:S(2)}, u32[]{:S(2)}) async-start(bf16[64,2,768]{2,1,0:T(2,128)(2,1)} %broadcast_in_dim.41), calls=%async_computation.5 | async-start | bytes 393216 | tf_op jit(solution)/shard_map/all_to_all | solution.py:48
  228.4 18.9 %copy-start.20 = (f32[64,1536]{1,0:T(8,128)S(1)}, f32[64,1536]{1,0:T(8,128)}, u32[]{:S(2)}) copy-start(f32[64,1536]{1,0:T(8,128)} %copy-done.18) | copy-start | bytes 1179652
  228.4 18.9 %copy-start.35 = (f32[1,1536]{1,0:T(1,128)S(1)}, f32[1,1536]{1,0:T(1,128)}, u32[]{:S(2)}) copy-start(f32[1,1536]{1,0:T(1,128)} %get-tuple-element.55.refs_9_.scale_ref) | copy-start | bytes 18436
  233.0 10.3 %collective-permute-start.2 = (bf16[64,1536]{1,0:T(8,128)(2,1)S(1)}, bf16[64,1536]{1,0:T(8,128)(2,1)S(1)}, u32[]{:S(2)}, u32[]{:S(2)}) collective-permute-start(bf16[64,1536]{1,0:T(8,128)(2,1)S(1)} %get-tuple-element.51), channel_id=1, source_target_pairs={{0,1},{1,2},{2,3},{3,0},{4,5},{5,6},{6,7},{7,4},{8,9},{9,10},{10,1... | collective-permute-start | bytes 589832 | tf_op jit(solution)/shard_map/ppermute | solution.py:479
  235.2 10.1 %collective-permute-start.3 = (bf16[64,1536]{1,0:T(8,128)(2,1)S(1)}, bf16[64,1536]{1,0:T(8,128)(2,1)S(1)}, u32[]{:S(2)}, u32[]{:S(2)}) collective-permute-start(bf16[64,1536]{1,0:T(8,128)(2,1)S(1)} %get-tuple-element.50), channel_id=1, source_target_pairs={{0,2},{1,3},{2,0},{3,1},{4,6},{5,7},{6,4},{7,5},{8,10},{9,11},{10,... | collective-permute-start | bytes 589832 | tf_op jit(solution)/shard_map/ppermute | solution.py:479
  238.9 8.4 %collective-permute-start.4 = (bf16[64,1536]{1,0:T(8,128)(2,1)S(1)}, bf16[64,1536]{1,0:T(8,128)(2,1)S(1)}, u32[]{:S(2)}, u32[]{:S(2)}) collective-permute-start(bf16[64,1536]{1,0:T(8,128)(2,1)S(1)} %get-tuple-element.49), channel_id=1, source_target_pairs={{0,3},{1,0},{2,1},{3,2},{4,7},{5,4},{6,5},{7,6},{8,11},{9,8},{10,9... | collective-permute-start | bytes 589832 | tf_op jit(solution)/shard_map/ppermute | solution.py:479
  247.9 16.5 %collective-permute-start.5 = (bf16[128,768]{1,0:T(8,128)(2,1)S(1)}, bf16[128,768]{1,0:T(8,128)(2,1)S(1)}, u32[]{:S(2)}, u32[]{:S(2)}) collective-permute-start(bf16[128,768]{1,0:T(8,128)(2,1)S(1)} %reshape.71), channel_id=1, source_target_pairs={{0,4},{4,0},{1,5},{5,1},{2,6},{6,2},{3,7},{7,3},{8,12},{12,8},{9,1... | collective-permute-start | bytes 589832 | tf_op jit(solution)/shard_map/ppermute | solution.py:469
  (17 other events, 24.3 us)
Sparse Core Ops, SparseCore 0:
  27.4 71.2 all-gather.1

commit v9 on v6

--- a/solution.py
+++ b/solution.py
@@ -46,6 +46,21 @@
 
 def spread(value, axes, n):
     return lax.all_to_all(jnp.broadcast_to(value[None], (n, *value.shape)), axes, 0, 0, tiled=True)
+
+
+def around(block, n):
+    here = lax.axis_index("z")
+    up = [(i, (i + 1) % n) for i in range(n)]
+    down = [(i, (i - 1) % n) for i in range(n)]
+    found = lax.dynamic_update_index_in_dim(jnp.zeros((n, *block.shape), block.dtype), block, here, 0)
+    left = right = block
+    for step in range(1, n // 2 + 1):
+        left = lax.ppermute(left, "z", up)
+        found = lax.dynamic_update_index_in_dim(found, left, (here - step) % n, 0)
+        if step < n // 2:
+            right = lax.ppermute(right, "z", down)
+            found = lax.dynamic_update_index_in_dim(found, right, (here + step) % n, 0)
+    return found
 
 
 def normalise(rows):
@@ -415,7 +430,6 @@
     sent = sent.reshape(thin, n_c, 2 * half).transpose(1, 0, 2)
     sent = jnp.broadcast_to(sent[None], (n_x, n_c, thin, 2 * half)).reshape(n_x * n_c, thin, 2 * half)
     near = lax.all_to_all(sent, ("x", "c"), 0, 0, tiled=True).reshape(n_x * n_c * thin, 2 * half)
-    own = lax.all_gather(near, "z", axis=0, tiled=True)
 
     count = live_block_count[0]
     wins = preferred_blocks[0]
@@ -442,7 +456,8 @@
     factor_other = lax.dynamic_slice_in_dim(factor_out, (1 - core) * half, half, axis=1)
     modded, low, low_split = prepare(preferred_blocks, tokens, modulation.reshape(6, width), a_turned)
 
-    own = after(own, [modded, low, low_split, factor_own, factor_other, x_own, t_own, gate, scale_own, mask])
+    near = after(near, [modded, low, low_split, factor_own, factor_other, x_own, t_own, gate, scale_own, mask])
+    own = around(near, n_z).reshape(width, 2 * half)
     other = lax.ppermute(own, "c", SWAP)
 
     pol_own, ref_own, slope_own = activate(modded, low, own, factor_own)

time: 260 us -> 266 us (1.023)
  starting transfers between devices: 67.4 us -> 128 us
  waiting for transfers between devices: 80 us -> 52.2 us
  blocking collectives: 39.2 us -> 21.8 us
  between operations: 18.6 us -> 5.49 us
  local copies, waits for them, and re-layouts: 27.7 us -> 30.8 us
    all_gather x1 -> x0, waiting for transfers between devices: 60.7 us -> none  [per_device(): own = lax.all_gather(near, 'z', axis=0, tiled=True)]
    ppermute x0 -> x15, starting transfers between devices: none -> 49.5 us  [the longest x7 34.1 us: around(): right = lax.ppermute(right, 'z', down)]
    ppermute x0 -> x15, waiting for transfers between devices: none -> 29.3 us  [the longest x8 29.3 us: around(): left = lax.ppermute(left, 'z', up)]
    all_to_all x1 -> x0, blocking collectives: 17.5 us -> none  [per_device(): lax.all_to_all(sent, ('x', 'c'), 0, 0, tiled=True)]
    all_to_all x0 -> x1, starting transfers between devices: none -> 10.2 us  [per_device(): lax.all_to_all(sent, ('x', 'c'), 0, 0, tiled=True)]
    ppermute x1, waiting for transfers between devices: 2.44 us -> 5.31 us  [per_device(): other = lax.ppermute(own, 'c', SWAP)]
    unnamed x71 -> x63, local copies, waits for them, and re-layouts: 18.3 us -> 18.3 us
  transfers between devices with their start and end apart: 14 -> 29, of which waited for: 9 -> 16; matrix products, arithmetic and copies ran while one was open for 4% -> 5% of each run, Pallas kernels for 3% -> 3%
where the time goes in v9:
time: 266 us; the launch traced here: 264 us
  starting transfers between devices  128 us (48%)
  waiting for transfers between devices  52.2 us (20%)
  local copies, waits for them, and re-layouts  30.8 us (12%)
  blocking collectives  21.8 us (8%)
  Pallas kernels  19.2 us (7%)
  other arithmetic  6.39 us (2%)
  between operations  5.49 us (2%)
    ppermute x7, starting transfers between devices, around(): right = lax.ppermute(right, 'z', down)  34.1 us
    ppermute x8, waiting for transfers between devices, around(): left = lax.ppermute(left, 'z', up)  29.3 us
    all_to_all x1, blocking collectives, per_device(): got_dy = lax.all_to_all(send, 't', 0, 0, tiled=True)  21.8 us
    unnamed x63, local copies, waits for them, and re-layouts  18.3 us
    ppermute x8, starting transfers between devices, around(): left = lax.ppermute(left, 'z', up)  15.4 us
    all_to_all x1, starting transfers between devices, spread(): lax.all_to_all(jnp.broadcast_to(value[None], (n, *value.shape)), axes, 0,...  12.8 us
    all_to_all x1, starting transfers between devices, per_device(): lax.all_to_all(pile.reshape(chips, 2 * rank // chips, half), CHIPS, 0, 0,...  11.3 us
    all_to_all x1, starting transfers between devices, per_device(): lax.all_to_all(sent, ('x', 'c'), 0, 0, tiled=True)  10.2 us
  transfers between devices with their start and end apart: 29, of which 16 were waited for; matrix products, arithmetic and copies ran while one was open for 5% of the time, Pallas kernels for 3%

profile of v9, /device:TPU:1, one launch (start us, length us, event | category | flops | bytes accessed | tf_op | source)
XLA Modules:
  0.0 264.2 jit_solution(7918036334672222462)
XLA Ops:
  3.3 10.2 %all-to-all-start = ((bf16[8,12,1536]{2,1,0:T(8,128)(2,1)}), bf16[8,12,1536]{2,1,0:T(8,128)(2,1)S(1)}, u32[]{:S(2)}, u32[]{:S(2)}) async-start(bf16[8,12,1536]{2,1,0:T(8,128)(2,1)} %bitcast.9), calls=%async_computation | async-start | bytes 786432 | tf_op jit(solution)/shard_map/all_to_all | solution.py:432
  33.6 6.7 %collective-permute-start.1 = (bf16[96,1536]{1,0:T(8,128)(2,1)}, bf16[96,1536]{1,0:T(8,128)(2,1)S(1)}, u32[]{:S(2)}, u32[]{:S(2)}) collective-permute-start(bf16[96,1536]{1,0:T(8,128)(2,1)} %shard_map.130), channel_id=1, source_target_pairs={{0,480},{32,0},{64,32},{96,64},{128,96},{160,128},{192,160},{224,1... | collective-permute-start | bytes 884744 | tf_op jit(solution)/shard_map/ppermute | solution.py:61
  40.9 5.1 %collective-permute-done = bf16[96,1536]{1,0:T(8,128)(2,1)S(1)} collective-permute-done((bf16[96,1536]{1,0:T(8,128)(2,1)}, bf16[96,1536]{1,0:T(8,128)(2,1)S(1)}, u32[]{:S(2)}, u32[]{:S(2)}) %collective-permute-start) | collective-permute-done | bytes 294944 | tf_op jit(solution)/shard_map/ppermute | solution.py:58
  47.9 4.6 %collective-permute-start.3 = (bf16[96,1536]{1,0:T(8,128)(2,1)S(1)}, bf16[96,1536]{1,0:T(8,128)(2,1)S(1)}, u32[]{:S(2)}, u32[]{:S(2)}) collective-permute-start(bf16[96,1536]{1,0:T(8,128)(2,1)S(1)} %collective-permute-done.1), channel_id=1, source_target_pairs={{0,480},{32,0},{64,32},{96,64},{128,96},{160,128},{192,160},{224,1... | collective-permute-start | bytes 884744 | tf_op jit(solution)/shard_map/ppermute | solution.py:61
  52.6 4.5 %collective-permute-done.2 = bf16[96,1536]{1,0:T(8,128)(2,1)S(1)} collective-permute-done((bf16[96,1536]{1,0:T(8,128)(2,1)S(1)}, bf16[96,1536]{1,0:T(8,128)(2,1)S(1)}, u32[]{:S(2)}, u32[]{:S(2)}) %collective-permute-start.2) | collective-permute-done | bytes 294944 | tf_op jit(solution)/shard_map/ppermute | solution.py:58
  59.0 4.6 %collective-permute-start.5 = (bf16[96,1536]{1,0:T(8,128)(2,1)S(1)}, bf16[96,1536]{1,0:T(8,128)(2,1)S(1)}, u32[]{:S(2)}, u32[]{:S(2)}) collective-permute-start(bf16[96,1536]{1,0:T(8,128)(2,1)S(1)} %collective-permute-done.3), channel_id=1, source_target_pairs={{0,480},{32,0},{64,32},{96,64},{128,96},{160,128},{192,160},{224,1... | collective-permute-start | bytes 884744 | tf_op jit(solution)/shard_map/ppermute | solution.py:61
  63.6 3.6 %collective-permute-done.4 = bf16[96,1536]{1,0:T(8,128)(2,1)S(1)} collective-permute-done((bf16[96,1536]{1,0:T(8,128)(2,1)S(1)}, bf16[96,1536]{1,0:T(8,128)(2,1)S(1)}, u32[]{:S(2)}, u32[]{:S(2)}) %collective-permute-start.4) | collective-permute-done | bytes 294944 | tf_op jit(solution)/shard_map/ppermute | solution.py:58
  69.1 4.6 %collective-permute-start.7 = (bf16[96,1536]{1,0:T(8,128)(2,1)S(1)}, bf16[96,1536]{1,0:T(8,128)(2,1)S(1)}, u32[]{:S(2)}, u32[]{:S(2)}) collective-permute-start(bf16[96,1536]{1,0:T(8,128)(2,1)S(1)} %collective-permute-done.5), channel_id=1, source_target_pairs={{0,480},{32,0},{64,32},{96,64},{128,96},{160,128},{192,160},{224,1... | collective-permute-start | bytes 884744 | tf_op jit(solution)/shard_map/ppermute | solution.py:61
  73.8 2.7 %collective-permute-done.6 = bf16[96,1536]{1,0:T(8,128)(2,1)S(1)} collective-permute-done((bf16[96,1536]{1,0:T(8,128)(2,1)S(1)}, bf16[96,1536]{1,0:T(8,128)(2,1)S(1)}, u32[]{:S(2)}, u32[]{:S(2)}) %collective-permute-start.6) | collective-permute-done | bytes 294944 | tf_op jit(solution)/shard_map/ppermute | solution.py:58
  78.4 4.6 %collective-permute-start.9 = (bf16[96,1536]{1,0:T(8,128)(2,1)S(1)}, bf16[96,1536]{1,0:T(8,128)(2,1)S(1)}, u32[]{:S(2)}, u32[]{:S(2)}) collective-permute-start(bf16[96,1536]{1,0:T(8,128)(2,1)S(1)} %collective-permute-done.7), channel_id=1, source_target_pairs={{0,480},{32,0},{64,32},{96,64},{128,96},{160,128},{192,160},{224,1... | collective-permute-start | bytes 884744 | tf_op jit(solution)/shard_map/ppermute | solution.py:61
  87.0 4.6 %collective-permute-start.11 = (bf16[96,1536]{1,0:T(8,128)(2,1)S(1)}, bf16[96,1536]{1,0:T(8,128)(2,1)S(1)}, u32[]{:S(2)}, u32[]{:S(2)}) collective-permute-start(bf16[96,1536]{1,0:T(8,128)(2,1)S(1)} %collective-permute-done.9), channel_id=1, source_target_pairs={{0,480},{32,0},{64,32},{96,64},{128,96},{160,128},{192,160},{224,1... | collective-permute-start | bytes 884744 | tf_op jit(solution)/shard_map/ppermute | solution.py:61
  95.7 4.6 %collective-permute-start.13 = (bf16[96,1536]{1,0:T(8,128)(2,1)S(1)}, bf16[96,1536]{1,0:T(8,128)(2,1)S(1)}, u32[]{:S(2)}, u32[]{:S(2)}) collective-permute-start(bf16[96,1536]{1,0:T(8,128)(2,1)S(1)} %collective-permute-done.11), channel_id=1, source_target_pairs={{0,480},{32,0},{64,32},{96,64},{128,96},{160,128},{192,160},{224,1... | collective-permute-start | bytes 884744 | tf_op jit(solution)/shard_map/ppermute | solution.py:61
  104.4 7.2 %collective-permute-done.14 = bf16[96,1536]{1,0:T(8,128)(2,1)S(1)} collective-permute-done((bf16[96,1536]{1,0:T(8,128)(2,1)S(1)}, bf16[96,1536]{1,0:T(8,128)(2,1)S(1)}, u32[]{:S(2)}, u32[]{:S(2)}) %collective-permute-start.14) | collective-permute-done | bytes 294944 | tf_op jit(solution)/shard_map/ppermute | solution.py:58
  111.7 9.7 %collective-permute-start.15 = (bf16[1536,1536]{1,0:T(8,128)(2,1)S(1)}, bf16[1536,1536]{1,0:T(8,128)(2,1)S(1)}, u32[]{:S(2)}, u32[]{:S(2)}) collective-permute-start(bf16[1536,1536]{1,0:T(8,128)(2,1)S(1)} %bitcast.80), channel_id=1, source_target_pairs={{0,4},{4,0},{1,5},{5,1},{2,6},{6,2},{3,7},{7,3},{8,12},{12,8},{9,1... | collective-permute-start | bytes 14155784 | tf_op jit(solution)/shard_map/ppermute | solution.py:461
  123.6 5.3 %collective-permute-done.15.up_ref.other_ref = bf16[1536,1536]{1,0:T(8,128)(2,1)S(1)} collective-permute-done((bf16[1536,1536]{1,0:T(8,128)(2,1)S(1)}, bf16[1536,1536]{1,0:T(8,128)(2,1)S(1)}, u32[]{:S(2)}, u32[]{:S(2)}) %collective-permute-start.15) | collective-permute-done | bytes 4718624 | tf_op jit(solution)/shard_map/ppermute | solution.py:461
  131.1 2.9 %shard_map.133 = bf16[256,1536]{1,0:T(8,128)(2,1)} custom-call(bf16[256,768]{1,0:T(8,128)(2,1)S(1)} %get-tuple-element.27.left_ref, bf16[256,768]{1,0:T(8,128)(2,1)S(1)} %get-tuple-element.28.right_ref, bf16[1536,1536]{1,0:T(8,128)(2,1)S(1)} %bitcast.82, bf16[1536,1536]{1,0:T(8,128)(2,1)S(1)} %collective-permute-done.15.up_ref.other_ref), custom_call_target="tpu_custom_call" | custom-call | flops 1207959552 | bytes 5505024 | tf_op jit(solution)/shard_map/pallas_call | solution.py:177
  134.0 4.2 %all-to-all-start.1 = ((bf16[4,64,1536]{2,1,0:T(8,128)(2,1)}), bf16[4,64,1536]{2,1,0:T(8,128)(2,1)S(1)}, u32[]{:S(2)}, u32[]{:S(2)}) async-start(bf16[4,64,1536]{2,1,0:T(8,128)(2,1)} %bitcast.30), calls=%async_computation.1 | async-start | bytes 1572864 | tf_op jit(solution)/shard_map/all_to_all | solution.py:466
  146.1 3.8 %all-to-all-done.1.got_ref = bf16[4,64,1536]{2,1,0:T(8,128)(2,1)S(1)} async-done(((bf16[4,64,1536]{2,1,0:T(8,128)(2,1)}), bf16[4,64,1536]{2,1,0:T(8,128)(2,1)S(1)}, u32[]{:S(2)}, u32[]{:S(2)}) %all-to-all-start.1) | async-done | bytes 786464 | tf_op jit(solution)/shard_map/all_to_all | solution.py:466
  150.4 21.8 %all_to_all.30.got_ref = bf16[4,128,1536]{2,1,0:T(8,128)(2,1)S(1)} all-to-all(bf16[4,128,1536]{2,1,0:T(8,128)(2,1)S(1)} %get-tuple-element.31), channel_id=1, replica_groups=mesh['z'=16,'x'=4,'c'=2,'t'=4] {'t'}, dimensions={0} | all-to-all | bytes 3145728 | tf_op jit(solution)/shard_map/all_to_all | solution.py:470
  174.4 4.4 %shard_map.136 = (bf16[256,768]{1,0:T(8,128)(2,1)S(1)}, bf16[256,768]{1,0:T(8,128)(2,1)S(1)}, bf16[256,64]{1,0:T(8,128)(2,1)S(1)}, bf16[4,80,256]{2,1,0:T(8,128)(2,1)S(1)}) custom-call(bf16[4,128,1536]{2,1,0:T(8,128)(2,1)S(1)} %all_to_all.30.got_ref, f32[64,1536]{1,0:T(8,128)S(1)} %get-tuple-element.32.unit_ref, bf16[64,1536]{1,0:T(8,128)(2,1)S(1)} %copy-done.9, ...), custom_call_target="tpu_custom_call" | custom-call | flops 1207959552 | bytes 7077888 | tf_op jit(solution)/shard_map/pallas_call | solution.py:268
  179.6 3.5 %all-to-all-start.3 = ((bf16[4,80,256]{2,1,0:T(8,128)(2,1)}), bf16[4,80,256]{2,1,0:T(8,128)(2,1)S(1)}, u32[]{:S(2)}, u32[]{:S(2)}) async-start(bf16[4,80,256]{2,1,0:T(8,128)(2,1)} %copy-done.27), calls=%async_computation.3 | async-start | bytes 327680 | tf_op jit(solution)/shard_map/all_to_all | solution.py:474
  184.7 3.3 %all-to-all-done.3.got_ref = bf16[4,80,256]{2,1,0:T(8,128)(2,1)S(1)} async-done(((bf16[4,80,256]{2,1,0:T(8,128)(2,1)}), bf16[4,80,256]{2,1,0:T(8,128)(2,1)S(1)}, u32[]{:S(2)}, u32[]{:S(2)}) %all-to-all-start.3) | async-done | bytes 163872 | tf_op jit(solution)/shard_map/all_to_all | solution.py:474
  188.8 5.6 %collective-permute-start.16 = (bf16[128,768]{1,0:T(8,128)(2,1)S(1)}, bf16[128,768]{1,0:T(8,128)(2,1)S(1)}, u32[]{:S(2)}, u32[]{:S(2)}) collective-permute-start(bf16[128,768]{1,0:T(8,128)(2,1)S(1)} %get-tuple-element.42), channel_id=1, source_target_pairs={{0,4},{4,0},{1,5},{5,1},{2,6},{6,2},{3,7},{7,3},{8,12},{12,8},{9,1... | collective-permute-start | bytes 589832 | tf_op jit(solution)/shard_map/ppermute | solution.py:481
  196.3 11.3 %all-to-all-start.4 = ((bf16[64,2,768]{2,1,0:T(2,128)(2,1)}), bf16[64,2,768]{2,1,0:T(2,128)(2,1)S(1)}, u32[]{:S(2)}, u32[]{:S(2)}) async-start(bf16[64,2,768]{2,1,0:T(2,128)(2,1)} %reshape.74), calls=%async_computation.4 | async-start | bytes 393216 | tf_op jit(solution)/shard_map/all_to_all | solution.py:484
  217.0 3.7 %collective-permute-start.18 = (bf16[64,1536]{1,0:T(8,128)(2,1)S(1)}, bf16[64,1536]{1,0:T(8,128)(2,1)S(1)}, u32[]{:S(2)}, u32[]{:S(2)}) collective-permute-start(bf16[64,1536]{1,0:T(8,128)(2,1)S(1)} %get-tuple-element.54), channel_id=1, source_target_pairs={{0,2},{1,3},{2,0},{3,1},{4,6},{5,7},{6,4},{7,5},{8,10},{9,11},{10,... | collective-permute-start | bytes 589832 | tf_op jit(solution)/shard_map/ppermute | solution.py:497
  220.7 2.7 %collective-permute-start.19 = (bf16[64,1536]{1,0:T(8,128)(2,1)S(1)}, bf16[64,1536]{1,0:T(8,128)(2,1)S(1)}, u32[]{:S(2)}, u32[]{:S(2)}) collective-permute-start(bf16[64,1536]{1,0:T(8,128)(2,1)S(1)} %get-tuple-element.53), channel_id=1, source_target_pairs={{0,3},{1,0},{2,1},{3,2},{4,7},{5,4},{6,5},{7,6},{8,11},{9,8},{10,9... | collective-permute-start | bytes 589832 | tf_op jit(solution)/shard_map/ppermute | solution.py:497
  226.2 12.8 %all-to-all-start.5 = ((bf16[64,2,768]{2,1,0:T(2,128)(2,1)}), bf16[64,2,768]{2,1,0:T(2,128)(2,1)S(1)}, u32[]{:S(2)}, u32[]{:S(2)}) async-start(bf16[64,2,768]{2,1,0:T(2,128)(2,1)} %broadcast_in_dim.110), calls=%async_computation.5 | async-start | bytes 393216 | tf_op jit(solution)/shard_map/all_to_all | solution.py:48
  241.3 2.8 %collective-permute-start.22 = (bf16[64,1536]{1,0:T(8,128)(2,1)S(1)}, bf16[64,1536]{1,0:T(8,128)(2,1)S(1)}, u32[]{:S(2)}, u32[]{:S(2)}) collective-permute-start(bf16[64,1536]{1,0:T(8,128)(2,1)S(1)} %shard_map.140), channel_id=1, source_target_pairs={{0,3},{1,0},{2,1},{3,2},{4,7},{5,4},{6,5},{7,6},{8,11},{9,8},{10,9... | collective-permute-start | bytes 589832 | tf_op jit(solution)/shard_map/ppermute | solution.py:499
  244.1 3.7 %collective-permute-start.21 = (bf16[64,1536]{1,0:T(8,128)(2,1)S(1)}, bf16[64,1536]{1,0:T(8,128)(2,1)S(1)}, u32[]{:S(2)}, u32[]{:S(2)}) collective-permute-start(bf16[64,1536]{1,0:T(8,128)(2,1)S(1)} %shard_map.140), channel_id=1, source_target_pairs={{0,2},{1,3},{2,0},{3,1},{4,6},{5,7},{6,4},{7,5},{8,10},{9,11},{10,... | collective-permute-start | bytes 589832 | tf_op jit(solution)/shard_map/ppermute | solution.py:499
  247.8 2.5 collective-permute-start.20
  252.3 5.6 %collective-permute-done.20 = bf16[64,1536]{1,0:T(8,128)(2,1)S(1)} collective-permute-done((bf16[64,1536]{1,0:T(8,128)(2,1)S(1)}, bf16[64,1536]{1,0:T(8,128)(2,1)S(1)}, u32[]{:S(2)}, u32[]{:S(2)}) %collective-permute-start.20) | collective-permute-done | bytes 196640 | tf_op jit(solution)/shard_map/ppermute | solution.py:499
  258.1 3.9 %collective-permute-start.23 = (bf16[128,768]{1,0:T(8,128)(2,1)S(1)}, bf16[128,768]{1,0:T(8,128)(2,1)S(1)}, u32[]{:S(2)}, u32[]{:S(2)}) collective-permute-start(bf16[128,768]{1,0:T(8,128)(2,1)S(1)} %reshape.75), channel_id=1, source_target_pairs={{0,4},{4,0},{1,5},{5,1},{2,6},{6,2},{3,7},{7,3},{8,12},{12,8},{9,1... | collective-permute-start | bytes 589832 | tf_op jit(solution)/shard_map/ppermute | solution.py:487
  (150 shorter events, 77.8 us)
Async XLA Ops:
  3.3 27.5 %all-to-all-start = ((bf16[8,12,1536]{2,1,0:T(8,128)(2,1)}), bf16[8,12,1536]{2,1,0:T(8,128)(2,1)S(1)}, u32[]{:S(2)}, u32[]{:S(2)}) async-start(bf16[8,12,1536]{2,1,0:T(8,128)(2,1)} %bitcast.9), calls=%async_computation | async-start | bytes 786432 | tf_op jit(solution)/shard_map/all_to_all | solution.py:432
  31.6 14.4 %collective-permute-start = (bf16[96,1536]{1,0:T(8,128)(2,1)}, bf16[96,1536]{1,0:T(8,128)(2,1)S(1)}, u32[]{:S(2)}, u32[]{:S(2)}) collective-permute-start(bf16[96,1536]{1,0:T(8,128)(2,1)} %shard_map.130), channel_id=1, source_target_pairs={{0,32},{32,64},{64,96},{96,128},{128,160},{160,192},{192,224},{224... | collective-permute-start | bytes 884744 | tf_op jit(solution)/shard_map/ppermute | solution.py:58
  33.6 14.3 %collective-permute-start.1 = (bf16[96,1536]{1,0:T(8,128)(2,1)}, bf16[96,1536]{1,0:T(8,128)(2,1)S(1)}, u32[]{:S(2)}, u32[]{:S(2)}) collective-permute-start(bf16[96,1536]{1,0:T(8,128)(2,1)} %shard_map.130), channel_id=1, source_target_pairs={{0,480},{32,0},{64,32},{96,64},{128,96},{160,128},{192,160},{224,1... | collective-permute-start | bytes 884744 | tf_op jit(solution)/shard_map/ppermute | solution.py:61
  40.8 80.6 %copy-start.8 = (bf16[256,1536]{1,0:T(8,128)(2,1)S(1)}, bf16[256,1536]{1,0:T(8,128)(2,1)}, u32[]{:S(2)}) copy-start(bf16[256,1536]{1,0:T(8,128)(2,1)} %copy-done.7) | copy-start | bytes 2359300
  40.8 80.6 %copy-start.12 = (bf16[64,768]{1,0:T(8,128)(2,1)S(1)}, bf16[64,768]{1,0:T(8,128)(2,1)}, u32[]{:S(2)}) copy-start(bf16[64,768]{1,0:T(8,128)(2,1)} %get-tuple-element.58.refs_4_.b_ref.bo_ref) | copy-start | bytes 294916
  40.8 80.6 %copy-start.21 = (bf16[256,64]{1,0:T(8,128)(2,1)S(1)}, bf16[256,64]{1,0:T(8,128)(2,1)}, u32[]{:S(2)}) copy-start(bf16[256,64]{1,0:T(8,128)(2,1)} %copy-done.20) | copy-start | bytes 98308
  46.0 11.1 %collective-permute-start.2 = (bf16[96,1536]{1,0:T(8,128)(2,1)S(1)}, bf16[96,1536]{1,0:T(8,128)(2,1)S(1)}, u32[]{:S(2)}, u32[]{:S(2)}) collective-permute-start(bf16[96,1536]{1,0:T(8,128)(2,1)S(1)} %collective-permute-done), channel_id=1, source_target_pairs={{0,32},{32,64},{64,96},{96,128},{128,160},{160,192},{192,224},{224... | collective-permute-start | bytes 884744 | tf_op jit(solution)/shard_map/ppermute | solution.py:58
  47.9 11.1 %collective-permute-start.3 = (bf16[96,1536]{1,0:T(8,128)(2,1)S(1)}, bf16[96,1536]{1,0:T(8,128)(2,1)S(1)}, u32[]{:S(2)}, u32[]{:S(2)}) collective-permute-start(bf16[96,1536]{1,0:T(8,128)(2,1)S(1)} %collective-permute-done.1), channel_id=1, source_target_pairs={{0,480},{32,0},{64,32},{96,64},{128,96},{160,128},{192,160},{224,1... | collective-permute-start | bytes 884744 | tf_op jit(solution)/shard_map/ppermute | solution.py:61
  57.1 10.2 %collective-permute-start.4 = (bf16[96,1536]{1,0:T(8,128)(2,1)S(1)}, bf16[96,1536]{1,0:T(8,128)(2,1)S(1)}, u32[]{:S(2)}, u32[]{:S(2)}) collective-permute-start(bf16[96,1536]{1,0:T(8,128)(2,1)S(1)} %collective-permute-done.2), channel_id=1, source_target_pairs={{0,32},{32,64},{64,96},{96,128},{128,160},{160,192},{192,224},{224... | collective-permute-start | bytes 884744 | tf_op jit(solution)/shard_map/ppermute | solution.py:58
  59.0 10.1 %collective-permute-start.5 = (bf16[96,1536]{1,0:T(8,128)(2,1)S(1)}, bf16[96,1536]{1,0:T(8,128)(2,1)S(1)}, u32[]{:S(2)}, u32[]{:S(2)}) collective-permute-start(bf16[96,1536]{1,0:T(8,128)(2,1)S(1)} %collective-permute-done.3), channel_id=1, source_target_pairs={{0,480},{32,0},{64,32},{96,64},{128,96},{160,128},{192,160},{224,1... | collective-permute-start | bytes 884744 | tf_op jit(solution)/shard_map/ppermute | solution.py:61
  67.2 9.2 %collective-permute-start.6 = (bf16[96,1536]{1,0:T(8,128)(2,1)S(1)}, bf16[96,1536]{1,0:T(8,128)(2,1)S(1)}, u32[]{:S(2)}, u32[]{:S(2)}) collective-permute-start(bf16[96,1536]{1,0:T(8,128)(2,1)S(1)} %collective-permute-done.4), channel_id=1, source_target_pairs={{0,32},{32,64},{64,96},{96,128},{128,160},{160,192},{192,224},{224... | collective-permute-start | bytes 884744 | tf_op jit(solution)/shard_map/ppermute | solution.py:58
  69.1 9.2 %collective-permute-start.7 = (bf16[96,1536]{1,0:T(8,128)(2,1)S(1)}, bf16[96,1536]{1,0:T(8,128)(2,1)S(1)}, u32[]{:S(2)}, u32[]{:S(2)}) collective-permute-start(bf16[96,1536]{1,0:T(8,128)(2,1)S(1)} %collective-permute-done.5), channel_id=1, source_target_pairs={{0,480},{32,0},{64,32},{96,64},{128,96},{160,128},{192,160},{224,1... | collective-permute-start | bytes 884744 | tf_op jit(solution)/shard_map/ppermute | solution.py:61
  76.4 8.7 %collective-permute-start.8 = (bf16[96,1536]{1,0:T(8,128)(2,1)S(1)}, bf16[96,1536]{1,0:T(8,128)(2,1)S(1)}, u32[]{:S(2)}, u32[]{:S(2)}) collective-permute-start(bf16[96,1536]{1,0:T(8,128)(2,1)S(1)} %collective-permute-done.6), channel_id=1, source_target_pairs={{0,32},{32,64},{64,96},{96,128},{128,160},{160,192},{192,224},{224... | collective-permute-start | bytes 884744 | tf_op jit(solution)/shard_map/ppermute | solution.py:58
  78.4 8.7 %collective-permute-start.9 = (bf16[96,1536]{1,0:T(8,128)(2,1)S(1)}, bf16[96,1536]{1,0:T(8,128)(2,1)S(1)}, u32[]{:S(2)}, u32[]{:S(2)}) collective-permute-start(bf16[96,1536]{1,0:T(8,128)(2,1)S(1)} %collective-permute-done.7), channel_id=1, source_target_pairs={{0,480},{32,0},{64,32},{96,64},{128,96},{160,128},{192,160},{224,1... | collective-permute-start | bytes 884744 | tf_op jit(solution)/shard_map/ppermute | solution.py:61
  85.1 8.7 %collective-permute-start.10 = (bf16[96,1536]{1,0:T(8,128)(2,1)S(1)}, bf16[96,1536]{1,0:T(8,128)(2,1)S(1)}, u32[]{:S(2)}, u32[]{:S(2)}) collective-permute-start(bf16[96,1536]{1,0:T(8,128)(2,1)S(1)} %collective-permute-done.8), channel_id=1, source_target_pairs={{0,32},{32,64},{64,96},{96,128},{128,160},{160,192},{192,224},{224... | collective-permute-start | bytes 884744 | tf_op jit(solution)/shard_map/ppermute | solution.py:58
  87.0 8.7 %collective-permute-start.11 = (bf16[96,1536]{1,0:T(8,128)(2,1)S(1)}, bf16[96,1536]{1,0:T(8,128)(2,1)S(1)}, u32[]{:S(2)}, u32[]{:S(2)}) collective-permute-start(bf16[96,1536]{1,0:T(8,128)(2,1)S(1)} %collective-permute-done.9), channel_id=1, source_target_pairs={{0,480},{32,0},{64,32},{96,64},{128,96},{160,128},{192,160},{224,1... | collective-permute-start | bytes 884744 | tf_op jit(solution)/shard_map/ppermute | solution.py:61
  93.8 8.7 %collective-permute-start.12 = (bf16[96,1536]{1,0:T(8,128)(2,1)S(1)}, bf16[96,1536]{1,0:T(8,128)(2,1)S(1)}, u32[]{:S(2)}, u32[]{:S(2)}) collective-permute-start(bf16[96,1536]{1,0:T(8,128)(2,1)S(1)} %collective-permute-done.10), channel_id=1, source_target_pairs={{0,32},{32,64},{64,96},{96,128},{128,160},{160,192},{192,224},{224... | collective-permute-start | bytes 884744 | tf_op jit(solution)/shard_map/ppermute | solution.py:58
  95.7 8.7 %collective-permute-start.13 = (bf16[96,1536]{1,0:T(8,128)(2,1)S(1)}, bf16[96,1536]{1,0:T(8,128)(2,1)S(1)}, u32[]{:S(2)}, u32[]{:S(2)}) collective-permute-start(bf16[96,1536]{1,0:T(8,128)(2,1)S(1)} %collective-permute-done.11), channel_id=1, source_target_pairs={{0,480},{32,0},{64,32},{96,64},{128,96},{160,128},{192,160},{224,1... | collective-permute-start | bytes 884744 | tf_op jit(solution)/shard_map/ppermute | solution.py:61
  102.4 9.2 %collective-permute-start.14 = (bf16[96,1536]{1,0:T(8,128)(2,1)S(1)}, bf16[96,1536]{1,0:T(8,128)(2,1)S(1)}, u32[]{:S(2)}, u32[]{:S(2)}) collective-permute-start(bf16[96,1536]{1,0:T(8,128)(2,1)S(1)} %collective-permute-done.12), channel_id=1, source_target_pairs={{0,32},{32,64},{64,96},{96,128},{128,160},{160,192},{192,224},{224... | collective-permute-start | bytes 884744 | tf_op jit(solution)/shard_map/ppermute | solution.py:58
  111.7 17.2 %collective-permute-start.15 = (bf16[1536,1536]{1,0:T(8,128)(2,1)S(1)}, bf16[1536,1536]{1,0:T(8,128)(2,1)S(1)}, u32[]{:S(2)}, u32[]{:S(2)}) collective-permute-start(bf16[1536,1536]{1,0:T(8,128)(2,1)S(1)} %bitcast.80), channel_id=1, source_target_pairs={{0,4},{4,0},{1,5},{5,1},{2,6},{6,2},{3,7},{7,3},{8,12},{12,8},{9,1... | collective-permute-start | bytes 14155784 | tf_op jit(solution)/shard_map/ppermute | solution.py:461
  134.0 15.9 %all-to-all-start.1 = ((bf16[4,64,1536]{2,1,0:T(8,128)(2,1)}), bf16[4,64,1536]{2,1,0:T(8,128)(2,1)S(1)}, u32[]{:S(2)}, u32[]{:S(2)}) async-start(bf16[4,64,1536]{2,1,0:T(8,128)(2,1)} %bitcast.30), calls=%async_computation.1 | async-start | bytes 1572864 | tf_op jit(solution)/shard_map/all_to_all | solution.py:466
  179.6 8.5 %all-to-all-start.3 = ((bf16[4,80,256]{2,1,0:T(8,128)(2,1)}), bf16[4,80,256]{2,1,0:T(8,128)(2,1)S(1)}, u32[]{:S(2)}, u32[]{:S(2)}) async-start(bf16[4,80,256]{2,1,0:T(8,128)(2,1)} %copy-done.27), calls=%async_computation.3 | async-start | bytes 327680 | tf_op jit(solution)/shard_map/all_to_all | solution.py:474
  188.8 6.7 %collective-permute-start.16 = (bf16[128,768]{1,0:T(8,128)(2,1)S(1)}, bf16[128,768]{1,0:T(8,128)(2,1)S(1)}, u32[]{:S(2)}, u32[]{:S(2)}) collective-permute-start(bf16[128,768]{1,0:T(8,128)(2,1)S(1)} %get-tuple-element.42), channel_id=1, source_target_pairs={{0,4},{4,0},{1,5},{5,1},{2,6},{6,2},{3,7},{7,3},{8,12},{12,8},{9,1... | collective-permute-start | bytes 589832 | tf_op jit(solution)/shard_map/ppermute | solution.py:481
  196.3 28.9 %all-to-all-start.4 = ((bf16[64,2,768]{2,1,0:T(2,128)(2,1)}), bf16[64,2,768]{2,1,0:T(2,128)(2,1)S(1)}, u32[]{:S(2)}, u32[]{:S(2)}) async-start(bf16[64,2,768]{2,1,0:T(2,128)(2,1)} %reshape.74), calls=%async_computation.4 | async-start | bytes 393216 | tf_op jit(solution)/shard_map/all_to_all | solution.py:484
  214.8 26.0 %collective-permute-start.17 = (bf16[64,1536]{1,0:T(8,128)(2,1)S(1)}, bf16[64,1536]{1,0:T(8,128)(2,1)S(1)}, u32[]{:S(2)}, u32[]{:S(2)}) collective-permute-start(bf16[64,1536]{1,0:T(8,128)(2,1)S(1)} %get-tuple-element.55), channel_id=1, source_target_pairs={{0,1},{1,2},{2,3},{3,0},{4,5},{5,6},{6,7},{7,4},{8,9},{9,10},{10,1... | collective-permute-start | bytes 589832 | tf_op jit(solution)/shard_map/ppermute | solution.py:497
  217.0 23.8 %collective-permute-start.18 = (bf16[64,1536]{1,0:T(8,128)(2,1)S(1)}, bf16[64,1536]{1,0:T(8,128)(2,1)S(1)}, u32[]{:S(2)}, u32[]{:S(2)}) collective-permute-start(bf16[64,1536]{1,0:T(8,128)(2,1)S(1)} %get-tuple-element.54), channel_id=1, source_target_pairs={{0,2},{1,3},{2,0},{3,1},{4,6},{5,7},{6,4},{7,5},{8,10},{9,11},{10,... | collective-permute-start | bytes 589832 | tf_op jit(solution)/shard_map/ppermute | solution.py:497
  220.7 20.1 %collective-permute-start.19 = (bf16[64,1536]{1,0:T(8,128)(2,1)S(1)}, bf16[64,1536]{1,0:T(8,128)(2,1)S(1)}, u32[]{:S(2)}, u32[]{:S(2)}) collective-permute-start(bf16[64,1536]{1,0:T(8,128)(2,1)S(1)} %get-tuple-element.53), channel_id=1, source_target_pairs={{0,3},{1,0},{2,1},{3,2},{4,7},{5,4},{6,5},{7,6},{8,11},{9,8},{10,9... | collective-permute-start | bytes 589832 | tf_op jit(solution)/shard_map/ppermute | solution.py:497
  226.2 31.9 %all-to-all-start.5 = ((bf16[64,2,768]{2,1,0:T(2,128)(2,1)}), bf16[64,2,768]{2,1,0:T(2,128)(2,1)S(1)}, u32[]{:S(2)}, u32[]{:S(2)}) async-start(bf16[64,2,768]{2,1,0:T(2,128)(2,1)} %broadcast_in_dim.110), calls=%async_computation.5 | async-start | bytes 393216 | tf_op jit(solution)/shard_map/all_to_all | solution.py:48
  241.3 9.0 %collective-permute-start.22 = (bf16[64,1536]{1,0:T(8,128)(2,1)S(1)}, bf16[64,1536]{1,0:T(8,128)(2,1)S(1)}, u32[]{:S(2)}, u32[]{:S(2)}) collective-permute-start(bf16[64,1536]{1,0:T(8,128)(2,1)S(1)} %shard_map.140), channel_id=1, source_target_pairs={{0,3},{1,0},{2,1},{3,2},{4,7},{5,4},{6,5},{7,6},{8,11},{9,8},{10,9... | collective-permute-start | bytes 589832 | tf_op jit(solution)/shard_map/ppermute | solution.py:499
  244.1 8.2 %collective-permute-start.21 = (bf16[64,1536]{1,0:T(8,128)(2,1)S(1)}, bf16[64,1536]{1,0:T(8,128)(2,1)S(1)}, u32[]{:S(2)}, u32[]{:S(2)}) collective-permute-start(bf16[64,1536]{1,0:T(8,128)(2,1)S(1)} %shard_map.140), channel_id=1, source_target_pairs={{0,2},{1,3},{2,0},{3,1},{4,6},{5,7},{6,4},{7,5},{8,10},{9,11},{10,... | collective-permute-start | bytes 589832 | tf_op jit(solution)/shard_map/ppermute | solution.py:499
  247.8 10.1 %collective-permute-start.20 = (bf16[64,1536]{1,0:T(8,128)(2,1)S(1)}, bf16[64,1536]{1,0:T(8,128)(2,1)S(1)}, u32[]{:S(2)}, u32[]{:S(2)}) collective-permute-start(bf16[64,1536]{1,0:T(8,128)(2,1)S(1)} %shard_map.140), channel_id=1, source_target_pairs={{0,1},{1,2},{2,3},{3,0},{4,5},{5,6},{6,7},{7,4},{8,9},{9,10},{10,1... | collective-permute-start | bytes 589832 | tf_op jit(solution)/shard_map/ppermute | solution.py:499
  258.1 5.0 %collective-permute-start.23 = (bf16[128,768]{1,0:T(8,128)(2,1)S(1)}, bf16[128,768]{1,0:T(8,128)(2,1)S(1)}, u32[]{:S(2)}, u32[]{:S(2)}) collective-permute-start(bf16[128,768]{1,0:T(8,128)(2,1)S(1)} %reshape.75), channel_id=1, source_target_pairs={{0,4},{4,0},{1,5},{5,1},{2,6},{6,2},{3,7},{7,3},{8,12},{12,8},{9,1... | collective-permute-start | bytes 589832 | tf_op jit(solution)/shard_map/ppermute | solution.py:487
  (28 other events, 217.8 us)

commit v10 on v9

--- a/solution.py
+++ b/solution.py
@@ -1,3 +1,5 @@
+import functools
+
 import jax
 import jax.numpy as jnp
 from jax import lax
@@ -116,6 +118,18 @@
     )(wins, tokens, mod, a_turned)
 
 
+def own_slot(ints_ref):
+    wins, count, slot = ints_ref[0], ints_ref[1], ints_ref[4]
+    first = slot < wins
+    last = jnp.where(first, wins - 1, count - 1)
+    tail = jnp.where(first, ints_ref[2], ints_ref[3])
+    return first, jnp.where(slot < count, jnp.where(slot == last, tail, BLK), 0)
+
+
+def pick(first, ref, line):
+    return jnp.where(first, ref[line : line + 1].astype(F32), ref[line + 3 : line + 4].astype(F32))
+
+
 def after_kernel(*refs):
     del refs
 
@@ -130,38 +144,47 @@
     )(value, *others)
 
 
-def up_kernel(modded_ref, low_ref, up_ref, b_ref, pol_ref, ref_ref, slope_ref):
+def half_of(core, step, half, size):
+    return pl.ds(pl.multiple_of(core * half + step * size, 128), size)
+
+
+def up_kernel(far, ints_ref, modded_ref, low_ref, up_ref, b_ref, pol_ref, ref_ref, slope_ref):
+    core = 1 - ints_ref[5] if far else ints_ref[5]
+    size = up_ref.shape[1]
+    cut = half_of(core, pl.program_id(0), size * pl.num_programs(0), size)
     pre_ref = product(modded_ref[...], up_ref[...])
-    pre_pol = pre_ref + product(low_ref[...], b_ref[...])
+    pre_pol = pre_ref + product(low_ref[...], b_ref[:, cut])
     act, slope = gelu_and_slope(pre_pol)
     pol_ref[...] = act.astype(BF16)
-    slope_ref[...] = slope
+    slope_ref[...] = slope.astype(BF16)
     ref_ref[...] = gelu(pre_ref).astype(BF16)
 
 
-def activate(modded, low, weights, factor):
+def activate(far, ints, modded, low, weights, factor):
     rows, width = modded.shape
-    rank, half = factor.shape
+    rank = factor.shape[0]
+    half = factor.shape[1] // 2
     step = 256
     cut = pl.BlockSpec((rows, step), lambda i: (0, i))
     return pl.pallas_call(
-        up_kernel,
+        functools.partial(up_kernel, far),
         grid=(half // step,),
         out_shape=[
             jax.ShapeDtypeStruct((rows, half), BF16),
             jax.ShapeDtypeStruct((rows, half), BF16),
-            jax.ShapeDtypeStruct((rows, half), F32),
+            jax.ShapeDtypeStruct((rows, half), BF16),
         ],
         in_specs=[
+            pl.BlockSpec(memory_space=SMEM),
             whole((rows, width)),
             whole((rows, rank)),
             pl.BlockSpec((width, step), lambda i: (0, i)),
-            pl.BlockSpec((rank, step), lambda i: (0, i)),
+            whole(factor.shape),
         ],
         out_specs=[cut, cut, cut],
         compiler_params=params(),
         cost_estimate=cost(2 * rows * width * half, 2 * width * half + 10 * rows * half, 2 * rows * half),
-    )(modded, low, weights, factor)
+    )(ints, modded, low, weights, factor)
 
 
 def down_kernel(left_ref, right_ref, own_ref, other_ref, out_ref):
@@ -185,10 +208,12 @@
     )(left, right, own, other)
 
 
-def miss_kernel(got_ref, ref_ref, x_ref, t_ref, gate_ref, mask_ref, unit_ref, send_ref):
+def miss_kernel(ints_ref, got_ref, ref_ref, x_ref, t_ref, mod_ref, unit_ref, send_ref):
+    first, live = own_slot(ints_ref)
     total = jnp.sum(got_ref[...].astype(F32), axis=0)
-    gate = gate_ref[...]
-    unit = 2.0 * mask_ref[...] * (x_ref[...].astype(F32) - t_ref[...].astype(F32) + gate * total)
+    gate = pick(first, mod_ref, 2)
+    unit = 2.0 * (x_ref[...].astype(F32) - t_ref[...].astype(F32) + gate * total)
+    unit = jnp.where(lax.broadcasted_iota(jnp.int32, unit.shape, 0) < live, unit, 0.0)
     unit_ref[...] = unit
     dy = (gate * unit).astype(BF16)
     for peer in range(send_ref.shape[0]):
@@ -196,7 +221,7 @@
         send_ref[peer, BLK:] = ref_ref[peer]
 
 
-def miss(got, part_ref, x_own, t_own, gate, mask):
+def miss(ints, got, part_ref, x_own, t_own, mod):
     groups, rows, width = got.shape
     return pl.pallas_call(
         miss_kernel,
@@ -204,24 +229,30 @@
             jax.ShapeDtypeStruct((rows, width), F32),
             jax.ShapeDtypeStruct((groups, 2 * rows, width), BF16),
         ],
+        in_specs=[pl.BlockSpec(memory_space=SMEM)] + [pl.BlockSpec(memory_space=pltpu.VMEM)] * 5,
         compiler_params=params(),
         cost_estimate=cost(20 * rows * width, 8 * groups * rows * width),
-    )(got, part_ref, x_own, t_own, gate, mask)
+    )(ints, got, part_ref, x_own, t_own, mod)
 
 
 def back_kernel(
-    got_ref, unit_ref, x_ref, t_ref, gate_ref, mask_ref, own_ref, other_ref, bo_ref, bt_ref, so_ref, st_ref,
+    ints_ref, got_ref, unit_ref, x_ref, t_ref, mod_ref, own_ref, other_ref, b_ref, so_ref, st_ref,
     do_ref, dt_ref, dlow_ref, send_ref, turned_scr, straight_scr,
 ):
     step = pl.program_id(0)
+    core = ints_ref[5]
     width = got_ref.shape[2]
+    size = so_ref.shape[1]
+    half = size * pl.num_programs(0)
+    b_own = b_ref[:, half_of(core, step, half, size)]
+    b_other = b_ref[:, half_of(1 - core, step, half, size)]
     dy = got_ref[:, :BLK].reshape(CAP * BLK, width)
-    d_own = (product(dy, own_ref[...]) * so_ref[...]).astype(BF16)
-    d_other = (product(dy, other_ref[...]) * st_ref[...]).astype(BF16)
+    d_own = (product(dy, own_ref[...]) * so_ref[...].astype(F32)).astype(BF16)
+    d_other = (product(dy, other_ref[...]) * st_ref[...].astype(F32)).astype(BF16)
     do_ref[...] = d_own
     dt_ref[...] = d_other
-    turned = rows_by_rows(bo_ref[...], d_own) + rows_by_rows(bt_ref[...], d_other)
-    straight = rows_by_rows(d_own, bo_ref[...]) + rows_by_rows(d_other, bt_ref[...])
+    turned = rows_by_rows(b_own, d_own) + rows_by_rows(b_other, d_other)
+    straight = rows_by_rows(d_own, b_own) + rows_by_rows(d_other, b_other)
 
     @pl.when(step == 0)
     def _():
@@ -237,9 +268,10 @@
     def _():
         rank = turned_scr.shape[0]
         dlow_ref[...] = straight_scr[...].astype(BF16)
-        mask = mask_ref[...]
+        first, live = own_slot(ints_ref)
         base = x_ref[...].astype(F32) - t_ref[...].astype(F32)
-        miss_ref = mask * (base + gate_ref[...] * jnp.sum(got_ref[:, BLK:].astype(F32), axis=0))
+        miss_ref = base + pick(first, mod_ref, 2) * jnp.sum(got_ref[:, BLK:].astype(F32), axis=0)
+        miss_ref = jnp.where(lax.broadcasted_iota(jnp.int32, miss_ref.shape, 0) < live, miss_ref, 0.0)
         miss_pol = 0.5 * unit_ref[...]
         parts = jnp.sum((miss_pol - miss_ref) * (miss_pol + miss_ref), axis=1, keepdims=True)
         excess = jnp.broadcast_to(jnp.sum(parts, axis=0, keepdims=True), (NOTE, CAP * BLK))
@@ -255,14 +287,13 @@
             send_ref[peer, rank:] = note
 
 
-def backward(got, unit, x_own, t_own, gate, mask, own, other, b_own, b_other, s_own, s_other):
+def backward(ints, got, unit, x_own, t_own, mod, own, other, factor, s_own, s_other):
     groups, _, width = got.shape
     half = s_own.shape[1]
-    rank = b_own.shape[0]
+    rank = factor.shape[0]
     rows = CAP * BLK
     step = 256
     weight = pl.BlockSpec((width, step), lambda i: (0, half // step + i))
-    factor = pl.BlockSpec((rank, step), lambda i: (0, i))
     cut = pl.BlockSpec((rows, step), lambda i: (0, i))
     block = whole((BLK, width))
     return pl.pallas_call(
@@ -275,14 +306,14 @@
             jax.ShapeDtypeStruct((groups, rank + NOTE, rows), BF16),
         ],
         in_specs=[
-            whole(got.shape), block, block, block, whole((1, width)), whole((BLK, 1)),
-            weight, weight, factor, factor, cut, cut,
+            pl.BlockSpec(memory_space=SMEM), whole(got.shape), block, block, block, whole(mod.shape),
+            weight, weight, whole(factor.shape), cut, cut,
         ],
         out_specs=[cut, cut, whole((rows, rank)), whole((groups, rank + NOTE, rows))],
         scratch_shapes=[pltpu.VMEM((rank, rows), F32), pltpu.VMEM((rows, rank), F32)],
         compiler_params=params(),
         cost_estimate=cost(4 * rows * width * half, 4 * width * half + 12 * rows * half),
-    )(got, unit, x_own, t_own, gate, mask, own, other, b_own, b_other, s_own, s_other)
+    )(ints, got, unit, x_own, t_own, mod, own, other, factor, s_own, s_other)
 
 
 def factor_kernel(split_ref, do_ref, dt_ref, own_ref, other_ref):
@@ -302,10 +333,10 @@
 
 
 def pile_kernel(
-    ints_ref, scales_ref, got_ref, modded_ref, own_ref, other_ref, keep_ref, give_ref, facts_ref
+    ints_ref, got_ref, modded_ref, own_ref, other_ref, keep_ref, give_ref, facts_ref
 ):
     wins = ints_ref[0]
-    core = ints_ref[1]
+    core = ints_ref[5]
     groups, lines, rows = got_ref.shape
     rank = lines - NOTE
     half = own_ref.shape[1]
@@ -316,8 +347,11 @@
         excess = note[0:1] + note[1:2] + note[2:3]
         gap_first += jnp.where(slot < wins, excess, 0.0)
         gap_second += jnp.where(slot < wins, 0.0, excess)
-    scale_first = scales_ref[0]
-    scale_second = scales_ref[1]
+    width = modded_ref.shape[1]
+    rows_first = (wins - 1) * BLK + ints_ref[2]
+    rows_second = (ints_ref[1] - wins - 1) * BLK + ints_ref[3]
+    scale_first = 1.0 / (width * jnp.full((1, rows), rows_first, jnp.int32).astype(F32))
+    scale_second = 1.0 / (width * jnp.full((1, rows), rows_second, jnp.int32).astype(F32))
     inside = -BETA * (gap_first * scale_first - gap_second * scale_second)
     losses = jnp.maximum(-inside, 0.0) + jnp.log1p(jnp.exp(-jnp.abs(inside)))
     weight = BETA * LOSS_SCALE * jax.nn.sigmoid(-inside)
@@ -338,7 +372,7 @@
     give_ref[rank:] = product(dlow, far).astype(BF16)
 
 
-def piles(ints, scales, got, modded, b_own, b_other):
+def piles(ints, got, modded, b_own, b_other):
     lines, half = b_own.shape
     rows = got.shape[2]
     return pl.pallas_call(
@@ -348,10 +382,10 @@
             jax.ShapeDtypeStruct((lines, half), BF16),
             jax.ShapeDtypeStruct((8, rows), F32),
         ],
-        in_specs=[pl.BlockSpec(memory_space=SMEM)] * 2 + [pl.BlockSpec(memory_space=pltpu.VMEM)] * 4,
+        in_specs=[pl.BlockSpec(memory_space=SMEM)] + [pl.BlockSpec(memory_space=pltpu.VMEM)] * 4,
         compiler_params=params(),
         cost_estimate=cost(2 * lines * half * rows, 16 * lines * half),
-    )(ints, scales, got, modded, b_own, b_other)
+    )(ints, got, modded, b_own, b_other)
 
 
 def dm_kernel(after_ref, do_ref, dt_ref, dlow_ref, own_ref, other_ref, a_ref, out_ref):
@@ -384,25 +418,28 @@
     )(after, d_own, d_other, dlow, own, other, a_turned)
 
 
-def token_kernel(one_ref, two_ref, three_ref, four_ref, x_ref, scale_ref, unit_ref, coef_ref, out_ref):
+def token_kernel(ints_ref, one_ref, two_ref, three_ref, four_ref, x_ref, mod_ref, unit_ref, facts_ref, out_ref):
     total = one_ref[...].astype(F32) + two_ref[...].astype(F32)
     total = total + three_ref[...].astype(F32) + four_ref[...].astype(F32)
     normed, inverse = normalise(x_ref[...])
-    dn = total * scale_ref[...]
+    first, _ = own_slot(ints_ref)
+    coef = jnp.where(first, facts_ref[1:2, :1], facts_ref[2:3, :1])
+    dn = total * (1.0 + pick(first, mod_ref, 1))
     mean_one = jnp.mean(dn, axis=-1, keepdims=True)
     mean_two = jnp.mean(dn * normed, axis=-1, keepdims=True)
-    grad = coef_ref[...] * (unit_ref[...] + inverse * (dn - mean_one - normed * mean_two))
+    grad = coef * (unit_ref[...] + inverse * (dn - mean_one - normed * mean_two))
     out_ref[...] = grad.astype(BF16)
 
 
-def token_gradient(pieces, x_own, scale, unit, coef):
+def token_gradient(ints, pieces, x_own, mod, unit, facts):
     rows, width = x_own.shape
     return pl.pallas_call(
         token_kernel,
         out_shape=jax.ShapeDtypeStruct((rows, width), BF16),
+        in_specs=[pl.BlockSpec(memory_space=SMEM)] + [pl.BlockSpec(memory_space=pltpu.VMEM)] * 8,
         compiler_params=params(),
         cost_estimate=cost(20 * rows * width, 20 * rows * width),
-    )(*pieces, x_own, scale, unit, coef)
+    )(ints, *pieces, x_own, mod, unit, facts)
 
 
 def per_device(
@@ -431,58 +468,43 @@
     sent = jnp.broadcast_to(sent[None], (n_x, n_c, thin, 2 * half)).reshape(n_x * n_c, thin, 2 * half)
     near = lax.all_to_all(sent, ("x", "c"), 0, 0, tiled=True).reshape(n_x * n_c * thin, 2 * half)
 
-    count = live_block_count[0]
-    wins = preferred_blocks[0]
-    slots = jnp.arange(CAP, dtype=jnp.int32)
-    flags = (slots >= wins).astype(jnp.int32)
-    last = jnp.where(flags == 0, wins - 1, count - 1)
-    tail = jnp.where(flags == 0, last_block_rows[0, 0], last_block_rows[0, 1])
-    live = jnp.where(slots < count, jnp.where(slots == last, tail, BLK), 0)
-    rows_first = jnp.sum(jnp.where(flags == 0, live, 0)).astype(F32)
-    rows_second = jnp.sum(jnp.where(flags == 1, live, 0)).astype(F32)
-    scales = 1.0 / (width * jnp.stack([rows_first, rows_second]))
-
-    own_first = group < wins
+    ints = [preferred_blocks[0], live_block_count[0], last_block_rows[0, 0], last_block_rows[0, 1], group, core]
+    ints = jnp.stack(ints).astype(jnp.int32)
     x_own = lax.dynamic_slice_in_dim(tokens, group * BLK, BLK, axis=0)
     t_own = lax.dynamic_slice_in_dim(targets, group * BLK, BLK, axis=0)
-    vec_own = jnp.where(own_first, modulation[0], modulation[1]).astype(F32)
-    live_own = lax.dynamic_slice_in_dim(live, group, 1)
-    mask = (jnp.arange(BLK, dtype=jnp.int32)[:, None] < live_own[None, :]).astype(F32)
-    gate = vec_own[2:3]
-    scale_own = 1.0 + vec_own[1:2]
-
+    mod = modulation.reshape(6, width)
     a_turned = factor_in.T
-    factor_own = lax.dynamic_slice_in_dim(factor_out, core * half, half, axis=1)
-    factor_other = lax.dynamic_slice_in_dim(factor_out, (1 - core) * half, half, axis=1)
-    modded, low, low_split = prepare(preferred_blocks, tokens, modulation.reshape(6, width), a_turned)
-
-    near = after(near, [modded, low, low_split, factor_own, factor_other, x_own, t_own, gate, scale_own, mask])
+    modded, low, low_split = prepare(ints, tokens, mod, a_turned)
+
+    near = after(near, [modded, low, low_split, x_own, t_own])
     own = around(near, n_z).reshape(width, 2 * half)
     other = lax.ppermute(own, "c", SWAP)
 
-    pol_own, ref_own, slope_own = activate(modded, low, own, factor_own)
-    pol_other, ref_other, slope_other = activate(modded, low, other, factor_other)
+    pol_own, ref_own, slope_own = activate(False, ints, modded, low, own, factor_out)
+    pol_other, ref_other, slope_other = activate(True, ints, modded, low, other, factor_out)
     part_pol = lower(pol_own, pol_other, own, other).reshape(CAP, BLK, width)
     got_pol = lax.all_to_all(part_pol, "t", 0, 0, tiled=True)
     part_ref = lower(ref_own, ref_other, own, other).reshape(CAP, BLK, width)
 
-    unit, send = miss(got_pol, part_ref, x_own, t_own, gate, mask)
+    unit, send = miss(ints, got_pol, part_ref, x_own, t_own, mod)
     got_dy = lax.all_to_all(send, "t", 0, 0, tiled=True)
     d_own, d_other, dlow_part, send = backward(
-        got_dy, unit, x_own, t_own, gate, mask, own, other, factor_own, factor_other, slope_own, slope_other
+        ints, got_dy, unit, x_own, t_own, mod, own, other, factor_out, slope_own, slope_other
     )
     got_low = lax.all_to_all(send, "t", 0, 0, tiled=True)
     b_own, b_other = factor_terms(low_split, d_own, d_other)
-    keep, give, facts = piles(
-        jnp.stack([wins, core]).astype(jnp.int32), scales, got_low, modded, b_own, b_other
-    )
+    keep, give, facts = piles(ints, got_low, modded, b_own, b_other)
     losses = facts[0, :1]
-    coef_own = jnp.where(own_first, facts[1:2, :1], facts[2:3, :1])
     pile = (keep + lax.ppermute(give, "c", SWAP).astype(F32)).astype(BF16)
 
     chips = n_z * n_x
     pieces = lax.all_to_all(pile.reshape(chips, 2 * rank // chips, half), CHIPS, 0, 0, tiled=True)
+    dm_part = dm_terms(pile, d_own, d_other, dlow_part, own, other, a_turned).reshape(CAP, BLK, width)
+    turns = [[(i, (i + step) % n_t) for i in range(n_t)] for step in range(n_t)]
+    chunks = [lax.dynamic_index_in_dim(dm_part, (group + step) % n_t, 0, False) for step in range(n_t)]
+    chunks = [chunks[0]] + [lax.ppermute(chunks[step], "t", turns[step]) for step in range(1, n_t)]
     total = (jnp.sum(pieces.astype(F32), axis=0) / n_dp).astype(BF16)
+    total = after(total, chunks[1:])
     mine = spread(total, CHIPS, chips).reshape(2 * rank, half)
     theirs = lax.ppermute(mine, "c", SWAP)
     ends = jnp.concatenate([mine, theirs], 1)
@@ -491,16 +513,8 @@
     sum_b = ends[:rank]
     sum_a = ends[rank:].T
 
-    dm_part = dm_terms(pile, d_own, d_other, dlow_part, own, other, a_turned).reshape(CAP, BLK, width)
-    turns = [[(i, (i + step) % n_t) for i in range(n_t)] for step in range(n_t)]
-    chunks = [lax.dynamic_index_in_dim(dm_part, (group + step) % n_t, 0, False) for step in range(n_t)]
-    chunks = [chunks[0]] + [lax.ppermute(chunks[step], "t", turns[step]) for step in range(1, n_t)]
-    grad_block = token_gradient(chunks, x_own, scale_own, unit, coef_own)
-    blocks = [grad_block] + [lax.ppermute(grad_block, "t", turns[step]) for step in range(1, n_t)]
-    blocks = jnp.stack(blocks)
-    grad_tokens = jnp.concatenate(
-        [lax.dynamic_index_in_dim(blocks, (group - slot) % n_t, 0, False) for slot in range(n_t)], 0
-    )
+    grad_block = token_gradient(ints, chunks, x_own, mod, unit, facts)
+    grad_tokens = lax.all_gather(grad_block, "t", axis=0, tiled=True)
     return losses, grad_tokens, sum_a, sum_b
 
 

time: 266 us -> 284 us (1.068)
  blocking collectives: 21.8 us -> 35 us
  waiting for transfers between devices: 52.2 us -> 61.4 us
  local copies, waits for them, and re-layouts: 30.8 us -> 36.1 us
  other arithmetic: 6.39 us -> 1.1 us
  starting transfers between devices: 128 us -> 123 us
    all_gather x0 -> x1, blocking collectives: none -> 13.3 us  [per_device(): grad_tokens = lax.all_gather(grad_block, 't', axis=0, tiled=True)]
    all_to_all x1, waiting for transfers between devices: 0.01 us -> 12.2 us  [spread(): lax.all_to_all(jnp.broadcast_to(value[None], (n, *value.shape)), axes, 0,...]
    ppermute x3 -> x0, starting transfers between devices: 8.94 us -> none  [per_device(): lax.ppermute(grad_block, 't', turns[step])]
    ppermute x3 -> x0, waiting for transfers between devices: 7.52 us -> none  [per_device(): lax.ppermute(grad_block, 't', turns[step])]
    unnamed x63 -> x72, local copies, waits for them, and re-layouts: 18.3 us -> 23.8 us
    ppermute x3, waiting for transfers between devices: 0.01 us -> 4.37 us  [per_device(): lax.ppermute(chunks[step], 't', turns[step])]
    ppermute x1, starting transfers between devices: 3.9 us -> 6.81 us  [per_device(): theirs = lax.ppermute(mine, 'c', SWAP)]
  transfers between devices with their start and end apart: 29 -> 26, of which waited for: 16 -> 16; matrix products, arithmetic and copies ran while one was open for 5% -> 3% of each run, Pallas kernels for 3% -> 4%
where the time goes in v10:
time: 284 us; the launch traced here: 281 us
  starting transfers between devices  123 us (43%)
  waiting for transfers between devices  61.4 us (22%)
  local copies, waits for them, and re-layouts  36.1 us (13%)
  blocking collectives  35 us (12%)
  Pallas kernels  21.6 us (8%)
    ppermute x7, starting transfers between devices, around(): right = lax.ppermute(right, 'z', down)  34.1 us
    ppermute x8, waiting for transfers between devices, around(): left = lax.ppermute(left, 'z', up)  29.3 us
    unnamed x72, local copies, waits for them, and re-layouts  23.8 us
    all_to_all x1, blocking collectives, per_device(): got_dy = lax.all_to_all(send, 't', 0, 0, tiled=True)  21.7 us
    ppermute x8, starting transfers between devices, around(): left = lax.ppermute(left, 'z', up)  15.4 us
    all_to_all x1, starting transfers between devices, spread(): lax.all_to_all(jnp.broadcast_to(value[None], (n, *value.shape)), axes, 0,...  14.2 us
    all_gather x1, blocking collectives, per_device(): grad_tokens = lax.all_gather(grad_block, 't', axis=0, tiled=True)  13.3 us
    all_to_all x1, waiting for transfers between devices, spread(): lax.all_to_all(jnp.broadcast_to(value[None], (n, *value.shape)), axes, 0,...  12.2 us
  transfers between devices with their start and end apart: 26, of which 16 were waited for; matrix products, arithmetic and copies ran while one was open for 3% of the time, Pallas kernels for 4%

profile of v10, /device:TPU:1, one launch (start us, length us, event | category | flops | bytes accessed | tf_op | source)
XLA Modules:
  0.0 281.4 jit_solution(15855901107501583802)
XLA Ops:
  3.3 10.2 %all-to-all-start = ((bf16[8,12,1536]{2,1,0:T(8,128)(2,1)}), bf16[8,12,1536]{2,1,0:T(8,128)(2,1)S(1)}, u32[]{:S(2)}, u32[]{:S(2)}) async-start(bf16[8,12,1536]{2,1,0:T(8,128)(2,1)} %bitcast.6), calls=%async_computation | async-start | bytes 786432 | tf_op jit(solution)/shard_map/all_to_all | solution.py:469
  28.7 6.7 %collective-permute-start.1 = (bf16[96,1536]{1,0:T(8,128)(2,1)}, bf16[96,1536]{1,0:T(8,128)(2,1)S(1)}, u32[]{:S(2)}, u32[]{:S(2)}) collective-permute-start(bf16[96,1536]{1,0:T(8,128)(2,1)} %shard_map.130), channel_id=1, source_target_pairs={{0,480},{32,0},{64,32},{96,64},{128,96},{160,128},{192,160},{224,1... | collective-permute-start | bytes 884744 | tf_op jit(solution)/shard_map/ppermute | solution.py:63
  35.9 5.1 %collective-permute-done = bf16[96,1536]{1,0:T(8,128)(2,1)S(1)} collective-permute-done((bf16[96,1536]{1,0:T(8,128)(2,1)}, bf16[96,1536]{1,0:T(8,128)(2,1)S(1)}, u32[]{:S(2)}, u32[]{:S(2)}) %collective-permute-start) | collective-permute-done | bytes 294944 | tf_op jit(solution)/shard_map/ppermute | solution.py:60
  42.9 4.6 %collective-permute-start.3 = (bf16[96,1536]{1,0:T(8,128)(2,1)S(1)}, bf16[96,1536]{1,0:T(8,128)(2,1)S(1)}, u32[]{:S(2)}, u32[]{:S(2)}) collective-permute-start(bf16[96,1536]{1,0:T(8,128)(2,1)S(1)} %collective-permute-done.1), channel_id=1, source_target_pairs={{0,480},{32,0},{64,32},{96,64},{128,96},{160,128},{192,160},{224,1... | collective-permute-start | bytes 884744 | tf_op jit(solution)/shard_map/ppermute | solution.py:63
  47.6 4.5 %collective-permute-done.2 = bf16[96,1536]{1,0:T(8,128)(2,1)S(1)} collective-permute-done((bf16[96,1536]{1,0:T(8,128)(2,1)S(1)}, bf16[96,1536]{1,0:T(8,128)(2,1)S(1)}, u32[]{:S(2)}, u32[]{:S(2)}) %collective-permute-start.2) | collective-permute-done | bytes 294944 | tf_op jit(solution)/shard_map/ppermute | solution.py:60
  54.0 4.6 %collective-permute-start.5 = (bf16[96,1536]{1,0:T(8,128)(2,1)S(1)}, bf16[96,1536]{1,0:T(8,128)(2,1)S(1)}, u32[]{:S(2)}, u32[]{:S(2)}) collective-permute-start(bf16[96,1536]{1,0:T(8,128)(2,1)S(1)} %collective-permute-done.3), channel_id=1, source_target_pairs={{0,480},{32,0},{64,32},{96,64},{128,96},{160,128},{192,160},{224,1... | collective-permute-start | bytes 884744 | tf_op jit(solution)/shard_map/ppermute | solution.py:63
  58.7 3.6 %collective-permute-done.4 = bf16[96,1536]{1,0:T(8,128)(2,1)S(1)} collective-permute-done((bf16[96,1536]{1,0:T(8,128)(2,1)S(1)}, bf16[96,1536]{1,0:T(8,128)(2,1)S(1)}, u32[]{:S(2)}, u32[]{:S(2)}) %collective-permute-start.4) | collective-permute-done | bytes 294944 | tf_op jit(solution)/shard_map/ppermute | solution.py:60
  64.2 4.6 %collective-permute-start.7 = (bf16[96,1536]{1,0:T(8,128)(2,1)S(1)}, bf16[96,1536]{1,0:T(8,128)(2,1)S(1)}, u32[]{:S(2)}, u32[]{:S(2)}) collective-permute-start(bf16[96,1536]{1,0:T(8,128)(2,1)S(1)} %collective-permute-done.5), channel_id=1, source_target_pairs={{0,480},{32,0},{64,32},{96,64},{128,96},{160,128},{192,160},{224,1... | collective-permute-start | bytes 884744 | tf_op jit(solution)/shard_map/ppermute | solution.py:63
  68.8 2.7 collective-permute-done.6
  73.4 4.6 %collective-permute-start.9 = (bf16[96,1536]{1,0:T(8,128)(2,1)S(1)}, bf16[96,1536]{1,0:T(8,128)(2,1)S(1)}, u32[]{:S(2)}, u32[]{:S(2)}) collective-permute-start(bf16[96,1536]{1,0:T(8,128)(2,1)S(1)} %collective-permute-done.7), channel_id=1, source_target_pairs={{0,480},{32,0},{64,32},{96,64},{128,96},{160,128},{192,160},{224,1... | collective-permute-start | bytes 884744 | tf_op jit(solution)/shard_map/ppermute | solution.py:63
  82.1 4.6 %collective-permute-start.11 = (bf16[96,1536]{1,0:T(8,128)(2,1)S(1)}, bf16[96,1536]{1,0:T(8,128)(2,1)S(1)}, u32[]{:S(2)}, u32[]{:S(2)}) collective-permute-start(bf16[96,1536]{1,0:T(8,128)(2,1)S(1)} %collective-permute-done.9), channel_id=1, source_target_pairs={{0,480},{32,0},{64,32},{96,64},{128,96},{160,128},{192,160},{224,1... | collective-permute-start | bytes 884744 | tf_op jit(solution)/shard_map/ppermute | solution.py:63
  90.7 4.6 %collective-permute-start.13 = (bf16[96,1536]{1,0:T(8,128)(2,1)S(1)}, bf16[96,1536]{1,0:T(8,128)(2,1)S(1)}, u32[]{:S(2)}, u32[]{:S(2)}) collective-permute-start(bf16[96,1536]{1,0:T(8,128)(2,1)S(1)} %collective-permute-done.11), channel_id=1, source_target_pairs={{0,480},{32,0},{64,32},{96,64},{128,96},{160,128},{192,160},{224,1... | collective-permute-start | bytes 884744 | tf_op jit(solution)/shard_map/ppermute | solution.py:63
  99.5 7.2 %collective-permute-done.14 = bf16[96,1536]{1,0:T(8,128)(2,1)S(1)} collective-permute-done((bf16[96,1536]{1,0:T(8,128)(2,1)S(1)}, bf16[96,1536]{1,0:T(8,128)(2,1)S(1)}, u32[]{:S(2)}, u32[]{:S(2)}) %collective-permute-start.14) | collective-permute-done | bytes 294944 | tf_op jit(solution)/shard_map/ppermute | solution.py:60
  106.7 9.7 %collective-permute-start.15 = (bf16[1536,1536]{1,0:T(8,128)(2,1)S(1)}, bf16[1536,1536]{1,0:T(8,128)(2,1)S(1)}, u32[]{:S(2)}, u32[]{:S(2)}) collective-permute-start(bf16[1536,1536]{1,0:T(8,128)(2,1)S(1)} %bitcast.54), channel_id=1, source_target_pairs={{0,4},{4,0},{1,5},{5,1},{2,6},{6,2},{3,7},{7,3},{8,12},{12,8},{9,1... | collective-permute-start | bytes 14155784 | tf_op jit(solution)/shard_map/ppermute | solution.py:481
  116.5 2.6 shard_map.131
  119.9 4.1 %collective-permute-done.15.up_ref.other_ref = bf16[1536,1536]{1,0:T(8,128)(2,1)S(1)} collective-permute-done((bf16[1536,1536]{1,0:T(8,128)(2,1)S(1)}, bf16[1536,1536]{1,0:T(8,128)(2,1)S(1)}, u32[]{:S(2)}, u32[]{:S(2)}) %collective-permute-start.15) | collective-permute-done | bytes 4718624 | tf_op jit(solution)/shard_map/ppermute | solution.py:481
  124.0 2.6 shard_map.132
  126.6 2.9 %shard_map.133 = bf16[256,1536]{1,0:T(8,128)(2,1)} custom-call(bf16[256,768]{1,0:T(8,128)(2,1)S(1)} %get-tuple-element.27.left_ref, bf16[256,768]{1,0:T(8,128)(2,1)S(1)} %get-tuple-element.28.right_ref, bf16[1536,1536]{1,0:T(8,128)(2,1)S(1)} %bitcast.56, bf16[1536,1536]{1,0:T(8,128)(2,1)S(1)} %collective-permute-done.15.up_ref.other_ref), custom_call_target="tpu_custom_call" | custom-call | flops 1207959552 | bytes 5505024 | tf_op jit(solution)/shard_map/pallas_call | solution.py:200
  129.5 4.2 %all-to-all-start.1 = ((bf16[4,64,1536]{2,1,0:T(8,128)(2,1)}), bf16[4,64,1536]{2,1,0:T(8,128)(2,1)S(1)}, u32[]{:S(2)}, u32[]{:S(2)}) async-start(bf16[4,64,1536]{2,1,0:T(8,128)(2,1)} %bitcast.24), calls=%async_computation.1 | async-start | bytes 1572864 | tf_op jit(solution)/shard_map/all_to_all | solution.py:486
  141.6 3.8 %all-to-all-done.1.got_ref = bf16[4,64,1536]{2,1,0:T(8,128)(2,1)S(1)} async-done(((bf16[4,64,1536]{2,1,0:T(8,128)(2,1)}), bf16[4,64,1536]{2,1,0:T(8,128)(2,1)S(1)}, u32[]{:S(2)}, u32[]{:S(2)}) %all-to-all-start.1) | async-done | bytes 786464 | tf_op jit(solution)/shard_map/all_to_all | solution.py:486
  146.3 21.7 %all_to_all.30.got_ref = bf16[4,128,1536]{2,1,0:T(8,128)(2,1)S(1)} all-to-all(bf16[4,128,1536]{2,1,0:T(8,128)(2,1)S(1)} %get-tuple-element.31), channel_id=1, replica_groups=mesh['z'=16,'x'=4,'c'=2,'t'=4] {'t'}, dimensions={0} | all-to-all | bytes 3145728 | tf_op jit(solution)/shard_map/all_to_all | solution.py:490
  171.3 4.4 %shard_map.136 = (bf16[256,768]{1,0:T(8,128)(2,1)S(1)}, bf16[256,768]{1,0:T(8,128)(2,1)S(1)}, bf16[256,64]{1,0:T(8,128)(2,1)S(1)}, bf16[4,80,256]{2,1,0:T(8,128)(2,1)}) custom-call(s32[6]{0:T(128)S(1)} %stack.14.wins_ref.ints_ref, bf16[4,128,1536]{2,1,0:T(8,128)(2,1)S(1)} %all_to_all.30.got_ref, f32[64,1536]{1,0:T(8,128)S(1)} %get-tuple-element.32.unit_ref, ...), custom_call_target="tpu_custom_call" | custom-call | flops 1207959552 | bytes 7077888 | tf_op jit(solution)/shard_map/pallas_call | solution.py:299
  175.7 3.5 %all-to-all-start.3 = ((bf16[4,80,256]{2,1,0:T(8,128)(2,1)}), bf16[4,80,256]{2,1,0:T(8,128)(2,1)S(1)}, u32[]{:S(2)}, u32[]{:S(2)}) async-start(bf16[4,80,256]{2,1,0:T(8,128)(2,1)} %get-tuple-element.35), calls=%async_computation.3 | async-start | bytes 327680 | tf_op jit(solution)/shard_map/all_to_all | solution.py:494
  179.5 4.7 %all-to-all-done.3.got_ref = bf16[4,80,256]{2,1,0:T(8,128)(2,1)S(1)} async-done(((bf16[4,80,256]{2,1,0:T(8,128)(2,1)}), bf16[4,80,256]{2,1,0:T(8,128)(2,1)S(1)}, u32[]{:S(2)}, u32[]{:S(2)}) %all-to-all-start.3) | async-done | bytes 163872 | tf_op jit(solution)/shard_map/all_to_all | solution.py:494
  184.9 5.6 %collective-permute-start.16 = (bf16[128,768]{1,0:T(8,128)(2,1)S(1)}, bf16[128,768]{1,0:T(8,128)(2,1)S(1)}, u32[]{:S(2)}, u32[]{:S(2)}) collective-permute-start(bf16[128,768]{1,0:T(8,128)(2,1)S(1)} %get-tuple-element.42), channel_id=1, source_target_pairs={{0,4},{4,0},{1,5},{5,1},{2,6},{6,2},{3,7},{7,3},{8,12},{12,8},{9,1... | collective-permute-start | bytes 589832 | tf_op jit(solution)/shard_map/ppermute | solution.py:498
  192.4 11.3 %all-to-all-start.4 = ((bf16[64,2,768]{2,1,0:T(2,128)(2,1)}), bf16[64,2,768]{2,1,0:T(2,128)(2,1)S(1)}, u32[]{:S(2)}, u32[]{:S(2)}) async-start(bf16[64,2,768]{2,1,0:T(2,128)(2,1)} %reshape.48), calls=%async_computation.4 | async-start | bytes 393216 | tf_op jit(solution)/shard_map/all_to_all | solution.py:501
  213.2 3.7 %collective-permute-start.18 = (bf16[64,1536]{1,0:T(8,128)(2,1)S(1)}, bf16[64,1536]{1,0:T(8,128)(2,1)S(1)}, u32[]{:S(2)}, u32[]{:S(2)}) collective-permute-start(bf16[64,1536]{1,0:T(8,128)(2,1)S(1)} %get-tuple-element.47), channel_id=1, source_target_pairs={{0,2},{1,3},{2,0},{3,1},{4,6},{5,7},{6,4},{7,5},{8,10},{9,11},{10,... | collective-permute-start | bytes 589832 | tf_op jit(solution)/shard_map/ppermute | solution.py:505
  223.6 2.9 %collective-permute-done.19.four_ref.refs_3_ = bf16[64,1536]{1,0:T(8,128)(2,1)S(1)} collective-permute-done((bf16[64,1536]{1,0:T(8,128)(2,1)S(1)}, bf16[64,1536]{1,0:T(8,128)(2,1)S(1)}, u32[]{:S(2)}, u32[]{:S(2)}) %collective-permute-start.19) | collective-permute-done | bytes 196640 | tf_op jit(solution)/shard_map/ppermute | solution.py:505
  228.6 14.2 %all-to-all-start.5 = ((bf16[64,2,768]{2,1,0:T(2,128)(2,1)}), bf16[64,2,768]{2,1,0:T(2,128)(2,1)S(1)}, u32[]{:S(2)}, u32[]{:S(2)}) async-start(bf16[64,2,768]{2,1,0:T(2,128)(2,1)} %broadcast_in_dim.82), calls=%async_computation.5 | async-start | bytes 393216 | tf_op jit(solution)/shard_map/all_to_all | solution.py:50
  247.1 12.2 %all-to-all-done.5 = bf16[64,2,768]{2,1,0:T(2,128)(2,1)S(1)} async-done(((bf16[64,2,768]{2,1,0:T(2,128)(2,1)}), bf16[64,2,768]{2,1,0:T(2,128)(2,1)S(1)}, u32[]{:S(2)}, u32[]{:S(2)}) %all-to-all-start.5) | async-done | bytes 196640 | tf_op jit(solution)/shard_map/all_to_all | solution.py:50
  259.4 6.8 %collective-permute-start.20 = (bf16[128,768]{1,0:T(8,128)(2,1)S(1)}, bf16[128,768]{1,0:T(8,128)(2,1)S(1)}, u32[]{:S(2)}, u32[]{:S(2)}) collective-permute-start(bf16[128,768]{1,0:T(8,128)(2,1)S(1)} %reshape.49), channel_id=1, source_target_pairs={{0,4},{4,0},{1,5},{5,1},{2,6},{6,2},{3,7},{7,3},{8,12},{12,8},{9,1... | collective-permute-start | bytes 589832 | tf_op jit(solution)/shard_map/ppermute | solution.py:509
  266.2 13.3 %all_gather.3 = bf16[256,1536]{1,0:T(8,128)(2,1)S(1)} all-gather(bf16[64,1536]{1,0:T(8,128)(2,1)S(1)} %shard_map.140), channel_id=1, replica_groups=mesh['z'=16,'x'=4,'c'=2,'t'=4] {'t'}, dimensions={0}, use_global_device_ids=true | all-gather | bytes 983040 | tf_op jit(solution)/shard_map/all_gather | solution.py:517
  (145 shorter events, 77.1 us)
Async XLA Ops:
  3.3 22.5 %all-to-all-start = ((bf16[8,12,1536]{2,1,0:T(8,128)(2,1)}), bf16[8,12,1536]{2,1,0:T(8,128)(2,1)S(1)}, u32[]{:S(2)}, u32[]{:S(2)}) async-start(bf16[8,12,1536]{2,1,0:T(8,128)(2,1)} %bitcast.6), calls=%async_computation | async-start | bytes 786432 | tf_op jit(solution)/shard_map/all_to_all | solution.py:469
  26.6 14.4 %collective-permute-start = (bf16[96,1536]{1,0:T(8,128)(2,1)}, bf16[96,1536]{1,0:T(8,128)(2,1)S(1)}, u32[]{:S(2)}, u32[]{:S(2)}) collective-permute-start(bf16[96,1536]{1,0:T(8,128)(2,1)} %shard_map.130), channel_id=1, source_target_pairs={{0,32},{32,64},{64,96},{96,128},{128,160},{160,192},{192,224},{224... | collective-permute-start | bytes 884744 | tf_op jit(solution)/shard_map/ppermute | solution.py:60
  28.7 14.3 %collective-permute-start.1 = (bf16[96,1536]{1,0:T(8,128)(2,1)}, bf16[96,1536]{1,0:T(8,128)(2,1)S(1)}, u32[]{:S(2)}, u32[]{:S(2)}) collective-permute-start(bf16[96,1536]{1,0:T(8,128)(2,1)} %shard_map.130), channel_id=1, source_target_pairs={{0,480},{32,0},{64,32},{96,64},{128,96},{160,128},{192,160},{224,1... | collective-permute-start | bytes 884744 | tf_op jit(solution)/shard_map/ppermute | solution.py:63
  35.8 80.6 %copy-start.9 = (bf16[256,1536]{1,0:T(8,128)(2,1)S(1)}, bf16[256,1536]{1,0:T(8,128)(2,1)}, u32[]{:S(2)}) copy-start(bf16[256,1536]{1,0:T(8,128)(2,1)} %copy-done.8) | copy-start | bytes 2359300
  35.8 80.6 %copy-start.12 = (bf16[64,1536]{1,0:T(8,128)(2,1)S(1)}, bf16[64,1536]{1,0:T(8,128)(2,1)}, u32[]{:S(2)}) copy-start(bf16[64,1536]{1,0:T(8,128)(2,1)} %b_ref.5) | copy-start | bytes 589828
  35.8 80.6 %copy-start.23 = (bf16[256,64]{1,0:T(8,128)(2,1)S(1)}, bf16[256,64]{1,0:T(8,128)(2,1)}, u32[]{:S(2)}) copy-start(bf16[256,64]{1,0:T(8,128)(2,1)} %copy-done.22) | copy-start | bytes 98308
  41.0 11.1 %collective-permute-start.2 = (bf16[96,1536]{1,0:T(8,128)(2,1)S(1)}, bf16[96,1536]{1,0:T(8,128)(2,1)S(1)}, u32[]{:S(2)}, u32[]{:S(2)}) collective-permute-start(bf16[96,1536]{1,0:T(8,128)(2,1)S(1)} %collective-permute-done), channel_id=1, source_target_pairs={{0,32},{32,64},{64,96},{96,128},{128,160},{160,192},{192,224},{224... | collective-permute-start | bytes 884744 | tf_op jit(solution)/shard_map/ppermute | solution.py:60
  42.9 11.1 %collective-permute-start.3 = (bf16[96,1536]{1,0:T(8,128)(2,1)S(1)}, bf16[96,1536]{1,0:T(8,128)(2,1)S(1)}, u32[]{:S(2)}, u32[]{:S(2)}) collective-permute-start(bf16[96,1536]{1,0:T(8,128)(2,1)S(1)} %collective-permute-done.1), channel_id=1, source_target_pairs={{0,480},{32,0},{64,32},{96,64},{128,96},{160,128},{192,160},{224,1... | collective-permute-start | bytes 884744 | tf_op jit(solution)/shard_map/ppermute | solution.py:63
  52.1 10.2 %collective-permute-start.4 = (bf16[96,1536]{1,0:T(8,128)(2,1)S(1)}, bf16[96,1536]{1,0:T(8,128)(2,1)S(1)}, u32[]{:S(2)}, u32[]{:S(2)}) collective-permute-start(bf16[96,1536]{1,0:T(8,128)(2,1)S(1)} %collective-permute-done.2), channel_id=1, source_target_pairs={{0,32},{32,64},{64,96},{96,128},{128,160},{160,192},{192,224},{224... | collective-permute-start | bytes 884744 | tf_op jit(solution)/shard_map/ppermute | solution.py:60
  54.0 10.1 %collective-permute-start.5 = (bf16[96,1536]{1,0:T(8,128)(2,1)S(1)}, bf16[96,1536]{1,0:T(8,128)(2,1)S(1)}, u32[]{:S(2)}, u32[]{:S(2)}) collective-permute-start(bf16[96,1536]{1,0:T(8,128)(2,1)S(1)} %collective-permute-done.3), channel_id=1, source_target_pairs={{0,480},{32,0},{64,32},{96,64},{128,96},{160,128},{192,160},{224,1... | collective-permute-start | bytes 884744 | tf_op jit(solution)/shard_map/ppermute | solution.py:63
  62.2 9.2 %collective-permute-start.6 = (bf16[96,1536]{1,0:T(8,128)(2,1)S(1)}, bf16[96,1536]{1,0:T(8,128)(2,1)S(1)}, u32[]{:S(2)}, u32[]{:S(2)}) collective-permute-start(bf16[96,1536]{1,0:T(8,128)(2,1)S(1)} %collective-permute-done.4), channel_id=1, source_target_pairs={{0,32},{32,64},{64,96},{96,128},{128,160},{160,192},{192,224},{224... | collective-permute-start | bytes 884744 | tf_op jit(solution)/shard_map/ppermute | solution.py:60
  64.2 9.2 %collective-permute-start.7 = (bf16[96,1536]{1,0:T(8,128)(2,1)S(1)}, bf16[96,1536]{1,0:T(8,128)(2,1)S(1)}, u32[]{:S(2)}, u32[]{:S(2)}) collective-permute-start(bf16[96,1536]{1,0:T(8,128)(2,1)S(1)} %collective-permute-done.5), channel_id=1, source_target_pairs={{0,480},{32,0},{64,32},{96,64},{128,96},{160,128},{192,160},{224,1... | collective-permute-start | bytes 884744 | tf_op jit(solution)/shard_map/ppermute | solution.py:63
  71.5 8.7 %collective-permute-start.8 = (bf16[96,1536]{1,0:T(8,128)(2,1)S(1)}, bf16[96,1536]{1,0:T(8,128)(2,1)S(1)}, u32[]{:S(2)}, u32[]{:S(2)}) collective-permute-start(bf16[96,1536]{1,0:T(8,128)(2,1)S(1)} %collective-permute-done.6), channel_id=1, source_target_pairs={{0,32},{32,64},{64,96},{96,128},{128,160},{160,192},{192,224},{224... | collective-permute-start | bytes 884744 | tf_op jit(solution)/shard_map/ppermute | solution.py:60
  73.4 8.7 %collective-permute-start.9 = (bf16[96,1536]{1,0:T(8,128)(2,1)S(1)}, bf16[96,1536]{1,0:T(8,128)(2,1)S(1)}, u32[]{:S(2)}, u32[]{:S(2)}) collective-permute-start(bf16[96,1536]{1,0:T(8,128)(2,1)S(1)} %collective-permute-done.7), channel_id=1, source_target_pairs={{0,480},{32,0},{64,32},{96,64},{128,96},{160,128},{192,160},{224,1... | collective-permute-start | bytes 884744 | tf_op jit(solution)/shard_map/ppermute | solution.py:63
  80.1 8.7 %collective-permute-start.10 = (bf16[96,1536]{1,0:T(8,128)(2,1)S(1)}, bf16[96,1536]{1,0:T(8,128)(2,1)S(1)}, u32[]{:S(2)}, u32[]{:S(2)}) collective-permute-start(bf16[96,1536]{1,0:T(8,128)(2,1)S(1)} %collective-permute-done.8), channel_id=1, source_target_pairs={{0,32},{32,64},{64,96},{96,128},{128,160},{160,192},{192,224},{224... | collective-permute-start | bytes 884744 | tf_op jit(solution)/shard_map/ppermute | solution.py:60
  82.1 8.7 %collective-permute-start.11 = (bf16[96,1536]{1,0:T(8,128)(2,1)S(1)}, bf16[96,1536]{1,0:T(8,128)(2,1)S(1)}, u32[]{:S(2)}, u32[]{:S(2)}) collective-permute-start(bf16[96,1536]{1,0:T(8,128)(2,1)S(1)} %collective-permute-done.9), channel_id=1, source_target_pairs={{0,480},{32,0},{64,32},{96,64},{128,96},{160,128},{192,160},{224,1... | collective-permute-start | bytes 884744 | tf_op jit(solution)/shard_map/ppermute | solution.py:63
  88.8 8.7 %collective-permute-start.12 = (bf16[96,1536]{1,0:T(8,128)(2,1)S(1)}, bf16[96,1536]{1,0:T(8,128)(2,1)S(1)}, u32[]{:S(2)}, u32[]{:S(2)}) collective-permute-start(bf16[96,1536]{1,0:T(8,128)(2,1)S(1)} %collective-permute-done.10), channel_id=1, source_target_pairs={{0,32},{32,64},{64,96},{96,128},{128,160},{160,192},{192,224},{224... | collective-permute-start | bytes 884744 | tf_op jit(solution)/shard_map/ppermute | solution.py:60
  90.7 8.7 %collective-permute-start.13 = (bf16[96,1536]{1,0:T(8,128)(2,1)S(1)}, bf16[96,1536]{1,0:T(8,128)(2,1)S(1)}, u32[]{:S(2)}, u32[]{:S(2)}) collective-permute-start(bf16[96,1536]{1,0:T(8,128)(2,1)S(1)} %collective-permute-done.11), channel_id=1, source_target_pairs={{0,480},{32,0},{64,32},{96,64},{128,96},{160,128},{192,160},{224,1... | collective-permute-start | bytes 884744 | tf_op jit(solution)/shard_map/ppermute | solution.py:63
  97.5 9.2 %collective-permute-start.14 = (bf16[96,1536]{1,0:T(8,128)(2,1)S(1)}, bf16[96,1536]{1,0:T(8,128)(2,1)S(1)}, u32[]{:S(2)}, u32[]{:S(2)}) collective-permute-start(bf16[96,1536]{1,0:T(8,128)(2,1)S(1)} %collective-permute-done.12), channel_id=1, source_target_pairs={{0,32},{32,64},{64,96},{96,128},{128,160},{160,192},{192,224},{224... | collective-permute-start | bytes 884744 | tf_op jit(solution)/shard_map/ppermute | solution.py:60
  106.7 17.2 %collective-permute-start.15 = (bf16[1536,1536]{1,0:T(8,128)(2,1)S(1)}, bf16[1536,1536]{1,0:T(8,128)(2,1)S(1)}, u32[]{:S(2)}, u32[]{:S(2)}) collective-permute-start(bf16[1536,1536]{1,0:T(8,128)(2,1)S(1)} %bitcast.54), channel_id=1, source_target_pairs={{0,4},{4,0},{1,5},{5,1},{2,6},{6,2},{3,7},{7,3},{8,12},{12,8},{9,1... | collective-permute-start | bytes 14155784 | tf_op jit(solution)/shard_map/ppermute | solution.py:481
  129.5 15.9 %all-to-all-start.1 = ((bf16[4,64,1536]{2,1,0:T(8,128)(2,1)}), bf16[4,64,1536]{2,1,0:T(8,128)(2,1)S(1)}, u32[]{:S(2)}, u32[]{:S(2)}) async-start(bf16[4,64,1536]{2,1,0:T(8,128)(2,1)} %bitcast.24), calls=%async_computation.1 | async-start | bytes 1572864 | tf_op jit(solution)/shard_map/all_to_all | solution.py:486
  145.5 22.5 %copy-start.2 = (bf16[16,96,1536]{2,1,0:T(8,128)(2,1)S(1)}, bf16[16,96,1536]{2,1,0:T(8,128)(2,1)}, u32[]{:S(2)}) copy-start(bf16[16,96,1536]{2,1,0:T(8,128)(2,1)} %copy-done) | copy-start | bytes 14155780
  145.5 22.5 %copy-start.25 = (bf16[256,768]{1,0:T(8,128)(2,1)S(1)}, bf16[256,768]{1,0:T(8,128)(2,1)}, u32[]{:S(2)}) copy-start(bf16[256,768]{1,0:T(8,128)(2,1)} %copy-done.24) | copy-start | bytes 1179652
  175.7 28.1 %copy-start.21 = (bf16[1536,64]{0,1:T(8,128)(2,1)S(1)}, bf16[1536,64]{0,1:T(8,128)(2,1)}, u32[]{:S(2)}) copy-start(bf16[1536,64]{0,1:T(8,128)(2,1)} %param.18) | copy-start | bytes 589828
  175.7 8.5 %all-to-all-start.3 = ((bf16[4,80,256]{2,1,0:T(8,128)(2,1)}), bf16[4,80,256]{2,1,0:T(8,128)(2,1)S(1)}, u32[]{:S(2)}, u32[]{:S(2)}) async-start(bf16[4,80,256]{2,1,0:T(8,128)(2,1)} %get-tuple-element.35), calls=%async_computation.3 | async-start | bytes 327680 | tf_op jit(solution)/shard_map/all_to_all | solution.py:494
  184.9 6.7 %collective-permute-start.16 = (bf16[128,768]{1,0:T(8,128)(2,1)S(1)}, bf16[128,768]{1,0:T(8,128)(2,1)S(1)}, u32[]{:S(2)}, u32[]{:S(2)}) collective-permute-start(bf16[128,768]{1,0:T(8,128)(2,1)S(1)} %get-tuple-element.42), channel_id=1, source_target_pairs={{0,4},{4,0},{1,5},{5,1},{2,6},{6,2},{3,7},{7,3},{8,12},{12,8},{9,1... | collective-permute-start | bytes 589832 | tf_op jit(solution)/shard_map/ppermute | solution.py:498
  192.4 28.9 %all-to-all-start.4 = ((bf16[64,2,768]{2,1,0:T(2,128)(2,1)}), bf16[64,2,768]{2,1,0:T(2,128)(2,1)S(1)}, u32[]{:S(2)}, u32[]{:S(2)}) async-start(bf16[64,2,768]{2,1,0:T(2,128)(2,1)} %reshape.48), calls=%async_computation.4 | async-start | bytes 393216 | tf_op jit(solution)/shard_map/all_to_all | solution.py:501
  210.9 11.2 %collective-permute-start.17 = (bf16[64,1536]{1,0:T(8,128)(2,1)S(1)}, bf16[64,1536]{1,0:T(8,128)(2,1)S(1)}, u32[]{:S(2)}, u32[]{:S(2)}) collective-permute-start(bf16[64,1536]{1,0:T(8,128)(2,1)S(1)} %get-tuple-element.48), channel_id=1, source_target_pairs={{0,1},{1,2},{2,3},{3,0},{4,5},{5,6},{6,7},{7,4},{8,9},{9,10},{10,1... | collective-permute-start | bytes 589832 | tf_op jit(solution)/shard_map/ppermute | solution.py:505
  213.2 10.4 %collective-permute-start.18 = (bf16[64,1536]{1,0:T(8,128)(2,1)S(1)}, bf16[64,1536]{1,0:T(8,128)(2,1)S(1)}, u32[]{:S(2)}, u32[]{:S(2)}) collective-permute-start(bf16[64,1536]{1,0:T(8,128)(2,1)S(1)} %get-tuple-element.47), channel_id=1, source_target_pairs={{0,2},{1,3},{2,0},{3,1},{4,6},{5,7},{6,4},{7,5},{8,10},{9,11},{10,... | collective-permute-start | bytes 589832 | tf_op jit(solution)/shard_map/ppermute | solution.py:505
  216.9 9.6 %collective-permute-start.19 = (bf16[64,1536]{1,0:T(8,128)(2,1)S(1)}, bf16[64,1536]{1,0:T(8,128)(2,1)S(1)}, u32[]{:S(2)}, u32[]{:S(2)}) collective-permute-start(bf16[64,1536]{1,0:T(8,128)(2,1)S(1)} %get-tuple-element.46), channel_id=1, source_target_pairs={{0,3},{1,0},{2,1},{3,2},{4,7},{5,4},{6,5},{7,6},{8,11},{9,8},{10,9... | collective-permute-start | bytes 589832 | tf_op jit(solution)/shard_map/ppermute | solution.py:505
  228.6 30.7 %all-to-all-start.5 = ((bf16[64,2,768]{2,1,0:T(2,128)(2,1)}), bf16[64,2,768]{2,1,0:T(2,128)(2,1)S(1)}, u32[]{:S(2)}, u32[]{:S(2)}) async-start(bf16[64,2,768]{2,1,0:T(2,128)(2,1)} %broadcast_in_dim.82), calls=%async_computation.5 | async-start | bytes 393216 | tf_op jit(solution)/shard_map/all_to_all | solution.py:50
  259.4 20.1 %collective-permute-start.20 = (bf16[128,768]{1,0:T(8,128)(2,1)S(1)}, bf16[128,768]{1,0:T(8,128)(2,1)S(1)}, u32[]{:S(2)}, u32[]{:S(2)}) collective-permute-start(bf16[128,768]{1,0:T(8,128)(2,1)S(1)} %reshape.49), channel_id=1, source_target_pairs={{0,4},{4,0},{1,5},{5,1},{2,6},{6,2},{3,7},{7,3},{8,12},{12,8},{9,1... | collective-permute-start | bytes 589832 | tf_op jit(solution)/shard_map/ppermute | solution.py:509
  (29 other events, 106.7 us)

commit v11 on v10

--- a/solution.py
+++ b/solution.py
@@ -196,7 +196,7 @@
     rows, half = left.shape
     width = own.shape[0]
     step = 512
-    cut = pl.BlockSpec((step, half), lambda i: (i, 1))
+    cut = pl.BlockSpec((step, half), lambda i: (i, 0))
     return pl.pallas_call(
         down_kernel,
         grid=(width // step,),
@@ -293,7 +293,7 @@
     rank = factor.shape[0]
     rows = CAP * BLK
     step = 256
-    weight = pl.BlockSpec((width, step), lambda i: (0, half // step + i))
+    weight = pl.BlockSpec((width, step), lambda i: (0, i))
     cut = pl.BlockSpec((rows, step), lambda i: (0, i))
     block = whole((BLK, width))
     return pl.pallas_call(
@@ -466,7 +466,10 @@
     sent = jnp.stack([up_rows.reshape(thin, n_c, half), down_rows.reshape(thin, n_c, half)], axis=2)
     sent = sent.reshape(thin, n_c, 2 * half).transpose(1, 0, 2)
     sent = jnp.broadcast_to(sent[None], (n_x, n_c, thin, 2 * half)).reshape(n_x * n_c, thin, 2 * half)
-    near = lax.all_to_all(sent, ("x", "c"), 0, 0, tiled=True).reshape(n_x * n_c * thin, 2 * half)
+    near = lax.all_to_all(sent, ("x", "c"), 0, 0, tiled=True)
+    near_up = near[:, :, :half].reshape(n_x * n_c * thin, half)
+    near_down = near[:, :, half:].reshape(n_x * n_c * thin, half)
+    down_own = lax.all_gather(near_down, "z", axis=0, tiled=True)
 
     ints = [preferred_blocks[0], live_block_count[0], last_block_rows[0, 0], last_block_rows[0, 1], group, core]
     ints = jnp.stack(ints).astype(jnp.int32)
@@ -476,20 +479,21 @@
     a_turned = factor_in.T
     modded, low, low_split = prepare(ints, tokens, mod, a_turned)
 
-    near = after(near, [modded, low, low_split, x_own, t_own])
-    own = around(near, n_z).reshape(width, 2 * half)
-    other = lax.ppermute(own, "c", SWAP)
-
-    pol_own, ref_own, slope_own = activate(False, ints, modded, low, own, factor_out)
-    pol_other, ref_other, slope_other = activate(True, ints, modded, low, other, factor_out)
-    part_pol = lower(pol_own, pol_other, own, other).reshape(CAP, BLK, width)
+    near_up = after(near_up, [modded, low, low_split, x_own, t_own])
+    up_own = around(near_up, n_z).reshape(width, half)
+    up_other = lax.ppermute(up_own, "c", SWAP)
+    down_other = lax.ppermute(down_own, "c", SWAP)
+
+    pol_own, ref_own, slope_own = activate(False, ints, modded, low, up_own, factor_out)
+    pol_other, ref_other, slope_other = activate(True, ints, modded, low, up_other, factor_out)
+    part_pol = lower(pol_own, pol_other, down_own, down_other).reshape(CAP, BLK, width)
     got_pol = lax.all_to_all(part_pol, "t", 0, 0, tiled=True)
-    part_ref = lower(ref_own, ref_other, own, other).reshape(CAP, BLK, width)
+    part_ref = lower(ref_own, ref_other, down_own, down_other).reshape(CAP, BLK, width)
 
     unit, send = miss(ints, got_pol, part_ref, x_own, t_own, mod)
     got_dy = lax.all_to_all(send, "t", 0, 0, tiled=True)
     d_own, d_other, dlow_part, send = backward(
-        ints, got_dy, unit, x_own, t_own, mod, own, other, factor_out, slope_own, slope_other
+        ints, got_dy, unit, x_own, t_own, mod, down_own, down_other, factor_out, slope_own, slope_other
     )
     got_low = lax.all_to_all(send, "t", 0, 0, tiled=True)
     b_own, b_other = factor_terms(low_split, d_own, d_other)
@@ -499,22 +503,22 @@
 
     chips = n_z * n_x
     pieces = lax.all_to_all(pile.reshape(chips, 2 * rank // chips, half), CHIPS, 0, 0, tiled=True)
-    dm_part = dm_terms(pile, d_own, d_other, dlow_part, own, other, a_turned).reshape(CAP, BLK, width)
+    dm_part = dm_terms(pile, d_own, d_other, dlow_part, up_own, up_other, a_turned).reshape(CAP, BLK, width)
     turns = [[(i, (i + step) % n_t) for i in range(n_t)] for step in range(n_t)]
     chunks = [lax.dynamic_index_in_dim(dm_part, (group + step) % n_t, 0, False) for step in range(n_t)]
     chunks = [chunks[0]] + [lax.ppermute(chunks[step], "t", turns[step]) for step in range(1, n_t)]
     total = (jnp.sum(pieces.astype(F32), axis=0) / n_dp).astype(BF16)
     total = after(total, chunks[1:])
     mine = spread(total, CHIPS, chips).reshape(2 * rank, half)
+    grad_block = token_gradient(ints, chunks, x_own, mod, unit, facts)
+    grad_tokens = lax.all_gather(grad_block, "t", axis=0, tiled=True)
+    mine = after(mine, [grad_tokens])
     theirs = lax.ppermute(mine, "c", SWAP)
     ends = jnp.concatenate([mine, theirs], 1)
     flipped = jnp.concatenate([theirs, mine], 1)
     ends = jnp.where(core == 0, ends, flipped).astype(F32)
     sum_b = ends[:rank]
     sum_a = ends[rank:].T
-
-    grad_block = token_gradient(ints, chunks, x_own, mod, unit, facts)
-    grad_tokens = lax.all_gather(grad_block, "t", axis=0, tiled=True)
     return losses, grad_tokens, sum_a, sum_b
 
 

time: 284 us -> 279 us (0.982)
  waiting for transfers between devices: 61.4 us -> 22.9 us
  blocking collectives: 35 us -> 52.8 us
  between operations: 2.76 us -> 16.5 us
  starting transfers between devices: 123 us -> 115 us
  local copies, waits for them, and re-layouts: 36.1 us -> 43.6 us
    ppermute x8, waiting for transfers between devices: 29.3 us -> 7.27 us  [around(): left = lax.ppermute(left, 'z', up)]
    all_to_all x0 -> x1, blocking collectives: none -> 17.3 us  [per_device(): near = lax.all_to_all(sent, ('x', 'c'), 0, 0, tiled=True)]
    all_to_all x1, waiting for transfers between devices: 12.2 us -> 0.01 us  [spread(): lax.all_to_all(jnp.broadcast_to(value[None], (n, *value.shape)), axes, 0,...]
    all_to_all x1 -> x0, starting transfers between devices: 10.2 us -> none  [per_device(): lax.all_to_all(sent, ('x', 'c'), 0, 0, tiled=True)]
    dynamic_update_slice x8, local copies, waits for them, and re-layouts: 0.21 us -> 5.41 us  [around(): found = lax.dynamic_update_index_in_dim(found, left, (here - step) % n, 0)]
    dynamic_update_slice x7, local copies, waits for them, and re-layouts: 0.19 us -> 4.68 us  [around(): found = lax.dynamic_update_index_in_dim(found, right, (here + step) % n, 0)]
    ppermute x1 -> x2, waiting for transfers between devices: 4.09 us -> 0.01 us  [the longest x1 0.01 us: per_device(): down_other = lax.ppermute(down_own, 'c', SWAP)]
    unnamed x72 -> x106, local copies, waits for them, and re-layouts: 23.8 us -> 19.7 us
  transfers between devices with their start and end apart: 26 -> 27, of which waited for: 16 -> 12; matrix products, arithmetic and copies ran while one was open for 3% -> 7% of each run, Pallas kernels for 4% -> 6%
where the time goes in v11:
time: 279 us; the launch traced here: 277 us
  starting transfers between devices  115 us (41%)
  blocking collectives  52.8 us (19%)
  local copies, waits for them, and re-layouts  43.6 us (16%)
  Pallas kernels  24.1 us (9%)
  waiting for transfers between devices  22.9 us (8%)
  between operations  16.5 us (6%)
    ppermute x7, starting transfers between devices, around(): right = lax.ppermute(right, 'z', down)  34.6 us
    all_to_all x1, blocking collectives, per_device(): got_dy = lax.all_to_all(send, 't', 0, 0, tiled=True)  21.6 us
    unnamed x106, local copies, waits for them, and re-layouts  19.7 us
    ppermute x8, starting transfers between devices, around(): left = lax.ppermute(left, 'z', up)  17.8 us
    all_to_all x1, blocking collectives, per_device(): near = lax.all_to_all(sent, ('x', 'c'), 0, 0, tiled=True)  17.3 us
    all_to_all x1, starting transfers between devices, spread(): lax.all_to_all(jnp.broadcast_to(value[None], (n, *value.shape)), axes, 0,...  14.2 us
    all_gather x1, blocking collectives, per_device(): grad_tokens = lax.all_gather(grad_block, 't', axis=0, tiled=True)  13.9 us
    all_to_all x1, starting transfers between devices, per_device(): lax.all_to_all(pile.reshape(chips, 2 * rank // chips, half), CHIPS, 0, 0,...  10 us
  transfers between devices with their start and end apart: 27, of which 12 were waited for; matrix products, arithmetic and copies ran while one was open for 7% of the time, Pallas kernels for 6%

profile of v11, /device:TPU:1, one launch (start us, length us, event | category | flops | bytes accessed | tf_op | source)
XLA Modules:
  0.0 277.4 jit_solution(9983458080682212892)
XLA Ops:
  9.3 17.3 %all_to_all.30 = bf16[8,12,1536]{2,1,0:T(8,128)(2,1)S(1)} all-to-all(bf16[8,12,1536]{2,1,0:T(8,128)(2,1)S(1)} %bitcast.59), channel_id=1, replica_groups=mesh['z'=16,'x'=4,'c'=2,'t'=4] {'x','c'}, dimensions={0} | all-to-all | bytes 589824 | tf_op jit(solution)/shard_map/all_to_all | solution.py:469
  35.9 2.0 collective-permute-start
  37.9 7.5 %collective-permute-start.1 = (bf16[96,768]{1,0:T(8,128)(2,1)}, bf16[96,768]{1,0:T(8,128)(2,1)S(1)}, u32[]{:S(2)}, u32[]{:S(2)}) collective-permute-start(bf16[96,768]{1,0:T(8,128)(2,1)} %shard_map.130), channel_id=1, source_target_pairs={{0,480},{32,0},{64,32},{96,64},{128,96},{160,128},{192,160},{224,1... | collective-permute-start | bytes 442376 | tf_op jit(solution)/shard_map/ppermute | solution.py:63
  49.8 4.6 %collective-permute-start.3 = (bf16[96,768]{1,0:T(8,128)(2,1)S(1)}, bf16[96,768]{1,0:T(8,128)(2,1)S(1)}, u32[]{:S(2)}, u32[]{:S(2)}) collective-permute-start(bf16[96,768]{1,0:T(8,128)(2,1)S(1)} %collective-permute-done.1), channel_id=1, source_target_pairs={{0,480},{32,0},{64,32},{96,64},{128,96},{160,128},{192,160},{224,1... | collective-permute-start | bytes 442376 | tf_op jit(solution)/shard_map/ppermute | solution.py:63
  56.9 2.7 collective-permute-start.4
  59.7 3.8 %collective-permute-start.5 = (bf16[96,768]{1,0:T(8,128)(2,1)S(1)}, bf16[96,768]{1,0:T(8,128)(2,1)S(1)}, u32[]{:S(2)}, u32[]{:S(2)}) collective-permute-start(bf16[96,768]{1,0:T(8,128)(2,1)S(1)} %collective-permute-done.3), channel_id=1, source_target_pairs={{0,480},{32,0},{64,32},{96,64},{128,96},{160,128},{192,160},{224,1... | collective-permute-start | bytes 442376 | tf_op jit(solution)/shard_map/ppermute | solution.py:63
  65.5 2.5 collective-permute-start.6
  68.0 4.0 %collective-permute-start.7 = (bf16[96,768]{1,0:T(8,128)(2,1)S(1)}, bf16[96,768]{1,0:T(8,128)(2,1)S(1)}, u32[]{:S(2)}, u32[]{:S(2)}) collective-permute-start(bf16[96,768]{1,0:T(8,128)(2,1)S(1)} %collective-permute-done.5), channel_id=1, source_target_pairs={{0,480},{32,0},{64,32},{96,64},{128,96},{160,128},{192,160},{224,1... | collective-permute-start | bytes 442376 | tf_op jit(solution)/shard_map/ppermute | solution.py:63
  73.9 2.5 collective-permute-start.8
  76.4 4.5 %collective-permute-start.9 = (bf16[96,768]{1,0:T(8,128)(2,1)S(1)}, bf16[96,768]{1,0:T(8,128)(2,1)S(1)}, u32[]{:S(2)}, u32[]{:S(2)}) collective-permute-start(bf16[96,768]{1,0:T(8,128)(2,1)S(1)} %collective-permute-done.7), channel_id=1, source_target_pairs={{0,480},{32,0},{64,32},{96,64},{128,96},{160,128},{192,160},{224,1... | collective-permute-start | bytes 442376 | tf_op jit(solution)/shard_map/ppermute | solution.py:63
  82.3 2.3 collective-permute-start.10
  84.7 4.8 %collective-permute-start.11 = (bf16[96,768]{1,0:T(8,128)(2,1)S(1)}, bf16[96,768]{1,0:T(8,128)(2,1)S(1)}, u32[]{:S(2)}, u32[]{:S(2)}) collective-permute-start(bf16[96,768]{1,0:T(8,128)(2,1)S(1)} %collective-permute-done.9), channel_id=1, source_target_pairs={{0,480},{32,0},{64,32},{96,64},{128,96},{160,128},{192,160},{224,1... | collective-permute-start | bytes 442376 | tf_op jit(solution)/shard_map/ppermute | solution.py:63
  93.5 5.5 %collective-permute-start.13 = (bf16[96,768]{1,0:T(8,128)(2,1)S(1)}, bf16[96,768]{1,0:T(8,128)(2,1)S(1)}, u32[]{:S(2)}, u32[]{:S(2)}) collective-permute-start(bf16[96,768]{1,0:T(8,128)(2,1)S(1)} %collective-permute-done.11), channel_id=1, source_target_pairs={{0,480},{32,0},{64,32},{96,64},{128,96},{160,128},{192,160},{224,1... | collective-permute-start | bytes 442376 | tf_op jit(solution)/shard_map/ppermute | solution.py:63
  103.7 4.0 %collective-permute-done.14 = bf16[96,768]{1,0:T(8,128)(2,1)S(1)} collective-permute-done((bf16[96,768]{1,0:T(8,128)(2,1)S(1)}, bf16[96,768]{1,0:T(8,128)(2,1)S(1)}, u32[]{:S(2)}, u32[]{:S(2)}) %collective-permute-start.14) | collective-permute-done | bytes 147488 | tf_op jit(solution)/shard_map/ppermute | solution.py:60
  108.3 9.4 %collective-permute-start.15 = (bf16[1536,768]{1,0:T(8,128)(2,1)}, bf16[1536,768]{1,0:T(8,128)(2,1)}, u32[]{:S(2)}, u32[]{:S(2)}) collective-permute-start(bf16[1536,768]{1,0:T(8,128)(2,1)} %bitcast.23.up_ref.own_ref), channel_id=1, source_target_pairs={{0,4},{4,0},{1,5},{5,1},{2,6},{6,2},{3,7},{7,3},{8,12},{12,8},{9,1... | collective-permute-start | bytes 7077896 | tf_op jit(solution)/shard_map/ppermute | solution.py:484
  119.8 3.6 %shard_map.131 = (bf16[256,768]{1,0:T(8,128)(2,1)S(1)}, bf16[256,768]{1,0:T(8,128)(2,1)S(1)}, bf16[256,768]{1,0:T(8,128)(2,1)S(1)}) custom-call(s32[6]{0:T(128)S(1)} %stack.14.wins_ref.ints_ref, bf16[256,1536]{1,0:T(8,128)(2,1)S(1)} %copy-done.5, bf16[256,64]{1,0:T(8,128)(2,1)S(1)} %copy-done.34, bf16[1536,768]{1,0:T(8,128)(2,1)} %bitcast.23.up_ref.own_ref, ...), custom_call_target="tpu_custom_call" | custom-call | flops 603979776 | bytes 4325376 | tf_op jit(solution)/shard_map/pallas_call | solution.py:169
  124.9 3.7 %shard_map.132 = (bf16[256,768]{1,0:T(8,128)(2,1)S(1)}, bf16[256,768]{1,0:T(8,128)(2,1)S(1)}, bf16[256,768]{1,0:T(8,128)(2,1)S(1)}) custom-call(s32[6]{0:T(128)S(1)} %stack.14.wins_ref.ints_ref, bf16[256,1536]{1,0:T(8,128)(2,1)S(1)} %copy-done.5, bf16[256,64]{1,0:T(8,128)(2,1)S(1)} %copy-done.34, bf16[1536,768]{1,0:T(8,128)(2,1)} %collective-permute-done.15.up_ref.other_ref, ...), custom_call_target="tpu_custom_call" | custom-call | flops 603979776 | bytes 4325376 | tf_op jit(solution)/shard_map/pallas_call | solution.py:169
  131.5 4.2 %all-to-all-start.1 = ((bf16[4,64,1536]{2,1,0:T(8,128)(2,1)}), bf16[4,64,1536]{2,1,0:T(8,128)(2,1)}, u32[]{:S(2)}, u32[]{:S(2)}) async-start(bf16[4,64,1536]{2,1,0:T(8,128)(2,1)} %bitcast.56), calls=%async_computation.1 | async-start | bytes 1572864 | tf_op jit(solution)/shard_map/all_to_all | solution.py:490
  142.1 5.5 %all-to-all-done.1.got_ref = bf16[4,64,1536]{2,1,0:T(8,128)(2,1)} async-done(((bf16[4,64,1536]{2,1,0:T(8,128)(2,1)}), bf16[4,64,1536]{2,1,0:T(8,128)(2,1)}, u32[]{:S(2)}, u32[]{:S(2)}) %all-to-all-start.1) | async-done | bytes 786464 | tf_op jit(solution)/shard_map/all_to_all | solution.py:490
  151.1 21.6 %all_to_all.31.got_ref = bf16[4,128,1536]{2,1,0:T(8,128)(2,1)S(1)} all-to-all(bf16[4,128,1536]{2,1,0:T(8,128)(2,1)S(1)} %get-tuple-element.31), channel_id=1, replica_groups=mesh['z'=16,'x'=4,'c'=2,'t'=4] {'t'}, dimensions={0} | all-to-all | bytes 3145728 | tf_op jit(solution)/shard_map/all_to_all | solution.py:494
  172.6 3.8 %shard_map.136 = (bf16[256,768]{1,0:T(8,128)(2,1)S(1)}, bf16[256,768]{1,0:T(8,128)(2,1)S(1)}, bf16[256,64]{1,0:T(8,128)(2,1)S(1)}, bf16[4,80,256]{2,1,0:T(8,128)(2,1)S(1)}) custom-call(s32[6]{0:T(128)S(1)} %stack.14.wins_ref.ints_ref, bf16[4,128,1536]{2,1,0:T(8,128)(2,1)S(1)} %all_to_all.31.got_ref, f32[64,1536]{1,0:T(8,128)S(1)} %get-tuple-element.32.unit_ref, ...), custom_call_target="tpu_custom_call" | custom-call | flops 1207959552 | bytes 7077888 | tf_op jit(solution)/shard_map/pallas_call | solution.py:299
  179.2 3.5 %all-to-all-start.3 = ((bf16[4,80,256]{2,1,0:T(8,128)(2,1)}), bf16[4,80,256]{2,1,0:T(8,128)(2,1)S(1)}, u32[]{:S(2)}, u32[]{:S(2)}) async-start(bf16[4,80,256]{2,1,0:T(8,128)(2,1)} %copy-done.45), calls=%async_computation.3 | async-start | bytes 327680 | tf_op jit(solution)/shard_map/all_to_all | solution.py:498
  188.5 5.6 %collective-permute-start.17 = (bf16[128,768]{1,0:T(8,128)(2,1)S(1)}, bf16[128,768]{1,0:T(8,128)(2,1)S(1)}, u32[]{:S(2)}, u32[]{:S(2)}) collective-permute-start(bf16[128,768]{1,0:T(8,128)(2,1)S(1)} %get-tuple-element.42), channel_id=1, source_target_pairs={{0,4},{4,0},{1,5},{5,1},{2,6},{6,2},{3,7},{7,3},{8,12},{12,8},{9,1... | collective-permute-start | bytes 589832 | tf_op jit(solution)/shard_map/ppermute | solution.py:502
  195.9 10.0 %all-to-all-start.4 = ((bf16[64,2,768]{2,1,0:T(2,128)(2,1)}), bf16[64,2,768]{2,1,0:T(2,128)(2,1)S(1)}, u32[]{:S(2)}, u32[]{:S(2)}) async-start(bf16[64,2,768]{2,1,0:T(2,128)(2,1)} %reshape.52), calls=%async_computation.4 | async-start | bytes 393216 | tf_op jit(solution)/shard_map/all_to_all | solution.py:505
  206.1 4.1 %shard_map.139 = bf16[256,1536]{1,0:T(8,128)(2,1)S(1)} custom-call(bf16[128,768]{1,0:T(8,128)(2,1)S(1)} %add_convert_fusion.after_ref, bf16[256,768]{1,0:T(8,128)(2,1)S(1)} %copy-done.17, bf16[256,768]{1,0:T(8,128)(2,1)S(1)} %copy-done.20, bf16[256,64]{1,0:T(8,128)(2,1)S(1)} %copy-done.47, bf16[1536,768]{1,0:T(8,128)(2,1)} %bitcast.23.up_ref.own_ref, ...), custom_call_target="tpu_custom_call" | custom-call | flops 1207959552 | bytes 5505024 | tf_op jit(solution)/shard_map/pallas_call | solution.py:402
  210.3 2.3 collective-permute-start.18
  212.6 3.7 %collective-permute-start.19 = (bf16[64,1536]{1,0:T(8,128)(2,1)S(1)}, bf16[64,1536]{1,0:T(8,128)(2,1)S(1)}, u32[]{:S(2)}, u32[]{:S(2)}) collective-permute-start(bf16[64,1536]{1,0:T(8,128)(2,1)S(1)} %get-tuple-element.47), channel_id=1, source_target_pairs={{0,2},{1,3},{2,0},{3,1},{4,6},{5,7},{6,4},{7,5},{8,10},{9,11},{10,... | collective-permute-start | bytes 589832 | tf_op jit(solution)/shard_map/ppermute | solution.py:509
  216.3 2.5 collective-permute-start.20
  218.9 4.7 %all-to-all-done.4 = bf16[64,2,768]{2,1,0:T(2,128)(2,1)S(1)} async-done(((bf16[64,2,768]{2,1,0:T(2,128)(2,1)}), bf16[64,2,768]{2,1,0:T(2,128)(2,1)S(1)}, u32[]{:S(2)}, u32[]{:S(2)}) %all-to-all-start.4) | async-done | bytes 196640 | tf_op jit(solution)/shard_map/all_to_all | solution.py:505
  228.1 14.2 %all-to-all-start.5 = ((bf16[64,2,768]{2,1,0:T(2,128)(2,1)}), bf16[64,2,768]{2,1,0:T(2,128)(2,1)S(1)}, u32[]{:S(2)}, u32[]{:S(2)}) async-start(bf16[64,2,768]{2,1,0:T(2,128)(2,1)} %broadcast_in_dim.82), calls=%async_computation.5 | async-start | bytes 393216 | tf_op jit(solution)/shard_map/all_to_all | solution.py:50
  246.1 13.9 %all_gather.7.refs_1_ = bf16[256,1536]{1,0:T(8,128)(2,1)} all-gather(bf16[64,1536]{1,0:T(8,128)(2,1)S(1)} %shard_map.140), channel_id=1, replica_groups=mesh['z'=16,'x'=4,'c'=2,'t'=4] {'t'}, dimensions={0}, use_global_device_ids=true | all-gather | bytes 983040 | tf_op jit(solution)/shard_map/all_gather | solution.py:514
  260.8 5.6 %collective-permute-start.21 = (bf16[128,768]{1,0:T(8,128)(2,1)}, bf16[128,768]{1,0:T(8,128)(2,1)S(1)}, u32[]{:S(2)}, u32[]{:S(2)}) collective-permute-start(bf16[128,768]{1,0:T(8,128)(2,1)} %shard_map.142), channel_id=1, source_target_pairs={{0,4},{4,0},{1,5},{5,1},{2,6},{6,2},{3,7},{7,3},{8,12},{12,8},{9,1... | collective-permute-start | bytes 589832 | tf_op jit(solution)/shard_map/ppermute | solution.py:516
  (186 shorter events, 70.9 us)
Async XLA Ops:
  7.2 110.6 %all-gather.2.cloned.1.call-start = ((), (), s32[]{:S(2)}) async-start(), calls=%async_computation.6 | async-start | bytes 2506752 | tf_op jit(solution)/shard_map/all_gather | solution.py:472
  35.9 11.9 %collective-permute-start = (bf16[96,768]{1,0:T(8,128)(2,1)}, bf16[96,768]{1,0:T(8,128)(2,1)S(1)}, u32[]{:S(2)}, u32[]{:S(2)}) collective-permute-start(bf16[96,768]{1,0:T(8,128)(2,1)} %shard_map.130), channel_id=1, source_target_pairs={{0,32},{32,64},{64,96},{96,128},{128,160},{160,192},{192,224},{224... | collective-permute-start | bytes 442376 | tf_op jit(solution)/shard_map/ppermute | solution.py:60
  37.9 11.8 %collective-permute-start.1 = (bf16[96,768]{1,0:T(8,128)(2,1)}, bf16[96,768]{1,0:T(8,128)(2,1)S(1)}, u32[]{:S(2)}, u32[]{:S(2)}) collective-permute-start(bf16[96,768]{1,0:T(8,128)(2,1)} %shard_map.130), channel_id=1, source_target_pairs={{0,480},{32,0},{64,32},{96,64},{128,96},{160,128},{192,160},{224,1... | collective-permute-start | bytes 442376 | tf_op jit(solution)/shard_map/ppermute | solution.py:63
  47.1 72.6 %copy-start.5 = (bf16[256,1536]{1,0:T(8,128)(2,1)S(1)}, bf16[256,1536]{1,0:T(8,128)(2,1)}, u32[]{:S(2)}) copy-start(bf16[256,1536]{1,0:T(8,128)(2,1)} %copy-done.4) | copy-start | bytes 2359300
  47.1 72.6 %copy-start.11 = (bf16[64,1536]{1,0:T(8,128)(2,1)S(1)}, bf16[64,1536]{1,0:T(8,128)(2,1)}, u32[]{:S(2)}) copy-start(bf16[64,1536]{1,0:T(8,128)(2,1)} %b_ref.5) | copy-start | bytes 589828
  47.1 72.6 %copy-start.34 = (bf16[256,64]{1,0:T(8,128)(2,1)S(1)}, bf16[256,64]{1,0:T(8,128)(2,1)}, u32[]{:S(2)}) copy-start(bf16[256,64]{1,0:T(8,128)(2,1)} %copy-done.33) | copy-start | bytes 98308
  47.8 9.1 %collective-permute-start.2 = (bf16[96,768]{1,0:T(8,128)(2,1)S(1)}, bf16[96,768]{1,0:T(8,128)(2,1)S(1)}, u32[]{:S(2)}, u32[]{:S(2)}) collective-permute-start(bf16[96,768]{1,0:T(8,128)(2,1)S(1)} %collective-permute-done), channel_id=1, source_target_pairs={{0,32},{32,64},{64,96},{96,128},{128,160},{160,192},{192,224},{224... | collective-permute-start | bytes 442376 | tf_op jit(solution)/shard_map/ppermute | solution.py:60
  49.8 9.9 %collective-permute-start.3 = (bf16[96,768]{1,0:T(8,128)(2,1)S(1)}, bf16[96,768]{1,0:T(8,128)(2,1)S(1)}, u32[]{:S(2)}, u32[]{:S(2)}) collective-permute-start(bf16[96,768]{1,0:T(8,128)(2,1)S(1)} %collective-permute-done.1), channel_id=1, source_target_pairs={{0,480},{32,0},{64,32},{96,64},{128,96},{160,128},{192,160},{224,1... | collective-permute-start | bytes 442376 | tf_op jit(solution)/shard_map/ppermute | solution.py:63
  56.9 8.6 %collective-permute-start.4 = (bf16[96,768]{1,0:T(8,128)(2,1)S(1)}, bf16[96,768]{1,0:T(8,128)(2,1)S(1)}, u32[]{:S(2)}, u32[]{:S(2)}) collective-permute-start(bf16[96,768]{1,0:T(8,128)(2,1)S(1)} %collective-permute-done.2), channel_id=1, source_target_pairs={{0,32},{32,64},{64,96},{96,128},{128,160},{160,192},{192,224},{224... | collective-permute-start | bytes 442376 | tf_op jit(solution)/shard_map/ppermute | solution.py:60
  59.7 8.3 %collective-permute-start.5 = (bf16[96,768]{1,0:T(8,128)(2,1)S(1)}, bf16[96,768]{1,0:T(8,128)(2,1)S(1)}, u32[]{:S(2)}, u32[]{:S(2)}) collective-permute-start(bf16[96,768]{1,0:T(8,128)(2,1)S(1)} %collective-permute-done.3), channel_id=1, source_target_pairs={{0,480},{32,0},{64,32},{96,64},{128,96},{160,128},{192,160},{224,1... | collective-permute-start | bytes 442376 | tf_op jit(solution)/shard_map/ppermute | solution.py:63
  65.5 8.4 %collective-permute-start.6 = (bf16[96,768]{1,0:T(8,128)(2,1)S(1)}, bf16[96,768]{1,0:T(8,128)(2,1)S(1)}, u32[]{:S(2)}, u32[]{:S(2)}) collective-permute-start(bf16[96,768]{1,0:T(8,128)(2,1)S(1)} %collective-permute-done.4), channel_id=1, source_target_pairs={{0,32},{32,64},{64,96},{96,128},{128,160},{160,192},{192,224},{224... | collective-permute-start | bytes 442376 | tf_op jit(solution)/shard_map/ppermute | solution.py:60
  68.0 8.4 %collective-permute-start.7 = (bf16[96,768]{1,0:T(8,128)(2,1)S(1)}, bf16[96,768]{1,0:T(8,128)(2,1)S(1)}, u32[]{:S(2)}, u32[]{:S(2)}) collective-permute-start(bf16[96,768]{1,0:T(8,128)(2,1)S(1)} %collective-permute-done.5), channel_id=1, source_target_pairs={{0,480},{32,0},{64,32},{96,64},{128,96},{160,128},{192,160},{224,1... | collective-permute-start | bytes 442376 | tf_op jit(solution)/shard_map/ppermute | solution.py:63
  73.9 8.4 %collective-permute-start.8 = (bf16[96,768]{1,0:T(8,128)(2,1)S(1)}, bf16[96,768]{1,0:T(8,128)(2,1)S(1)}, u32[]{:S(2)}, u32[]{:S(2)}) collective-permute-start(bf16[96,768]{1,0:T(8,128)(2,1)S(1)} %collective-permute-done.6), channel_id=1, source_target_pairs={{0,32},{32,64},{64,96},{96,128},{128,160},{160,192},{192,224},{224... | collective-permute-start | bytes 442376 | tf_op jit(solution)/shard_map/ppermute | solution.py:60
  76.4 8.2 %collective-permute-start.9 = (bf16[96,768]{1,0:T(8,128)(2,1)S(1)}, bf16[96,768]{1,0:T(8,128)(2,1)S(1)}, u32[]{:S(2)}, u32[]{:S(2)}) collective-permute-start(bf16[96,768]{1,0:T(8,128)(2,1)S(1)} %collective-permute-done.7), channel_id=1, source_target_pairs={{0,480},{32,0},{64,32},{96,64},{128,96},{160,128},{192,160},{224,1... | collective-permute-start | bytes 442376 | tf_op jit(solution)/shard_map/ppermute | solution.py:63
  82.3 9.2 %collective-permute-start.10 = (bf16[96,768]{1,0:T(8,128)(2,1)S(1)}, bf16[96,768]{1,0:T(8,128)(2,1)S(1)}, u32[]{:S(2)}, u32[]{:S(2)}) collective-permute-start(bf16[96,768]{1,0:T(8,128)(2,1)S(1)} %collective-permute-done.8), channel_id=1, source_target_pairs={{0,32},{32,64},{64,96},{96,128},{128,160},{160,192},{192,224},{224... | collective-permute-start | bytes 442376 | tf_op jit(solution)/shard_map/ppermute | solution.py:60
  84.7 8.8 %collective-permute-start.11 = (bf16[96,768]{1,0:T(8,128)(2,1)S(1)}, bf16[96,768]{1,0:T(8,128)(2,1)S(1)}, u32[]{:S(2)}, u32[]{:S(2)}) collective-permute-start(bf16[96,768]{1,0:T(8,128)(2,1)S(1)} %collective-permute-done.9), channel_id=1, source_target_pairs={{0,480},{32,0},{64,32},{96,64},{128,96},{160,128},{192,160},{224,1... | collective-permute-start | bytes 442376 | tf_op jit(solution)/shard_map/ppermute | solution.py:63
  91.5 8.9 %collective-permute-start.12 = (bf16[96,768]{1,0:T(8,128)(2,1)S(1)}, bf16[96,768]{1,0:T(8,128)(2,1)S(1)}, u32[]{:S(2)}, u32[]{:S(2)}) collective-permute-start(bf16[96,768]{1,0:T(8,128)(2,1)S(1)} %collective-permute-done.10), channel_id=1, source_target_pairs={{0,32},{32,64},{64,96},{96,128},{128,160},{160,192},{192,224},{224... | collective-permute-start | bytes 442376 | tf_op jit(solution)/shard_map/ppermute | solution.py:60
  93.5 9.5 %collective-permute-start.13 = (bf16[96,768]{1,0:T(8,128)(2,1)S(1)}, bf16[96,768]{1,0:T(8,128)(2,1)S(1)}, u32[]{:S(2)}, u32[]{:S(2)}) collective-permute-start(bf16[96,768]{1,0:T(8,128)(2,1)S(1)} %collective-permute-done.11), channel_id=1, source_target_pairs={{0,480},{32,0},{64,32},{96,64},{128,96},{160,128},{192,160},{224,1... | collective-permute-start | bytes 442376 | tf_op jit(solution)/shard_map/ppermute | solution.py:63
  100.4 7.3 %collective-permute-start.14 = (bf16[96,768]{1,0:T(8,128)(2,1)S(1)}, bf16[96,768]{1,0:T(8,128)(2,1)S(1)}, u32[]{:S(2)}, u32[]{:S(2)}) collective-permute-start(bf16[96,768]{1,0:T(8,128)(2,1)S(1)} %collective-permute-done.12), channel_id=1, source_target_pairs={{0,32},{32,64},{64,96},{96,128},{128,160},{160,192},{192,224},{224... | collective-permute-start | bytes 442376 | tf_op jit(solution)/shard_map/ppermute | solution.py:60
  108.3 16.5 %collective-permute-start.15 = (bf16[1536,768]{1,0:T(8,128)(2,1)}, bf16[1536,768]{1,0:T(8,128)(2,1)}, u32[]{:S(2)}, u32[]{:S(2)}) collective-permute-start(bf16[1536,768]{1,0:T(8,128)(2,1)} %bitcast.23.up_ref.own_ref), channel_id=1, source_target_pairs={{0,4},{4,0},{1,5},{5,1},{2,6},{6,2},{3,7},{7,3},{8,12},{12,8},{9,1... | collective-permute-start | bytes 7077896 | tf_op jit(solution)/shard_map/ppermute | solution.py:484
  117.8 10.8 %collective-permute-start.16 = (bf16[1536,768]{1,0:T(8,128)(2,1)}, bf16[1536,768]{1,0:T(8,128)(2,1)S(1)}, u32[]{:S(2)}, u32[]{:S(2)}) collective-permute-start(bf16[1536,768]{1,0:T(8,128)(2,1)} %all-gather.2.cloned.1.call-done.own_ref), channel_id=1, source_target_pairs={{0,4},{4,0},{1,5},{5,1},{2,6},{6,2},{3,7},{7,3},{8,12},{12,8},{9,1... | collective-permute-start | bytes 7077896 | tf_op jit(solution)/shard_map/ppermute | solution.py:485
  131.5 16.2 %all-to-all-start.1 = ((bf16[4,64,1536]{2,1,0:T(8,128)(2,1)}), bf16[4,64,1536]{2,1,0:T(8,128)(2,1)}, u32[]{:S(2)}, u32[]{:S(2)}) async-start(bf16[4,64,1536]{2,1,0:T(8,128)(2,1)} %bitcast.56), calls=%async_computation.1 | async-start | bytes 1572864 | tf_op jit(solution)/shard_map/all_to_all | solution.py:490
  179.2 8.5 %all-to-all-start.3 = ((bf16[4,80,256]{2,1,0:T(8,128)(2,1)}), bf16[4,80,256]{2,1,0:T(8,128)(2,1)S(1)}, u32[]{:S(2)}, u32[]{:S(2)}) async-start(bf16[4,80,256]{2,1,0:T(8,128)(2,1)} %copy-done.45), calls=%async_computation.3 | async-start | bytes 327680 | tf_op jit(solution)/shard_map/all_to_all | solution.py:498
  188.5 6.7 %collective-permute-start.17 = (bf16[128,768]{1,0:T(8,128)(2,1)S(1)}, bf16[128,768]{1,0:T(8,128)(2,1)S(1)}, u32[]{:S(2)}, u32[]{:S(2)}) collective-permute-start(bf16[128,768]{1,0:T(8,128)(2,1)S(1)} %get-tuple-element.42), channel_id=1, source_target_pairs={{0,4},{4,0},{1,5},{5,1},{2,6},{6,2},{3,7},{7,3},{8,12},{12,8},{9,1... | collective-permute-start | bytes 589832 | tf_op jit(solution)/shard_map/ppermute | solution.py:502
  195.9 27.6 %all-to-all-start.4 = ((bf16[64,2,768]{2,1,0:T(2,128)(2,1)}), bf16[64,2,768]{2,1,0:T(2,128)(2,1)S(1)}, u32[]{:S(2)}, u32[]{:S(2)}) async-start(bf16[64,2,768]{2,1,0:T(2,128)(2,1)} %reshape.52), calls=%async_computation.4 | async-start | bytes 393216 | tf_op jit(solution)/shard_map/all_to_all | solution.py:505
  210.2 32.1 %copy-start.14 = (f32[64,1536]{1,0:T(8,128)S(1)}, f32[64,1536]{1,0:T(8,128)}, u32[]{:S(2)}) copy-start(f32[64,1536]{1,0:T(8,128)} %copy-done.13) | copy-start | bytes 1179652
  210.2 32.1 %copy-start.32 = (bf16[6,1536]{1,0:T(8,128)(2,1)S(1)}, bf16[6,1536]{1,0:T(8,128)(2,1)}, u32[]{:S(2)}) copy-start(bf16[6,1536]{1,0:T(8,128)(2,1)} %copy-done.30) | copy-start | bytes 55300
  210.3 14.0 %collective-permute-start.18 = (bf16[64,1536]{1,0:T(8,128)(2,1)S(1)}, bf16[64,1536]{1,0:T(8,128)(2,1)S(1)}, u32[]{:S(2)}, u32[]{:S(2)}) collective-permute-start(bf16[64,1536]{1,0:T(8,128)(2,1)S(1)} %get-tuple-element.48), channel_id=1, source_target_pairs={{0,1},{1,2},{2,3},{3,0},{4,5},{5,6},{6,7},{7,4},{8,9},{9,10},{10,1... | collective-permute-start | bytes 589832 | tf_op jit(solution)/shard_map/ppermute | solution.py:509
  212.6 11.7 %collective-permute-start.19 = (bf16[64,1536]{1,0:T(8,128)(2,1)S(1)}, bf16[64,1536]{1,0:T(8,128)(2,1)S(1)}, u32[]{:S(2)}, u32[]{:S(2)}) collective-permute-start(bf16[64,1536]{1,0:T(8,128)(2,1)S(1)} %get-tuple-element.47), channel_id=1, source_target_pairs={{0,2},{1,3},{2,0},{3,1},{4,6},{5,7},{6,4},{7,5},{8,10},{9,11},{10,... | collective-permute-start | bytes 589832 | tf_op jit(solution)/shard_map/ppermute | solution.py:509
  216.3 9.6 %collective-permute-start.20 = (bf16[64,1536]{1,0:T(8,128)(2,1)S(1)}, bf16[64,1536]{1,0:T(8,128)(2,1)S(1)}, u32[]{:S(2)}, u32[]{:S(2)}) collective-permute-start(bf16[64,1536]{1,0:T(8,128)(2,1)S(1)} %get-tuple-element.46), channel_id=1, source_target_pairs={{0,3},{1,0},{2,1},{3,2},{4,7},{5,4},{6,5},{7,6},{8,11},{9,8},{10,9... | collective-permute-start | bytes 589832 | tf_op jit(solution)/shard_map/ppermute | solution.py:509
  228.1 31.9 %all-to-all-start.5 = ((bf16[64,2,768]{2,1,0:T(2,128)(2,1)}), bf16[64,2,768]{2,1,0:T(2,128)(2,1)S(1)}, u32[]{:S(2)}, u32[]{:S(2)}) async-start(bf16[64,2,768]{2,1,0:T(2,128)(2,1)} %broadcast_in_dim.82), calls=%async_computation.5 | async-start | bytes 393216 | tf_op jit(solution)/shard_map/all_to_all | solution.py:50
  260.8 6.8 %collective-permute-start.21 = (bf16[128,768]{1,0:T(8,128)(2,1)}, bf16[128,768]{1,0:T(8,128)(2,1)S(1)}, u32[]{:S(2)}, u32[]{:S(2)}) collective-permute-start(bf16[128,768]{1,0:T(8,128)(2,1)} %shard_map.142), channel_id=1, source_target_pairs={{0,4},{4,0},{1,5},{5,1},{2,6},{6,2},{3,7},{7,3},{8,12},{12,8},{9,1... | collective-permute-start | bytes 589832 | tf_op jit(solution)/shard_map/ppermute | solution.py:516
  (47 other events, 394.6 us)
Sparse Core Ops, SparseCore 0:
  27.5 68.0 all-gather.1

commit v12 on v10

--- a/solution.py
+++ b/solution.py
@@ -48,21 +48,6 @@
 
 def spread(value, axes, n):
     return lax.all_to_all(jnp.broadcast_to(value[None], (n, *value.shape)), axes, 0, 0, tiled=True)
-
-
-def around(block, n):
-    here = lax.axis_index("z")
-    up = [(i, (i + 1) % n) for i in range(n)]
-    down = [(i, (i - 1) % n) for i in range(n)]
-    found = lax.dynamic_update_index_in_dim(jnp.zeros((n, *block.shape), block.dtype), block, here, 0)
-    left = right = block
-    for step in range(1, n // 2 + 1):
-        left = lax.ppermute(left, "z", up)
-        found = lax.dynamic_update_index_in_dim(found, left, (here - step) % n, 0)
-        if step < n // 2:
-            right = lax.ppermute(right, "z", down)
-            found = lax.dynamic_update_index_in_dim(found, right, (here + step) % n, 0)
-    return found
 
 
 def normalise(rows):
@@ -293,7 +278,7 @@
     rank = factor.shape[0]
     rows = CAP * BLK
     step = 256
-    weight = pl.BlockSpec((width, step), lambda i: (0, half // step + i))
+    weight = pl.BlockSpec((width, step), lambda i: (0, i))
     cut = pl.BlockSpec((rows, step), lambda i: (0, i))
     block = whole((BLK, width))
     return pl.pallas_call(
@@ -467,6 +452,7 @@
     sent = sent.reshape(thin, n_c, 2 * half).transpose(1, 0, 2)
     sent = jnp.broadcast_to(sent[None], (n_x, n_c, thin, 2 * half)).reshape(n_x * n_c, thin, 2 * half)
     near = lax.all_to_all(sent, ("x", "c"), 0, 0, tiled=True).reshape(n_x * n_c * thin, 2 * half)
+    own = lax.all_gather(near, "z", axis=0, tiled=True)
 
     ints = [preferred_blocks[0], live_block_count[0], last_block_rows[0, 0], last_block_rows[0, 1], group, core]
     ints = jnp.stack(ints).astype(jnp.int32)
@@ -476,8 +462,7 @@
     a_turned = factor_in.T
     modded, low, low_split = prepare(ints, tokens, mod, a_turned)
 
-    near = after(near, [modded, low, low_split, x_own, t_own])
-    own = around(near, n_z).reshape(width, 2 * half)
+    own = after(own, [modded, low, low_split, x_own, t_own])
     other = lax.ppermute(own, "c", SWAP)
 
     pol_own, ref_own, slope_own = activate(False, ints, modded, low, own, factor_out)
@@ -487,9 +472,11 @@
     part_ref = lower(ref_own, ref_other, own, other).reshape(CAP, BLK, width)
 
     unit, send = miss(ints, got_pol, part_ref, x_own, t_own, mod)
+    down_own, down_other = own[:, half:], other[:, half:]
+    send = after(send, [down_own, down_other])
     got_dy = lax.all_to_all(send, "t", 0, 0, tiled=True)
     d_own, d_other, dlow_part, send = backward(
-        ints, got_dy, unit, x_own, t_own, mod, own, other, factor_out, slope_own, slope_other
+        ints, got_dy, unit, x_own, t_own, mod, down_own, down_other, factor_out, slope_own, slope_other
     )
     got_low = lax.all_to_all(send, "t", 0, 0, tiled=True)
     b_own, b_other = factor_terms(low_split, d_own, d_other)
@@ -506,15 +493,15 @@
     total = (jnp.sum(pieces.astype(F32), axis=0) / n_dp).astype(BF16)
     total = after(total, chunks[1:])
     mine = spread(total, CHIPS, chips).reshape(2 * rank, half)
+    grad_block = token_gradient(ints, chunks, x_own, mod, unit, facts)
+    grad_tokens = lax.all_gather(grad_block, "t", axis=0, tiled=True)
+    mine = after(mine, [grad_tokens])
     theirs = lax.ppermute(mine, "c", SWAP)
     ends = jnp.concatenate([mine, theirs], 1)
     flipped = jnp.concatenate([theirs, mine], 1)
     ends = jnp.where(core == 0, ends, flipped).astype(F32)
     sum_b = ends[:rank]
     sum_a = ends[rank:].T
-
-    grad_block = token_gradient(ints, chunks, x_own, mod, unit, facts)
-    grad_tokens = lax.all_gather(grad_block, "t", axis=0, tiled=True)
     return losses, grad_tokens, sum_a, sum_b
 
 

time: 284 us -> 276 us (0.972)
  starting transfers between devices: 123 us -> 61.9 us
  blocking collectives: 35 us -> 54.3 us
  waiting for transfers between devices: 61.4 us -> 77.1 us
  between operations: 2.76 us -> 15.9 us
  local copies, waits for them, and re-layouts: 36.1 us -> 42.4 us
    all_gather x0 -> x1, waiting for transfers between devices: none -> 62.7 us  [per_device(): own = lax.all_gather(near, 'z', axis=0, tiled=True)]
    ppermute x15 -> x0, starting transfers between devices: 49.5 us -> none  [the longest x7 34.1 us: around(): right = lax.ppermute(right, 'z', down)]
    ppermute x15 -> x0, waiting for transfers between devices: 29.3 us -> none  [the longest x8 29.3 us: around(): left = lax.ppermute(left, 'z', up)]
    all_to_all x0 -> x1, blocking collectives: none -> 17.3 us  [per_device(): lax.all_to_all(sent, ('x', 'c'), 0, 0, tiled=True)]
    all_to_all x1, waiting for transfers between devices: 12.2 us -> 0.01 us  [spread(): lax.all_to_all(jnp.broadcast_to(value[None], (n, *value.shape)), axes, 0,...]
    all_to_all x1 -> x0, starting transfers between devices: 10.2 us -> none  [per_device(): lax.all_to_all(sent, ('x', 'c'), 0, 0, tiled=True)]
    slice x0 -> x2, local copies, waits for them, and re-layouts: none -> 6.76 us  [per_device(): down_own, down_other = (own[:, half:], other[:, half:])]
    unnamed x72 -> x114, local copies, waits for them, and re-layouts: 23.8 us -> 24.8 us
  transfers between devices with their start and end apart: 26 -> 11, of which waited for: 16 -> 9; matrix products, arithmetic and copies ran while one was open for 3% -> 4% of each run, Pallas kernels for 4% -> 4%
where the time goes in v12:
time: 276 us; the launch traced here: 275 us
  waiting for transfers between devices  77.1 us (28%)
  starting transfers between devices  61.9 us (22%)
  blocking collectives  54.3 us (20%)
  local copies, waits for them, and re-layouts  42.4 us (15%)
  Pallas kernels  20.8 us (8%)
  between operations  15.9 us (6%)
    all_gather x1, waiting for transfers between devices, per_device(): own = lax.all_gather(near, 'z', axis=0, tiled=True)  62.7 us
    unnamed x114, local copies, waits for them, and re-layouts  24.8 us
    all_to_all x1, blocking collectives, per_device(): got_dy = lax.all_to_all(send, 't', 0, 0, tiled=True)  23 us
    all_to_all x1, blocking collectives, per_device(): lax.all_to_all(sent, ('x', 'c'), 0, 0, tiled=True)  17.3 us
    all_to_all x1, starting transfers between devices, spread(): lax.all_to_all(jnp.broadcast_to(value[None], (n, *value.shape)), axes, 0,...  14.2 us
    all_gather x1, blocking collectives, per_device(): grad_tokens = lax.all_gather(grad_block, 't', axis=0, tiled=True)  13.9 us
    ppermute x1, starting transfers between devices, per_device(): other = lax.ppermute(own, 'c', SWAP)  10.6 us
    all_to_all x1, starting transfers between devices, per_device(): lax.all_to_all(pile.reshape(chips, 2 * rank // chips, half), CHIPS, 0, 0,...  9.97 us
  transfers between devices with their start and end apart: 11, of which 9 were waited for; matrix products, arithmetic and copies ran while one was open for 4% of the time, Pallas kernels for 4%

profile of v12, /device:TPU:1, one launch (start us, length us, event | category | flops | bytes accessed | tf_op | source)
XLA Modules:
  0.0 274.5 jit_solution(15437367496164678892)
XLA Ops:
  9.3 17.3 %all_to_all.30 = bf16[8,12,1536]{2,1,0:T(8,128)(2,1)S(1)} all-to-all(bf16[8,12,1536]{2,1,0:T(8,128)(2,1)S(1)} %bitcast.27), channel_id=1, replica_groups=mesh['z'=16,'x'=4,'c'=2,'t'=4] {'x','c'}, dimensions={0} | all-to-all | bytes 589824 | tf_op jit(solution)/shard_map/all_to_all | solution.py:454
  34.4 1.7 constant_dynamic-slice_fusion
  36.1 62.7 %all-gather.2.cloned.1.call-done.refs_0_ = bf16[1536,1536]{1,0:T(8,128)(2,1)} async-done(((bf16[96,1536]{1,0:T(8,128)(2,1)}), bf16[1536,1536]{1,0:T(8,128)(2,1)}) %all-gather.2.cloned.1.call-update) | async-done | bytes 4718608 | tf_op jit(solution)/shard_map/all_gather | solution.py:455
  98.9 10.6 %collective-permute-start = (bf16[1536,1536]{1,0:T(8,128)(2,1)}, bf16[1536,1536]{1,0:T(8,128)(2,1)S(1)}, u32[]{:S(2)}, u32[]{:S(2)}) collective-permute-start(bf16[1536,1536]{1,0:T(8,128)(2,1)} %shard_map.130.up_ref.own_ref), channel_id=1, source_target_pairs={{0,4},{4,0},{1,5},{5,1},{2,6},{6,2},{3,7},{7,3},{8,12},{12,8},{9,1... | collective-permute-start | bytes 14155784 | tf_op jit(solution)/shard_map/ppermute | solution.py:466
  109.5 2.3 copy-done
  111.9 2.6 shard_map.131
  114.5 2.7 collective-permute-done.up_ref.other_ref
  117.2 2.6 shard_map.132
  120.6 2.9 %shard_map.133 = bf16[256,1536]{1,0:T(8,128)(2,1)} custom-call(bf16[256,768]{1,0:T(8,128)(2,1)S(1)} %get-tuple-element.27.left_ref, bf16[256,768]{1,0:T(8,128)(2,1)S(1)} %get-tuple-element.28.right_ref, bf16[1536,1536]{1,0:T(8,128)(2,1)S(1)} %copy-done.1, bf16[1536,1536]{1,0:T(8,128)(2,1)S(1)} %collective-permute-done.up_ref.other_ref), custom_call_target="tpu_custom_call" | custom-call | flops 1207959552 | bytes 5505024 | tf_op jit(solution)/shard_map/pallas_call | solution.py:185
  123.5 3.9 %all-to-all-start.1 = ((bf16[4,64,1536]{2,1,0:T(8,128)(2,1)}), bf16[4,64,1536]{2,1,0:T(8,128)(2,1)S(1)}, u32[]{:S(2)}, u32[]{:S(2)}) async-start(bf16[4,64,1536]{2,1,0:T(8,128)(2,1)} %bitcast.7), calls=%async_computation.1 | async-start | bytes 1572864 | tf_op jit(solution)/shard_map/all_to_all | solution.py:471
  127.4 3.4 %slice.28.refs_1_.own_ref = bf16[1536,768]{1,0:T(8,128)(2,1)} slice(bf16[1536,1536]{1,0:T(8,128)(2,1)} %shard_map.130.up_ref.own_ref), slice={[0:1536], [768:1536]} | slice | bytes 4718592 | tf_op jit(solution)/shard_map/slice | solution.py:475
  130.8 3.3 %slice.29.refs_2_.other_ref = bf16[1536,768]{1,0:T(8,128)(2,1)} slice(bf16[1536,1536]{1,0:T(8,128)(2,1)} %copy-done.3), slice={[0:1536], [768:1536]} | slice | bytes 4718592 | tf_op jit(solution)/shard_map/slice | solution.py:475
  135.2 2.2 shard_map.134
  137.4 1.7 all-to-all-done.1.got_ref
  141.8 23.0 %all_to_all.31.got_ref = bf16[4,128,1536]{2,1,0:T(8,128)(2,1)S(1)} all-to-all(bf16[4,128,1536]{2,1,0:T(8,128)(2,1)} %shard_map.136), channel_id=1, replica_groups=mesh['z'=16,'x'=4,'c'=2,'t'=4] {'t'}, dimensions={0} | all-to-all | bytes 3145728 | tf_op jit(solution)/shard_map/all_to_all | solution.py:477
  166.9 3.7 %shard_map.137 = (bf16[256,768]{1,0:T(8,128)(2,1)S(1)}, bf16[256,768]{1,0:T(8,128)(2,1)S(1)}, bf16[256,64]{1,0:T(8,128)(2,1)S(1)}, bf16[4,80,256]{2,1,0:T(8,128)(2,1)S(1)}) custom-call(s32[6]{0:T(128)S(1)} %stack.14.wins_ref.ints_ref, bf16[4,128,1536]{2,1,0:T(8,128)(2,1)S(1)} %all_to_all.31.got_ref, f32[64,1536]{1,0:T(8,128)S(1)} %copy-done.16, ...), custom_call_target="tpu_custom_call" | custom-call | flops 1207959552 | bytes 7077888 | tf_op jit(solution)/shard_map/pallas_call | solution.py:284
  173.4 3.5 %all-to-all-start.3 = ((bf16[4,80,256]{2,1,0:T(8,128)(2,1)}), bf16[4,80,256]{2,1,0:T(8,128)(2,1)S(1)}, u32[]{:S(2)}, u32[]{:S(2)}) async-start(bf16[4,80,256]{2,1,0:T(8,128)(2,1)} %copy-done.48), calls=%async_computation.3 | async-start | bytes 327680 | tf_op jit(solution)/shard_map/all_to_all | solution.py:481
  180.0 1.9 all-to-all-done.3.got_ref
  182.7 5.6 %collective-permute-start.1 = (bf16[128,768]{1,0:T(8,128)(2,1)S(1)}, bf16[128,768]{1,0:T(8,128)(2,1)S(1)}, u32[]{:S(2)}, u32[]{:S(2)}) collective-permute-start(bf16[128,768]{1,0:T(8,128)(2,1)S(1)} %get-tuple-element.42), channel_id=1, source_target_pairs={{0,4},{4,0},{1,5},{5,1},{2,6},{6,2},{3,7},{7,3},{8,12},{12,8},{9,1... | collective-permute-start | bytes 589832 | tf_op jit(solution)/shard_map/ppermute | solution.py:485
  190.2 10.0 %all-to-all-start.4 = ((bf16[64,2,768]{2,1,0:T(2,128)(2,1)}), bf16[64,2,768]{2,1,0:T(2,128)(2,1)S(1)}, u32[]{:S(2)}, u32[]{:S(2)}) async-start(bf16[64,2,768]{2,1,0:T(2,128)(2,1)} %reshape.44), calls=%async_computation.4 | async-start | bytes 393216 | tf_op jit(solution)/shard_map/all_to_all | solution.py:488
  200.2 2.3 copy-done.2
  202.6 2.3 copy-done.5
  204.9 2.4 shard_map.140
  207.4 2.3 collective-permute-start.2
  209.8 3.7 %collective-permute-start.3 = (bf16[64,1536]{1,0:T(8,128)(2,1)S(1)}, bf16[64,1536]{1,0:T(8,128)(2,1)S(1)}, u32[]{:S(2)}, u32[]{:S(2)}) collective-permute-start(bf16[64,1536]{1,0:T(8,128)(2,1)S(1)} %get-tuple-element.47), channel_id=1, source_target_pairs={{0,2},{1,3},{2,0},{3,1},{4,6},{5,7},{6,4},{7,5},{8,10},{9,11},{10,... | collective-permute-start | bytes 589832 | tf_op jit(solution)/shard_map/ppermute | solution.py:492
  213.5 2.5 collective-permute-start.4
  216.0 1.7 all-to-all-done.4
  218.5 1.7 collective-permute-done.3.three_ref.refs_2_
  220.2 2.9 %collective-permute-done.4.four_ref.refs_3_ = bf16[64,1536]{1,0:T(8,128)(2,1)S(1)} collective-permute-done((bf16[64,1536]{1,0:T(8,128)(2,1)S(1)}, bf16[64,1536]{1,0:T(8,128)(2,1)S(1)}, u32[]{:S(2)}, u32[]{:S(2)}) %collective-permute-start.4) | collective-permute-done | bytes 196640 | tf_op jit(solution)/shard_map/ppermute | solution.py:492
  225.2 14.2 %all-to-all-start.5 = ((bf16[64,2,768]{2,1,0:T(2,128)(2,1)}), bf16[64,2,768]{2,1,0:T(2,128)(2,1)S(1)}, u32[]{:S(2)}, u32[]{:S(2)}) async-start(bf16[64,2,768]{2,1,0:T(2,128)(2,1)} %broadcast_in_dim.5), calls=%async_computation.5 | async-start | bytes 393216 | tf_op jit(solution)/shard_map/all_to_all | solution.py:50
  243.2 13.9 %all_gather.7.refs_1_ = bf16[256,1536]{1,0:T(8,128)(2,1)} all-gather(bf16[64,1536]{1,0:T(8,128)(2,1)S(1)} %shard_map.141), channel_id=1, replica_groups=mesh['z'=16,'x'=4,'c'=2,'t'=4] {'t'}, dimensions={0}, use_global_device_ids=true | all-gather | bytes 983040 | tf_op jit(solution)/shard_map/all_gather | solution.py:497
  257.9 5.6 %collective-permute-start.5 = (bf16[128,768]{1,0:T(8,128)(2,1)}, bf16[128,768]{1,0:T(8,128)(2,1)S(1)}, u32[]{:S(2)}, u32[]{:S(2)}) collective-permute-start(bf16[128,768]{1,0:T(8,128)(2,1)} %shard_map.143), channel_id=1, source_target_pairs={{0,4},{4,0},{1,5},{5,1},{2,6},{6,2},{3,7},{7,3},{8,12},{12,8},{9,1... | collective-permute-start | bytes 589832 | tf_op jit(solution)/shard_map/ppermute | solution.py:499
  (147 shorter events, 35.2 us)
Async XLA Ops:
  7.2 21.6 %copy-start.52 = (bf16[2,3,1536]{2,0,1:T(2,128)(2,1)S(1)}, bf16[2,3,1536]{2,0,1:T(2,128)(2,1)}, u32[]{:S(2)}) copy-start(bf16[2,3,1536]{2,0,1:T(2,128)(2,1)} %param.12) | copy-start | bytes 55300
  7.2 21.6 %copy-start.53 = (s32[1,2]{1,0:T(1,128)S(1)}, s32[1,2]{1,0:T(1,128)}, u32[]{:S(2)}) copy-start(s32[1,2]{1,0:T(1,128)} %param.15) | copy-start | bytes 28
  7.2 23.6 %copy-start.24 = (bf16[256,1536]{1,0:T(8,128)(2,1)S(1)}, bf16[256,1536]{1,0:T(8,128)(2,1)}, u32[]{:S(2)}) copy-start(bf16[256,1536]{1,0:T(8,128)(2,1)} %x_ref.1) | copy-start | bytes 2359300
  7.2 23.6 %copy-start.31 = (bf16[1536,64]{0,1:T(8,128)(2,1)S(1)}, bf16[1536,64]{0,1:T(8,128)(2,1)}, u32[]{:S(2)}) copy-start(bf16[1536,64]{0,1:T(8,128)(2,1)} %param.18) | copy-start | bytes 589828
  7.2 91.7 %all-gather.2.cloned.1.call-start = ((), (), s32[]{:S(2)}) async-start(), calls=%async_computation.6 | async-start | bytes 5013504 | tf_op jit(solution)/shard_map/all_gather | solution.py:455
  28.8 110.4 %copy-start.33 = (bf16[6,1536]{1,0:T(8,128)(2,1)}, bf16[6,1536]{1,0:T(8,128)(2,1)S(1)}, u32[]{:S(2)}) copy-start(bf16[6,1536]{1,0:T(8,128)(2,1)S(1)} %reshape.37.mod_ref) | copy-start | bytes 55300
  98.9 10.6 %copy-start.9 = (bf16[256,1536]{1,0:T(8,128)(2,1)S(1)}, bf16[256,1536]{1,0:T(8,128)(2,1)}, u32[]{:S(2)}) copy-start(bf16[256,1536]{1,0:T(8,128)(2,1)} %copy-done.8) | copy-start | bytes 2359300
  98.9 10.7 %copy-start.13 = (bf16[64,1536]{1,0:T(8,128)(2,1)S(1)}, bf16[64,1536]{1,0:T(8,128)(2,1)}, u32[]{:S(2)}) copy-start(bf16[64,1536]{1,0:T(8,128)(2,1)} %b_ref.5) | copy-start | bytes 589828
  98.9 10.7 %copy-start.37 = (bf16[256,64]{1,0:T(8,128)(2,1)S(1)}, bf16[256,64]{1,0:T(8,128)(2,1)}, u32[]{:S(2)}) copy-start(bf16[256,64]{1,0:T(8,128)(2,1)} %copy-done.36) | copy-start | bytes 98308
  98.9 18.4 %collective-permute-start = (bf16[1536,1536]{1,0:T(8,128)(2,1)}, bf16[1536,1536]{1,0:T(8,128)(2,1)S(1)}, u32[]{:S(2)}, u32[]{:S(2)}) collective-permute-start(bf16[1536,1536]{1,0:T(8,128)(2,1)} %shard_map.130.up_ref.own_ref), channel_id=1, source_target_pairs={{0,4},{4,0},{1,5},{5,1},{2,6},{6,2},{3,7},{7,3},{8,12},{12,8},{9,1... | collective-permute-start | bytes 14155784 | tf_op jit(solution)/shard_map/ppermute | solution.py:466
  123.5 10.7 %slice-start = ((s8[4718592]{0:T(1024)(128)(4,1)}), s8[524288]{0:T(1024)(128)(4,1)S(1)}, s32[]{:S(2)}) async-start(s8[4718592]{0:T(1024)(128)(4,1)} %bitcast.21), calls=%async_computation.7 | async-start | bytes 1048576
  123.5 15.6 %all-to-all-start.1 = ((bf16[4,64,1536]{2,1,0:T(8,128)(2,1)}), bf16[4,64,1536]{2,1,0:T(8,128)(2,1)S(1)}, u32[]{:S(2)}, u32[]{:S(2)}) async-start(bf16[4,64,1536]{2,1,0:T(8,128)(2,1)} %bitcast.7), calls=%async_computation.1 | async-start | bytes 1572864 | tf_op jit(solution)/shard_map/all_to_all | solution.py:471
  141.8 23.1 %copy-start.7 = (bf16[1536,768]{1,0:T(8,128)(2,1)S(1)}, bf16[1536,768]{1,0:T(8,128)(2,1)}, u32[]{:S(2)}) copy-start(bf16[1536,768]{1,0:T(8,128)(2,1)} %slice.29.refs_2_.other_ref) | copy-start | bytes 7077892
  141.8 23.1 %copy-start.6 = (bf16[1536,768]{1,0:T(8,128)(2,1)S(1)}, bf16[1536,768]{1,0:T(8,128)(2,1)}, u32[]{:S(2)}) copy-start(bf16[1536,768]{1,0:T(8,128)(2,1)} %slice.28.refs_1_.own_ref) | copy-start | bytes 7077892
  141.8 23.1 %copy-start.14 = (bf16[64,1536]{1,0:T(8,128)(2,1)S(1)}, bf16[64,1536]{1,0:T(8,128)(2,1)}, u32[]{:S(2)}) copy-start(bf16[64,1536]{1,0:T(8,128)(2,1)} %b_ref.5) | copy-start | bytes 589828
  141.8 23.1 %copy-start.16 = (f32[64,1536]{1,0:T(8,128)S(1)}, f32[64,1536]{1,0:T(8,128)}, u32[]{:S(2)}) copy-start(f32[64,1536]{1,0:T(8,128)} %copy-done.15) | copy-start | bytes 1179652
  141.8 23.1 %copy-start.34 = (bf16[6,1536]{1,0:T(8,128)(2,1)S(1)}, bf16[6,1536]{1,0:T(8,128)(2,1)}, u32[]{:S(2)}) copy-start(bf16[6,1536]{1,0:T(8,128)(2,1)} %copy-done.33) | copy-start | bytes 55300
  173.4 26.8 %copy-start.32 = (bf16[1536,64]{0,1:T(8,128)(2,1)S(1)}, bf16[1536,64]{0,1:T(8,128)(2,1)}, u32[]{:S(2)}) copy-start(bf16[1536,64]{0,1:T(8,128)(2,1)} %param.18) | copy-start | bytes 589828
  173.4 26.8 %copy-start.50 = (bf16[256,64]{1,0:T(8,128)(2,1)S(1)}, bf16[256,64]{1,0:T(8,128)(2,1)}, u32[]{:S(2)}) copy-start(bf16[256,64]{1,0:T(8,128)(2,1)} %copy-done.49) | copy-start | bytes 98308
  173.4 8.5 %all-to-all-start.3 = ((bf16[4,80,256]{2,1,0:T(8,128)(2,1)}), bf16[4,80,256]{2,1,0:T(8,128)(2,1)S(1)}, u32[]{:S(2)}, u32[]{:S(2)}) async-start(bf16[4,80,256]{2,1,0:T(8,128)(2,1)} %copy-done.48), calls=%async_computation.3 | async-start | bytes 327680 | tf_op jit(solution)/shard_map/all_to_all | solution.py:481
  179.7 20.5 %copy-start.20 = (bf16[256,768]{1,0:T(8,128)(2,1)S(1)}, bf16[256,768]{1,0:T(8,128)(2,1)}, u32[]{:S(2)}) copy-start(bf16[256,768]{1,0:T(8,128)(2,1)} %copy-done.18) | copy-start | bytes 1179652
  179.7 20.5 %copy-start.23 = (bf16[256,768]{1,0:T(8,128)(2,1)S(1)}, bf16[256,768]{1,0:T(8,128)(2,1)}, u32[]{:S(2)}) copy-start(bf16[256,768]{1,0:T(8,128)(2,1)} %copy-done.21) | copy-start | bytes 1179652
  182.7 6.7 %collective-permute-start.1 = (bf16[128,768]{1,0:T(8,128)(2,1)S(1)}, bf16[128,768]{1,0:T(8,128)(2,1)S(1)}, u32[]{:S(2)}, u32[]{:S(2)}) collective-permute-start(bf16[128,768]{1,0:T(8,128)(2,1)S(1)} %get-tuple-element.42), channel_id=1, source_target_pairs={{0,4},{4,0},{1,5},{5,1},{2,6},{6,2},{3,7},{7,3},{8,12},{12,8},{9,1... | collective-permute-start | bytes 589832 | tf_op jit(solution)/shard_map/ppermute | solution.py:485
  190.2 27.6 %all-to-all-start.4 = ((bf16[64,2,768]{2,1,0:T(2,128)(2,1)}), bf16[64,2,768]{2,1,0:T(2,128)(2,1)S(1)}, u32[]{:S(2)}, u32[]{:S(2)}) async-start(bf16[64,2,768]{2,1,0:T(2,128)(2,1)} %reshape.44), calls=%async_computation.4 | async-start | bytes 393216 | tf_op jit(solution)/shard_map/all_to_all | solution.py:488
  207.3 32.1 %copy-start.17 = (f32[64,1536]{1,0:T(8,128)S(1)}, f32[64,1536]{1,0:T(8,128)}, u32[]{:S(2)}) copy-start(f32[64,1536]{1,0:T(8,128)} %copy-done.15) | copy-start | bytes 1179652
  207.3 32.1 %copy-start.35 = (bf16[6,1536]{1,0:T(8,128)(2,1)S(1)}, bf16[6,1536]{1,0:T(8,128)(2,1)}, u32[]{:S(2)}) copy-start(bf16[6,1536]{1,0:T(8,128)(2,1)} %copy-done.33) | copy-start | bytes 55300
  207.4 11.1 %collective-permute-start.2 = (bf16[64,1536]{1,0:T(8,128)(2,1)S(1)}, bf16[64,1536]{1,0:T(8,128)(2,1)S(1)}, u32[]{:S(2)}, u32[]{:S(2)}) collective-permute-start(bf16[64,1536]{1,0:T(8,128)(2,1)S(1)} %get-tuple-element.48), channel_id=1, source_target_pairs={{0,1},{1,2},{2,3},{3,0},{4,5},{5,6},{6,7},{7,4},{8,9},{9,10},{10,1... | collective-permute-start | bytes 589832 | tf_op jit(solution)/shard_map/ppermute | solution.py:492
  209.8 10.4 %collective-permute-start.3 = (bf16[64,1536]{1,0:T(8,128)(2,1)S(1)}, bf16[64,1536]{1,0:T(8,128)(2,1)S(1)}, u32[]{:S(2)}, u32[]{:S(2)}) collective-permute-start(bf16[64,1536]{1,0:T(8,128)(2,1)S(1)} %get-tuple-element.47), channel_id=1, source_target_pairs={{0,2},{1,3},{2,0},{3,1},{4,6},{5,7},{6,4},{7,5},{8,10},{9,11},{10,... | collective-permute-start | bytes 589832 | tf_op jit(solution)/shard_map/ppermute | solution.py:492
  213.5 9.6 %collective-permute-start.4 = (bf16[64,1536]{1,0:T(8,128)(2,1)S(1)}, bf16[64,1536]{1,0:T(8,128)(2,1)S(1)}, u32[]{:S(2)}, u32[]{:S(2)}) collective-permute-start(bf16[64,1536]{1,0:T(8,128)(2,1)S(1)} %get-tuple-element.46), channel_id=1, source_target_pairs={{0,3},{1,0},{2,1},{3,2},{4,7},{5,4},{6,5},{7,6},{8,11},{9,8},{10,9... | collective-permute-start | bytes 589832 | tf_op jit(solution)/shard_map/ppermute | solution.py:492
  225.2 31.9 %all-to-all-start.5 = ((bf16[64,2,768]{2,1,0:T(2,128)(2,1)}), bf16[64,2,768]{2,1,0:T(2,128)(2,1)S(1)}, u32[]{:S(2)}, u32[]{:S(2)}) async-start(bf16[64,2,768]{2,1,0:T(2,128)(2,1)} %broadcast_in_dim.5), calls=%async_computation.5 | async-start | bytes 393216 | tf_op jit(solution)/shard_map/all_to_all | solution.py:50
  257.2 9.6 %copy-start.51 = (bf16[256,1536]{1,0:T(8,128)(2,1)S(1)}, bf16[256,1536]{1,0:T(8,128)(2,1)}, u32[]{:S(2)}) copy-start(bf16[256,1536]{1,0:T(8,128)(2,1)} %all_gather.7.refs_1_) | copy-start | bytes 2359300
  257.9 6.8 %collective-permute-start.5 = (bf16[128,768]{1,0:T(8,128)(2,1)}, bf16[128,768]{1,0:T(8,128)(2,1)S(1)}, u32[]{:S(2)}, u32[]{:S(2)}) collective-permute-start(bf16[128,768]{1,0:T(8,128)(2,1)} %shard_map.143), channel_id=1, source_target_pairs={{0,4},{4,0},{1,5},{5,1},{2,6},{6,2},{3,7},{7,3},{8,12},{12,8},{9,1... | collective-permute-start | bytes 589832 | tf_op jit(solution)/shard_map/ppermute | solution.py:499
  (35 other events, 79.2 us)
Sparse Core Ops, SparseCore 0:
  27.6 71.2 all-gather.1

commit v13 on v11

--- a/solution.py
+++ b/solution.py
@@ -48,21 +48,6 @@
 
 def spread(value, axes, n):
     return lax.all_to_all(jnp.broadcast_to(value[None], (n, *value.shape)), axes, 0, 0, tiled=True)
-
-
-def around(block, n):
-    here = lax.axis_index("z")
-    up = [(i, (i + 1) % n) for i in range(n)]
-    down = [(i, (i - 1) % n) for i in range(n)]
-    found = lax.dynamic_update_index_in_dim(jnp.zeros((n, *block.shape), block.dtype), block, here, 0)
-    left = right = block
-    for step in range(1, n // 2 + 1):
-        left = lax.ppermute(left, "z", up)
-        found = lax.dynamic_update_index_in_dim(found, left, (here - step) % n, 0)
-        if step < n // 2:
-            right = lax.ppermute(right, "z", down)
-            found = lax.dynamic_update_index_in_dim(found, right, (here + step) % n, 0)
-    return found
 
 
 def normalise(rows):
@@ -463,13 +448,16 @@
     half = hidden // n_c
     rank = factor_in.shape[1]
 
-    sent = jnp.stack([up_rows.reshape(thin, n_c, half), down_rows.reshape(thin, n_c, half)], axis=2)
-    sent = sent.reshape(thin, n_c, 2 * half).transpose(1, 0, 2)
-    sent = jnp.broadcast_to(sent[None], (n_x, n_c, thin, 2 * half)).reshape(n_x * n_c, thin, 2 * half)
+    sent = down_rows.reshape(thin, n_c, half).transpose(1, 0, 2)
+    sent = jnp.broadcast_to(sent[None], (n_x, n_c, thin, half)).reshape(n_x * n_c, thin, half)
     near = lax.all_to_all(sent, ("x", "c"), 0, 0, tiled=True)
-    near_up = near[:, :, :half].reshape(n_x * n_c * thin, half)
-    near_down = near[:, :, half:].reshape(n_x * n_c * thin, half)
-    down_own = lax.all_gather(near_down, "z", axis=0, tiled=True)
+    down_own = lax.all_gather(near.reshape(n_x * n_c * thin, half), "z", axis=0, tiled=True)
+
+    up_rows, near = lax.optimization_barrier((up_rows, near))
+    keep = lax.dynamic_slice_in_dim(up_rows, core * half, half, axis=1)
+    got = lax.ppermute(lax.dynamic_slice_in_dim(up_rows, (1 - core) * half, half, axis=1), "c", SWAP)
+    pair = jnp.where(core == 0, jnp.concatenate([keep, got], 0), jnp.concatenate([got, keep], 0))
+    line = lax.all_gather(pair, "z", axis=0, tiled=True)
 
     ints = [preferred_blocks[0], live_block_count[0], last_block_rows[0, 0], last_block_rows[0, 1], group, core]
     ints = jnp.stack(ints).astype(jnp.int32)
@@ -479,8 +467,8 @@
     a_turned = factor_in.T
     modded, low, low_split = prepare(ints, tokens, mod, a_turned)
 
-    near_up = after(near_up, [modded, low, low_split, x_own, t_own])
-    up_own = around(near_up, n_z).reshape(width, half)
+    blocks = after(spread(line, "x", n_x), [modded, low, low_split, x_own, t_own])
+    up_own = blocks.reshape(n_x, n_z, n_c * thin, half).transpose(1, 0, 2, 3).reshape(width, half)
     up_other = lax.ppermute(up_own, "c", SWAP)
     down_other = lax.ppermute(down_own, "c", SWAP)
 
@@ -508,11 +496,13 @@
     chunks = [lax.dynamic_index_in_dim(dm_part, (group + step) % n_t, 0, False) for step in range(n_t)]
     chunks = [chunks[0]] + [lax.ppermute(chunks[step], "t", turns[step]) for step in range(1, n_t)]
     total = (jnp.sum(pieces.astype(F32), axis=0) / n_dp).astype(BF16)
-    total = after(total, chunks[1:])
     mine = spread(total, CHIPS, chips).reshape(2 * rank, half)
     grad_block = token_gradient(ints, chunks, x_own, mod, unit, facts)
-    grad_tokens = lax.all_gather(grad_block, "t", axis=0, tiled=True)
-    mine = after(mine, [grad_tokens])
+    shares = [grad_block] + [lax.ppermute(grad_block, "t", turns[step]) for step in range(1, n_t)]
+    shares = jnp.stack(shares)
+    grad_tokens = jnp.concatenate(
+        [lax.dynamic_index_in_dim(shares, (group - slot) % n_t, 0, False) for slot in range(n_t)], 0
+    )
     theirs = lax.ppermute(mine, "c", SWAP)
     ends = jnp.concatenate([mine, theirs], 1)
     flipped = jnp.concatenate([theirs, mine], 1)

time: 279 us -> 249 us (0.89)
  starting transfers between devices: 115 us -> 70.9 us
  blocking collectives: 52.8 us -> 70.4 us
  local copies, waits for them, and re-layouts: 43.6 us -> 32.2 us
  waiting for transfers between devices: 22.9 us -> 32.9 us
    ppermute x15 -> x4, starting transfers between devices: 52.4 us -> 13 us  [the longest x3 10.1 us: per_device(): lax.ppermute(grad_block, 't', turns[step])]
    all_gather x1, blocking collectives: 13.9 us -> 31.9 us  [per_device(): line = lax.all_gather(pair, 'z', axis=0, tiled=True)]
    all_to_all x1 -> x2, waiting for transfers between devices: 0.01 us -> 14 us  [spread(): lax.all_to_all(jnp.broadcast_to(value[None], (n, *value.shape)), axes, 0,...]
    dynamic_update_slice x16 -> x0, local copies, waits for them, and re-layouts: 10.8 us -> none  [the longest x8 5.41 us: around(): found = lax.dynamic_update_index_in_dim(found, left, (here - step) % n, 0)]
    all_to_all x1, starting transfers between devices: 10 us -> 4.6 us  [per_device(): lax.all_to_all(pile.reshape(chips, 2 * rank // chips, half), CHIPS, 0, 0,...]
    reshape x3, local copies, waits for them, and re-layouts: 1.45 us -> 4.92 us  [the longest x1 3.4 us: per_device(): blocks.reshape(n_x, n_z, n_c * thin, half).transpose(1, 0, 2, 3)]
    ppermute x15 -> x4, waiting for transfers between devices: 7.37 us -> 5.08 us  [the longest x3 4.26 us: per_device(): lax.ppermute(grad_block, 't', turns[step])]
    unnamed x106 -> x93, local copies, waits for them, and re-layouts: 19.7 us -> 18.1 us
  transfers between devices with their start and end apart: 27 -> 17, of which waited for: 12 -> 9; matrix products, arithmetic and copies ran while one was open for 7% -> 5% of each run, Pallas kernels for 6% -> 6%
where the time goes in v13:
time: 249 us; the launch traced here: 248 us
  starting transfers between devices  70.9 us (28%)
  blocking collectives  70.4 us (28%)
  waiting for transfers between devices  32.9 us (13%)
  local copies, waits for them, and re-layouts  32.2 us (13%)
  Pallas kernels  24 us (10%)
  between operations  16.1 us (6%)
    all_gather x1, blocking collectives, per_device(): line = lax.all_gather(pair, 'z', axis=0, tiled=True)  31.9 us
    all_to_all x1, blocking collectives, per_device(): got_dy = lax.all_to_all(send, 't', 0, 0, tiled=True)  23.4 us
    unnamed x93, local copies, waits for them, and re-layouts  18.1 us
    all_to_all x1, blocking collectives, per_device(): near = lax.all_to_all(sent, ('x', 'c'), 0, 0, tiled=True)  15.2 us
    all_to_all x2, waiting for transfers between devices, spread(): lax.all_to_all(jnp.broadcast_to(value[None], (n, *value.shape)), axes, 0,...  14 us
    all_to_all x2, starting transfers between devices, spread(): lax.all_to_all(jnp.broadcast_to(value[None], (n, *value.shape)), axes, 0,...  12.8 us
    ppermute x3, starting transfers between devices, per_device(): lax.ppermute(grad_block, 't', turns[step])  10.1 us
    ppermute x1, starting transfers between devices, per_device(): up_other = lax.ppermute(up_own, 'c', SWAP)  9.25 us
  transfers between devices with their start and end apart: 17, of which 9 were waited for; matrix products, arithmetic and copies ran while one was open for 5% of the time, Pallas kernels for 6%

profile of v13, /device:TPU:1, one launch (start us, length us, event | category | flops | bytes accessed | tf_op | source)
XLA Modules:
  0.0 247.9 jit_solution(9621062848078339446)
XLA Ops:
  8.1 15.2 %all_to_all.35 = bf16[8,12,768]{2,1,0:T(8,128)(2,1)S(1)} all-to-all(bf16[8,12,768]{2,1,0:T(8,128)(2,1)S(1)} %bitcast.44), channel_id=1, replica_groups=mesh['z'=16,'x'=4,'c'=2,'t'=4] {'x','c'}, dimensions={0} | all-to-all | bytes 294912 | tf_op jit(solution)/shard_map/all_to_all | solution.py:453
  24.7 2.8 %collective-permute-start = (bf16[12,768]{1,0:T(8,128)(2,1)S(1)}, bf16[12,768]{1,0:T(8,128)(2,1)S(1)}, u32[]{:S(2)}, u32[]{:S(2)}) collective-permute-start(bf16[12,768]{1,0:T(8,128)(2,1)S(1)} %get-tuple-element.57), channel_id=1, source_target_pairs={{0,4},{4,0},{1,5},{5,1},{2,6},{6,2},{3,7},{7,3},{8,12},{12,8},{9,1... | collective-permute-start | bytes 55304 | tf_op jit(solution)/shard_map/ppermute | solution.py:458
  28.4 31.9 %all_gather.6 = bf16[384,768]{1,0:T(8,128)(2,1)S(1)} all-gather(bf16[24,768]{1,0:T(8,128)(2,1)S(1)} %maximum_select_fusion.1), channel_id=1, replica_groups=mesh['z'=16,'x'=4,'c'=2,'t'=4] {'z'}, dimensions={0}, use_global_device_ids=true | all-gather | bytes 626688 | tf_op jit(solution)/shard_map/all_gather | solution.py:460
  61.8 3.8 %all-to-all-start.1 = ((bf16[4,384,768]{2,1,0:T(8,128)(2,1)}), bf16[4,384,768]{2,1,0:T(8,128)(2,1)S(1)}, u32[]{:S(2)}, u32[]{:S(2)}) async-start(bf16[4,384,768]{2,1,0:T(8,128)(2,1)} %broadcast_in_dim.7), calls=%async_computation.1 | async-start | bytes 4718592 | tf_op jit(solution)/shard_map/all_to_all | solution.py:50
  72.6 1.7 constant_dynamic-slice_fusion
  74.3 14.0 %all-to-all-done.1.refs_0_ = bf16[4,384,768]{2,1,0:T(8,128)(2,1)S(1)} async-done(((bf16[4,384,768]{2,1,0:T(8,128)(2,1)}), bf16[4,384,768]{2,1,0:T(8,128)(2,1)S(1)}, u32[]{:S(2)}, u32[]{:S(2)}) %all-to-all-start.1) | async-done | bytes 2359328 | tf_op jit(solution)/shard_map/all_to_all | solution.py:50
  89.8 3.4 %copy.20 = bf16[4,16,24,768]{3,2,0,1:T(8,128)(2,1)} copy(bf16[4,16,24,768]{3,2,1,0:T(8,128)(2,1)} %bitcast.43) | data formatting | bytes 4718592 | tf_op jit(solution)/shard_map/reshape | solution.py:471
  93.2 9.3 %collective-permute-start.1 = (bf16[1536,768]{1,0:T(8,128)(2,1)}, bf16[1536,768]{1,0:T(8,128)(2,1)}, u32[]{:S(2)}, u32[]{:S(2)}) collective-permute-start(bf16[1536,768]{1,0:T(8,128)(2,1)} %bitcast.9.up_ref.own_ref), channel_id=1, source_target_pairs={{0,4},{4,0},{1,5},{5,1},{2,6},{6,2},{3,7},{7,3},{8,12},{12,8},{9,1... | collective-permute-start | bytes 7077896 | tf_op jit(solution)/shard_map/ppermute | solution.py:472
  102.5 1.9 collective-permute-start.2
  104.4 3.6 %shard_map.131 = (bf16[256,768]{1,0:T(8,128)(2,1)S(1)}, bf16[256,768]{1,0:T(8,128)(2,1)S(1)}, bf16[256,768]{1,0:T(8,128)(2,1)S(1)}) custom-call(s32[6]{0:T(128)S(1)} %stack.26.wins_ref.ints_ref, bf16[256,1536]{1,0:T(8,128)(2,1)S(1)} %copy-done.5, bf16[256,64]{1,0:T(8,128)(2,1)S(1)} %copy-done.29, bf16[1536,768]{1,0:T(8,128)(2,1)} %bitcast.9.up_ref.own_ref, ...), custom_call_target="tpu_custom_call" | custom-call | flops 603979776 | bytes 4325376 | tf_op jit(solution)/shard_map/pallas_call | solution.py:154
  109.5 3.7 %shard_map.132 = (bf16[256,768]{1,0:T(8,128)(2,1)S(1)}, bf16[256,768]{1,0:T(8,128)(2,1)S(1)}, bf16[256,768]{1,0:T(8,128)(2,1)S(1)}) custom-call(s32[6]{0:T(128)S(1)} %stack.26.wins_ref.ints_ref, bf16[256,1536]{1,0:T(8,128)(2,1)S(1)} %copy-done.5, bf16[256,64]{1,0:T(8,128)(2,1)S(1)} %copy-done.29, bf16[1536,768]{1,0:T(8,128)(2,1)} %collective-permute-done.1.up_ref.other_ref, ...), custom_call_target="tpu_custom_call" | custom-call | flops 603979776 | bytes 4325376 | tf_op jit(solution)/shard_map/pallas_call | solution.py:154
  113.3 1.9 shard_map.133
  116.1 4.9 %all-to-all-start.2 = ((bf16[4,64,1536]{2,1,0:T(8,128)(2,1)}), bf16[4,64,1536]{2,1,0:T(8,128)(2,1)}, u32[]{:S(2)}, u32[]{:S(2)}) async-start(bf16[4,64,1536]{2,1,0:T(8,128)(2,1)} %bitcast.39), calls=%async_computation.2 | async-start | bytes 1572864 | tf_op jit(solution)/shard_map/all_to_all | solution.py:478
  124.7 1.9 shard_map.134
  127.5 5.3 %all-to-all-done.2.got_ref = bf16[4,64,1536]{2,1,0:T(8,128)(2,1)} async-done(((bf16[4,64,1536]{2,1,0:T(8,128)(2,1)}), bf16[4,64,1536]{2,1,0:T(8,128)(2,1)}, u32[]{:S(2)}, u32[]{:S(2)}) %all-to-all-start.2) | async-done | bytes 786464 | tf_op jit(solution)/shard_map/all_to_all | solution.py:478
  136.1 23.4 %all_to_all.36.got_ref = bf16[4,128,1536]{2,1,0:T(8,128)(2,1)S(1)} all-to-all(bf16[4,128,1536]{2,1,0:T(8,128)(2,1)S(1)} %get-tuple-element.33), channel_id=1, replica_groups=mesh['z'=16,'x'=4,'c'=2,'t'=4] {'t'}, dimensions={0} | all-to-all | bytes 3145728 | tf_op jit(solution)/shard_map/all_to_all | solution.py:482
  159.5 3.8 %shard_map.136 = (bf16[256,768]{1,0:T(8,128)(2,1)S(1)}, bf16[256,768]{1,0:T(8,128)(2,1)S(1)}, bf16[256,64]{1,0:T(8,128)(2,1)S(1)}, bf16[4,80,256]{2,1,0:T(8,128)(2,1)S(1)}) custom-call(s32[6]{0:T(128)S(1)} %stack.26.wins_ref.ints_ref, bf16[4,128,1536]{2,1,0:T(8,128)(2,1)S(1)} %all_to_all.36.got_ref, f32[64,1536]{1,0:T(8,128)S(1)} %get-tuple-element.34.unit_ref, ...), custom_call_target="tpu_custom_call" | custom-call | flops 1207959552 | bytes 7077888 | tf_op jit(solution)/shard_map/pallas_call | solution.py:284
  166.1 3.3 %all-to-all-start.4 = ((bf16[4,80,256]{2,1,0:T(8,128)(2,1)}), bf16[4,80,256]{2,1,0:T(8,128)(2,1)S(1)}, u32[]{:S(2)}, u32[]{:S(2)}) async-start(bf16[4,80,256]{2,1,0:T(8,128)(2,1)} %copy-done.40), calls=%async_computation.4 | async-start | bytes 327680 | tf_op jit(solution)/shard_map/all_to_all | solution.py:486
  172.5 1.9 all-to-all-done.4.got_ref
  175.2 5.6 %collective-permute-start.3 = (bf16[128,768]{1,0:T(8,128)(2,1)S(1)}, bf16[128,768]{1,0:T(8,128)(2,1)S(1)}, u32[]{:S(2)}, u32[]{:S(2)}) collective-permute-start(bf16[128,768]{1,0:T(8,128)(2,1)S(1)} %get-tuple-element.44), channel_id=1, source_target_pairs={{0,4},{4,0},{1,5},{5,1},{2,6},{6,2},{3,7},{7,3},{8,12},{12,8},{9,1... | collective-permute-start | bytes 589832 | tf_op jit(solution)/shard_map/ppermute | solution.py:490
  182.7 4.6 %all-to-all-start.5 = ((bf16[64,2,768]{2,1,0:T(2,128)(2,1)}), bf16[64,2,768]{2,1,0:T(2,128)(2,1)S(1)}, u32[]{:S(2)}, u32[]{:S(2)}) async-start(bf16[64,2,768]{2,1,0:T(2,128)(2,1)} %reshape.56), calls=%async_computation.5 | async-start | bytes 393216 | tf_op jit(solution)/shard_map/all_to_all | solution.py:493
  187.4 4.1 %shard_map.139 = bf16[256,1536]{1,0:T(8,128)(2,1)S(1)} custom-call(bf16[128,768]{1,0:T(8,128)(2,1)S(1)} %add_convert_fusion.after_ref, bf16[256,768]{1,0:T(8,128)(2,1)S(1)} %copy-done.17, bf16[256,768]{1,0:T(8,128)(2,1)S(1)} %copy-done.20, bf16[256,64]{1,0:T(8,128)(2,1)S(1)} %copy-done.42, bf16[1536,768]{1,0:T(8,128)(2,1)} %bitcast.9.up_ref.own_ref, ...), custom_call_target="tpu_custom_call" | custom-call | flops 1207959552 | bytes 5505024 | tf_op jit(solution)/shard_map/pallas_call | solution.py:387
  191.6 2.3 collective-permute-start.4
  193.9 3.7 %collective-permute-start.5 = (bf16[64,1536]{1,0:T(8,128)(2,1)S(1)}, bf16[64,1536]{1,0:T(8,128)(2,1)S(1)}, u32[]{:S(2)}, u32[]{:S(2)}) collective-permute-start(bf16[64,1536]{1,0:T(8,128)(2,1)S(1)} %get-tuple-element.53), channel_id=1, source_target_pairs={{0,2},{1,3},{2,0},{3,1},{4,6},{5,7},{6,4},{7,5},{8,10},{9,11},{10,... | collective-permute-start | bytes 589832 | tf_op jit(solution)/shard_map/ppermute | solution.py:497
  197.6 2.5 %collective-permute-start.6 = (bf16[64,1536]{1,0:T(8,128)(2,1)S(1)}, bf16[64,1536]{1,0:T(8,128)(2,1)S(1)}, u32[]{:S(2)}, u32[]{:S(2)}) collective-permute-start(bf16[64,1536]{1,0:T(8,128)(2,1)S(1)} %get-tuple-element.52), channel_id=1, source_target_pairs={{0,3},{1,0},{2,1},{3,2},{4,7},{5,4},{6,5},{7,6},{8,11},{9,8},{10,9... | collective-permute-start | bytes 589832 | tf_op jit(solution)/shard_map/ppermute | solution.py:497
  200.2 5.5 %all-to-all-done.5 = bf16[64,2,768]{2,1,0:T(2,128)(2,1)S(1)} async-done(((bf16[64,2,768]{2,1,0:T(2,128)(2,1)}), bf16[64,2,768]{2,1,0:T(2,128)(2,1)S(1)}, u32[]{:S(2)}, u32[]{:S(2)}) %all-to-all-start.5) | async-done | bytes 196640 | tf_op jit(solution)/shard_map/all_to_all | solution.py:493
  206.7 9.0 %all-to-all-start.6 = ((bf16[64,2,768]{2,1,0:T(2,128)(2,1)}), bf16[64,2,768]{2,1,0:T(2,128)(2,1)S(1)}, u32[]{:S(2)}, u32[]{:S(2)}) async-start(bf16[64,2,768]{2,1,0:T(2,128)(2,1)} %broadcast_in_dim.8), calls=%async_computation.6 | async-start | bytes 393216 | tf_op jit(solution)/shard_map/all_to_all | solution.py:50
  216.8 2.8 %collective-permute-start.7 = (bf16[64,1536]{1,0:T(8,128)(2,1)S(1)}, bf16[64,1536]{1,0:T(8,128)(2,1)S(1)}, u32[]{:S(2)}, u32[]{:S(2)}) collective-permute-start(bf16[64,1536]{1,0:T(8,128)(2,1)S(1)} %shard_map.140), channel_id=1, source_target_pairs={{0,1},{1,2},{2,3},{3,0},{4,5},{5,6},{6,7},{7,4},{8,9},{9,10},{10,1... | collective-permute-start | bytes 589832 | tf_op jit(solution)/shard_map/ppermute | solution.py:501
  219.5 3.4 %collective-permute-start.8 = (bf16[64,1536]{1,0:T(8,128)(2,1)S(1)}, bf16[64,1536]{1,0:T(8,128)(2,1)S(1)}, u32[]{:S(2)}, u32[]{:S(2)}) collective-permute-start(bf16[64,1536]{1,0:T(8,128)(2,1)S(1)} %shard_map.140), channel_id=1, source_target_pairs={{0,2},{1,3},{2,0},{3,1},{4,6},{5,7},{6,4},{7,5},{8,10},{9,11},{10,... | collective-permute-start | bytes 589832 | tf_op jit(solution)/shard_map/ppermute | solution.py:501
  223.0 4.0 %collective-permute-start.9 = (bf16[64,1536]{1,0:T(8,128)(2,1)S(1)}, bf16[64,1536]{1,0:T(8,128)(2,1)S(1)}, u32[]{:S(2)}, u32[]{:S(2)}) collective-permute-start(bf16[64,1536]{1,0:T(8,128)(2,1)S(1)} %shard_map.140), channel_id=1, source_target_pairs={{0,3},{1,0},{2,1},{3,2},{4,7},{5,4},{6,5},{7,6},{8,11},{9,8},{10,9... | collective-permute-start | bytes 589832 | tf_op jit(solution)/shard_map/ppermute | solution.py:501
  228.9 2.9 %collective-permute-done.9 = bf16[64,1536]{1,0:T(8,128)(2,1)S(1)} collective-permute-done((bf16[64,1536]{1,0:T(8,128)(2,1)S(1)}, bf16[64,1536]{1,0:T(8,128)(2,1)S(1)}, u32[]{:S(2)}, u32[]{:S(2)}) %collective-permute-start.9) | collective-permute-done | bytes 196640 | tf_op jit(solution)/shard_map/ppermute | solution.py:501
  232.1 6.9 %collective-permute-start.10 = (bf16[128,768]{1,0:T(8,128)(2,1)S(1)}, bf16[128,768]{1,0:T(8,128)(2,1)S(1)}, u32[]{:S(2)}, u32[]{:S(2)}) collective-permute-start(bf16[128,768]{1,0:T(8,128)(2,1)S(1)} %reshape.57), channel_id=1, source_target_pairs={{0,4},{4,0},{1,5},{5,1},{2,6},{6,2},{3,7},{7,3},{8,12},{12,8},{9,1... | collective-permute-start | bytes 589832 | tf_op jit(solution)/shard_map/ppermute | solution.py:506
  (136 shorter events, 37.0 us)
Async XLA Ops:
  7.2 95.3 %all-gather.2.cloned.1.call-start = ((), (), s32[]{:S(2)}) async-start(), calls=%async_computation.7 | async-start | bytes 2506752 | tf_op jit(solution)/shard_map/all_gather | solution.py:454
  24.7 3.7 %collective-permute-start = (bf16[12,768]{1,0:T(8,128)(2,1)S(1)}, bf16[12,768]{1,0:T(8,128)(2,1)S(1)}, u32[]{:S(2)}, u32[]{:S(2)}) collective-permute-start(bf16[12,768]{1,0:T(8,128)(2,1)S(1)} %get-tuple-element.57), channel_id=1, source_target_pairs={{0,4},{4,0},{1,5},{5,1},{2,6},{6,2},{3,7},{7,3},{8,12},{12,8},{9,1... | collective-permute-start | bytes 55304 | tf_op jit(solution)/shard_map/ppermute | solution.py:458
  61.8 26.5 %all-to-all-start.1 = ((bf16[4,384,768]{2,1,0:T(8,128)(2,1)}), bf16[4,384,768]{2,1,0:T(8,128)(2,1)S(1)}, u32[]{:S(2)}, u32[]{:S(2)}) async-start(bf16[4,384,768]{2,1,0:T(8,128)(2,1)} %broadcast_in_dim.7), calls=%async_computation.1 | async-start | bytes 4718592 | tf_op jit(solution)/shard_map/all_to_all | solution.py:50
  67.0 22.8 %copy-start.24 = (bf16[6,1536]{1,0:T(8,128)(2,1)}, bf16[6,1536]{1,0:T(8,128)(2,1)S(1)}, u32[]{:S(2)}) copy-start(bf16[6,1536]{1,0:T(8,128)(2,1)S(1)} %reshape.47.mod_ref) | copy-start | bytes 55300
  89.8 14.6 %copy-start.5 = (bf16[256,1536]{1,0:T(8,128)(2,1)S(1)}, bf16[256,1536]{1,0:T(8,128)(2,1)}, u32[]{:S(2)}) copy-start(bf16[256,1536]{1,0:T(8,128)(2,1)} %copy-done.4) | copy-start | bytes 2359300
  89.8 14.6 %copy-start.11 = (bf16[64,1536]{1,0:T(8,128)(2,1)S(1)}, bf16[64,1536]{1,0:T(8,128)(2,1)}, u32[]{:S(2)}) copy-start(bf16[64,1536]{1,0:T(8,128)(2,1)} %b_ref.5) | copy-start | bytes 589828
  89.8 14.6 %copy-start.29 = (bf16[256,64]{1,0:T(8,128)(2,1)S(1)}, bf16[256,64]{1,0:T(8,128)(2,1)}, u32[]{:S(2)}) copy-start(bf16[256,64]{1,0:T(8,128)(2,1)} %copy-done.28) | copy-start | bytes 98308
  93.2 16.4 %collective-permute-start.1 = (bf16[1536,768]{1,0:T(8,128)(2,1)}, bf16[1536,768]{1,0:T(8,128)(2,1)}, u32[]{:S(2)}, u32[]{:S(2)}) collective-permute-start(bf16[1536,768]{1,0:T(8,128)(2,1)} %bitcast.9.up_ref.own_ref), channel_id=1, source_target_pairs={{0,4},{4,0},{1,5},{5,1},{2,6},{6,2},{3,7},{7,3},{8,12},{12,8},{9,1... | collective-permute-start | bytes 7077896 | tf_op jit(solution)/shard_map/ppermute | solution.py:472
  102.5 10.8 %collective-permute-start.2 = (bf16[1536,768]{1,0:T(8,128)(2,1)}, bf16[1536,768]{1,0:T(8,128)(2,1)S(1)}, u32[]{:S(2)}, u32[]{:S(2)}) collective-permute-start(bf16[1536,768]{1,0:T(8,128)(2,1)} %all-gather.2.cloned.1.call-done.own_ref), channel_id=1, source_target_pairs={{0,4},{4,0},{1,5},{5,1},{2,6},{6,2},{3,7},{7,3},{8,12},{12,8},{9,1... | collective-permute-start | bytes 7077896 | tf_op jit(solution)/shard_map/ppermute | solution.py:473
  116.1 16.6 %all-to-all-start.2 = ((bf16[4,64,1536]{2,1,0:T(8,128)(2,1)}), bf16[4,64,1536]{2,1,0:T(8,128)(2,1)}, u32[]{:S(2)}, u32[]{:S(2)}) async-start(bf16[4,64,1536]{2,1,0:T(8,128)(2,1)} %bitcast.39), calls=%async_computation.2 | async-start | bytes 1572864 | tf_op jit(solution)/shard_map/all_to_all | solution.py:478
  134.6 24.9 %copy-start.33 = (bf16[256,768]{1,0:T(8,128)(2,1)S(1)}, bf16[256,768]{1,0:T(8,128)(2,1)}, u32[]{:S(2)}) copy-start(bf16[256,768]{1,0:T(8,128)(2,1)} %copy-done.32) | copy-start | bytes 1179652
  136.0 23.4 %copy-start.13 = (f32[64,1536]{1,0:T(8,128)}, f32[64,1536]{1,0:T(8,128)S(1)}, u32[]{:S(2)}) copy-start(f32[64,1536]{1,0:T(8,128)S(1)} %get-tuple-element.34.unit_ref) | copy-start | bytes 1179652
  136.0 23.4 %copy-start.3 = (bf16[1536,768]{1,0:T(8,128)(2,1)S(1)}, bf16[1536,768]{1,0:T(8,128)(2,1)}, u32[]{:S(2)}) copy-start(bf16[1536,768]{1,0:T(8,128)(2,1)} %copy-done.1) | copy-start | bytes 7077892
  136.1 23.4 %copy-start.12 = (bf16[64,1536]{1,0:T(8,128)(2,1)S(1)}, bf16[64,1536]{1,0:T(8,128)(2,1)}, u32[]{:S(2)}) copy-start(bf16[64,1536]{1,0:T(8,128)(2,1)} %b_ref.5) | copy-start | bytes 589828
  136.1 23.4 %copy-start.26 = (bf16[6,1536]{1,0:T(8,128)(2,1)S(1)}, bf16[6,1536]{1,0:T(8,128)(2,1)}, u32[]{:S(2)}) copy-start(bf16[6,1536]{1,0:T(8,128)(2,1)} %copy-done.24) | copy-start | bytes 55300
  136.1 23.4 %copy-start.31 = (bf16[256,768]{1,0:T(8,128)(2,1)S(1)}, bf16[256,768]{1,0:T(8,128)(2,1)}, u32[]{:S(2)}) copy-start(bf16[256,768]{1,0:T(8,128)(2,1)} %copy-done.30) | copy-start | bytes 1179652
  166.1 8.3 %all-to-all-start.4 = ((bf16[4,80,256]{2,1,0:T(8,128)(2,1)}), bf16[4,80,256]{2,1,0:T(8,128)(2,1)S(1)}, u32[]{:S(2)}, u32[]{:S(2)}) async-start(bf16[4,80,256]{2,1,0:T(8,128)(2,1)} %copy-done.40), calls=%async_computation.4 | async-start | bytes 327680 | tf_op jit(solution)/shard_map/all_to_all | solution.py:486
  174.4 12.9 %copy-start.20 = (bf16[256,768]{1,0:T(8,128)(2,1)S(1)}, bf16[256,768]{1,0:T(8,128)(2,1)}, u32[]{:S(2)}) copy-start(bf16[256,768]{1,0:T(8,128)(2,1)} %copy-done.18) | copy-start | bytes 1179652
  174.4 13.0 %copy-start.23 = (bf16[1536,64]{0,1:T(8,128)(2,1)S(1)}, bf16[1536,64]{0,1:T(8,128)(2,1)}, u32[]{:S(2)}) copy-start(bf16[1536,64]{0,1:T(8,128)(2,1)} %param.18) | copy-start | bytes 589828
  174.4 13.0 %copy-start.42 = (bf16[256,64]{1,0:T(8,128)(2,1)S(1)}, bf16[256,64]{1,0:T(8,128)(2,1)}, u32[]{:S(2)}) copy-start(bf16[256,64]{1,0:T(8,128)(2,1)} %copy-done.41) | copy-start | bytes 98308
  175.2 6.6 %collective-permute-start.3 = (bf16[128,768]{1,0:T(8,128)(2,1)S(1)}, bf16[128,768]{1,0:T(8,128)(2,1)S(1)}, u32[]{:S(2)}, u32[]{:S(2)}) collective-permute-start(bf16[128,768]{1,0:T(8,128)(2,1)S(1)} %get-tuple-element.44), channel_id=1, source_target_pairs={{0,4},{4,0},{1,5},{5,1},{2,6},{6,2},{3,7},{7,3},{8,12},{12,8},{9,1... | collective-permute-start | bytes 589832 | tf_op jit(solution)/shard_map/ppermute | solution.py:490
  182.7 23.0 %all-to-all-start.5 = ((bf16[64,2,768]{2,1,0:T(2,128)(2,1)}), bf16[64,2,768]{2,1,0:T(2,128)(2,1)S(1)}, u32[]{:S(2)}, u32[]{:S(2)}) async-start(bf16[64,2,768]{2,1,0:T(2,128)(2,1)} %reshape.56), calls=%async_computation.5 | async-start | bytes 393216 | tf_op jit(solution)/shard_map/all_to_all | solution.py:493
  191.5 24.2 %copy-start.14 = (f32[64,1536]{1,0:T(8,128)S(1)}, f32[64,1536]{1,0:T(8,128)}, u32[]{:S(2)}) copy-start(f32[64,1536]{1,0:T(8,128)} %copy-done.13) | copy-start | bytes 1179652
  191.5 24.2 %copy-start.27 = (bf16[6,1536]{1,0:T(8,128)(2,1)S(1)}, bf16[6,1536]{1,0:T(8,128)(2,1)}, u32[]{:S(2)}) copy-start(bf16[6,1536]{1,0:T(8,128)(2,1)} %copy-done.24) | copy-start | bytes 55300
  191.6 24.1 %collective-permute-start.4 = (bf16[64,1536]{1,0:T(8,128)(2,1)S(1)}, bf16[64,1536]{1,0:T(8,128)(2,1)S(1)}, u32[]{:S(2)}, u32[]{:S(2)}) collective-permute-start(bf16[64,1536]{1,0:T(8,128)(2,1)S(1)} %get-tuple-element.54), channel_id=1, source_target_pairs={{0,1},{1,2},{2,3},{3,0},{4,5},{5,6},{6,7},{7,4},{8,9},{9,10},{10,1... | collective-permute-start | bytes 589832 | tf_op jit(solution)/shard_map/ppermute | solution.py:497
  193.9 21.8 %collective-permute-start.5 = (bf16[64,1536]{1,0:T(8,128)(2,1)S(1)}, bf16[64,1536]{1,0:T(8,128)(2,1)S(1)}, u32[]{:S(2)}, u32[]{:S(2)}) collective-permute-start(bf16[64,1536]{1,0:T(8,128)(2,1)S(1)} %get-tuple-element.53), channel_id=1, source_target_pairs={{0,2},{1,3},{2,0},{3,1},{4,6},{5,7},{6,4},{7,5},{8,10},{9,11},{10,... | collective-permute-start | bytes 589832 | tf_op jit(solution)/shard_map/ppermute | solution.py:497
  197.6 18.1 %collective-permute-start.6 = (bf16[64,1536]{1,0:T(8,128)(2,1)S(1)}, bf16[64,1536]{1,0:T(8,128)(2,1)S(1)}, u32[]{:S(2)}, u32[]{:S(2)}) collective-permute-start(bf16[64,1536]{1,0:T(8,128)(2,1)S(1)} %get-tuple-element.52), channel_id=1, source_target_pairs={{0,3},{1,0},{2,1},{3,2},{4,7},{5,4},{6,5},{7,6},{8,11},{9,8},{10,9... | collective-permute-start | bytes 589832 | tf_op jit(solution)/shard_map/ppermute | solution.py:497
  206.7 25.3 %all-to-all-start.6 = ((bf16[64,2,768]{2,1,0:T(2,128)(2,1)}), bf16[64,2,768]{2,1,0:T(2,128)(2,1)S(1)}, u32[]{:S(2)}, u32[]{:S(2)}) async-start(bf16[64,2,768]{2,1,0:T(2,128)(2,1)} %broadcast_in_dim.8), calls=%async_computation.6 | async-start | bytes 393216 | tf_op jit(solution)/shard_map/all_to_all | solution.py:50
  216.8 10.7 %collective-permute-start.7 = (bf16[64,1536]{1,0:T(8,128)(2,1)S(1)}, bf16[64,1536]{1,0:T(8,128)(2,1)S(1)}, u32[]{:S(2)}, u32[]{:S(2)}) collective-permute-start(bf16[64,1536]{1,0:T(8,128)(2,1)S(1)} %shard_map.140), channel_id=1, source_target_pairs={{0,1},{1,2},{2,3},{3,0},{4,5},{5,6},{6,7},{7,4},{8,9},{9,10},{10,1... | collective-permute-start | bytes 589832 | tf_op jit(solution)/shard_map/ppermute | solution.py:501
  219.5 9.4 %collective-permute-start.8 = (bf16[64,1536]{1,0:T(8,128)(2,1)S(1)}, bf16[64,1536]{1,0:T(8,128)(2,1)S(1)}, u32[]{:S(2)}, u32[]{:S(2)}) collective-permute-start(bf16[64,1536]{1,0:T(8,128)(2,1)S(1)} %shard_map.140), channel_id=1, source_target_pairs={{0,2},{1,3},{2,0},{3,1},{4,6},{5,7},{6,4},{7,5},{8,10},{9,11},{10,... | collective-permute-start | bytes 589832 | tf_op jit(solution)/shard_map/ppermute | solution.py:501
  223.0 8.8 %collective-permute-start.9 = (bf16[64,1536]{1,0:T(8,128)(2,1)S(1)}, bf16[64,1536]{1,0:T(8,128)(2,1)S(1)}, u32[]{:S(2)}, u32[]{:S(2)}) collective-permute-start(bf16[64,1536]{1,0:T(8,128)(2,1)S(1)} %shard_map.140), channel_id=1, source_target_pairs={{0,3},{1,0},{2,1},{3,2},{4,7},{5,4},{6,5},{7,6},{8,11},{9,8},{10,9... | collective-permute-start | bytes 589832 | tf_op jit(solution)/shard_map/ppermute | solution.py:501
  232.1 8.0 %collective-permute-start.10 = (bf16[128,768]{1,0:T(8,128)(2,1)S(1)}, bf16[128,768]{1,0:T(8,128)(2,1)S(1)}, u32[]{:S(2)}, u32[]{:S(2)}) collective-permute-start(bf16[128,768]{1,0:T(8,128)(2,1)S(1)} %reshape.57), channel_id=1, source_target_pairs={{0,4},{4,0},{1,5},{5,1},{2,6},{6,2},{3,7},{7,3},{8,12},{12,8},{9,1... | collective-permute-start | bytes 589832 | tf_op jit(solution)/shard_map/ppermute | solution.py:506
  (31 other events, 81.1 us)
Sparse Core Ops, SparseCore 0:
  24.1 66.2 all-gather.1

commit v14 on v13

--- a/solution.py
+++ b/solution.py
@@ -127,6 +127,42 @@
         out_specs=pl.BlockSpec(memory_space=pl.ANY),
         input_output_aliases={0: 0},
     )(value, *others)
+
+
+def swapped(index, outer, inner, unit):
+    first = sum((index >= k * inner * unit).astype(jnp.int32) for k in range(1, outer))
+    rest = index - first * (inner * unit)
+    second = sum((rest >= k * unit).astype(jnp.int32) for k in range(1, inner))
+    return second * (outer * unit) + first * unit + rest - second * unit
+
+
+def places(start, size, width, outer, inner, unit):
+    column = swapped(lax.broadcasted_iota(jnp.int32, (1, size), 1) + start, outer, inner, unit)
+    line = lax.broadcasted_iota(jnp.int32, (width, size), 0)
+    return jnp.where(line == column, 1.0, 0.0).astype(BF16)
+
+
+def reorder_kernel(order, modded_ref, a_ref, modded_out, a_out):
+    size = modded_out.shape[1]
+    turn = places(pl.program_id(0) * size, size, modded_ref.shape[1], *order)
+    modded_out[...] = product(modded_ref[...], turn).astype(BF16)
+    a_out[...] = product(a_ref[...], turn).astype(BF16)
+
+
+def reorder(order, modded, a_turned):
+    rows, width = modded.shape
+    rank = a_turned.shape[0]
+    step = 256
+    cuts = [pl.BlockSpec((rows, step), lambda i: (0, i)), pl.BlockSpec((rank, step), lambda i: (0, i))]
+    return pl.pallas_call(
+        functools.partial(reorder_kernel, order),
+        grid=(width // step,),
+        out_shape=[jax.ShapeDtypeStruct((rows, width), BF16), jax.ShapeDtypeStruct((rank, width), BF16)],
+        in_specs=[whole((rows, width)), whole((rank, width))],
+        out_specs=cuts,
+        compiler_params=params(),
+        cost_estimate=cost(2 * (rows + rank) * width * width, 8 * rows * width),
+    )(modded, a_turned)
 
 
 def half_of(core, step, half, size):
@@ -373,19 +409,29 @@
     )(ints, got, modded, b_own, b_other)
 
 
-def dm_kernel(after_ref, do_ref, dt_ref, dlow_ref, own_ref, other_ref, a_ref, out_ref):
+def dm_kernel(order, after_ref, do_ref, dt_ref, dlow_ref, own_ref, other_ref, a_ref, out_ref, total_scr):
+    step = pl.program_id(0)
+    size = own_ref.shape[0]
+    width = out_ref.shape[1]
     total = rows_by_rows(do_ref[...], own_ref[...]) + rows_by_rows(dt_ref[...], other_ref[...])
-    out_ref[...] = (total + product(dlow_ref[...], a_ref[...])).astype(BF16)
-
-
-def dm_terms(after, d_own, d_other, dlow, own, other, a_turned):
+    total = total + product(dlow_ref[...], a_ref[...])
+    total_scr[:, pl.ds(pl.multiple_of(step * size, 128), size)] = total.astype(BF16)
+
+    @pl.when(step == pl.num_programs(0) - 1)
+    def _():
+        for start in range(0, width, 256):
+            turn = places(start, 256, width, *order)
+            out_ref[:, start : start + 256] = product(total_scr[...], turn).astype(BF16)
+
+
+def dm_terms(order, after, d_own, d_other, dlow, own, other, a_order):
     rows, half = d_own.shape
     width = own.shape[0]
     rank = dlow.shape[1]
     step = 512
     cut = pl.BlockSpec((step, half), lambda i: (i, 0))
     return pl.pallas_call(
-        dm_kernel,
+        functools.partial(dm_kernel, order),
         grid=(width // step,),
         out_shape=jax.ShapeDtypeStruct((rows, width), BF16),
         in_specs=[
@@ -397,10 +443,11 @@
             cut,
             pl.BlockSpec((rank, step), lambda i: (0, i)),
         ],
-        out_specs=pl.BlockSpec((rows, step), lambda i: (0, i)),
+        out_specs=whole((rows, width)),
+        scratch_shapes=[pltpu.VMEM((rows, width), BF16)],
         compiler_params=params(),
         cost_estimate=cost(4 * rows * width * half, 4 * width * half + 2 * rows * width),
-    )(after, d_own, d_other, dlow, own, other, a_turned)
+    )(after, d_own, d_other, dlow, own, other, a_order)
 
 
 def token_kernel(ints_ref, one_ref, two_ref, three_ref, four_ref, x_ref, mod_ref, unit_ref, facts_ref, out_ref):
@@ -467,13 +514,14 @@
     a_turned = factor_in.T
     modded, low, low_split = prepare(ints, tokens, mod, a_turned)
 
-    blocks = after(spread(line, "x", n_x), [modded, low, low_split, x_own, t_own])
-    up_own = blocks.reshape(n_x, n_z, n_c * thin, half).transpose(1, 0, 2, 3).reshape(width, half)
+    modded_order, a_order = reorder((n_x, n_z, n_c * thin), modded, a_turned)
+    blocks = after(spread(line, "x", n_x), [modded_order, a_order, low, low_split, x_own, t_own])
+    up_own = blocks.reshape(width, half)
     up_other = lax.ppermute(up_own, "c", SWAP)
     down_other = lax.ppermute(down_own, "c", SWAP)
 
-    pol_own, ref_own, slope_own = activate(False, ints, modded, low, up_own, factor_out)
-    pol_other, ref_other, slope_other = activate(True, ints, modded, low, up_other, factor_out)
+    pol_own, ref_own, slope_own = activate(False, ints, modded_order, low, up_own, factor_out)
+    pol_other, ref_other, slope_other = activate(True, ints, modded_order, low, up_other, factor_out)
     part_pol = lower(pol_own, pol_other, down_own, down_other).reshape(CAP, BLK, width)
     got_pol = lax.all_to_all(part_pol, "t", 0, 0, tiled=True)
     part_ref = lower(ref_own, ref_other, down_own, down_other).reshape(CAP, BLK, width)
@@ -491,7 +539,9 @@
 
     chips = n_z * n_x
     pieces = lax.all_to_all(pile.reshape(chips, 2 * rank // chips, half), CHIPS, 0, 0, tiled=True)
-    dm_part = dm_terms(pile, d_own, d_other, dlow_part, up_own, up_other, a_turned).reshape(CAP, BLK, width)
+    dm_part = dm_terms(
+        (n_z, n_x, n_c * thin), pile, d_own, d_other, dlow_part, up_own, up_other, a_order
+    ).reshape(CAP, BLK, width)
     turns = [[(i, (i + step) % n_t) for i in range(n_t)] for step in range(n_t)]
     chunks = [lax.dynamic_index_in_dim(dm_part, (group + step) % n_t, 0, False) for step in range(n_t)]
     chunks = [chunks[0]] + [lax.ppermute(chunks[step], "t", turns[step]) for step in range(1, n_t)]

time: 249 us -> 256 us (1.028)
  starting transfers between devices: 70.9 us -> 78.3 us
  waiting for transfers between devices: 32.9 us -> 26.5 us
  Pallas kernels: 24 us -> 28.5 us
    pallas_call x1 -> x2, Pallas kernels: 4.13 us -> 8.53 us  [the longest x1 5.09 us: dm_terms(): pl.pallas_call(functools.partial(dm_kernel, order), grid=(width // step,)...]
    all_to_all x1, starting transfers between devices: 4.6 us -> 8.51 us  [per_device(): lax.all_to_all(pile.reshape(chips, 2 * rank // chips, half), CHIPS, 0, 0,...]
    all_to_all x1, waiting for transfers between devices: 5.5 us -> 1.71 us  [per_device(): lax.all_to_all(pile.reshape(chips, 2 * rank // chips, half), CHIPS, 0, 0,...]
    all_to_all x2, waiting for transfers between devices: 14 us -> 10.3 us  [spread(): lax.all_to_all(jnp.broadcast_to(value[None], (n, *value.shape)), axes, 0,...]
    all_to_all x2, starting transfers between devices: 12.8 us -> 16.5 us  [spread(): lax.all_to_all(jnp.broadcast_to(value[None], (n, *value.shape)), axes, 0,...]
    reshape x1 -> x0, local copies, waits for them, and re-layouts: 3.4 us -> none  [per_device(): blocks.reshape(n_x, n_z, n_c * thin, half).transpose(1, 0, 2, 3)]
    unnamed x93 -> x99, local copies, waits for them, and re-layouts: 18.1 us -> 21.3 us
  transfers between devices with their start and end apart: 17 -> 17, of which waited for: 9 -> 10; matrix products, arithmetic and copies ran while one was open for 5% -> 4% of each run, Pallas kernels for 6% -> 8%
where the time goes in v14:
time: 256 us; the launch traced here: 254 us
  starting transfers between devices  78.3 us (31%)
  blocking collectives  70.4 us (28%)
  local copies, waits for them, and re-layouts  32.1 us (13%)
  Pallas kernels  28.5 us (11%)
  waiting for transfers between devices  26.5 us (10%)
  between operations  16.1 us (6%)
    all_gather x1, blocking collectives, per_device(): line = lax.all_gather(pair, 'z', axis=0, tiled=True)  31.9 us
    all_to_all x1, blocking collectives, per_device(): got_dy = lax.all_to_all(send, 't', 0, 0, tiled=True)  23.4 us
    unnamed x99, local copies, waits for them, and re-layouts  21.3 us
    all_to_all x2, starting transfers between devices, spread(): lax.all_to_all(jnp.broadcast_to(value[None], (n, *value.shape)), axes, 0,...  16.5 us
    all_to_all x1, blocking collectives, per_device(): near = lax.all_to_all(sent, ('x', 'c'), 0, 0, tiled=True)  15.2 us
    all_to_all x2, waiting for transfers between devices, spread(): lax.all_to_all(jnp.broadcast_to(value[None], (n, *value.shape)), axes, 0,...  10.3 us
    ppermute x3, starting transfers between devices, per_device(): lax.ppermute(grad_block, 't', turns[step])  10.1 us
    ppermute x1, starting transfers between devices, per_device(): up_other = lax.ppermute(up_own, 'c', SWAP)  9.38 us
  transfers between devices with their start and end apart: 17, of which 10 were waited for; matrix products, arithmetic and copies ran while one was open for 4% of the time, Pallas kernels for 8%

profile of v14, /device:TPU:1, one launch (start us, length us, event | category | flops | bytes accessed | tf_op | source)
XLA Modules:
  0.0 254.2 jit_solution(2646926697927977936)
XLA Ops:
  8.1 15.2 %all_to_all.35 = bf16[8,12,768]{2,1,0:T(8,128)(2,1)S(1)} all-to-all(bf16[8,12,768]{2,1,0:T(8,128)(2,1)S(1)} %bitcast.42), channel_id=1, replica_groups=mesh['z'=16,'x'=4,'c'=2,'t'=4] {'x','c'}, dimensions={0} | all-to-all | bytes 294912 | tf_op jit(solution)/shard_map/all_to_all | solution.py:500
  24.7 2.8 %collective-permute-start = (bf16[12,768]{1,0:T(8,128)(2,1)S(1)}, bf16[12,768]{1,0:T(8,128)(2,1)S(1)}, u32[]{:S(2)}, u32[]{:S(2)}) collective-permute-start(bf16[12,768]{1,0:T(8,128)(2,1)S(1)} %get-tuple-element.61), channel_id=1, source_target_pairs={{0,4},{4,0},{1,5},{5,1},{2,6},{6,2},{3,7},{7,3},{8,12},{12,8},{9,1... | collective-permute-start | bytes 55304 | tf_op jit(solution)/shard_map/ppermute | solution.py:505
  28.4 31.9 %all_gather.6 = bf16[384,768]{1,0:T(8,128)(2,1)S(1)} all-gather(bf16[24,768]{1,0:T(8,128)(2,1)S(1)} %maximum_select_fusion.1), channel_id=1, replica_groups=mesh['z'=16,'x'=4,'c'=2,'t'=4] {'z'}, dimensions={0}, use_global_device_ids=true | all-gather | bytes 626688 | tf_op jit(solution)/shard_map/all_gather | solution.py:507
  61.8 3.8 %all-to-all-start.1 = ((bf16[4,384,768]{2,1,0:T(8,128)(2,1)}), bf16[4,384,768]{2,1,0:T(8,128)(2,1)S(1)}, u32[]{:S(2)}, u32[]{:S(2)}) async-start(bf16[4,384,768]{2,1,0:T(8,128)(2,1)} %broadcast_in_dim.7), calls=%async_computation.1 | async-start | bytes 4718592 | tf_op jit(solution)/shard_map/all_to_all | solution.py:50
  71.7 3.4 %shard_map.130 = (bf16[256,1536]{1,0:T(8,128)(2,1)S(1)}, bf16[64,1536]{1,0:T(8,128)(2,1)S(1)}) custom-call(bf16[256,1536]{1,0:T(8,128)(2,1)S(1)} %get-tuple-element.27.modded_ref, bf16[64,1536]{1,0:T(8,128)(2,1)S(1)} %bitcast.41), custom_call_target="tpu_custom_call" | custom-call | flops 1509949440 | bytes 3145728 | tf_op jit(solution)/shard_map/pallas_call | solution.py:157
  76.8 1.7 constant_dynamic-slice_fusion
  78.5 9.8 %all-to-all-done.1.refs_0_ = bf16[4,384,768]{2,1,0:T(8,128)(2,1)S(1)} async-done(((bf16[4,384,768]{2,1,0:T(8,128)(2,1)}), bf16[4,384,768]{2,1,0:T(8,128)(2,1)S(1)}, u32[]{:S(2)}, u32[]{:S(2)}) %all-to-all-start.1) | async-done | bytes 2359328 | tf_op jit(solution)/shard_map/all_to_all | solution.py:50
  89.8 9.4 %collective-permute-start.1 = (bf16[1536,768]{1,0:T(8,128)(2,1)}, bf16[1536,768]{1,0:T(8,128)(2,1)}, u32[]{:S(2)}, u32[]{:S(2)}) collective-permute-start(bf16[1536,768]{1,0:T(8,128)(2,1)} %bitcast.34), channel_id=1, source_target_pairs={{0,4},{4,0},{1,5},{5,1},{2,6},{6,2},{3,7},{7,3},{8,12},{12,8},{9,1... | collective-permute-start | bytes 7077896 | tf_op jit(solution)/shard_map/ppermute | solution.py:520
  99.2 1.9 collective-permute-start.2
  102.8 2.6 %shard_map.132 = (bf16[256,768]{1,0:T(8,128)(2,1)S(1)}, bf16[256,768]{1,0:T(8,128)(2,1)S(1)}, bf16[256,768]{1,0:T(8,128)(2,1)S(1)}) custom-call(s32[6]{0:T(128)S(1)} %stack.26.wins_ref.ints_ref, bf16[256,1536]{1,0:T(8,128)(2,1)S(1)} %copy-done.8, bf16[256,64]{1,0:T(8,128)(2,1)S(1)} %copy-done.28, bf16[1536,768]{1,0:T(8,128)(2,1)S(1)} %bitcast.35, ...), custom_call_target="tpu_custom_call" | custom-call | flops 603979776 | bytes 4325376 | tf_op jit(solution)/shard_map/pallas_call | solution.py:190
  107.0 3.7 %shard_map.133 = (bf16[256,768]{1,0:T(8,128)(2,1)S(1)}, bf16[256,768]{1,0:T(8,128)(2,1)S(1)}, bf16[256,768]{1,0:T(8,128)(2,1)S(1)}) custom-call(s32[6]{0:T(128)S(1)} %stack.26.wins_ref.ints_ref, bf16[256,1536]{1,0:T(8,128)(2,1)S(1)} %copy-done.8, bf16[256,64]{1,0:T(8,128)(2,1)S(1)} %copy-done.28, bf16[1536,768]{1,0:T(8,128)(2,1)} %collective-permute-done.1.up_ref.other_ref, ...), custom_call_target="tpu_custom_call" | custom-call | flops 603979776 | bytes 4325376 | tf_op jit(solution)/shard_map/pallas_call | solution.py:190
  110.8 3.0 %shard_map.134 = bf16[256,1536]{1,0:T(8,128)(2,1)} custom-call(bf16[256,768]{1,0:T(8,128)(2,1)S(1)} %get-tuple-element.33.left_ref, bf16[256,768]{1,0:T(8,128)(2,1)S(1)} %get-tuple-element.34.right_ref, bf16[1536,768]{1,0:T(8,128)(2,1)S(1)} %copy-done.3, bf16[1536,768]{1,0:T(8,128)(2,1)S(1)} %collective-permute-done.2.other_ref), custom_call_target="tpu_custom_call" | custom-call | flops 1207959552 | bytes 5505024 | tf_op jit(solution)/shard_map/pallas_call | solution.py:221
  113.8 4.9 %all-to-all-start.2 = ((bf16[4,64,1536]{2,1,0:T(8,128)(2,1)}), bf16[4,64,1536]{2,1,0:T(8,128)(2,1)}, u32[]{:S(2)}, u32[]{:S(2)}) async-start(bf16[4,64,1536]{2,1,0:T(8,128)(2,1)} %bitcast.8), calls=%async_computation.2 | async-start | bytes 1572864 | tf_op jit(solution)/shard_map/all_to_all | solution.py:526
  122.4 1.9 shard_map.135
  124.2 6.1 %all-to-all-done.2.got_ref = bf16[4,64,1536]{2,1,0:T(8,128)(2,1)} async-done(((bf16[4,64,1536]{2,1,0:T(8,128)(2,1)}), bf16[4,64,1536]{2,1,0:T(8,128)(2,1)}, u32[]{:S(2)}, u32[]{:S(2)}) %all-to-all-start.2) | async-done | bytes 786464 | tf_op jit(solution)/shard_map/all_to_all | solution.py:526
  132.6 23.4 %all_to_all.36.got_ref = bf16[4,128,1536]{2,1,0:T(8,128)(2,1)S(1)} all-to-all(bf16[4,128,1536]{2,1,0:T(8,128)(2,1)S(1)} %get-tuple-element.37), channel_id=1, replica_groups=mesh['z'=16,'x'=4,'c'=2,'t'=4] {'t'}, dimensions={0} | all-to-all | bytes 3145728 | tf_op jit(solution)/shard_map/all_to_all | solution.py:530
  156.1 3.8 %shard_map.137 = (bf16[256,768]{1,0:T(8,128)(2,1)S(1)}, bf16[256,768]{1,0:T(8,128)(2,1)S(1)}, bf16[256,64]{1,0:T(8,128)(2,1)S(1)}, bf16[4,80,256]{2,1,0:T(8,128)(2,1)S(1)}) custom-call(s32[6]{0:T(128)S(1)} %stack.26.wins_ref.ints_ref, bf16[4,128,1536]{2,1,0:T(8,128)(2,1)S(1)} %all_to_all.36.got_ref, f32[64,1536]{1,0:T(8,128)S(1)} %get-tuple-element.38.unit_ref, ...), custom_call_target="tpu_custom_call" | custom-call | flops 1207959552 | bytes 7077888 | tf_op jit(solution)/shard_map/pallas_call | solution.py:320
  161.9 3.3 %all-to-all-start.4 = ((bf16[4,80,256]{2,1,0:T(8,128)(2,1)}), bf16[4,80,256]{2,1,0:T(8,128)(2,1)S(1)}, u32[]{:S(2)}, u32[]{:S(2)}) async-start(bf16[4,80,256]{2,1,0:T(8,128)(2,1)} %copy-done.44), calls=%async_computation.4 | async-start | bytes 327680 | tf_op jit(solution)/shard_map/all_to_all | solution.py:534
  168.0 2.2 all-to-all-done.4.got_ref
  174.1 5.7 %collective-permute-start.3 = (bf16[128,768]{1,0:T(8,128)(2,1)S(1)}, bf16[128,768]{1,0:T(8,128)(2,1)S(1)}, u32[]{:S(2)}, u32[]{:S(2)}) collective-permute-start(bf16[128,768]{1,0:T(8,128)(2,1)S(1)} %get-tuple-element.48), channel_id=1, source_target_pairs={{0,4},{4,0},{1,5},{5,1},{2,6},{6,2},{3,7},{7,3},{8,12},{12,8},{9,1... | collective-permute-start | bytes 589832 | tf_op jit(solution)/shard_map/ppermute | solution.py:538
  181.7 8.5 %all-to-all-start.5 = ((bf16[64,2,768]{2,1,0:T(2,128)(2,1)}), bf16[64,2,768]{2,1,0:T(2,128)(2,1)}, u32[]{:S(2)}, u32[]{:S(2)}) async-start(bf16[64,2,768]{2,1,0:T(2,128)(2,1)} %reshape.52), calls=%async_computation.5 | async-start | bytes 393216 | tf_op jit(solution)/shard_map/all_to_all | solution.py:541
  192.0 5.1 %shard_map.140 = bf16[256,1536]{1,0:T(8,128)(2,1)S(1)} custom-call(bf16[128,768]{1,0:T(8,128)(2,1)S(1)} %add_convert_fusion.after_ref, bf16[256,768]{1,0:T(8,128)(2,1)S(1)} %get-tuple-element.42.do_ref, bf16[256,768]{1,0:T(8,128)(2,1)S(1)} %copy-done.17, bf16[256,64]{1,0:T(8,128)(2,1)S(1)} %copy-done.46, bf16[1536,768]{1,0:T(8,128)(2,1)S(1)} %bitcast.36, ...), custom_call_target="tpu_custom_call" | custom-call | flops 1207959552 | bytes 5505024 | tf_op jit(solution)/shard_map/pallas_call | solution.py:433
  197.2 2.3 collective-permute-start.4
  199.6 3.7 %collective-permute-start.5 = (bf16[64,1536]{1,0:T(8,128)(2,1)S(1)}, bf16[64,1536]{1,0:T(8,128)(2,1)S(1)}, u32[]{:S(2)}, u32[]{:S(2)}) collective-permute-start(bf16[64,1536]{1,0:T(8,128)(2,1)S(1)} %get-tuple-element.57), channel_id=1, source_target_pairs={{0,2},{1,3},{2,0},{3,1},{4,6},{5,7},{6,4},{7,5},{8,10},{9,11},{10,... | collective-permute-start | bytes 589832 | tf_op jit(solution)/shard_map/ppermute | solution.py:547
  203.3 2.5 collective-permute-start.6
  205.8 1.7 all-to-all-done.5
  209.4 12.8 %all-to-all-start.6 = ((bf16[64,2,768]{2,1,0:T(2,128)(2,1)}), bf16[64,2,768]{2,1,0:T(2,128)(2,1)S(1)}, u32[]{:S(2)}, u32[]{:S(2)}) async-start(bf16[64,2,768]{2,1,0:T(2,128)(2,1)} %broadcast_in_dim.8), calls=%async_computation.6 | async-start | bytes 393216 | tf_op jit(solution)/shard_map/all_to_all | solution.py:50
  223.3 2.8 %collective-permute-start.7 = (bf16[64,1536]{1,0:T(8,128)(2,1)S(1)}, bf16[64,1536]{1,0:T(8,128)(2,1)S(1)}, u32[]{:S(2)}, u32[]{:S(2)}) collective-permute-start(bf16[64,1536]{1,0:T(8,128)(2,1)S(1)} %shard_map.141), channel_id=1, source_target_pairs={{0,1},{1,2},{2,3},{3,0},{4,5},{5,6},{6,7},{7,4},{8,9},{9,10},{10,1... | collective-permute-start | bytes 589832 | tf_op jit(solution)/shard_map/ppermute | solution.py:551
  226.0 3.4 %collective-permute-start.8 = (bf16[64,1536]{1,0:T(8,128)(2,1)S(1)}, bf16[64,1536]{1,0:T(8,128)(2,1)S(1)}, u32[]{:S(2)}, u32[]{:S(2)}) collective-permute-start(bf16[64,1536]{1,0:T(8,128)(2,1)S(1)} %shard_map.141), channel_id=1, source_target_pairs={{0,2},{1,3},{2,0},{3,1},{4,6},{5,7},{6,4},{7,5},{8,10},{9,11},{10,... | collective-permute-start | bytes 589832 | tf_op jit(solution)/shard_map/ppermute | solution.py:551
  229.5 4.0 %collective-permute-start.9 = (bf16[64,1536]{1,0:T(8,128)(2,1)S(1)}, bf16[64,1536]{1,0:T(8,128)(2,1)S(1)}, u32[]{:S(2)}, u32[]{:S(2)}) collective-permute-start(bf16[64,1536]{1,0:T(8,128)(2,1)S(1)} %shard_map.141), channel_id=1, source_target_pairs={{0,3},{1,0},{2,1},{3,2},{4,7},{5,4},{6,5},{7,6},{8,11},{9,8},{10,9... | collective-permute-start | bytes 589832 | tf_op jit(solution)/shard_map/ppermute | solution.py:551
  235.5 2.7 %collective-permute-done.9 = bf16[64,1536]{1,0:T(8,128)(2,1)S(1)} collective-permute-done((bf16[64,1536]{1,0:T(8,128)(2,1)S(1)}, bf16[64,1536]{1,0:T(8,128)(2,1)S(1)}, u32[]{:S(2)}, u32[]{:S(2)}) %collective-permute-start.9) | collective-permute-done | bytes 196640 | tf_op jit(solution)/shard_map/ppermute | solution.py:551
  238.8 6.4 %collective-permute-start.10 = (bf16[128,768]{1,0:T(8,128)(2,1)S(1)}, bf16[128,768]{1,0:T(8,128)(2,1)S(1)}, u32[]{:S(2)}, u32[]{:S(2)}) collective-permute-start(bf16[128,768]{1,0:T(8,128)(2,1)S(1)} %reshape.53), channel_id=1, source_target_pairs={{0,4},{4,0},{1,5},{5,1},{2,6},{6,2},{3,7},{7,3},{8,12},{12,8},{9,1... | collective-permute-start | bytes 589832 | tf_op jit(solution)/shard_map/ppermute | solution.py:556
  (142 shorter events, 41.7 us)
Async XLA Ops:
  7.2 92.0 %all-gather.2.cloned.1.call-start = ((), (), s32[]{:S(2)}) async-start(), calls=%async_computation.7 | async-start | bytes 2506752 | tf_op jit(solution)/shard_map/all_gather | solution.py:501
  24.7 3.7 %collective-permute-start = (bf16[12,768]{1,0:T(8,128)(2,1)S(1)}, bf16[12,768]{1,0:T(8,128)(2,1)S(1)}, u32[]{:S(2)}, u32[]{:S(2)}) collective-permute-start(bf16[12,768]{1,0:T(8,128)(2,1)S(1)} %get-tuple-element.61), channel_id=1, source_target_pairs={{0,4},{4,0},{1,5},{5,1},{2,6},{6,2},{3,7},{7,3},{8,12},{12,8},{9,1... | collective-permute-start | bytes 55304 | tf_op jit(solution)/shard_map/ppermute | solution.py:505
  61.8 26.5 %all-to-all-start.1 = ((bf16[4,384,768]{2,1,0:T(8,128)(2,1)}), bf16[4,384,768]{2,1,0:T(8,128)(2,1)S(1)}, u32[]{:S(2)}, u32[]{:S(2)}) async-start(bf16[4,384,768]{2,1,0:T(8,128)(2,1)} %broadcast_in_dim.7), calls=%async_computation.1 | async-start | bytes 4718592 | tf_op jit(solution)/shard_map/all_to_all | solution.py:50
  67.0 8.2 %copy-start.23 = (bf16[6,1536]{1,0:T(8,128)(2,1)}, bf16[6,1536]{1,0:T(8,128)(2,1)S(1)}, u32[]{:S(2)}) copy-start(bf16[6,1536]{1,0:T(8,128)(2,1)S(1)} %reshape.44.mod_ref) | copy-start | bytes 55300
  89.8 11.4 %copy-start.8 = (bf16[256,1536]{1,0:T(8,128)(2,1)S(1)}, bf16[256,1536]{1,0:T(8,128)(2,1)}, u32[]{:S(2)}) copy-start(bf16[256,1536]{1,0:T(8,128)(2,1)} %copy-done.7) | copy-start | bytes 2359300
  89.8 11.4 %copy-start.11 = (bf16[64,1536]{1,0:T(8,128)(2,1)S(1)}, bf16[64,1536]{1,0:T(8,128)(2,1)}, u32[]{:S(2)}) copy-start(bf16[64,1536]{1,0:T(8,128)(2,1)} %b_ref.5) | copy-start | bytes 589828
  89.8 11.4 %copy-start.28 = (bf16[256,64]{1,0:T(8,128)(2,1)S(1)}, bf16[256,64]{1,0:T(8,128)(2,1)}, u32[]{:S(2)}) copy-start(bf16[256,64]{1,0:T(8,128)(2,1)} %copy-done.27) | copy-start | bytes 98308
  89.8 17.2 %collective-permute-start.1 = (bf16[1536,768]{1,0:T(8,128)(2,1)}, bf16[1536,768]{1,0:T(8,128)(2,1)}, u32[]{:S(2)}, u32[]{:S(2)}) collective-permute-start(bf16[1536,768]{1,0:T(8,128)(2,1)} %bitcast.34), channel_id=1, source_target_pairs={{0,4},{4,0},{1,5},{5,1},{2,6},{6,2},{3,7},{7,3},{8,12},{12,8},{9,1... | collective-permute-start | bytes 7077896 | tf_op jit(solution)/shard_map/ppermute | solution.py:520
  99.2 11.5 %collective-permute-start.2 = (bf16[1536,768]{1,0:T(8,128)(2,1)}, bf16[1536,768]{1,0:T(8,128)(2,1)S(1)}, u32[]{:S(2)}, u32[]{:S(2)}) collective-permute-start(bf16[1536,768]{1,0:T(8,128)(2,1)} %all-gather.2.cloned.1.call-done.own_ref), channel_id=1, source_target_pairs={{0,4},{4,0},{1,5},{5,1},{2,6},{6,2},{3,7},{7,3},{8,12},{12,8},{9,1... | collective-permute-start | bytes 7077896 | tf_op jit(solution)/shard_map/ppermute | solution.py:521
  113.8 16.6 %all-to-all-start.2 = ((bf16[4,64,1536]{2,1,0:T(8,128)(2,1)}), bf16[4,64,1536]{2,1,0:T(8,128)(2,1)}, u32[]{:S(2)}, u32[]{:S(2)}) async-start(bf16[4,64,1536]{2,1,0:T(8,128)(2,1)} %bitcast.8), calls=%async_computation.2 | async-start | bytes 1572864 | tf_op jit(solution)/shard_map/all_to_all | solution.py:526
  131.1 24.9 %copy-start.32 = (bf16[256,768]{1,0:T(8,128)(2,1)S(1)}, bf16[256,768]{1,0:T(8,128)(2,1)}, u32[]{:S(2)}) copy-start(bf16[256,768]{1,0:T(8,128)(2,1)} %copy-done.31) | copy-start | bytes 1179652
  132.6 23.5 %copy-start.13 = (f32[64,1536]{1,0:T(8,128)}, f32[64,1536]{1,0:T(8,128)S(1)}, u32[]{:S(2)}) copy-start(f32[64,1536]{1,0:T(8,128)S(1)} %get-tuple-element.38.unit_ref) | copy-start | bytes 1179652
  132.6 23.4 %copy-start.6 = (bf16[1536,768]{1,0:T(8,128)(2,1)S(1)}, bf16[1536,768]{1,0:T(8,128)(2,1)}, u32[]{:S(2)}) copy-start(bf16[1536,768]{1,0:T(8,128)(2,1)} %copy-done.4) | copy-start | bytes 7077892
  132.6 23.4 %copy-start.12 = (bf16[64,1536]{1,0:T(8,128)(2,1)S(1)}, bf16[64,1536]{1,0:T(8,128)(2,1)}, u32[]{:S(2)}) copy-start(bf16[64,1536]{1,0:T(8,128)(2,1)} %b_ref.5) | copy-start | bytes 589828
  132.6 23.4 %copy-start.25 = (bf16[6,1536]{1,0:T(8,128)(2,1)S(1)}, bf16[6,1536]{1,0:T(8,128)(2,1)}, u32[]{:S(2)}) copy-start(bf16[6,1536]{1,0:T(8,128)(2,1)} %copy-done.23) | copy-start | bytes 55300
  132.6 23.4 %copy-start.30 = (bf16[256,768]{1,0:T(8,128)(2,1)S(1)}, bf16[256,768]{1,0:T(8,128)(2,1)}, u32[]{:S(2)}) copy-start(bf16[256,768]{1,0:T(8,128)(2,1)} %copy-done.29) | copy-start | bytes 1179652
  156.0 9.2 %copy-start.42 = (bf16[128,256]{1,0:T(8,128)(2,1)S(1)}, bf16[128,256]{1,0:T(8,128)(2,1)}, u32[]{:S(2)}) copy-start(bf16[128,256]{1,0:T(8,128)(2,1)} %copy-done.41) | copy-start | bytes 196612
  161.9 8.3 %all-to-all-start.4 = ((bf16[4,80,256]{2,1,0:T(8,128)(2,1)}), bf16[4,80,256]{2,1,0:T(8,128)(2,1)S(1)}, u32[]{:S(2)}, u32[]{:S(2)}) async-start(bf16[4,80,256]{2,1,0:T(8,128)(2,1)} %copy-done.44), calls=%async_computation.4 | async-start | bytes 327680 | tf_op jit(solution)/shard_map/all_to_all | solution.py:534
  173.3 16.9 %copy-start.2 = (bf16[4,384,768]{2,1,0:T(8,128)(2,1)S(1)}, bf16[4,384,768]{2,1,0:T(8,128)(2,1)}, u32[]{:S(2)}) copy-start(bf16[4,384,768]{2,1,0:T(8,128)(2,1)} %shard_map.131) | copy-start | bytes 7077892
  173.3 16.9 %copy-start.17 = (bf16[256,768]{1,0:T(8,128)(2,1)S(1)}, bf16[256,768]{1,0:T(8,128)(2,1)}, u32[]{:S(2)}) copy-start(bf16[256,768]{1,0:T(8,128)(2,1)} %copy-done.15) | copy-start | bytes 1179652
  174.1 6.8 %collective-permute-start.3 = (bf16[128,768]{1,0:T(8,128)(2,1)S(1)}, bf16[128,768]{1,0:T(8,128)(2,1)S(1)}, u32[]{:S(2)}, u32[]{:S(2)}) collective-permute-start(bf16[128,768]{1,0:T(8,128)(2,1)S(1)} %get-tuple-element.48), channel_id=1, source_target_pairs={{0,4},{4,0},{1,5},{5,1},{2,6},{6,2},{3,7},{7,3},{8,12},{12,8},{9,1... | collective-permute-start | bytes 589832 | tf_op jit(solution)/shard_map/ppermute | solution.py:538
  181.7 25.8 %all-to-all-start.5 = ((bf16[64,2,768]{2,1,0:T(2,128)(2,1)}), bf16[64,2,768]{2,1,0:T(2,128)(2,1)}, u32[]{:S(2)}, u32[]{:S(2)}) async-start(bf16[64,2,768]{2,1,0:T(2,128)(2,1)} %reshape.52), calls=%async_computation.5 | async-start | bytes 393216 | tf_op jit(solution)/shard_map/all_to_all | solution.py:541
  197.1 25.1 %copy-start.14 = (f32[64,1536]{1,0:T(8,128)S(1)}, f32[64,1536]{1,0:T(8,128)}, u32[]{:S(2)}) copy-start(f32[64,1536]{1,0:T(8,128)} %copy-done.13) | copy-start | bytes 1179652
  197.2 25.1 %copy-start.26 = (bf16[6,1536]{1,0:T(8,128)(2,1)S(1)}, bf16[6,1536]{1,0:T(8,128)(2,1)}, u32[]{:S(2)}) copy-start(bf16[6,1536]{1,0:T(8,128)(2,1)} %copy-done.23) | copy-start | bytes 55300
  197.2 25.0 %collective-permute-start.4 = (bf16[64,1536]{1,0:T(8,128)(2,1)S(1)}, bf16[64,1536]{1,0:T(8,128)(2,1)S(1)}, u32[]{:S(2)}, u32[]{:S(2)}) collective-permute-start(bf16[64,1536]{1,0:T(8,128)(2,1)S(1)} %get-tuple-element.58), channel_id=1, source_target_pairs={{0,1},{1,2},{2,3},{3,0},{4,5},{5,6},{6,7},{7,4},{8,9},{9,10},{10,1... | collective-permute-start | bytes 589832 | tf_op jit(solution)/shard_map/ppermute | solution.py:547
  199.6 22.6 %collective-permute-start.5 = (bf16[64,1536]{1,0:T(8,128)(2,1)S(1)}, bf16[64,1536]{1,0:T(8,128)(2,1)S(1)}, u32[]{:S(2)}, u32[]{:S(2)}) collective-permute-start(bf16[64,1536]{1,0:T(8,128)(2,1)S(1)} %get-tuple-element.57), channel_id=1, source_target_pairs={{0,2},{1,3},{2,0},{3,1},{4,6},{5,7},{6,4},{7,5},{8,10},{9,11},{10,... | collective-permute-start | bytes 589832 | tf_op jit(solution)/shard_map/ppermute | solution.py:547
  203.3 19.0 %collective-permute-start.6 = (bf16[64,1536]{1,0:T(8,128)(2,1)S(1)}, bf16[64,1536]{1,0:T(8,128)(2,1)S(1)}, u32[]{:S(2)}, u32[]{:S(2)}) collective-permute-start(bf16[64,1536]{1,0:T(8,128)(2,1)S(1)} %get-tuple-element.56), channel_id=1, source_target_pairs={{0,3},{1,0},{2,1},{3,2},{4,7},{5,4},{6,5},{7,6},{8,11},{9,8},{10,9... | collective-permute-start | bytes 589832 | tf_op jit(solution)/shard_map/ppermute | solution.py:547
  209.4 29.3 %all-to-all-start.6 = ((bf16[64,2,768]{2,1,0:T(2,128)(2,1)}), bf16[64,2,768]{2,1,0:T(2,128)(2,1)S(1)}, u32[]{:S(2)}, u32[]{:S(2)}) async-start(bf16[64,2,768]{2,1,0:T(2,128)(2,1)} %broadcast_in_dim.8), calls=%async_computation.6 | async-start | bytes 393216 | tf_op jit(solution)/shard_map/all_to_all | solution.py:50
  223.3 10.7 %collective-permute-start.7 = (bf16[64,1536]{1,0:T(8,128)(2,1)S(1)}, bf16[64,1536]{1,0:T(8,128)(2,1)S(1)}, u32[]{:S(2)}, u32[]{:S(2)}) collective-permute-start(bf16[64,1536]{1,0:T(8,128)(2,1)S(1)} %shard_map.141), channel_id=1, source_target_pairs={{0,1},{1,2},{2,3},{3,0},{4,5},{5,6},{6,7},{7,4},{8,9},{9,10},{10,1... | collective-permute-start | bytes 589832 | tf_op jit(solution)/shard_map/ppermute | solution.py:551
  226.0 9.4 %collective-permute-start.8 = (bf16[64,1536]{1,0:T(8,128)(2,1)S(1)}, bf16[64,1536]{1,0:T(8,128)(2,1)S(1)}, u32[]{:S(2)}, u32[]{:S(2)}) collective-permute-start(bf16[64,1536]{1,0:T(8,128)(2,1)S(1)} %shard_map.141), channel_id=1, source_target_pairs={{0,2},{1,3},{2,0},{3,1},{4,6},{5,7},{6,4},{7,5},{8,10},{9,11},{10,... | collective-permute-start | bytes 589832 | tf_op jit(solution)/shard_map/ppermute | solution.py:551
  229.5 8.7 %collective-permute-start.9 = (bf16[64,1536]{1,0:T(8,128)(2,1)S(1)}, bf16[64,1536]{1,0:T(8,128)(2,1)S(1)}, u32[]{:S(2)}, u32[]{:S(2)}) collective-permute-start(bf16[64,1536]{1,0:T(8,128)(2,1)S(1)} %shard_map.141), channel_id=1, source_target_pairs={{0,3},{1,0},{2,1},{3,2},{4,7},{5,4},{6,5},{7,6},{8,11},{9,8},{10,9... | collective-permute-start | bytes 589832 | tf_op jit(solution)/shard_map/ppermute | solution.py:551
  238.8 7.5 %collective-permute-start.10 = (bf16[128,768]{1,0:T(8,128)(2,1)S(1)}, bf16[128,768]{1,0:T(8,128)(2,1)S(1)}, u32[]{:S(2)}, u32[]{:S(2)}) collective-permute-start(bf16[128,768]{1,0:T(8,128)(2,1)S(1)} %reshape.53), channel_id=1, source_target_pairs={{0,4},{4,0},{1,5},{5,1},{2,6},{6,2},{3,7},{7,3},{8,12},{12,8},{9,1... | collective-permute-start | bytes 589832 | tf_op jit(solution)/shard_map/ppermute | solution.py:556
  (34 other events, 78.2 us)
Sparse Core Ops, SparseCore 0:
  24.1 65.6 all-gather.1

commit v15 on v14

--- a/solution.py
+++ b/solution.py
@@ -337,30 +337,12 @@
     )(ints, got, unit, x_own, t_own, mod, own, other, factor, s_own, s_other)
 
 
-def factor_kernel(split_ref, do_ref, dt_ref, own_ref, other_ref):
-    own_ref[...] = product(split_ref[...], do_ref[...])
-    other_ref[...] = product(split_ref[...], dt_ref[...])
-
-
-def factor_terms(split, d_own, d_other):
-    lines, rows = split.shape
-    half = d_own.shape[1]
-    return pl.pallas_call(
-        factor_kernel,
-        out_shape=[jax.ShapeDtypeStruct((lines, half), F32)] * 2,
-        compiler_params=params(),
-        cost_estimate=cost(4 * lines * rows * half, 8 * lines * half),
-    )(split, d_own, d_other)
-
-
-def pile_kernel(
-    ints_ref, got_ref, modded_ref, own_ref, other_ref, keep_ref, give_ref, facts_ref
-):
+def pile_kernel(ints_ref, got_ref, modded_ref, split_ref, do_ref, dt_ref, keep_ref, give_ref, facts_ref):
     wins = ints_ref[0]
     core = ints_ref[5]
     groups, lines, rows = got_ref.shape
     rank = lines - NOTE
-    half = own_ref.shape[1]
+    half = do_ref.shape[1]
     gap_first = jnp.zeros((1, rows), F32)
     gap_second = jnp.zeros((1, rows), F32)
     for slot in range(groups):
@@ -387,14 +369,17 @@
     two = second[:, :1]
     near = modded_ref[:, pl.ds(pl.multiple_of(core * half, 128), half)]
     far = modded_ref[:, pl.ds(pl.multiple_of((1 - core) * half, 128), half)]
-    keep_ref[:rank] = one * own_ref[:rank] + two * own_ref[rank:]
+    b_own = product(split_ref[...], do_ref[...])
+    b_other = product(split_ref[...], dt_ref[...])
+    keep_ref[:rank] = one * b_own[:rank] + two * b_own[rank:]
     keep_ref[rank:] = product(dlow, near)
-    give_ref[:rank] = (one * other_ref[:rank] + two * other_ref[rank:]).astype(BF16)
+    give_ref[:rank] = (one * b_other[:rank] + two * b_other[rank:]).astype(BF16)
     give_ref[rank:] = product(dlow, far).astype(BF16)
 
 
-def piles(ints, got, modded, b_own, b_other):
-    lines, half = b_own.shape
+def piles(ints, got, modded, split, d_own, d_other):
+    lines = split.shape[0]
+    half = d_own.shape[1]
     rows = got.shape[2]
     return pl.pallas_call(
         pile_kernel,
@@ -403,10 +388,10 @@
             jax.ShapeDtypeStruct((lines, half), BF16),
             jax.ShapeDtypeStruct((8, rows), F32),
         ],
-        in_specs=[pl.BlockSpec(memory_space=SMEM)] + [pl.BlockSpec(memory_space=pltpu.VMEM)] * 4,
-        compiler_params=params(),
-        cost_estimate=cost(2 * lines * half * rows, 16 * lines * half),
-    )(ints, got, modded, b_own, b_other)
+        in_specs=[pl.BlockSpec(memory_space=SMEM)] + [pl.BlockSpec(memory_space=pltpu.VMEM)] * 5,
+        compiler_params=params(),
+        cost_estimate=cost(6 * lines * half * rows, 16 * lines * half),
+    )(ints, got, modded, split, d_own, d_other)
 
 
 def dm_kernel(order, after_ref, do_ref, dt_ref, dlow_ref, own_ref, other_ref, a_ref, out_ref, total_scr):
@@ -532,8 +517,7 @@
         ints, got_dy, unit, x_own, t_own, mod, down_own, down_other, factor_out, slope_own, slope_other
     )
     got_low = lax.all_to_all(send, "t", 0, 0, tiled=True)
-    b_own, b_other = factor_terms(low_split, d_own, d_other)
-    keep, give, facts = piles(ints, got_low, modded, b_own, b_other)
+    keep, give, facts = piles(ints, got_low, modded, low_split, d_own, d_other)
     losses = facts[0, :1]
     pile = (keep + lax.ppermute(give, "c", SWAP).astype(F32)).astype(BF16)
 

time: 256 us -> 250 us (0.977)
  local copies, waits for them, and re-layouts: 32.1 us -> 24.4 us
  blocking collectives: 70.4 us -> 77.7 us
  starting transfers between devices: 78.3 us -> 75.1 us
    unnamed x99 -> x87, local copies, waits for them, and re-layouts: 21.3 us -> 13.7 us
    all_to_all x0 -> x1, blocking collectives: none -> 7.36 us  [per_device(): got_low = lax.all_to_all(send, 't', 0, 0, tiled=True)]
    all_to_all x1 -> x0, starting transfers between devices: 3.34 us -> none  [per_device(): got_low = lax.all_to_all(send, 't', 0, 0, tiled=True)]
  transfers between devices with their start and end apart: 17 -> 16, of which waited for: 10 -> 9; matrix products, arithmetic and copies ran while one was open for 4% -> 4% of each run, Pallas kernels for 8% -> 8%
where the time goes in v15:
time: 250 us; the launch traced here: 248 us
  blocking collectives  77.7 us (31%)
  starting transfers between devices  75.1 us (30%)
  Pallas kernels  28.4 us (11%)
  waiting for transfers between devices  24.5 us (10%)
  local copies, waits for them, and re-layouts  24.4 us (10%)
  between operations  16.1 us (6%)
    all_gather x1, blocking collectives, per_device(): line = lax.all_gather(pair, 'z', axis=0, tiled=True)  31.9 us
    all_to_all x1, blocking collectives, per_device(): got_dy = lax.all_to_all(send, 't', 0, 0, tiled=True)  23.4 us
    all_to_all x2, starting transfers between devices, spread(): lax.all_to_all(jnp.broadcast_to(value[None], (n, *value.shape)), axes, 0,...  16.6 us
    all_to_all x1, blocking collectives, per_device(): near = lax.all_to_all(sent, ('x', 'c'), 0, 0, tiled=True)  15.2 us
    unnamed x87, local copies, waits for them, and re-layouts  13.7 us
    all_to_all x2, waiting for transfers between devices, spread(): lax.all_to_all(jnp.broadcast_to(value[None], (n, *value.shape)), axes, 0,...  10.4 us
    ppermute x3, starting transfers between devices, per_device(): lax.ppermute(grad_block, 't', turns[step])  9.96 us
    ppermute x1, starting transfers between devices, per_device(): up_other = lax.ppermute(up_own, 'c', SWAP)  9.39 us
  transfers between devices with their start and end apart: 16, of which 9 were waited for; matrix products, arithmetic and copies ran while one was open for 4% of the time, Pallas kernels for 8%

profile of v15, /device:TPU:1, one launch (start us, length us, event | category | flops | bytes accessed | tf_op | source)
XLA Modules:
  0.0 248.5 jit_solution(7201432118844775021)
XLA Ops:
  8.1 15.2 %all_to_all.35 = bf16[8,12,768]{2,1,0:T(8,128)(2,1)S(1)} all-to-all(bf16[8,12,768]{2,1,0:T(8,128)(2,1)S(1)} %bitcast.42), channel_id=1, replica_groups=mesh['z'=16,'x'=4,'c'=2,'t'=4] {'x','c'}, dimensions={0} | all-to-all | bytes 294912 | tf_op jit(solution)/shard_map/all_to_all | solution.py:485
  24.7 2.8 %collective-permute-start = (bf16[12,768]{1,0:T(8,128)(2,1)S(1)}, bf16[12,768]{1,0:T(8,128)(2,1)S(1)}, u32[]{:S(2)}, u32[]{:S(2)}) collective-permute-start(bf16[12,768]{1,0:T(8,128)(2,1)S(1)} %get-tuple-element.57), channel_id=1, source_target_pairs={{0,4},{4,0},{1,5},{5,1},{2,6},{6,2},{3,7},{7,3},{8,12},{12,8},{9,1... | collective-permute-start | bytes 55304 | tf_op jit(solution)/shard_map/ppermute | solution.py:490
  28.4 31.9 %all_gather.6 = bf16[384,768]{1,0:T(8,128)(2,1)S(1)} all-gather(bf16[24,768]{1,0:T(8,128)(2,1)S(1)} %maximum_select_fusion.1), channel_id=1, replica_groups=mesh['z'=16,'x'=4,'c'=2,'t'=4] {'z'}, dimensions={0}, use_global_device_ids=true | all-gather | bytes 626688 | tf_op jit(solution)/shard_map/all_gather | solution.py:492
  61.8 3.8 %all-to-all-start.1 = ((bf16[4,384,768]{2,1,0:T(8,128)(2,1)}), bf16[4,384,768]{2,1,0:T(8,128)(2,1)S(1)}, u32[]{:S(2)}, u32[]{:S(2)}) async-start(bf16[4,384,768]{2,1,0:T(8,128)(2,1)} %broadcast_in_dim.7), calls=%async_computation.1 | async-start | bytes 4718592 | tf_op jit(solution)/shard_map/all_to_all | solution.py:50
  71.7 3.4 %shard_map.130 = (bf16[256,1536]{1,0:T(8,128)(2,1)S(1)}, bf16[64,1536]{1,0:T(8,128)(2,1)S(1)}) custom-call(bf16[256,1536]{1,0:T(8,128)(2,1)S(1)} %get-tuple-element.25.modded_ref, bf16[64,1536]{1,0:T(8,128)(2,1)S(1)} %bitcast.41), custom_call_target="tpu_custom_call" | custom-call | flops 1509949440 | bytes 3145728 | tf_op jit(solution)/shard_map/pallas_call | solution.py:157
  76.8 1.7 constant_dynamic-slice_fusion
  78.5 9.9 %all-to-all-done.1.refs_0_ = bf16[4,384,768]{2,1,0:T(8,128)(2,1)S(1)} async-done(((bf16[4,384,768]{2,1,0:T(8,128)(2,1)}), bf16[4,384,768]{2,1,0:T(8,128)(2,1)S(1)}, u32[]{:S(2)}, u32[]{:S(2)}) %all-to-all-start.1) | async-done | bytes 2359328 | tf_op jit(solution)/shard_map/all_to_all | solution.py:50
  89.8 9.4 %collective-permute-start.1 = (bf16[1536,768]{1,0:T(8,128)(2,1)}, bf16[1536,768]{1,0:T(8,128)(2,1)}, u32[]{:S(2)}, u32[]{:S(2)}) collective-permute-start(bf16[1536,768]{1,0:T(8,128)(2,1)} %bitcast.34), channel_id=1, source_target_pairs={{0,4},{4,0},{1,5},{5,1},{2,6},{6,2},{3,7},{7,3},{8,12},{12,8},{9,1... | collective-permute-start | bytes 7077896 | tf_op jit(solution)/shard_map/ppermute | solution.py:505
  99.2 1.9 collective-permute-start.2
  102.9 2.6 %shard_map.132 = (bf16[256,768]{1,0:T(8,128)(2,1)S(1)}, bf16[256,768]{1,0:T(8,128)(2,1)S(1)}, bf16[256,768]{1,0:T(8,128)(2,1)S(1)}) custom-call(s32[6]{0:T(128)S(1)} %stack.26.wins_ref.ints_ref, bf16[256,1536]{1,0:T(8,128)(2,1)S(1)} %copy-done.8, bf16[256,64]{1,0:T(8,128)(2,1)S(1)} %copy-done.27, bf16[1536,768]{1,0:T(8,128)(2,1)S(1)} %bitcast.35, ...), custom_call_target="tpu_custom_call" | custom-call | flops 603979776 | bytes 4325376 | tf_op jit(solution)/shard_map/pallas_call | solution.py:190
  107.0 3.7 %shard_map.133 = (bf16[256,768]{1,0:T(8,128)(2,1)S(1)}, bf16[256,768]{1,0:T(8,128)(2,1)S(1)}, bf16[256,768]{1,0:T(8,128)(2,1)S(1)}) custom-call(s32[6]{0:T(128)S(1)} %stack.26.wins_ref.ints_ref, bf16[256,1536]{1,0:T(8,128)(2,1)S(1)} %copy-done.8, bf16[256,64]{1,0:T(8,128)(2,1)S(1)} %copy-done.27, bf16[1536,768]{1,0:T(8,128)(2,1)} %collective-permute-done.1.up_ref.other_ref, ...), custom_call_target="tpu_custom_call" | custom-call | flops 603979776 | bytes 4325376 | tf_op jit(solution)/shard_map/pallas_call | solution.py:190
  110.8 3.0 %shard_map.134 = bf16[256,1536]{1,0:T(8,128)(2,1)} custom-call(bf16[256,768]{1,0:T(8,128)(2,1)S(1)} %get-tuple-element.31.left_ref, bf16[256,768]{1,0:T(8,128)(2,1)S(1)} %get-tuple-element.32.right_ref, bf16[1536,768]{1,0:T(8,128)(2,1)S(1)} %copy-done.3, bf16[1536,768]{1,0:T(8,128)(2,1)S(1)} %collective-permute-done.2.other_ref), custom_call_target="tpu_custom_call" | custom-call | flops 1207959552 | bytes 5505024 | tf_op jit(solution)/shard_map/pallas_call | solution.py:221
  113.8 4.9 %all-to-all-start.2 = ((bf16[4,64,1536]{2,1,0:T(8,128)(2,1)}), bf16[4,64,1536]{2,1,0:T(8,128)(2,1)}, u32[]{:S(2)}, u32[]{:S(2)}) async-start(bf16[4,64,1536]{2,1,0:T(8,128)(2,1)} %bitcast.8), calls=%async_computation.2 | async-start | bytes 1572864 | tf_op jit(solution)/shard_map/all_to_all | solution.py:511
  118.7 1.7 copy-done.5
  122.4 1.9 shard_map.135
  124.2 6.2 %all-to-all-done.2.got_ref = bf16[4,64,1536]{2,1,0:T(8,128)(2,1)} async-done(((bf16[4,64,1536]{2,1,0:T(8,128)(2,1)}), bf16[4,64,1536]{2,1,0:T(8,128)(2,1)}, u32[]{:S(2)}, u32[]{:S(2)}) %all-to-all-start.2) | async-done | bytes 786464 | tf_op jit(solution)/shard_map/all_to_all | solution.py:511
  132.6 23.4 %all_to_all.36.got_ref = bf16[4,128,1536]{2,1,0:T(8,128)(2,1)S(1)} all-to-all(bf16[4,128,1536]{2,1,0:T(8,128)(2,1)S(1)} %get-tuple-element.35), channel_id=1, replica_groups=mesh['z'=16,'x'=4,'c'=2,'t'=4] {'t'}, dimensions={0} | all-to-all | bytes 3145728 | tf_op jit(solution)/shard_map/all_to_all | solution.py:515
  156.1 3.8 %shard_map.137 = (bf16[256,768]{1,0:T(8,128)(2,1)S(1)}, bf16[256,768]{1,0:T(8,128)(2,1)S(1)}, bf16[256,64]{1,0:T(8,128)(2,1)S(1)}, bf16[4,80,256]{2,1,0:T(8,128)(2,1)S(1)}) custom-call(s32[6]{0:T(128)S(1)} %stack.26.wins_ref.ints_ref, bf16[4,128,1536]{2,1,0:T(8,128)(2,1)S(1)} %all_to_all.36.got_ref, f32[64,1536]{1,0:T(8,128)S(1)} %get-tuple-element.36.unit_ref, ...), custom_call_target="tpu_custom_call" | custom-call | flops 1207959552 | bytes 7077888 | tf_op jit(solution)/shard_map/pallas_call | solution.py:320
  159.8 7.4 %all_to_all.37.got_ref = bf16[4,80,256]{2,1,0:T(8,128)(2,1)S(1)} all-to-all(bf16[4,80,256]{2,1,0:T(8,128)(2,1)S(1)} %get-tuple-element.39), channel_id=1, replica_groups=mesh['z'=16,'x'=4,'c'=2,'t'=4] {'t'}, dimensions={0} | all-to-all | bytes 327680 | tf_op jit(solution)/shard_map/all_to_all | solution.py:519
  168.1 5.6 %collective-permute-start.3 = (bf16[128,768]{1,0:T(8,128)(2,1)S(1)}, bf16[128,768]{1,0:T(8,128)(2,1)S(1)}, u32[]{:S(2)}, u32[]{:S(2)}) collective-permute-start(bf16[128,768]{1,0:T(8,128)(2,1)S(1)} %get-tuple-element.44), channel_id=1, source_target_pairs={{0,4},{4,0},{1,5},{5,1},{2,6},{6,2},{3,7},{7,3},{8,12},{12,8},{9,1... | collective-permute-start | bytes 589832 | tf_op jit(solution)/shard_map/ppermute | solution.py:522
  175.6 8.5 %all-to-all-start.5 = ((bf16[64,2,768]{2,1,0:T(2,128)(2,1)}), bf16[64,2,768]{2,1,0:T(2,128)(2,1)}, u32[]{:S(2)}, u32[]{:S(2)}) async-start(bf16[64,2,768]{2,1,0:T(2,128)(2,1)} %reshape.52), calls=%async_computation.5 | async-start | bytes 393216 | tf_op jit(solution)/shard_map/all_to_all | solution.py:525
  185.9 5.1 %shard_map.139 = bf16[256,1536]{1,0:T(8,128)(2,1)S(1)} custom-call(bf16[128,768]{1,0:T(8,128)(2,1)S(1)} %add_convert_fusion.after_ref, bf16[256,768]{1,0:T(8,128)(2,1)S(1)} %get-tuple-element.40.do_ref, bf16[256,768]{1,0:T(8,128)(2,1)S(1)} %copy-done.16, bf16[256,64]{1,0:T(8,128)(2,1)S(1)} %copy-done.40, bf16[1536,768]{1,0:T(8,128)(2,1)S(1)} %bitcast.36, ...), custom_call_target="tpu_custom_call" | custom-call | flops 1207959552 | bytes 5505024 | tf_op jit(solution)/shard_map/pallas_call | solution.py:418
  191.1 2.3 collective-permute-start.4
  193.4 3.7 %collective-permute-start.5 = (bf16[64,1536]{1,0:T(8,128)(2,1)S(1)}, bf16[64,1536]{1,0:T(8,128)(2,1)S(1)}, u32[]{:S(2)}, u32[]{:S(2)}) collective-permute-start(bf16[64,1536]{1,0:T(8,128)(2,1)S(1)} %get-tuple-element.53), channel_id=1, source_target_pairs={{0,2},{1,3},{2,0},{3,1},{4,6},{5,7},{6,4},{7,5},{8,10},{9,11},{10,... | collective-permute-start | bytes 589832 | tf_op jit(solution)/shard_map/ppermute | solution.py:531
  197.1 2.7 %collective-permute-start.6 = (bf16[64,1536]{1,0:T(8,128)(2,1)S(1)}, bf16[64,1536]{1,0:T(8,128)(2,1)S(1)}, u32[]{:S(2)}, u32[]{:S(2)}) collective-permute-start(bf16[64,1536]{1,0:T(8,128)(2,1)S(1)} %get-tuple-element.52), channel_id=1, source_target_pairs={{0,3},{1,0},{2,1},{3,2},{4,7},{5,4},{6,5},{7,6},{8,11},{9,8},{10,9... | collective-permute-start | bytes 589832 | tf_op jit(solution)/shard_map/ppermute | solution.py:531
  199.8 1.7 all-to-all-done.5
  203.4 12.8 %all-to-all-start.6 = ((bf16[64,2,768]{2,1,0:T(2,128)(2,1)}), bf16[64,2,768]{2,1,0:T(2,128)(2,1)S(1)}, u32[]{:S(2)}, u32[]{:S(2)}) async-start(bf16[64,2,768]{2,1,0:T(2,128)(2,1)} %broadcast_in_dim.8), calls=%async_computation.6 | async-start | bytes 393216 | tf_op jit(solution)/shard_map/all_to_all | solution.py:50
  217.3 2.6 %collective-permute-start.7 = (bf16[64,1536]{1,0:T(8,128)(2,1)S(1)}, bf16[64,1536]{1,0:T(8,128)(2,1)S(1)}, u32[]{:S(2)}, u32[]{:S(2)}) collective-permute-start(bf16[64,1536]{1,0:T(8,128)(2,1)S(1)} %shard_map.140), channel_id=1, source_target_pairs={{0,1},{1,2},{2,3},{3,0},{4,5},{5,6},{6,7},{7,4},{8,9},{9,10},{10,1... | collective-permute-start | bytes 589832 | tf_op jit(solution)/shard_map/ppermute | solution.py:535
  219.9 3.4 %collective-permute-start.8 = (bf16[64,1536]{1,0:T(8,128)(2,1)S(1)}, bf16[64,1536]{1,0:T(8,128)(2,1)S(1)}, u32[]{:S(2)}, u32[]{:S(2)}) collective-permute-start(bf16[64,1536]{1,0:T(8,128)(2,1)S(1)} %shard_map.140), channel_id=1, source_target_pairs={{0,2},{1,3},{2,0},{3,1},{4,6},{5,7},{6,4},{7,5},{8,10},{9,11},{10,... | collective-permute-start | bytes 589832 | tf_op jit(solution)/shard_map/ppermute | solution.py:535
  223.3 4.0 %collective-permute-start.9 = (bf16[64,1536]{1,0:T(8,128)(2,1)S(1)}, bf16[64,1536]{1,0:T(8,128)(2,1)S(1)}, u32[]{:S(2)}, u32[]{:S(2)}) collective-permute-start(bf16[64,1536]{1,0:T(8,128)(2,1)S(1)} %shard_map.140), channel_id=1, source_target_pairs={{0,3},{1,0},{2,1},{3,2},{4,7},{5,4},{6,5},{7,6},{8,11},{9,8},{10,9... | collective-permute-start | bytes 589832 | tf_op jit(solution)/shard_map/ppermute | solution.py:535
  229.3 2.8 %collective-permute-done.9 = bf16[64,1536]{1,0:T(8,128)(2,1)S(1)} collective-permute-done((bf16[64,1536]{1,0:T(8,128)(2,1)S(1)}, bf16[64,1536]{1,0:T(8,128)(2,1)S(1)}, u32[]{:S(2)}, u32[]{:S(2)}) %collective-permute-start.9) | collective-permute-done | bytes 196640 | tf_op jit(solution)/shard_map/ppermute | solution.py:535
  232.9 6.6 %collective-permute-start.10 = (bf16[128,768]{1,0:T(8,128)(2,1)S(1)}, bf16[128,768]{1,0:T(8,128)(2,1)S(1)}, u32[]{:S(2)}, u32[]{:S(2)}) collective-permute-start(bf16[128,768]{1,0:T(8,128)(2,1)S(1)} %reshape.53), channel_id=1, source_target_pairs={{0,4},{4,0},{1,5},{5,1},{2,6},{6,2},{3,7},{7,3},{8,12},{12,8},{9,1... | collective-permute-start | bytes 589832 | tf_op jit(solution)/shard_map/ppermute | solution.py:540
  (128 shorter events, 32.3 us)
Async XLA Ops:
  7.2 92.1 %all-gather.2.cloned.1.call-start = ((), (), s32[]{:S(2)}) async-start(), calls=%async_computation.7 | async-start | bytes 2506752 | tf_op jit(solution)/shard_map/all_gather | solution.py:486
  24.7 3.7 %collective-permute-start = (bf16[12,768]{1,0:T(8,128)(2,1)S(1)}, bf16[12,768]{1,0:T(8,128)(2,1)S(1)}, u32[]{:S(2)}, u32[]{:S(2)}) collective-permute-start(bf16[12,768]{1,0:T(8,128)(2,1)S(1)} %get-tuple-element.57), channel_id=1, source_target_pairs={{0,4},{4,0},{1,5},{5,1},{2,6},{6,2},{3,7},{7,3},{8,12},{12,8},{9,1... | collective-permute-start | bytes 55304 | tf_op jit(solution)/shard_map/ppermute | solution.py:490
  61.8 26.5 %all-to-all-start.1 = ((bf16[4,384,768]{2,1,0:T(8,128)(2,1)}), bf16[4,384,768]{2,1,0:T(8,128)(2,1)S(1)}, u32[]{:S(2)}, u32[]{:S(2)}) async-start(bf16[4,384,768]{2,1,0:T(8,128)(2,1)} %broadcast_in_dim.7), calls=%async_computation.1 | async-start | bytes 4718592 | tf_op jit(solution)/shard_map/all_to_all | solution.py:50
  89.8 11.4 %copy-start.8 = (bf16[256,1536]{1,0:T(8,128)(2,1)S(1)}, bf16[256,1536]{1,0:T(8,128)(2,1)}, u32[]{:S(2)}) copy-start(bf16[256,1536]{1,0:T(8,128)(2,1)} %copy-done.7) | copy-start | bytes 2359300
  89.8 11.4 %copy-start.11 = (bf16[64,1536]{1,0:T(8,128)(2,1)S(1)}, bf16[64,1536]{1,0:T(8,128)(2,1)}, u32[]{:S(2)}) copy-start(bf16[64,1536]{1,0:T(8,128)(2,1)} %b_ref.5) | copy-start | bytes 589828
  89.8 11.4 %copy-start.27 = (bf16[256,64]{1,0:T(8,128)(2,1)S(1)}, bf16[256,64]{1,0:T(8,128)(2,1)}, u32[]{:S(2)}) copy-start(bf16[256,64]{1,0:T(8,128)(2,1)} %copy-done.26) | copy-start | bytes 98308
  89.8 17.2 %collective-permute-start.1 = (bf16[1536,768]{1,0:T(8,128)(2,1)}, bf16[1536,768]{1,0:T(8,128)(2,1)}, u32[]{:S(2)}, u32[]{:S(2)}) collective-permute-start(bf16[1536,768]{1,0:T(8,128)(2,1)} %bitcast.34), channel_id=1, source_target_pairs={{0,4},{4,0},{1,5},{5,1},{2,6},{6,2},{3,7},{7,3},{8,12},{12,8},{9,1... | collective-permute-start | bytes 7077896 | tf_op jit(solution)/shard_map/ppermute | solution.py:505
  99.2 11.5 %collective-permute-start.2 = (bf16[1536,768]{1,0:T(8,128)(2,1)}, bf16[1536,768]{1,0:T(8,128)(2,1)S(1)}, u32[]{:S(2)}, u32[]{:S(2)}) collective-permute-start(bf16[1536,768]{1,0:T(8,128)(2,1)} %all-gather.2.cloned.1.call-done.own_ref), channel_id=1, source_target_pairs={{0,4},{4,0},{1,5},{5,1},{2,6},{6,2},{3,7},{7,3},{8,12},{12,8},{9,1... | collective-permute-start | bytes 7077896 | tf_op jit(solution)/shard_map/ppermute | solution.py:506
  113.8 16.6 %all-to-all-start.2 = ((bf16[4,64,1536]{2,1,0:T(8,128)(2,1)}), bf16[4,64,1536]{2,1,0:T(8,128)(2,1)}, u32[]{:S(2)}, u32[]{:S(2)}) async-start(bf16[4,64,1536]{2,1,0:T(8,128)(2,1)} %bitcast.8), calls=%async_computation.2 | async-start | bytes 1572864 | tf_op jit(solution)/shard_map/all_to_all | solution.py:511
  131.1 24.9 %copy-start.31 = (bf16[256,768]{1,0:T(8,128)(2,1)S(1)}, bf16[256,768]{1,0:T(8,128)(2,1)}, u32[]{:S(2)}) copy-start(bf16[256,768]{1,0:T(8,128)(2,1)} %copy-done.30) | copy-start | bytes 1179652
  132.6 23.4 %copy-start.13 = (f32[64,1536]{1,0:T(8,128)}, f32[64,1536]{1,0:T(8,128)S(1)}, u32[]{:S(2)}) copy-start(f32[64,1536]{1,0:T(8,128)S(1)} %get-tuple-element.36.unit_ref) | copy-start | bytes 1179652
  132.6 23.4 %copy-start.6 = (bf16[1536,768]{1,0:T(8,128)(2,1)S(1)}, bf16[1536,768]{1,0:T(8,128)(2,1)}, u32[]{:S(2)}) copy-start(bf16[1536,768]{1,0:T(8,128)(2,1)} %copy-done.4) | copy-start | bytes 7077892
  132.6 23.4 %copy-start.12 = (bf16[64,1536]{1,0:T(8,128)(2,1)S(1)}, bf16[64,1536]{1,0:T(8,128)(2,1)}, u32[]{:S(2)}) copy-start(bf16[64,1536]{1,0:T(8,128)(2,1)} %b_ref.5) | copy-start | bytes 589828
  132.6 23.4 %copy-start.24 = (bf16[6,1536]{1,0:T(8,128)(2,1)S(1)}, bf16[6,1536]{1,0:T(8,128)(2,1)}, u32[]{:S(2)}) copy-start(bf16[6,1536]{1,0:T(8,128)(2,1)} %copy-done.22) | copy-start | bytes 55300
  132.6 23.4 %copy-start.29 = (bf16[256,768]{1,0:T(8,128)(2,1)S(1)}, bf16[256,768]{1,0:T(8,128)(2,1)}, u32[]{:S(2)}) copy-start(bf16[256,768]{1,0:T(8,128)(2,1)} %copy-done.28) | copy-start | bytes 1179652
  156.0 11.2 %copy-start.21 = (bf16[256,1536]{1,0:T(8,128)(2,1)S(1)}, bf16[256,1536]{1,0:T(8,128)(2,1)}, u32[]{:S(2)}) copy-start(bf16[256,1536]{1,0:T(8,128)(2,1)} %copy-done.20) | copy-start | bytes 2359300
  156.0 11.2 %copy-start.37 = (bf16[128,256]{1,0:T(8,128)(2,1)S(1)}, bf16[128,256]{1,0:T(8,128)(2,1)}, u32[]{:S(2)}) copy-start(bf16[128,256]{1,0:T(8,128)(2,1)} %copy-done.36) | copy-start | bytes 196612
  159.8 14.9 %copy-start.15 = (bf16[256,768]{1,0:T(8,128)(2,1)}, bf16[256,768]{1,0:T(8,128)(2,1)S(1)}, u32[]{:S(2)}) copy-start(bf16[256,768]{1,0:T(8,128)(2,1)S(1)} %get-tuple-element.41.dt_ref) | copy-start | bytes 1179652
  159.8 14.9 %copy-start.39 = (bf16[256,64]{1,0:T(8,128)(2,1)}, bf16[256,64]{1,0:T(8,128)(2,1)S(1)}, u32[]{:S(2)}) copy-start(bf16[256,64]{1,0:T(8,128)(2,1)S(1)} %get-tuple-element.45.dlow_ref) | copy-start | bytes 98308
  167.2 16.9 %copy-start.2 = (bf16[4,384,768]{2,1,0:T(8,128)(2,1)S(1)}, bf16[4,384,768]{2,1,0:T(8,128)(2,1)}, u32[]{:S(2)}) copy-start(bf16[4,384,768]{2,1,0:T(8,128)(2,1)} %shard_map.131) | copy-start | bytes 7077892
  168.1 6.6 %collective-permute-start.3 = (bf16[128,768]{1,0:T(8,128)(2,1)S(1)}, bf16[128,768]{1,0:T(8,128)(2,1)S(1)}, u32[]{:S(2)}, u32[]{:S(2)}) collective-permute-start(bf16[128,768]{1,0:T(8,128)(2,1)S(1)} %get-tuple-element.44), channel_id=1, source_target_pairs={{0,4},{4,0},{1,5},{5,1},{2,6},{6,2},{3,7},{7,3},{8,12},{12,8},{9,1... | collective-permute-start | bytes 589832 | tf_op jit(solution)/shard_map/ppermute | solution.py:522
  175.6 26.0 %all-to-all-start.5 = ((bf16[64,2,768]{2,1,0:T(2,128)(2,1)}), bf16[64,2,768]{2,1,0:T(2,128)(2,1)}, u32[]{:S(2)}, u32[]{:S(2)}) async-start(bf16[64,2,768]{2,1,0:T(2,128)(2,1)} %reshape.52), calls=%async_computation.5 | async-start | bytes 393216 | tf_op jit(solution)/shard_map/all_to_all | solution.py:525
  191.0 25.3 %copy-start.14 = (f32[64,1536]{1,0:T(8,128)S(1)}, f32[64,1536]{1,0:T(8,128)}, u32[]{:S(2)}) copy-start(f32[64,1536]{1,0:T(8,128)} %copy-done.13) | copy-start | bytes 1179652
  191.0 25.3 %copy-start.25 = (bf16[6,1536]{1,0:T(8,128)(2,1)S(1)}, bf16[6,1536]{1,0:T(8,128)(2,1)}, u32[]{:S(2)}) copy-start(bf16[6,1536]{1,0:T(8,128)(2,1)} %copy-done.22) | copy-start | bytes 55300
  191.1 25.2 %collective-permute-start.4 = (bf16[64,1536]{1,0:T(8,128)(2,1)S(1)}, bf16[64,1536]{1,0:T(8,128)(2,1)S(1)}, u32[]{:S(2)}, u32[]{:S(2)}) collective-permute-start(bf16[64,1536]{1,0:T(8,128)(2,1)S(1)} %get-tuple-element.54), channel_id=1, source_target_pairs={{0,1},{1,2},{2,3},{3,0},{4,5},{5,6},{6,7},{7,4},{8,9},{9,10},{10,1... | collective-permute-start | bytes 589832 | tf_op jit(solution)/shard_map/ppermute | solution.py:531
  193.4 22.8 %collective-permute-start.5 = (bf16[64,1536]{1,0:T(8,128)(2,1)S(1)}, bf16[64,1536]{1,0:T(8,128)(2,1)S(1)}, u32[]{:S(2)}, u32[]{:S(2)}) collective-permute-start(bf16[64,1536]{1,0:T(8,128)(2,1)S(1)} %get-tuple-element.53), channel_id=1, source_target_pairs={{0,2},{1,3},{2,0},{3,1},{4,6},{5,7},{6,4},{7,5},{8,10},{9,11},{10,... | collective-permute-start | bytes 589832 | tf_op jit(solution)/shard_map/ppermute | solution.py:531
  197.1 19.1 %collective-permute-start.6 = (bf16[64,1536]{1,0:T(8,128)(2,1)S(1)}, bf16[64,1536]{1,0:T(8,128)(2,1)S(1)}, u32[]{:S(2)}, u32[]{:S(2)}) collective-permute-start(bf16[64,1536]{1,0:T(8,128)(2,1)S(1)} %get-tuple-element.52), channel_id=1, source_target_pairs={{0,3},{1,0},{2,1},{3,2},{4,7},{5,4},{6,5},{7,6},{8,11},{9,8},{10,9... | collective-permute-start | bytes 589832 | tf_op jit(solution)/shard_map/ppermute | solution.py:531
  203.4 29.4 %all-to-all-start.6 = ((bf16[64,2,768]{2,1,0:T(2,128)(2,1)}), bf16[64,2,768]{2,1,0:T(2,128)(2,1)S(1)}, u32[]{:S(2)}, u32[]{:S(2)}) async-start(bf16[64,2,768]{2,1,0:T(2,128)(2,1)} %broadcast_in_dim.8), calls=%async_computation.6 | async-start | bytes 393216 | tf_op jit(solution)/shard_map/all_to_all | solution.py:50
  217.3 10.6 %collective-permute-start.7 = (bf16[64,1536]{1,0:T(8,128)(2,1)S(1)}, bf16[64,1536]{1,0:T(8,128)(2,1)S(1)}, u32[]{:S(2)}, u32[]{:S(2)}) collective-permute-start(bf16[64,1536]{1,0:T(8,128)(2,1)S(1)} %shard_map.140), channel_id=1, source_target_pairs={{0,1},{1,2},{2,3},{3,0},{4,5},{5,6},{6,7},{7,4},{8,9},{9,10},{10,1... | collective-permute-start | bytes 589832 | tf_op jit(solution)/shard_map/ppermute | solution.py:535
  219.9 9.4 %collective-permute-start.8 = (bf16[64,1536]{1,0:T(8,128)(2,1)S(1)}, bf16[64,1536]{1,0:T(8,128)(2,1)S(1)}, u32[]{:S(2)}, u32[]{:S(2)}) collective-permute-start(bf16[64,1536]{1,0:T(8,128)(2,1)S(1)} %shard_map.140), channel_id=1, source_target_pairs={{0,2},{1,3},{2,0},{3,1},{4,6},{5,7},{6,4},{7,5},{8,10},{9,11},{10,... | collective-permute-start | bytes 589832 | tf_op jit(solution)/shard_map/ppermute | solution.py:535
  223.3 8.8 %collective-permute-start.9 = (bf16[64,1536]{1,0:T(8,128)(2,1)S(1)}, bf16[64,1536]{1,0:T(8,128)(2,1)S(1)}, u32[]{:S(2)}, u32[]{:S(2)}) collective-permute-start(bf16[64,1536]{1,0:T(8,128)(2,1)S(1)} %shard_map.140), channel_id=1, source_target_pairs={{0,3},{1,0},{2,1},{3,2},{4,7},{5,4},{6,5},{7,6},{8,11},{9,8},{10,9... | collective-permute-start | bytes 589832 | tf_op jit(solution)/shard_map/ppermute | solution.py:535
  232.9 7.7 %collective-permute-start.10 = (bf16[128,768]{1,0:T(8,128)(2,1)S(1)}, bf16[128,768]{1,0:T(8,128)(2,1)S(1)}, u32[]{:S(2)}, u32[]{:S(2)}) collective-permute-start(bf16[128,768]{1,0:T(8,128)(2,1)S(1)} %reshape.53), channel_id=1, source_target_pairs={{0,4},{4,0},{1,5},{5,1},{2,6},{6,2},{3,7},{7,3},{8,12},{12,8},{9,1... | collective-permute-start | bytes 589832 | tf_op jit(solution)/shard_map/ppermute | solution.py:540
  (27 other events, 88.1 us)
Sparse Core Ops, SparseCore 0:
  24.1 66.2 all-gather.1

commit v16 on v13

--- a/solution.py
+++ b/solution.py
@@ -301,30 +301,12 @@
     )(ints, got, unit, x_own, t_own, mod, own, other, factor, s_own, s_other)
 
 
-def factor_kernel(split_ref, do_ref, dt_ref, own_ref, other_ref):
-    own_ref[...] = product(split_ref[...], do_ref[...])
-    other_ref[...] = product(split_ref[...], dt_ref[...])
-
-
-def factor_terms(split, d_own, d_other):
-    lines, rows = split.shape
-    half = d_own.shape[1]
-    return pl.pallas_call(
-        factor_kernel,
-        out_shape=[jax.ShapeDtypeStruct((lines, half), F32)] * 2,
-        compiler_params=params(),
-        cost_estimate=cost(4 * lines * rows * half, 8 * lines * half),
-    )(split, d_own, d_other)
-
-
-def pile_kernel(
-    ints_ref, got_ref, modded_ref, own_ref, other_ref, keep_ref, give_ref, facts_ref
-):
+def pile_kernel(ints_ref, got_ref, modded_ref, split_ref, do_ref, dt_ref, keep_ref, give_ref, facts_ref):
     wins = ints_ref[0]
     core = ints_ref[5]
     groups, lines, rows = got_ref.shape
     rank = lines - NOTE
-    half = own_ref.shape[1]
+    half = do_ref.shape[1]
     gap_first = jnp.zeros((1, rows), F32)
     gap_second = jnp.zeros((1, rows), F32)
     for slot in range(groups):
@@ -351,14 +333,17 @@
     two = second[:, :1]
     near = modded_ref[:, pl.ds(pl.multiple_of(core * half, 128), half)]
     far = modded_ref[:, pl.ds(pl.multiple_of((1 - core) * half, 128), half)]
-    keep_ref[:rank] = one * own_ref[:rank] + two * own_ref[rank:]
+    b_own = product(split_ref[...], do_ref[...])
+    b_other = product(split_ref[...], dt_ref[...])
+    keep_ref[:rank] = one * b_own[:rank] + two * b_own[rank:]
     keep_ref[rank:] = product(dlow, near)
-    give_ref[:rank] = (one * other_ref[:rank] + two * other_ref[rank:]).astype(BF16)
+    give_ref[:rank] = (one * b_other[:rank] + two * b_other[rank:]).astype(BF16)
     give_ref[rank:] = product(dlow, far).astype(BF16)
 
 
-def piles(ints, got, modded, b_own, b_other):
-    lines, half = b_own.shape
+def piles(ints, got, modded, split, d_own, d_other):
+    lines = split.shape[0]
+    half = d_own.shape[1]
     rows = got.shape[2]
     return pl.pallas_call(
         pile_kernel,
@@ -367,10 +352,10 @@
             jax.ShapeDtypeStruct((lines, half), BF16),
             jax.ShapeDtypeStruct((8, rows), F32),
         ],
-        in_specs=[pl.BlockSpec(memory_space=SMEM)] + [pl.BlockSpec(memory_space=pltpu.VMEM)] * 4,
-        compiler_params=params(),
-        cost_estimate=cost(2 * lines * half * rows, 16 * lines * half),
-    )(ints, got, modded, b_own, b_other)
+        in_specs=[pl.BlockSpec(memory_space=SMEM)] + [pl.BlockSpec(memory_space=pltpu.VMEM)] * 5,
+        compiler_params=params(),
+        cost_estimate=cost(6 * lines * half * rows, 16 * lines * half),
+    )(ints, got, modded, split, d_own, d_other)
 
 
 def dm_kernel(after_ref, do_ref, dt_ref, dlow_ref, own_ref, other_ref, a_ref, out_ref):
@@ -484,8 +469,7 @@
         ints, got_dy, unit, x_own, t_own, mod, down_own, down_other, factor_out, slope_own, slope_other
     )
     got_low = lax.all_to_all(send, "t", 0, 0, tiled=True)
-    b_own, b_other = factor_terms(low_split, d_own, d_other)
-    keep, give, facts = piles(ints, got_low, modded, b_own, b_other)
+    keep, give, facts = piles(ints, got_low, modded, low_split, d_own, d_other)
     losses = facts[0, :1]
     pile = (keep + lax.ppermute(give, "c", SWAP).astype(F32)).astype(BF16)
 

time: 249 us -> 248 us (level)
  blocking collectives: 70.4 us -> 77.8 us
  local copies, waits for them, and re-layouts: 32.2 us -> 28.5 us
  waiting for transfers between devices: 32.9 us -> 29.9 us
    all_to_all x0 -> x1, blocking collectives: none -> 7.36 us  [per_device(): got_low = lax.all_to_all(send, 't', 0, 0, tiled=True)]
    unnamed x93 -> x87, local copies, waits for them, and re-layouts: 18.1 us -> 14.3 us
    all_to_all x1 -> x0, starting transfers between devices: 3.34 us -> none  [per_device(): got_low = lax.all_to_all(send, 't', 0, 0, tiled=True)]
  transfers between devices with their start and end apart: 17 -> 16, of which waited for: 9 -> 9; matrix products, arithmetic and copies ran while one was open for 5% -> 5% of each run, Pallas kernels for 6% -> 6%
where the time goes in v16:
time: 248 us; the launch traced here: 246 us
  blocking collectives  77.8 us (31%)
  starting transfers between devices  68.7 us (28%)
  waiting for transfers between devices  29.9 us (12%)
  local copies, waits for them, and re-layouts  28.5 us (11%)
  Pallas kernels  23.8 us (10%)
  between operations  16.1 us (6%)
    all_gather x1, blocking collectives, per_device(): line = lax.all_gather(pair, 'z', axis=0, tiled=True)  31.9 us
    all_to_all x1, blocking collectives, per_device(): got_dy = lax.all_to_all(send, 't', 0, 0, tiled=True)  23.4 us
    all_to_all x1, blocking collectives, per_device(): near = lax.all_to_all(sent, ('x', 'c'), 0, 0, tiled=True)  15.2 us
    all_to_all x2, waiting for transfers between devices, spread(): lax.all_to_all(jnp.broadcast_to(value[None], (n, *value.shape)), axes, 0,...  14.5 us
    all_to_all x2, starting transfers between devices, spread(): lax.all_to_all(jnp.broadcast_to(value[None], (n, *value.shape)), axes, 0,...  14.4 us
    unnamed x87, local copies, waits for them, and re-layouts  14.3 us
    ppermute x3, starting transfers between devices, per_device(): lax.ppermute(grad_block, 't', turns[step])  9.96 us
    ppermute x1, starting transfers between devices, per_device(): up_other = lax.ppermute(up_own, 'c', SWAP)  9.25 us
  transfers between devices with their start and end apart: 16, of which 9 were waited for; matrix products, arithmetic and copies ran while one was open for 5% of the time, Pallas kernels for 6%

profile of v16, /device:TPU:1, one launch (start us, length us, event | category | flops | bytes accessed | tf_op | source)
XLA Modules:
  0.0 246.1 jit_solution(4232491410299118075)
XLA Ops:
  8.1 15.2 %all_to_all.35 = bf16[8,12,768]{2,1,0:T(8,128)(2,1)S(1)} all-to-all(bf16[8,12,768]{2,1,0:T(8,128)(2,1)S(1)} %bitcast.44), channel_id=1, replica_groups=mesh['z'=16,'x'=4,'c'=2,'t'=4] {'x','c'}, dimensions={0} | all-to-all | bytes 294912 | tf_op jit(solution)/shard_map/all_to_all | solution.py:438
  24.7 2.8 %collective-permute-start = (bf16[12,768]{1,0:T(8,128)(2,1)S(1)}, bf16[12,768]{1,0:T(8,128)(2,1)S(1)}, u32[]{:S(2)}, u32[]{:S(2)}) collective-permute-start(bf16[12,768]{1,0:T(8,128)(2,1)S(1)} %get-tuple-element.53), channel_id=1, source_target_pairs={{0,4},{4,0},{1,5},{5,1},{2,6},{6,2},{3,7},{7,3},{8,12},{12,8},{9,1... | collective-permute-start | bytes 55304 | tf_op jit(solution)/shard_map/ppermute | solution.py:443
  28.4 31.9 %all_gather.6 = bf16[384,768]{1,0:T(8,128)(2,1)S(1)} all-gather(bf16[24,768]{1,0:T(8,128)(2,1)S(1)} %maximum_select_fusion.1), channel_id=1, replica_groups=mesh['z'=16,'x'=4,'c'=2,'t'=4] {'z'}, dimensions={0}, use_global_device_ids=true | all-gather | bytes 626688 | tf_op jit(solution)/shard_map/all_gather | solution.py:445
  61.9 3.8 %all-to-all-start.1 = ((bf16[4,384,768]{2,1,0:T(8,128)(2,1)}), bf16[4,384,768]{2,1,0:T(8,128)(2,1)S(1)}, u32[]{:S(2)}, u32[]{:S(2)}) async-start(bf16[4,384,768]{2,1,0:T(8,128)(2,1)} %broadcast_in_dim.7), calls=%async_computation.1 | async-start | bytes 4718592 | tf_op jit(solution)/shard_map/all_to_all | solution.py:50
  72.7 1.7 constant_dynamic-slice_fusion
  74.4 14.0 %all-to-all-done.1.refs_0_ = bf16[4,384,768]{2,1,0:T(8,128)(2,1)S(1)} async-done(((bf16[4,384,768]{2,1,0:T(8,128)(2,1)}), bf16[4,384,768]{2,1,0:T(8,128)(2,1)S(1)}, u32[]{:S(2)}, u32[]{:S(2)}) %all-to-all-start.1) | async-done | bytes 2359328 | tf_op jit(solution)/shard_map/all_to_all | solution.py:50
  89.8 3.4 %copy.20 = bf16[4,16,24,768]{3,2,0,1:T(8,128)(2,1)} copy(bf16[4,16,24,768]{3,2,1,0:T(8,128)(2,1)} %bitcast.43) | data formatting | bytes 4718592 | tf_op jit(solution)/shard_map/reshape | solution.py:456
  93.2 9.3 %collective-permute-start.1 = (bf16[1536,768]{1,0:T(8,128)(2,1)}, bf16[1536,768]{1,0:T(8,128)(2,1)}, u32[]{:S(2)}, u32[]{:S(2)}) collective-permute-start(bf16[1536,768]{1,0:T(8,128)(2,1)} %bitcast.9.up_ref.own_ref), channel_id=1, source_target_pairs={{0,4},{4,0},{1,5},{5,1},{2,6},{6,2},{3,7},{7,3},{8,12},{12,8},{9,1... | collective-permute-start | bytes 7077896 | tf_op jit(solution)/shard_map/ppermute | solution.py:457
  102.5 1.9 collective-permute-start.2
  104.4 3.6 %shard_map.131 = (bf16[256,768]{1,0:T(8,128)(2,1)S(1)}, bf16[256,768]{1,0:T(8,128)(2,1)S(1)}, bf16[256,768]{1,0:T(8,128)(2,1)S(1)}) custom-call(s32[6]{0:T(128)S(1)} %stack.26.wins_ref.ints_ref, bf16[256,1536]{1,0:T(8,128)(2,1)S(1)} %copy-done.5, bf16[256,64]{1,0:T(8,128)(2,1)S(1)} %copy-done.27, bf16[1536,768]{1,0:T(8,128)(2,1)} %bitcast.9.up_ref.own_ref, ...), custom_call_target="tpu_custom_call" | custom-call | flops 603979776 | bytes 4325376 | tf_op jit(solution)/shard_map/pallas_call | solution.py:154
  109.6 3.7 %shard_map.132 = (bf16[256,768]{1,0:T(8,128)(2,1)S(1)}, bf16[256,768]{1,0:T(8,128)(2,1)S(1)}, bf16[256,768]{1,0:T(8,128)(2,1)S(1)}) custom-call(s32[6]{0:T(128)S(1)} %stack.26.wins_ref.ints_ref, bf16[256,1536]{1,0:T(8,128)(2,1)S(1)} %copy-done.5, bf16[256,64]{1,0:T(8,128)(2,1)S(1)} %copy-done.27, bf16[1536,768]{1,0:T(8,128)(2,1)} %collective-permute-done.1.up_ref.other_ref, ...), custom_call_target="tpu_custom_call" | custom-call | flops 603979776 | bytes 4325376 | tf_op jit(solution)/shard_map/pallas_call | solution.py:154
  113.4 1.9 shard_map.133
  116.2 4.9 %all-to-all-start.2 = ((bf16[4,64,1536]{2,1,0:T(8,128)(2,1)}), bf16[4,64,1536]{2,1,0:T(8,128)(2,1)}, u32[]{:S(2)}, u32[]{:S(2)}) async-start(bf16[4,64,1536]{2,1,0:T(8,128)(2,1)} %bitcast.39), calls=%async_computation.2 | async-start | bytes 1572864 | tf_op jit(solution)/shard_map/all_to_all | solution.py:463
  121.1 1.7 copy-done.2
  124.7 1.9 shard_map.134
  127.5 5.3 %all-to-all-done.2.got_ref = bf16[4,64,1536]{2,1,0:T(8,128)(2,1)} async-done(((bf16[4,64,1536]{2,1,0:T(8,128)(2,1)}), bf16[4,64,1536]{2,1,0:T(8,128)(2,1)}, u32[]{:S(2)}, u32[]{:S(2)}) %all-to-all-start.2) | async-done | bytes 786464 | tf_op jit(solution)/shard_map/all_to_all | solution.py:463
  136.1 23.4 %all_to_all.36.got_ref = bf16[4,128,1536]{2,1,0:T(8,128)(2,1)S(1)} all-to-all(bf16[4,128,1536]{2,1,0:T(8,128)(2,1)S(1)} %get-tuple-element.31), channel_id=1, replica_groups=mesh['z'=16,'x'=4,'c'=2,'t'=4] {'t'}, dimensions={0} | all-to-all | bytes 3145728 | tf_op jit(solution)/shard_map/all_to_all | solution.py:467
  159.6 3.8 %shard_map.136 = (bf16[256,768]{1,0:T(8,128)(2,1)S(1)}, bf16[256,768]{1,0:T(8,128)(2,1)S(1)}, bf16[256,64]{1,0:T(8,128)(2,1)S(1)}, bf16[4,80,256]{2,1,0:T(8,128)(2,1)S(1)}) custom-call(s32[6]{0:T(128)S(1)} %stack.26.wins_ref.ints_ref, bf16[4,128,1536]{2,1,0:T(8,128)(2,1)S(1)} %all_to_all.36.got_ref, f32[64,1536]{1,0:T(8,128)S(1)} %get-tuple-element.32.unit_ref, ...), custom_call_target="tpu_custom_call" | custom-call | flops 1207959552 | bytes 7077888 | tf_op jit(solution)/shard_map/pallas_call | solution.py:284
  163.4 7.4 %all_to_all.37.got_ref = bf16[4,80,256]{2,1,0:T(8,128)(2,1)S(1)} all-to-all(bf16[4,80,256]{2,1,0:T(8,128)(2,1)S(1)} %get-tuple-element.35), channel_id=1, replica_groups=mesh['z'=16,'x'=4,'c'=2,'t'=4] {'t'}, dimensions={0} | all-to-all | bytes 327680 | tf_op jit(solution)/shard_map/all_to_all | solution.py:471
  171.6 5.6 %collective-permute-start.3 = (bf16[128,768]{1,0:T(8,128)(2,1)S(1)}, bf16[128,768]{1,0:T(8,128)(2,1)S(1)}, u32[]{:S(2)}, u32[]{:S(2)}) collective-permute-start(bf16[128,768]{1,0:T(8,128)(2,1)S(1)} %get-tuple-element.40), channel_id=1, source_target_pairs={{0,4},{4,0},{1,5},{5,1},{2,6},{6,2},{3,7},{7,3},{8,12},{12,8},{9,1... | collective-permute-start | bytes 589832 | tf_op jit(solution)/shard_map/ppermute | solution.py:474
  179.1 4.6 %all-to-all-start.5 = ((bf16[64,2,768]{2,1,0:T(2,128)(2,1)}), bf16[64,2,768]{2,1,0:T(2,128)(2,1)S(1)}, u32[]{:S(2)}, u32[]{:S(2)}) async-start(bf16[64,2,768]{2,1,0:T(2,128)(2,1)} %reshape.56), calls=%async_computation.5 | async-start | bytes 393216 | tf_op jit(solution)/shard_map/all_to_all | solution.py:477
  185.6 4.1 %shard_map.138 = bf16[256,1536]{1,0:T(8,128)(2,1)S(1)} custom-call(bf16[128,768]{1,0:T(8,128)(2,1)S(1)} %add_convert_fusion.after_ref, bf16[256,768]{1,0:T(8,128)(2,1)S(1)} %copy-done.16, bf16[256,768]{1,0:T(8,128)(2,1)S(1)} %copy-done.18, bf16[256,64]{1,0:T(8,128)(2,1)S(1)} %copy-done.39, bf16[1536,768]{1,0:T(8,128)(2,1)} %bitcast.9.up_ref.own_ref, ...), custom_call_target="tpu_custom_call" | custom-call | flops 1207959552 | bytes 5505024 | tf_op jit(solution)/shard_map/pallas_call | solution.py:372
  189.8 2.3 collective-permute-start.4
  192.2 3.7 %collective-permute-start.5 = (bf16[64,1536]{1,0:T(8,128)(2,1)S(1)}, bf16[64,1536]{1,0:T(8,128)(2,1)S(1)}, u32[]{:S(2)}, u32[]{:S(2)}) collective-permute-start(bf16[64,1536]{1,0:T(8,128)(2,1)S(1)} %get-tuple-element.49), channel_id=1, source_target_pairs={{0,2},{1,3},{2,0},{3,1},{4,6},{5,7},{6,4},{7,5},{8,10},{9,11},{10,... | collective-permute-start | bytes 589832 | tf_op jit(solution)/shard_map/ppermute | solution.py:481
  195.9 2.7 %collective-permute-start.6 = (bf16[64,1536]{1,0:T(8,128)(2,1)S(1)}, bf16[64,1536]{1,0:T(8,128)(2,1)S(1)}, u32[]{:S(2)}, u32[]{:S(2)}) collective-permute-start(bf16[64,1536]{1,0:T(8,128)(2,1)S(1)} %get-tuple-element.48), channel_id=1, source_target_pairs={{0,3},{1,0},{2,1},{3,2},{4,7},{5,4},{6,5},{7,6},{8,11},{9,8},{10,9... | collective-permute-start | bytes 589832 | tf_op jit(solution)/shard_map/ppermute | solution.py:481
  198.6 3.9 %all-to-all-done.5 = bf16[64,2,768]{2,1,0:T(2,128)(2,1)S(1)} async-done(((bf16[64,2,768]{2,1,0:T(2,128)(2,1)}), bf16[64,2,768]{2,1,0:T(2,128)(2,1)S(1)}, u32[]{:S(2)}, u32[]{:S(2)}) %all-to-all-start.5) | async-done | bytes 196640 | tf_op jit(solution)/shard_map/all_to_all | solution.py:477
  203.5 10.7 %all-to-all-start.6 = ((bf16[64,2,768]{2,1,0:T(2,128)(2,1)}), bf16[64,2,768]{2,1,0:T(2,128)(2,1)S(1)}, u32[]{:S(2)}, u32[]{:S(2)}) async-start(bf16[64,2,768]{2,1,0:T(2,128)(2,1)} %broadcast_in_dim.8), calls=%async_computation.6 | async-start | bytes 393216 | tf_op jit(solution)/shard_map/all_to_all | solution.py:50
  215.2 2.6 %collective-permute-start.7 = (bf16[64,1536]{1,0:T(8,128)(2,1)S(1)}, bf16[64,1536]{1,0:T(8,128)(2,1)S(1)}, u32[]{:S(2)}, u32[]{:S(2)}) collective-permute-start(bf16[64,1536]{1,0:T(8,128)(2,1)S(1)} %shard_map.139), channel_id=1, source_target_pairs={{0,1},{1,2},{2,3},{3,0},{4,5},{5,6},{6,7},{7,4},{8,9},{9,10},{10,1... | collective-permute-start | bytes 589832 | tf_op jit(solution)/shard_map/ppermute | solution.py:485
  217.8 3.4 %collective-permute-start.8 = (bf16[64,1536]{1,0:T(8,128)(2,1)S(1)}, bf16[64,1536]{1,0:T(8,128)(2,1)S(1)}, u32[]{:S(2)}, u32[]{:S(2)}) collective-permute-start(bf16[64,1536]{1,0:T(8,128)(2,1)S(1)} %shard_map.139), channel_id=1, source_target_pairs={{0,2},{1,3},{2,0},{3,1},{4,6},{5,7},{6,4},{7,5},{8,10},{9,11},{10,... | collective-permute-start | bytes 589832 | tf_op jit(solution)/shard_map/ppermute | solution.py:485
  221.2 4.0 %collective-permute-start.9 = (bf16[64,1536]{1,0:T(8,128)(2,1)S(1)}, bf16[64,1536]{1,0:T(8,128)(2,1)S(1)}, u32[]{:S(2)}, u32[]{:S(2)}) collective-permute-start(bf16[64,1536]{1,0:T(8,128)(2,1)S(1)} %shard_map.139), channel_id=1, source_target_pairs={{0,3},{1,0},{2,1},{3,2},{4,7},{5,4},{6,5},{7,6},{8,11},{9,8},{10,9... | collective-permute-start | bytes 589832 | tf_op jit(solution)/shard_map/ppermute | solution.py:485
  227.2 2.9 %collective-permute-done.9 = bf16[64,1536]{1,0:T(8,128)(2,1)S(1)} collective-permute-done((bf16[64,1536]{1,0:T(8,128)(2,1)S(1)}, bf16[64,1536]{1,0:T(8,128)(2,1)S(1)}, u32[]{:S(2)}, u32[]{:S(2)}) %collective-permute-start.9) | collective-permute-done | bytes 196640 | tf_op jit(solution)/shard_map/ppermute | solution.py:485
  230.8 6.4 %collective-permute-start.10 = (bf16[128,768]{1,0:T(8,128)(2,1)S(1)}, bf16[128,768]{1,0:T(8,128)(2,1)S(1)}, u32[]{:S(2)}, u32[]{:S(2)}) collective-permute-start(bf16[128,768]{1,0:T(8,128)(2,1)S(1)} %reshape.57), channel_id=1, source_target_pairs={{0,4},{4,0},{1,5},{5,1},{2,6},{6,2},{3,7},{7,3},{8,12},{12,8},{9,1... | collective-permute-start | bytes 589832 | tf_op jit(solution)/shard_map/ppermute | solution.py:490
  (128 shorter events, 31.9 us)
Async XLA Ops:
  7.2 95.3 %all-gather.2.cloned.1.call-start = ((), (), s32[]{:S(2)}) async-start(), calls=%async_computation.7 | async-start | bytes 2506752 | tf_op jit(solution)/shard_map/all_gather | solution.py:439
  24.7 3.7 %collective-permute-start = (bf16[12,768]{1,0:T(8,128)(2,1)S(1)}, bf16[12,768]{1,0:T(8,128)(2,1)S(1)}, u32[]{:S(2)}, u32[]{:S(2)}) collective-permute-start(bf16[12,768]{1,0:T(8,128)(2,1)S(1)} %get-tuple-element.53), channel_id=1, source_target_pairs={{0,4},{4,0},{1,5},{5,1},{2,6},{6,2},{3,7},{7,3},{8,12},{12,8},{9,1... | collective-permute-start | bytes 55304 | tf_op jit(solution)/shard_map/ppermute | solution.py:443
  61.9 26.5 %all-to-all-start.1 = ((bf16[4,384,768]{2,1,0:T(8,128)(2,1)}), bf16[4,384,768]{2,1,0:T(8,128)(2,1)S(1)}, u32[]{:S(2)}, u32[]{:S(2)}) async-start(bf16[4,384,768]{2,1,0:T(8,128)(2,1)} %broadcast_in_dim.7), calls=%async_computation.1 | async-start | bytes 4718592 | tf_op jit(solution)/shard_map/all_to_all | solution.py:50
  67.0 22.8 %copy-start.22 = (bf16[6,1536]{1,0:T(8,128)(2,1)}, bf16[6,1536]{1,0:T(8,128)(2,1)S(1)}, u32[]{:S(2)}) copy-start(bf16[6,1536]{1,0:T(8,128)(2,1)S(1)} %reshape.47.mod_ref) | copy-start | bytes 55300
  89.8 14.6 %copy-start.5 = (bf16[256,1536]{1,0:T(8,128)(2,1)S(1)}, bf16[256,1536]{1,0:T(8,128)(2,1)}, u32[]{:S(2)}) copy-start(bf16[256,1536]{1,0:T(8,128)(2,1)} %copy-done.4) | copy-start | bytes 2359300
  89.8 14.6 %copy-start.11 = (bf16[64,1536]{1,0:T(8,128)(2,1)S(1)}, bf16[64,1536]{1,0:T(8,128)(2,1)}, u32[]{:S(2)}) copy-start(bf16[64,1536]{1,0:T(8,128)(2,1)} %b_ref.5) | copy-start | bytes 589828
  89.8 14.7 %copy-start.27 = (bf16[256,64]{1,0:T(8,128)(2,1)S(1)}, bf16[256,64]{1,0:T(8,128)(2,1)}, u32[]{:S(2)}) copy-start(bf16[256,64]{1,0:T(8,128)(2,1)} %copy-done.26) | copy-start | bytes 98308
  93.2 16.4 %collective-permute-start.1 = (bf16[1536,768]{1,0:T(8,128)(2,1)}, bf16[1536,768]{1,0:T(8,128)(2,1)}, u32[]{:S(2)}, u32[]{:S(2)}) collective-permute-start(bf16[1536,768]{1,0:T(8,128)(2,1)} %bitcast.9.up_ref.own_ref), channel_id=1, source_target_pairs={{0,4},{4,0},{1,5},{5,1},{2,6},{6,2},{3,7},{7,3},{8,12},{12,8},{9,1... | collective-permute-start | bytes 7077896 | tf_op jit(solution)/shard_map/ppermute | solution.py:457
  102.5 10.9 %collective-permute-start.2 = (bf16[1536,768]{1,0:T(8,128)(2,1)}, bf16[1536,768]{1,0:T(8,128)(2,1)S(1)}, u32[]{:S(2)}, u32[]{:S(2)}) collective-permute-start(bf16[1536,768]{1,0:T(8,128)(2,1)} %all-gather.2.cloned.1.call-done.own_ref), channel_id=1, source_target_pairs={{0,4},{4,0},{1,5},{5,1},{2,6},{6,2},{3,7},{7,3},{8,12},{12,8},{9,1... | collective-permute-start | bytes 7077896 | tf_op jit(solution)/shard_map/ppermute | solution.py:458
  116.2 16.6 %all-to-all-start.2 = ((bf16[4,64,1536]{2,1,0:T(8,128)(2,1)}), bf16[4,64,1536]{2,1,0:T(8,128)(2,1)}, u32[]{:S(2)}, u32[]{:S(2)}) async-start(bf16[4,64,1536]{2,1,0:T(8,128)(2,1)} %bitcast.39), calls=%async_computation.2 | async-start | bytes 1572864 | tf_op jit(solution)/shard_map/all_to_all | solution.py:463
  134.6 24.9 %copy-start.31 = (bf16[256,768]{1,0:T(8,128)(2,1)S(1)}, bf16[256,768]{1,0:T(8,128)(2,1)}, u32[]{:S(2)}) copy-start(bf16[256,768]{1,0:T(8,128)(2,1)} %copy-done.30) | copy-start | bytes 1179652
  136.1 23.4 %copy-start.13 = (f32[64,1536]{1,0:T(8,128)}, f32[64,1536]{1,0:T(8,128)S(1)}, u32[]{:S(2)}) copy-start(f32[64,1536]{1,0:T(8,128)S(1)} %get-tuple-element.32.unit_ref) | copy-start | bytes 1179652
  136.1 23.4 %copy-start.3 = (bf16[1536,768]{1,0:T(8,128)(2,1)S(1)}, bf16[1536,768]{1,0:T(8,128)(2,1)}, u32[]{:S(2)}) copy-start(bf16[1536,768]{1,0:T(8,128)(2,1)} %copy-done.1) | copy-start | bytes 7077892
  136.1 23.4 %copy-start.12 = (bf16[64,1536]{1,0:T(8,128)(2,1)S(1)}, bf16[64,1536]{1,0:T(8,128)(2,1)}, u32[]{:S(2)}) copy-start(bf16[64,1536]{1,0:T(8,128)(2,1)} %b_ref.5) | copy-start | bytes 589828
  136.1 23.4 %copy-start.24 = (bf16[6,1536]{1,0:T(8,128)(2,1)S(1)}, bf16[6,1536]{1,0:T(8,128)(2,1)}, u32[]{:S(2)}) copy-start(bf16[6,1536]{1,0:T(8,128)(2,1)} %copy-done.22) | copy-start | bytes 55300
  136.1 23.4 %copy-start.29 = (bf16[256,768]{1,0:T(8,128)(2,1)S(1)}, bf16[256,768]{1,0:T(8,128)(2,1)}, u32[]{:S(2)}) copy-start(bf16[256,768]{1,0:T(8,128)(2,1)} %copy-done.28) | copy-start | bytes 1179652
  163.3 14.9 %copy-start.15 = (bf16[256,768]{1,0:T(8,128)(2,1)}, bf16[256,768]{1,0:T(8,128)(2,1)S(1)}, u32[]{:S(2)}) copy-start(bf16[256,768]{1,0:T(8,128)(2,1)S(1)} %get-tuple-element.36.do_ref) | copy-start | bytes 1179652
  163.3 14.9 %copy-start.17 = (bf16[256,768]{1,0:T(8,128)(2,1)}, bf16[256,768]{1,0:T(8,128)(2,1)S(1)}, u32[]{:S(2)}) copy-start(bf16[256,768]{1,0:T(8,128)(2,1)S(1)} %get-tuple-element.37.dt_ref) | copy-start | bytes 1179652
  163.3 14.9 %copy-start.38 = (bf16[256,64]{1,0:T(8,128)(2,1)}, bf16[256,64]{1,0:T(8,128)(2,1)S(1)}, u32[]{:S(2)}) copy-start(bf16[256,64]{1,0:T(8,128)(2,1)S(1)} %get-tuple-element.41.dlow_ref) | copy-start | bytes 98308
  170.7 13.0 %copy-start.21 = (bf16[1536,64]{0,1:T(8,128)(2,1)S(1)}, bf16[1536,64]{0,1:T(8,128)(2,1)}, u32[]{:S(2)}) copy-start(bf16[1536,64]{0,1:T(8,128)(2,1)} %param.18) | copy-start | bytes 589828
  171.6 6.6 %collective-permute-start.3 = (bf16[128,768]{1,0:T(8,128)(2,1)S(1)}, bf16[128,768]{1,0:T(8,128)(2,1)S(1)}, u32[]{:S(2)}, u32[]{:S(2)}) collective-permute-start(bf16[128,768]{1,0:T(8,128)(2,1)S(1)} %get-tuple-element.40), channel_id=1, source_target_pairs={{0,4},{4,0},{1,5},{5,1},{2,6},{6,2},{3,7},{7,3},{8,12},{12,8},{9,1... | collective-permute-start | bytes 589832 | tf_op jit(solution)/shard_map/ppermute | solution.py:474
  179.1 23.4 %all-to-all-start.5 = ((bf16[64,2,768]{2,1,0:T(2,128)(2,1)}), bf16[64,2,768]{2,1,0:T(2,128)(2,1)S(1)}, u32[]{:S(2)}, u32[]{:S(2)}) async-start(bf16[64,2,768]{2,1,0:T(2,128)(2,1)} %reshape.56), calls=%async_computation.5 | async-start | bytes 393216 | tf_op jit(solution)/shard_map/all_to_all | solution.py:477
  189.7 24.4 %copy-start.14 = (f32[64,1536]{1,0:T(8,128)S(1)}, f32[64,1536]{1,0:T(8,128)}, u32[]{:S(2)}) copy-start(f32[64,1536]{1,0:T(8,128)} %copy-done.13) | copy-start | bytes 1179652
  189.8 24.4 %copy-start.25 = (bf16[6,1536]{1,0:T(8,128)(2,1)S(1)}, bf16[6,1536]{1,0:T(8,128)(2,1)}, u32[]{:S(2)}) copy-start(bf16[6,1536]{1,0:T(8,128)(2,1)} %copy-done.22) | copy-start | bytes 55300
  189.8 24.3 %collective-permute-start.4 = (bf16[64,1536]{1,0:T(8,128)(2,1)S(1)}, bf16[64,1536]{1,0:T(8,128)(2,1)S(1)}, u32[]{:S(2)}, u32[]{:S(2)}) collective-permute-start(bf16[64,1536]{1,0:T(8,128)(2,1)S(1)} %get-tuple-element.50), channel_id=1, source_target_pairs={{0,1},{1,2},{2,3},{3,0},{4,5},{5,6},{6,7},{7,4},{8,9},{9,10},{10,1... | collective-permute-start | bytes 589832 | tf_op jit(solution)/shard_map/ppermute | solution.py:481
  192.2 22.0 %collective-permute-start.5 = (bf16[64,1536]{1,0:T(8,128)(2,1)S(1)}, bf16[64,1536]{1,0:T(8,128)(2,1)S(1)}, u32[]{:S(2)}, u32[]{:S(2)}) collective-permute-start(bf16[64,1536]{1,0:T(8,128)(2,1)S(1)} %get-tuple-element.49), channel_id=1, source_target_pairs={{0,2},{1,3},{2,0},{3,1},{4,6},{5,7},{6,4},{7,5},{8,10},{9,11},{10,... | collective-permute-start | bytes 589832 | tf_op jit(solution)/shard_map/ppermute | solution.py:481
  195.9 18.3 %collective-permute-start.6 = (bf16[64,1536]{1,0:T(8,128)(2,1)S(1)}, bf16[64,1536]{1,0:T(8,128)(2,1)S(1)}, u32[]{:S(2)}, u32[]{:S(2)}) collective-permute-start(bf16[64,1536]{1,0:T(8,128)(2,1)S(1)} %get-tuple-element.48), channel_id=1, source_target_pairs={{0,3},{1,0},{2,1},{3,2},{4,7},{5,4},{6,5},{7,6},{8,11},{9,8},{10,9... | collective-permute-start | bytes 589832 | tf_op jit(solution)/shard_map/ppermute | solution.py:481
  203.5 27.2 %all-to-all-start.6 = ((bf16[64,2,768]{2,1,0:T(2,128)(2,1)}), bf16[64,2,768]{2,1,0:T(2,128)(2,1)S(1)}, u32[]{:S(2)}, u32[]{:S(2)}) async-start(bf16[64,2,768]{2,1,0:T(2,128)(2,1)} %broadcast_in_dim.8), calls=%async_computation.6 | async-start | bytes 393216 | tf_op jit(solution)/shard_map/all_to_all | solution.py:50
  215.2 10.6 %collective-permute-start.7 = (bf16[64,1536]{1,0:T(8,128)(2,1)S(1)}, bf16[64,1536]{1,0:T(8,128)(2,1)S(1)}, u32[]{:S(2)}, u32[]{:S(2)}) collective-permute-start(bf16[64,1536]{1,0:T(8,128)(2,1)S(1)} %shard_map.139), channel_id=1, source_target_pairs={{0,1},{1,2},{2,3},{3,0},{4,5},{5,6},{6,7},{7,4},{8,9},{9,10},{10,1... | collective-permute-start | bytes 589832 | tf_op jit(solution)/shard_map/ppermute | solution.py:485
  217.8 9.4 %collective-permute-start.8 = (bf16[64,1536]{1,0:T(8,128)(2,1)S(1)}, bf16[64,1536]{1,0:T(8,128)(2,1)S(1)}, u32[]{:S(2)}, u32[]{:S(2)}) collective-permute-start(bf16[64,1536]{1,0:T(8,128)(2,1)S(1)} %shard_map.139), channel_id=1, source_target_pairs={{0,2},{1,3},{2,0},{3,1},{4,6},{5,7},{6,4},{7,5},{8,10},{9,11},{10,... | collective-permute-start | bytes 589832 | tf_op jit(solution)/shard_map/ppermute | solution.py:485
  221.2 8.8 %collective-permute-start.9 = (bf16[64,1536]{1,0:T(8,128)(2,1)S(1)}, bf16[64,1536]{1,0:T(8,128)(2,1)S(1)}, u32[]{:S(2)}, u32[]{:S(2)}) collective-permute-start(bf16[64,1536]{1,0:T(8,128)(2,1)S(1)} %shard_map.139), channel_id=1, source_target_pairs={{0,3},{1,0},{2,1},{3,2},{4,7},{5,4},{6,5},{7,6},{8,11},{9,8},{10,9... | collective-permute-start | bytes 589832 | tf_op jit(solution)/shard_map/ppermute | solution.py:485
  230.8 7.4 %collective-permute-start.10 = (bf16[128,768]{1,0:T(8,128)(2,1)S(1)}, bf16[128,768]{1,0:T(8,128)(2,1)S(1)}, u32[]{:S(2)}, u32[]{:S(2)}) collective-permute-start(bf16[128,768]{1,0:T(8,128)(2,1)S(1)} %reshape.57), channel_id=1, source_target_pairs={{0,4},{4,0},{1,5},{5,1},{2,6},{6,2},{3,7},{7,3},{8,12},{12,8},{9,1... | collective-permute-start | bytes 589832 | tf_op jit(solution)/shard_map/ppermute | solution.py:490
  (27 other events, 81.1 us)
Sparse Core Ops, SparseCore 0:
  24.1 66.2 all-gather.1
